TPU v7x, 32 devices: a whole 2x2x4 slice. The times are simulated.
32 devices in a mesh: stream: 4 (over z), girth: 8 (over y, x, core).
Axes of the slice: x: 2, y: 2, z: 4, core: 2. Of those that a mesh axis runs over, the one named last changes fastest.
Arguments:
- velocity: float32 [3, 16, 64, 256], P(None, 'stream', 'girth'), may hold values from -6 to 6
- pressure: float32 [16, 64, 256], P('stream', 'girth'), may hold values from -6 to 6
- kinetic_energy: float32 [16, 64, 256], P('stream', 'girth'), may hold values from 0.01 to 1
- dissipation_rate: float32 [16, 64, 256], P('stream', 'girth'), may hold values from 0.5 to 20
- corner_ids: int32 [128, 1024], replicated, may hold values from 0 to 30462, as said below
- fractions: float32 [3, 128, 1024], replicated, may hold values from 0 to 1
- sector_owner: int32 [64, 1], replicated, may hold values from 0 to 7; in each aligned block of 64 rows (0 to 63, 64 to 127, ...) at most 24 rows name the same one
Outputs:
- new_velocity: float32 [3, 16, 64, 256], P(None, 'stream', 'girth')
- new_energy: float32 [16, 64, 256], P('stream', 'girth')
- new_rate: float32 [16, 64, 256], P('stream', 'girth')
- harmonics: float32 [128, 768], P(('stream', 'girth'))
Inputs may be any that keep to these rules, and one draw needn't show every extreme that they name: `corner_ids`: each entry is s * 8 * 256 + g * 256 + q with s from 0 to 14, g from 0 to 6 and q from 0 to 254. `sector_owner`: sector s covers azimuths s * 16 to (s + 1) * 16 - 1. Every girth index owns at least one sector and at most 24, and some girth index owns exactly 24.
All inputs are finite; a program needn't handle non-finite values.
Results may differ from a plain program's by a relative error of at most 0.000076.
Values sent between devices are 32-bit elements; how exact they have to be, the bound alone decides.
No kernel may reach another device: no remote copies, remote signals or barrier semaphores. Data moves between devices by JAX's collectives and lax.ppermute only.
A program may use at most 192 MiB of HBM per device.

v0:
```python
import math

import jax
import jax.numpy as jnp
from jax import lax
from jax.sharding import PartitionSpec as P

NH = 128


base_viscosity = 0.05
time_step = 0.2
beta_star = 0.09
beta_rate = 0.075
alpha_rate = 0.52
wall_rate = 1.0


def extended_2(shard, sides, width):
    for axis, dim in sides:
        devices, length = (lax.axis_size(axis), shard.shape[dim])
        up = [(i, (i + 1) % devices) for i in range(devices - 1)]
        down = [(j, i) for i, j in up]
        last = lax.slice_in_dim(shard, length - width, length, axis=dim)
        leading = lax.slice_in_dim(shard, 0, width, axis=dim)
        before = lax.ppermute(last, axis, up)
        after = lax.ppermute(leading, axis, down)
        shard = jnp.concatenate([before, shard, after], axis=dim)
    return shard


def shifted(values, offsets):
    extent = values.shape
    return values[
        2 + offsets[0] : extent[0] - 2 + offsets[0],
        2 + offsets[1] : extent[1] - 2 + offsets[1],
        2 + offsets[2] : extent[2] - 2 + offsets[2],
    ]


def offset_of(direction, amount):
    offsets = [0, 0, 0]
    offsets[direction] = amount
    return tuple(offsets)


def derivative(values, direction):
    near_pair = shifted(values, offset_of(direction, 1)) - shifted(values, offset_of(direction, -1))
    far_pair = shifted(values, offset_of(direction, 2)) - shifted(values, offset_of(direction, -2))
    return (8.0 * near_pair - far_pair) / 12.0


def diffusion(values, viscosity, direction):
    center = shifted(values, (0, 0, 0))
    middle = shifted(viscosity, (0, 0, 0))
    upper_face = 0.5 * (middle + shifted(viscosity, offset_of(direction, 1)))
    lower_face = 0.5 * (middle + shifted(viscosity, offset_of(direction, -1)))
    return upper_face * (shifted(values, offset_of(direction, 1)) - center) - lower_face * (
        center - shifted(values, offset_of(direction, -1))
    )


def advance(padded):
    viscosity = base_viscosity + padded[4] / (padded[5] + wall_rate)
    centers = [shifted(padded[component], (0, 0, 0)) for component in range(6)]
    strain = jnp.zeros_like(centers[0])
    updated = []
    for component in range(3):
        change = -derivative(padded[3], component)
        for direction in range(3):
            gradient = derivative(padded[component], direction)
            strain = strain + gradient * gradient
            change = (
                change
                - centers[direction] * gradient
                + diffusion(padded[component], viscosity, direction)
            )
        updated.append(centers[component] + time_step * change)
    eddy_viscosity = centers[4] / (centers[5] + wall_rate)
    energy_change = eddy_viscosity * strain - beta_star * centers[4] * centers[5]
    rate_change = alpha_rate * strain - beta_rate * centers[5] * centers[5]
    for direction in range(3):
        energy_change = (
            energy_change
            - centers[direction] * derivative(padded[4], direction)
            + diffusion(padded[4], viscosity, direction)
        )
        rate_change = (
            rate_change
            - centers[direction] * derivative(padded[5], direction)
            + diffusion(padded[5], viscosity, direction)
        )
    return (
        jnp.stack(updated),
        centers[4] + time_step * energy_change,
        centers[5] + time_step * rate_change,
    )


def side_weight(fraction, upper_side):
    if upper_side:
        return fraction
    return 1.0 - fraction


def sample_points(
    flat_field,
    cell_ids,
    fracs,
    valid_cols,
    stream_first,
    cells_s,
    cells_g,
    cells_r,
    lowest_corner,
    highest_corner,
):
    plane_cells = cells_g * cells_r
    stream_cell = cell_ids // plane_cells
    remainder = cell_ids - stream_cell * plane_cells
    girth_cell = remainder // cells_r
    radial_cell = remainder - girth_cell * cells_r
    local_stream = stream_cell - stream_first
    counted = (local_stream >= lowest_corner) & (local_stream <= highest_corner)
    sampled = jnp.zeros((3,) + cell_ids.shape, jnp.float32)
    for along_s in (0, 1):
        for along_g in (0, 1):
            for along_r in (0, 1):
                weight = (
                    side_weight(fracs[0], along_s)
                    * side_weight(fracs[1], along_g)
                    * side_weight(fracs[2], along_r)
                )
                layer = local_stream + along_s
                inside = (layer >= 0) & (layer < cells_s) & counted & valid_cols[None, :]
                position = (
                    (jnp.clip(layer, 0, cells_s - 1) * cells_g + girth_cell + along_g) * cells_r
                    + radial_cell
                    + along_r
                )
                picked = jnp.take(flat_field, position.reshape(-1), axis=1).reshape(
                    (3,) + cell_ids.shape
                )
                sampled = sampled + jnp.where(inside, weight, 0.0) * picked
    return sampled


def fourier_table(azimuth_list, azimuths, modes):
    orders = lax.broadcasted_iota(jnp.int32, (1, modes), 1)
    phase_index = azimuth_list[:, None] * orders % azimuths
    angles = phase_index.astype(jnp.float32) * (2.0 * math.pi / azimuths)
    normalizer = 1.0 / math.sqrt(azimuths)
    return jnp.concatenate([jnp.cos(angles), -jnp.sin(angles)], axis=1) * normalizer


def body(velocity, pressure, kinetic_energy, dissipation_rate, corner_ids, fractions, sector_owner):
    stacked = jnp.concatenate(
        [velocity, pressure[None], kinetic_energy[None], dissipation_rate[None]], axis=0
    )
    extended = extended_2(stacked, (("stream", 1), ("girth", 2)), 2)
    padded = jnp.pad(extended, ((0, 0), (0, 0), (0, 0), (2, 2)))
    new_velocity, new_energy, new_rate = advance(padded)
    cells_s = velocity.shape[1]
    cells_g = velocity.shape[2]
    cells_r = velocity.shape[3]
    radii = corner_ids.shape[0]
    azimuths = corner_ids.shape[1]
    sectors = sector_owner.shape[0]
    width = azimuths // sectors
    girth_count = lax.axis_size("girth")
    stream_count = lax.axis_size("stream")
    girth_me = lax.axis_index("girth")
    stream_first = lax.axis_index("stream") * cells_s
    owners = sector_owner[:, 0]
    row_count = radii // (stream_count * girth_count)
    flat_field = new_velocity.reshape(3, -1)
    capacity = 3 * sectors // girth_count
    mine = (owners == girth_me).astype(jnp.int32)
    order = jnp.argsort(1 - mine, stable=True)[:capacity]
    live = mine[order]
    cell_ids = corner_ids.reshape(radii, sectors, width)[:, order].reshape(radii, capacity * width)
    fracs = fractions.reshape(3, radii, sectors, width)[:, :, order].reshape(
        3, radii, capacity * width
    )
    valid_cols = jnp.broadcast_to(live[:, None] > 0, (capacity, width)).reshape(-1)
    sector_pos = lax.broadcasted_iota(jnp.int32, (capacity, sectors), 1)
    chooser = ((order[:, None] == sector_pos) & (live[:, None] > 0)).astype(jnp.float32)
    sampled = sample_points(
        flat_field,
        cell_ids,
        fracs,
        valid_cols,
        stream_first,
        cells_s,
        cells_g,
        cells_r,
        -1,
        cells_s - 1,
    )
    spread = jnp.einsum(
        "crkw,ks->crsw",
        sampled.reshape(3, radii, capacity, width),
        chooser,
        precision=lax.Precision.HIGHEST,
    )
    disk = spread.reshape(3, radii, azimuths)
    own_rows = lax.psum_scatter(
        jnp.transpose(disk, (1, 0, 2)).reshape(
            row_count * lax.axis_size(("stream", "girth")), 3 * azimuths
        ),
        ("stream", "girth"),
        scatter_dimension=0,
        tiled=True,
    )
    full_table = fourier_table(lax.broadcasted_iota(jnp.int32, (azimuths,), 0), azimuths, NH)
    harmonics = jnp.dot(
        own_rows.reshape(row_count * 3, azimuths), full_table, precision=lax.Precision.HIGHEST
    ).reshape(row_count, 6 * NH)
    return (new_velocity, new_energy, new_rate, harmonics)


def solution(mesh):
    return jax.shard_map(
        body,
        mesh=mesh,
        in_specs=(
            P(None, "stream", "girth", None),
            P("stream", "girth", None),
            P("stream", "girth", None),
            P("stream", "girth", None),
            P(),
            P(),
            P(),
        ),
        out_specs=(
            P(None, "stream", "girth", None),
            P("stream", "girth", None),
            P("stream", "girth", None),
            P(("stream", "girth"), None),
        ),
        check_vma=False,
    )
```

profile of v0, /device:TPU:0, one launch (start us, length us, event | category | flops | bytes accessed | tf_op | source)
XLA Modules:
  0.0 1828.2 jit_solution(10930063836291134191)
XLA Ops:
  10.2 6.2 collective-permute-start
  18.3 2.0 sort.17
  33.8 3.0 collective-permute-start.2
  47.8 2.9 copy.81
  50.7 179.8 %gather_fusion.10 = f32[49152,3]{1,0:T(8,128)} fusion(f32[3,8192]{0,1:T(8,128)} %copy.81, s32[49152]{0:T(1024)} %get-tuple-element.63), kind=kCustom, calls=%fused_computation.7.clone | custom fusion | bytes 1376256 | tf_op jit(solution)/shard_map/jit(_take)/gather | solution.py:141
  230.5 25.1 %broadcast_select_fusion = f32[49152,3]{1,0:T(8,128)} fusion(f32[49152,3]{1,0:T(8,128)} %gather_fusion.10, pred[49152]{0:T(1024)(128)(4,1)} %get-tuple-element.72), kind=kLoop, calls=%fused_computation.11 | loop fusion | flops 147456 | bytes 1228800 | tf_op jit(solution)/shard_map/jit(_take)/select_n | solution.py:141
  255.8 16.0 copy.103
  271.8 164.1 %gather_fusion.9 = f32[49152,3]{1,0:T(8,128)} fusion(f32[3,8192]{0,1:T(8,128)} %copy.81, s32[49152]{0:T(1024)S(1)} %get-tuple-element.62), kind=kCustom, calls=%fused_computation.6.clone | custom fusion | bytes 1376256 | tf_op jit(solution)/shard_map/jit(_take)/gather | solution.py:141
  435.9 164.0 %gather_fusion.7 = f32[49152,3]{1,0:T(8,128)} fusion(f32[3,8192]{0,1:T(8,128)} %copy.81, s32[49152]{0:T(1024)S(1)} %copy-done.13), kind=kCustom, calls=%fused_computation.4.clone | custom fusion | bytes 1376256 | tf_op jit(solution)/shard_map/jit(_take)/gather | solution.py:141
  599.9 34.4 %broadcast_select_fusion.1 = (f32[49152,3]{1,0:T(8,128)}, f32[49152,3]{1,0:T(8,128)}) fusion(f32[49152,3]{1,0:T(8,128)} %gather_fusion.9, pred[49152]{0:T(1024)(128)(4,1)S(1)} %copy-done.21, f32[49152,3]{1,0:T(8,128)} %gather_fusion.7, pred[49152]{0:T(1024)(128)(4,1)S(1)} %copy-done.22), kind=kLoop, calls=%fused_computation.12 | loop fusion | flops 294912 | bytes 2457600 | tf_op jit(solution)/shard_map/jit(_take)/select_n | solution.py:141
  634.3 15.1 copy.100
  649.4 164.1 %gather_fusion.8 = f32[49152,3]{1,0:T(8,128)} fusion(f32[3,8192]{0,1:T(8,128)} %copy.81, s32[49152]{0:T(1024)S(1)} %get-tuple-element.61), kind=kCustom, calls=%fused_computation.5.clone | custom fusion | bytes 1376256 | tf_op jit(solution)/shard_map/jit(_take)/gather | solution.py:141
  813.5 27.5 %broadcast_select_fusion.2 = f32[49152,3]{1,0:T(8,128)} fusion(f32[49152,3]{1,0:T(8,128)} %gather_fusion.8, pred[49152]{0:T(1024)(128)(4,1)S(1)} %copy-done.25), kind=kLoop, calls=%fused_computation.13 | loop fusion | flops 147456 | bytes 1228800 | tf_op jit(solution)/shard_map/jit(_take)/select_n | solution.py:141
  841.0 15.1 copy.97
  856.1 15.1 copy.94
  871.2 164.1 %gather_fusion.6 = f32[49152,3]{1,0:T(8,128)} fusion(f32[3,8192]{0,1:T(8,128)} %copy.81, s32[49152]{0:T(1024)S(1)} %get-tuple-element.59), kind=kCustom, calls=%fused_computation.3.clone | custom fusion | bytes 1376256 | tf_op jit(solution)/shard_map/jit(_take)/gather | solution.py:141
  1035.3 27.7 %broadcast_select_fusion.4 = f32[49152,3]{1,0:T(8,128)} fusion(f32[49152,3]{1,0:T(8,128)} %gather_fusion.6, pred[49152]{0:T(1024)(128)(4,1)S(1)} %copy-done.24), kind=kLoop, calls=%fused_computation.15 | loop fusion | flops 147456 | bytes 1228800 | tf_op jit(solution)/shard_map/jit(_take)/select_n | solution.py:141
  1063.0 15.1 copy.91
  1078.1 164.0 %gather_fusion.5 = f32[49152,3]{1,0:T(8,128)} fusion(f32[3,8192]{0,1:T(8,128)} %copy.81, s32[49152]{0:T(1024)S(1)} %get-tuple-element.58), kind=kCustom, calls=%fused_computation.2.clone | custom fusion | bytes 1376256 | tf_op jit(solution)/shard_map/jit(_take)/gather | solution.py:141
  1242.2 164.1 %gather_fusion.3 = f32[49152,3]{1,0:T(8,128)} fusion(f32[3,8192]{0,1:T(8,128)} %copy.81, s32[49152]{0:T(1024)S(1)} %get-tuple-element.50), kind=kCustom, calls=%fused_computation.clone | custom fusion | bytes 1376256 | tf_op jit(solution)/shard_map/jit(_take)/gather | solution.py:141
  1406.3 34.4 %broadcast_select_fusion.5 = (f32[49152,3]{1,0:T(8,128)}, f32[49152,3]{1,0:T(8,128)}) fusion(f32[49152,3]{1,0:T(8,128)} %gather_fusion.5, pred[49152]{0:T(1024)(128)(4,1)S(1)} %copy-done.20, f32[49152,3]{1,0:T(8,128)} %gather_fusion.3, pred[49152]{0:T(1024)(128)(4,1)S(1)} %copy-done.19), kind=kLoop, calls=%fused_computation.16 | loop fusion | flops 294912 | bytes 2457600 | tf_op jit(solution)/shard_map/jit(_take)/select_n | solution.py:141
  1440.7 15.1 copy.88
  1455.9 164.0 %gather_fusion.4 = f32[49152,3]{1,0:T(8,128)} fusion(f32[3,8192]{0,1:T(8,128)} %copy.81, s32[49152]{0:T(1024)S(1)} %copy-done.12), kind=kCustom, calls=%fused_computation.1.clone | custom fusion | bytes 1376256 | tf_op jit(solution)/shard_map/jit(_take)/gather | solution.py:141
  1619.9 27.4 %broadcast_select_fusion.6 = f32[49152,3]{1,0:T(8,128)} fusion(f32[49152,3]{1,0:T(8,128)} %gather_fusion.4, pred[49152]{0:T(1024)(128)(4,1)S(1)} %copy-done.23), kind=kLoop, calls=%fused_computation.17 | loop fusion | flops 147456 | bytes 1228800 | tf_op jit(solution)/shard_map/jit(_take)/select_n | solution.py:141
  1647.3 16.0 copy.85
  1663.3 16.1 copy.82
  1679.4 2.9 convolution_bitcast_fusion
  1682.4 2.1 copy.104
  1684.5 2.1 sine_negate_fusion
  1688.0 2.9 fusion.80
  1690.9 126.5 %all-reduce.4.cloned.1.call-done = f32[128,3072]{0,1:T(8,128)} async-done(((f32[128,3072]{0,1:T(8,128)}), f32[128,3072]{0,1:T(8,128)}) %all-reduce.4.cloned.1.call-update) | async-done | bytes 1572880
  1817.4 1.9 constant_dynamic-slice_fusion
  (115 shorter events, 32.3 us)
Async XLA Ops:
  7.2 24.1 %copy-start.14 = (f32[4,8,256]{2,1,0:T(8,128)S(1)}, f32[4,8,256]{2,1,0:T(8,128)}, u32[]{:S(2)}) copy-start(f32[4,8,256]{2,1,0:T(8,128)} %param.12) | copy-start | bytes 98308
  7.2 24.1 %copy-start.15 = (f32[4,8,256]{2,1,0:T(8,128)S(1)}, f32[4,8,256]{2,1,0:T(8,128)}, u32[]{:S(2)}) copy-start(f32[4,8,256]{2,1,0:T(8,128)} %param.11) | copy-start | bytes 98308
  7.2 24.1 %copy-start.5 = (f32[3,4,8,256]{3,2,1,0:T(8,128)S(1)}, f32[3,4,8,256]{3,2,1,0:T(8,128)}, u32[]{:S(2)}) copy-start(f32[3,4,8,256]{3,2,1,0:T(8,128)} %param.9) | copy-start | bytes 294916
  7.2 1810.2 %all-reduce.4.cloned.1.call-start = ((), (), s32[]{:S(2)}) async-start(), calls=%async_computation | async-start | bytes 3145728
  8.9 22.4 %collective-permute-start.1 = (f32[6,2,8,256]{3,2,1,0:T(8,128)}, f32[6,2,8,256]{3,2,1,0:T(8,128)}, u32[]{:S(2)}, u32[]{:S(2)}) collective-permute-start(f32[6,2,8,256]{3,2,1,0:T(8,128)} %get-tuple-element.65), channel_id=1, source_target_pairs={{8,0},{16,8},{24,16},{9,1},{17,9},{25,17},{10,2},{18,10},{26,18},{... | collective-permute-start | bytes 294920 | tf_op jit(solution)/shard_map/ppermute | solution.py:27
  10.2 21.1 %collective-permute-start = (f32[6,2,8,256]{3,2,1,0:T(8,128)}, f32[6,2,8,256]{3,2,1,0:T(8,128)}, u32[]{:S(2)}, u32[]{:S(2)}) collective-permute-start(f32[6,2,8,256]{3,2,1,0:T(8,128)} %get-tuple-element.64), channel_id=1, source_target_pairs={{0,8},{8,16},{16,24},{1,9},{9,17},{17,25},{2,10},{10,18},{18,26},{... | collective-permute-start | bytes 294920 | tf_op jit(solution)/shard_map/ppermute | solution.py:26
  30.9 224.7 %copy-start.26 = (pred[24]{0:T(512)(128)(4,1)}, pred[24]{0:T(512)(128)(4,1)S(1)}, u32[]{:S(2)}) copy-start(pred[24]{0:T(512)(128)(4,1)S(1)} %broadcast_compare_fusion) | copy-start | bytes 76
  32.5 10.6 collective-permute-start.3
  33.8 9.3 collective-permute-start.2
  45.1 210.5 %copy-start = (f32[8,12,260]{2,1,0:T(8,128)}, f32[8,12,260]{2,1,0:T(8,128)S(1)}, u32[]{:S(2)}) copy-start(f32[8,12,260]{2,1,0:T(8,128)S(1)} %get-tuple-element.45) | copy-start | bytes 299524
  45.2 210.5 %copy-start.1 = (f32[8,12,260]{2,1,0:T(8,128)}, f32[8,12,260]{2,1,0:T(8,128)S(1)}, u32[]{:S(2)}) copy-start(f32[8,12,260]{2,1,0:T(8,128)S(1)} %get-tuple-element.46) | copy-start | bytes 299524
  45.2 210.5 %copy-start.2 = (f32[8,12,260]{2,1,0:T(8,128)}, f32[8,12,260]{2,1,0:T(8,128)S(1)}, u32[]{:S(2)}) copy-start(f32[8,12,260]{2,1,0:T(8,128)S(1)} %get-tuple-element.47) | copy-start | bytes 299524
  47.0 208.7 %copy-start.6 = (f32[4,8,256]{2,1,0:T(8,128)}, f32[4,8,256]{2,1,0:T(8,128)S(1)}, u32[]{:S(2)}) copy-start(f32[4,8,256]{2,1,0:T(8,128)S(1)} %get-tuple-element.26) | copy-start | bytes 98308
  47.0 208.7 %copy-start.7 = (f32[4,8,256]{2,1,0:T(8,128)}, f32[4,8,256]{2,1,0:T(8,128)S(1)}, u32[]{:S(2)}) copy-start(f32[4,8,256]{2,1,0:T(8,128)S(1)} %get-tuple-element.27) | copy-start | bytes 98308
  47.0 208.7 %copy-start.8 = (f32[4,8,256]{2,1,0:T(8,128)}, f32[4,8,256]{2,1,0:T(8,128)S(1)}, u32[]{:S(2)}) copy-start(f32[4,8,256]{2,1,0:T(8,128)S(1)} %get-tuple-element.29) | copy-start | bytes 98308
  47.0 208.7 %copy-start.9 = (f32[4,8,256]{2,1,0:T(8,128)}, f32[4,8,256]{2,1,0:T(8,128)S(1)}, u32[]{:S(2)}) copy-start(f32[4,8,256]{2,1,0:T(8,128)S(1)} %get-tuple-element.30) | copy-start | bytes 98308
  47.0 208.7 %copy-start.10 = (f32[4,8,256]{2,1,0:T(8,128)}, f32[4,8,256]{2,1,0:T(8,128)S(1)}, u32[]{:S(2)}) copy-start(f32[4,8,256]{2,1,0:T(8,128)S(1)} %get-tuple-element.32) | copy-start | bytes 98308
  47.0 208.7 %copy-start.11 = (f32[4,8,256]{2,1,0:T(8,128)}, f32[4,8,256]{2,1,0:T(8,128)S(1)}, u32[]{:S(2)}) copy-start(f32[4,8,256]{2,1,0:T(8,128)S(1)} %get-tuple-element.33) | copy-start | bytes 98308
  47.2 208.6 %copy-start.16 = (f32[4,8,256]{2,1,0:T(8,128)}, f32[4,8,256]{2,1,0:T(8,128)S(1)}, u32[]{:S(2)}) copy-start(f32[4,8,256]{2,1,0:T(8,128)S(1)} %fusion.107) | copy-start | bytes 98308
  47.4 208.3 %copy-start.17 = (f32[4,8,256]{2,1,0:T(8,128)}, f32[4,8,256]{2,1,0:T(8,128)S(1)}, u32[]{:S(2)}) copy-start(f32[4,8,256]{2,1,0:T(8,128)S(1)} %fusion.125) | copy-start | bytes 98308
  47.7 208.1 %copy-start.18 = (f32[4,8,256]{2,1,0:T(8,128)}, f32[4,8,256]{2,1,0:T(8,128)S(1)}, u32[]{:S(2)}) copy-start(f32[4,8,256]{2,1,0:T(8,128)S(1)} %fusion.149) | copy-start | bytes 98308
  255.8 180.1 %copy-start.13 = (s32[49152]{0:T(1024)S(1)}, s32[49152]{0:T(1024)}, u32[]{:S(2)}) copy-start(s32[49152]{0:T(1024)} %get-tuple-element.60) | copy-start | bytes 589828
  255.8 344.1 %copy-start.21 = (pred[49152]{0:T(1024)(128)(4,1)S(1)}, pred[49152]{0:T(1024)(128)(4,1)}, u32[]{:S(2)}) copy-start(pred[49152]{0:T(1024)(128)(4,1)} %get-tuple-element.52) | copy-start | bytes 147460
  255.8 344.1 %copy-start.22 = (pred[49152]{0:T(1024)(128)(4,1)S(1)}, pred[49152]{0:T(1024)(128)(4,1)}, u32[]{:S(2)}) copy-start(pred[49152]{0:T(1024)(128)(4,1)} %get-tuple-element.56) | copy-start | bytes 147460
  634.3 179.2 %copy-start.25 = (pred[49152]{0:T(1024)(128)(4,1)S(1)}, pred[49152]{0:T(1024)(128)(4,1)}, u32[]{:S(2)}) copy-start(pred[49152]{0:T(1024)(128)(4,1)} %get-tuple-element.73) | copy-start | bytes 147460
  841.0 194.3 %copy-start.24 = (pred[49152]{0:T(1024)(128)(4,1)S(1)}, pred[49152]{0:T(1024)(128)(4,1)}, u32[]{:S(2)}) copy-start(pred[49152]{0:T(1024)(128)(4,1)} %get-tuple-element.74) | copy-start | bytes 147460
  1063.0 343.3 %copy-start.19 = (pred[49152]{0:T(1024)(128)(4,1)S(1)}, pred[49152]{0:T(1024)(128)(4,1)}, u32[]{:S(2)}) copy-start(pred[49152]{0:T(1024)(128)(4,1)} %get-tuple-element.7) | copy-start | bytes 147460
  1063.0 343.3 %copy-start.20 = (pred[49152]{0:T(1024)(128)(4,1)S(1)}, pred[49152]{0:T(1024)(128)(4,1)}, u32[]{:S(2)}) copy-start(pred[49152]{0:T(1024)(128)(4,1)} %get-tuple-element.54) | copy-start | bytes 147460
  1440.7 179.2 %copy-start.23 = (pred[49152]{0:T(1024)(128)(4,1)S(1)}, pred[49152]{0:T(1024)(128)(4,1)}, u32[]{:S(2)}) copy-start(pred[49152]{0:T(1024)(128)(4,1)} %get-tuple-element.75) | copy-start | bytes 147460
  1647.3 32.1 %copy-start.3 = (f32[3,128,24,16]{1,2,3,0:T(8,128)S(1)}, f32[3,128,24,16]{1,2,3,0:T(8,128)}, u32[]{:S(2)}) copy-start(f32[3,128,24,16]{1,2,3,0:T(8,128)} %copy.103) | copy-start | bytes 1769476
  1647.3 32.1 %copy-start.27 = (pred[24]{0:T(512)(128)(4,1)S(1)}, pred[24]{0:T(512)(128)(4,1)}, u32[]{:S(2)}) copy-start(pred[24]{0:T(512)(128)(4,1)} %copy-done.26) | copy-start | bytes 76
  1647.3 32.1 %copy-start.28 = (s32[24]{0:T(128)S(1)}, s32[24]{0:T(128)}, u32[]{:S(2)}) copy-start(s32[24]{0:T(128)} %get-tuple-element.66) | copy-start | bytes 292
  (2 other events, 15.8 us)
Sparse Core Ops, SparseCore 0:
  1684.6 132.7 all-reduce.3
where the time goes:
time: 1840 us; the launch traced here: 1830 us
  local copies, waits for them, and re-layouts  1470 us (80%)
  other arithmetic  197 us (11%)
  waiting for transfers between devices  127 us (7%)
    gather x8, local copies, waits for them, and re-layouts, sample_points(): jnp.take(flat_field, position.reshape(-1), axis=1)  1330 us
    select_n x6, other arithmetic, sample_points(): jnp.take(flat_field, position.reshape(-1), axis=1)  176 us
    unnamed x2, waiting for transfers between devices  127 us
    reshape x8, local copies, waits for them, and re-layouts, sample_points(): jnp.take(flat_field, position.reshape(-1), axis=1)  124 us
  transfers between devices with their start and end apart: 5, of which 1 were waited for; matrix products, arithmetic and copies ran while one was open for 1% of the time, Pallas kernels for 0%

commit v1 on v0

v1 whole, which is shorter than its diff:
```python
import functools
import math

import jax
import jax.numpy as jnp
import numpy as np
from jax import lax
from jax.experimental import pallas as pl
from jax.experimental.pallas import tpu as pltpu
from jax.sharding import PartitionSpec as P

NH = 128

base_viscosity = 0.05
time_step = 0.2
beta_star = 0.09
beta_rate = 0.075
alpha_rate = 0.52
wall_rate = 1.0

LANES = 128
ROWS = 8
VMEM_LIMIT = 48 * 1024 * 1024


def prepare_kernel(cells_s, cells_g, cells_r, ids_ref, frac_ref, q_ref, fr_ref, xg_ref, hs_ref):
    stream_first = lax.axis_index("stream") * cells_s
    plane_cells = cells_g * cells_r
    azimuths = ids_ref.shape[1]
    for block in range(azimuths // LANES):
        cols = pl.ds(block * LANES, LANES)
        ids = ids_ref[:, cols].T
        fs = frac_ref[0, :, cols].T
        fg = frac_ref[1, :, cols].T
        fr = frac_ref[2, :, cols].T
        stream_cell = ids // plane_cells
        remainder = ids - stream_cell * plane_cells
        girth_cell = remainder // cells_r
        q_ref[cols, :] = remainder - girth_cell * cells_r
        fr_ref[cols, :] = fr
        xg_ref[cols, :] = girth_cell.astype(jnp.float32) + fg
        local = stream_cell - stream_first
        for layer in range(cells_s):
            hs_ref[layer, cols, :] = jnp.where(
                local == layer, 1.0 - fs, jnp.where(local == layer - 1, fs, 0.0)
            )


def prepare(corner_ids, fractions, cells_s, cells_g, cells_r):
    radii, azimuths = corner_ids.shape
    shape = jax.ShapeDtypeStruct
    return pl.pallas_call(
        functools.partial(prepare_kernel, cells_s, cells_g, cells_r),
        out_shape=(
            shape((azimuths, radii), jnp.int32),
            shape((azimuths, radii), jnp.float32),
            shape((azimuths, radii), jnp.float32),
            shape((cells_s, azimuths, radii), jnp.float32),
        ),
        compiler_params=pltpu.CompilerParams(vmem_limit_bytes=VMEM_LIMIT),
        cost_estimate=pl.CostEstimate(
            flops=20 * radii * azimuths, bytes_accessed=44 * radii * azimuths, transcendentals=0
        ),
        name="prepare_points",
    )(corner_ids, fractions)


def radial(values, amount, fill):
    extent = values.shape[-1]
    rolled = pltpu.roll(values, (-amount) % extent, values.ndim - 1)
    position = lax.broadcasted_iota(jnp.int32, values.shape, values.ndim - 1) + amount
    return jnp.where((position >= 0) & (position < extent), rolled, fill)


def advance(own, before, after, left, right, ext_ref, visc_ref):
    cells_s, cells_g, _ = own[0].shape
    mid = ROWS

    def along_s(stack, amount):
        return stack[2 + amount : 2 + amount + cells_s]

    def along_g(ref, amount):
        return ref[:, mid + amount : mid + amount + cells_g, :]

    def viscosity(energy, rate):
        return base_viscosity + energy / (rate + wall_rate)

    stacks = [jnp.concatenate([before[f], own[f], after[f]], axis=0) for f in range(6)]
    for f in range(6):
        ext_ref[f, :, mid - 2 : mid, :] = left[f]
        ext_ref[f, :, mid : mid + cells_g, :] = own[f]
        ext_ref[f, :, mid + cells_g : mid + cells_g + 2, :] = right[f]
    middle = viscosity(own[4], own[5])
    visc_stack = viscosity(stacks[4], stacks[5])
    visc_ref[:, mid - 2 : mid, :] = viscosity(left[4], left[5])
    visc_ref[:, mid : mid + cells_g, :] = middle
    visc_ref[:, mid + cells_g : mid + cells_g + 2, :] = viscosity(right[4], right[5])
    faces = [
        (
            0.5 * (middle + along_s(visc_stack, 1)),
            0.5 * (middle + along_s(visc_stack, -1)),
        ),
        (
            0.5 * (middle + along_g(visc_ref, 1)),
            0.5 * (middle + along_g(visc_ref, -1)),
        ),
        (
            0.5 * (middle + radial(middle, 1, base_viscosity)),
            0.5 * (middle + radial(middle, -1, base_viscosity)),
        ),
    ]

    def neighbour(f, direction, amount):
        if direction == 0:
            return along_s(stacks[f], amount)
        if direction == 1:
            return along_g(ext_ref.at[f], amount)
        return radial(own[f], amount, 0.0)

    def terms(f, direction):
        up, down = neighbour(f, direction, 1), neighbour(f, direction, -1)
        far = neighbour(f, direction, 2) - neighbour(f, direction, -2)
        gradient = (8.0 * (up - down) - far) * (1.0 / 12.0)
        above, below = faces[direction]
        return gradient, above * (up - own[f]) - below * (own[f] - down)

    strain = None
    updated = []
    for f in range(3):
        change = -terms(3, f)[0]
        for direction in range(3):
            gradient, spread = terms(f, direction)
            strain = gradient * gradient if strain is None else strain + gradient * gradient
            change = change - own[direction] * gradient + spread
        updated.append(own[f] + time_step * change)
    energy = own[4] / (own[5] + wall_rate) * strain - beta_star * own[4] * own[5]
    rate = alpha_rate * strain - beta_rate * own[5] * own[5]
    for direction in range(3):
        gradient, spread = terms(4, direction)
        energy = energy - own[direction] * gradient + spread
        gradient, spread = terms(5, direction)
        rate = rate - own[direction] * gradient + spread
    return updated, own[4] + time_step * energy, own[5] + time_step * rate


def section_kernel(
    owner_ref,
    vel_ref,
    p_ref,
    k_ref,
    w_ref,
    before_ref,
    after_ref,
    left_ref,
    right_ref,
    q_ref,
    fr_ref,
    xg_ref,
    hs_ref,
    table_ref,
    new_vel_ref,
    new_k_ref,
    new_w_ref,
    harm_ref,
    ext_ref,
    visc_ref,
    field_ref,
    slope_ref,
    disk_ref,
    chosen_ref,
):
    cells_s, cells_g, cells_r = p_ref.shape
    halves = cells_r // LANES
    sectors = owner_ref.shape[0]
    width = q_ref.shape[0] // sectors
    me = lax.axis_index("girth")

    own = [vel_ref[0], vel_ref[1], vel_ref[2], p_ref[...], k_ref[...], w_ref[...]]
    six = range(6)
    updated, energy, rate = advance(
        own,
        [before_ref[f] for f in six],
        [after_ref[f] for f in six],
        [left_ref[f] for f in six],
        [right_ref[f] for f in six],
        ext_ref,
        visc_ref,
    )
    new_k_ref[...] = energy
    new_w_ref[...] = rate
    for c in range(3):
        new_vel_ref[c] = updated[c]
        slope = radial(updated[c], 1, 0.0) - updated[c]
        for h in range(halves):
            lanes = slice(h * LANES, (h + 1) * LANES)
            field_ref[c, :, h] = updated[c][:, :, lanes]
            slope_ref[c, :, h] = slope[:, :, lanes]

    disk_ref[...] = jnp.zeros_like(disk_ref)
    chosen_ref[...] = jnp.zeros_like(chosen_ref)
    girth_row = lax.broadcasted_iota(jnp.int32, (cells_g, LANES), 0).astype(jnp.float32)

    def pick(ref, c, s, index, half_of):
        out = None
        for h in range(halves):
            got = jnp.take_along_axis(ref[c, s, h], index, axis=1, mode="promise_in_bounds")
            out = got if out is None else jnp.where(half_of[h], got, out)
        return out

    def spread(row):
        return jnp.broadcast_to(row, (cells_g, LANES))

    def eight(source, target):
        rows = pl.ds(pl.multiple_of(source, ROWS), ROWS)
        q8, fr8, xg8 = q_ref[rows, :], fr_ref[rows, :], xg_ref[rows, :]
        hs8 = [hs_ref[s, rows, :] for s in range(cells_s)]
        for j in range(ROWS):
            q = spread(q8[j : j + 1])
            fr = spread(fr8[j : j + 1])
            hg = jnp.maximum(1.0 - jnp.abs(spread(xg8[j : j + 1]) - girth_row), 0.0)
            hs = [spread(hs8[s][j : j + 1]) for s in range(cells_s)]
            index = q % LANES
            half_of = [q >= h * LANES for h in range(halves)]
            for c in range(3):
                total = None
                for s in range(cells_s):
                    value = pick(field_ref, c, s, index, half_of)
                    value = value + fr * pick(slope_ref, c, s, index, half_of)
                    total = hs[s] * value if total is None else total + hs[s] * value
                disk_ref[c, pl.ds(target + j, 1), :] = jnp.sum(hg * total, axis=0, keepdims=True)

    def sector(number, count):
        mine = owner_ref[number] == me

        @pl.when(mine)
        def _():
            source = pl.multiple_of(number * width, width)
            target = pl.multiple_of(count * width, width)
            chosen_ref[pl.ds(target, width), :] = table_ref[pl.ds(source, width), :]
            for part in range(width // ROWS):
                eight(source + part * ROWS, target + part * ROWS)

        return count + mine.astype(jnp.int32)

    lax.fori_loop(0, sectors, sector, jnp.int32(0))

    for c in range(3):
        harm_ref[:, c * 2 * NH : (c + 1) * 2 * NH] = lax.dot_general(
            disk_ref[c],
            chosen_ref[...],
            (((0,), (0,)), ((), ())),
            precision=lax.Precision.HIGHEST,
            preferred_element_type=jnp.float32,
        )


def section(
    owners, velocity, pressure, energy, rate, before, after, left, right, points, table, girth_count
):
    _, cells_s, cells_g, cells_r = velocity.shape
    azimuths, radii = points[0].shape
    sectors = owners.shape[0]
    columns = 3 * sectors // girth_count * (azimuths // sectors)
    shape = functools.partial(jax.ShapeDtypeStruct, dtype=jnp.float32)
    scratch = lambda *dims: pltpu.VMEM(dims, jnp.float32)
    vmem = pl.BlockSpec(memory_space=pltpu.VMEM)
    smem = pl.BlockSpec(memory_space=pltpu.SMEM)
    return pl.pallas_call(
        section_kernel,
        out_shape=(
            shape(velocity.shape),
            shape(energy.shape),
            shape(rate.shape),
            shape((radii, 6 * NH)),
        ),
        in_specs=[smem] + [vmem] * 13,
        scratch_shapes=[
            scratch(6, cells_s, 3 * ROWS, cells_r),
            scratch(cells_s, 3 * ROWS, cells_r),
            scratch(3, cells_s, cells_r // LANES, cells_g, LANES),
            scratch(3, cells_s, cells_r // LANES, cells_g, LANES),
            scratch(3, columns, radii),
            scratch(columns, 2 * NH),
        ],
        compiler_params=pltpu.CompilerParams(vmem_limit_bytes=VMEM_LIMIT),
        name="section_and_disk",
    )(owners, velocity, pressure, energy, rate, before, after, left, right, *points, table)


def fourier_table(azimuths, modes):
    phase = np.arange(azimuths)[:, None] * np.arange(modes)[None, :] % azimuths
    angles = phase * (2.0 * math.pi / azimuths)
    table = np.concatenate([np.cos(angles), -np.sin(angles)], axis=1) / math.sqrt(azimuths)
    return jnp.asarray(table.astype(np.float32))


def body(velocity, pressure, kinetic_energy, dissipation_rate, corner_ids, fractions, sector_owner):
    _, cells_s, cells_g, cells_r = velocity.shape
    radii, azimuths = corner_ids.shape
    stream_count, girth_count = lax.axis_size("stream"), lax.axis_size("girth")
    devices = stream_count * girth_count

    def slab(dim, start):
        def cut(values, at):
            return lax.slice_in_dim(values, start, start + 2, axis=at)

        scalars = [cut(x, dim)[None] for x in (pressure, kinetic_energy, dissipation_rate)]
        return jnp.concatenate([cut(velocity, dim + 1)] + scalars, axis=0)

    def send(values, axis, count, step):
        pairs = [(i, i + step) for i in range(count) if 0 <= i + step < count]
        return lax.ppermute(values, axis, pairs)

    before = send(slab(0, cells_s - 2), "stream", stream_count, 1)
    after = send(slab(0, 0), "stream", stream_count, -1)
    left = send(slab(1, cells_g - 2), "girth", girth_count, 1)
    right = send(slab(1, 0), "girth", girth_count, -1)
    points = prepare(corner_ids, fractions, cells_s, cells_g, cells_r)
    new_velocity, new_energy, new_rate, partial = section(
        sector_owner[:, 0],
        velocity,
        pressure,
        kinetic_energy,
        dissipation_rate,
        before,
        after,
        left,
        right,
        points,
        fourier_table(azimuths, NH),
        girth_count,
    )
    shares = lax.all_to_all(
        partial.reshape(devices, radii // devices, 6 * NH),
        ("stream", "girth"),
        split_axis=0,
        concat_axis=0,
        tiled=True,
    )
    return new_velocity, new_energy, new_rate, jnp.sum(shares, axis=0)


def solution(mesh):
    return jax.shard_map(
        body,
        mesh=mesh,
        in_specs=(
            P(None, "stream", "girth", None),
            P("stream", "girth", None),
            P("stream", "girth", None),
            P("stream", "girth", None),
            P(),
            P(),
            P(),
        ),
        out_specs=(
            P(None, "stream", "girth", None),
            P("stream", "girth", None),
            P("stream", "girth", None),
            P(("stream", "girth"), None),
        ),
        check_vma=False,
    )
```

time: 1840 us -> 66.9 us (0.04)
  local copies, waits for them, and re-layouts: 1470 us -> 7.65 us
  other arithmetic: 197 us -> 0.75 us
  waiting for transfers between devices: 127 us -> 0.96 us
  blocking collectives: 0 us -> 40.5 us
    gather x13 -> x0, local copies, waits for them, and re-layouts: 1330 us -> none  [the longest x8 1330 us: sample_points(): jnp.take(flat_field, position.reshape(-1), axis=1)]
    select_n x8 -> x0, other arithmetic: 177 us -> none  [the longest x6 176 us: sample_points(): jnp.take(flat_field, position.reshape(-1), axis=1)]
    unnamed x2 -> x0, waiting for transfers between devices: 127 us -> none
    reshape x11 -> x1, local copies, waits for them, and re-layouts: 125 us -> 0.11 us  [body(): partial.reshape(devices, radii // devices, 6 * NH)]
    all_to_all x0 -> x1, blocking collectives: none -> 40.5 us  [body(): lax.all_to_all(partial.reshape(devices, radii // devices, 6 * NH), ('stre...]
  transfers between devices with their start and end apart: 5 -> 4, of which waited for: 1 -> 1; matrix products, arithmetic and copies ran while one was open for 1% -> 4% of each run, Pallas kernels for 0% -> 2%
where the time goes in v1:
time: 66.9 us
  blocking collectives  40.5 us (61%)
  starting transfers between devices  9.26 us (14%)
  local copies, waits for them, and re-layouts  7.65 us (11%)
  Pallas kernels  6.89 us (10%)
  waiting for transfers between devices  0.96 us (1%)
  between operations  0.81 us (1%)
  other arithmetic  0.75 us (1%)
    all_to_all x1, blocking collectives, body(): lax.all_to_all(partial.reshape(devices, radii // devices, 6 * NH), ('stre...  40.5 us
    ppermute x4, starting transfers between devices, send(): return lax.ppermute(values, axis, pairs)  9.26 us
    pallas_call x1, Pallas kernels, section(): pl.pallas_call(section_kernel, out_shape=(shape(velocity.shape), shape(en...  5.87 us
    broadcast_in_dim x4, local copies, waits for them, and re-layouts, slab(): cut(x, dim)[None]  3.25 us
    unnamed x16, local copies, waits for them, and re-layouts  2.48 us
    slice x2, local copies, waits for them, and re-layouts, cut(): return lax.slice_in_dim(values, start, start + 2, axis=at)  1.82 us
  transfers between devices with their start and end apart: 4, of which 1 were waited for; matrix products, arithmetic and copies ran while one was open for 4% of the time, Pallas kernels for 2%

profile of v1, /device:TPU:0, one launch (start us, length us, event | category | flops | bytes accessed | tf_op | source)
XLA Modules:
  0.0 66.9 jit_solution(11916097359269624807)
XLA Ops:
  0.6 0.0 copy-start.1
  0.6 0.0 copy-start.4
  0.7 0.0 copy-start.2
  0.7 0.0 copy-start.5
  0.7 0.9 %slice_bitcast_fusion.8 = (f32[1,4,2,256]{3,2,1,0:T(2,128)S(1)}, f32[1,4,2,256]{3,2,1,0:T(2,128)S(1)}) fusion(f32[4,8,256]{2,1,0:T(8,128)} %p_ref.1), kind=kLoop, calls=%fused_computation.12 | loop fusion | bytes 32768 | tf_op jit(solution)/shard_map/broadcast_in_dim | solution.py:307
  1.6 1.0 %fusion = (f32[3,4,2,256]{3,2,1,0:T(2,128)S(1)}, f32[3,4,2,256]{3,2,1,0:T(2,128)S(1)}) fusion(f32[3,4,8,256]{3,2,1,0:T(8,128)} %vel_ref.1), kind=kLoop, calls=%fused_computation.16 | loop fusion | bytes 98304 | tf_op jit(solution)/shard_map/slice | solution.py:305
  2.5 0.9 %slice_bitcast_fusion.6 = (f32[1,4,2,256]{3,2,1,0:T(2,128)S(1)}, f32[1,4,2,256]{3,2,1,0:T(2,128)S(1)}, f32[1,4,2,256]{3,2,1,0:T(2,128)S(1)}, f32[1,4,2,256]{3,2,1,0:T(2,128)S(1)}) fusion(f32[4,8,256]{2,1,0:T(8,128)} %w_ref.1, f32[4,8,256]{2,1,0:T(8,128)} %k_ref.1), kind=kLoop, calls=%fused_computation.10 | loop fusion | bytes 65536 | tf_op jit(solution)/shard_map/broadcast_in_dim | solution.py:307
  3.4 2.4 %collective-permute-start.2 = (f32[6,4,2,256]{3,2,1,0:T(2,128)S(1)}, f32[6,4,2,256]{3,2,1,0:T(2,128)S(1)}, u32[]{:S(2)}, u32[]{:S(2)}) collective-permute-start(f32[6,4,2,256]{3,2,1,0:T(2,128)S(1)} %pad_maximum_fusion.2), channel_id=1, source_target_pairs={{0,1},{1,2},{2,3},{3,4},{4,5},{5,6},{6,7},{8,9},{9,10},{10,11},{11... | collective-permute-start | bytes 147464 | tf_op jit(solution)/shard_map/ppermute | solution.py:312
  5.8 0.7 %slice_bitcast_fusion.2 = (f32[1,2,8,256]{3,2,1,0:T(8,128)S(1)}, f32[1,2,8,256]{3,2,1,0:T(8,128)S(1)}) fusion(f32[4,8,256]{2,1,0:T(8,128)} %p_ref.1), kind=kLoop, calls=%fused_computation.6 | loop fusion | bytes 65536 | tf_op jit(solution)/shard_map/broadcast_in_dim | solution.py:307
  6.5 0.8 %slice_bitcast_fusion = (f32[1,2,8,256]{3,2,1,0:T(8,128)S(1)}, f32[1,2,8,256]{3,2,1,0:T(8,128)S(1)}, f32[1,2,8,256]{3,2,1,0:T(8,128)S(1)}, f32[1,2,8,256]{3,2,1,0:T(8,128)S(1)}) fusion(f32[4,8,256]{2,1,0:T(8,128)} %w_ref.1, f32[4,8,256]{2,1,0:T(8,128)} %k_ref.1), kind=kLoop, calls=%fused_computation.4 | loop fusion | bytes 131072 | tf_op jit(solution)/shard_map/broadcast_in_dim | solution.py:307
  7.3 0.8 %fusion.1 = (f32[3,2,8,256]{3,2,1,0:T(8,128)S(1)}, f32[3,2,8,256]{3,2,1,0:T(8,128)S(1)}) fusion(f32[3,4,8,256]{3,2,1,0:T(8,128)} %vel_ref.1), kind=kLoop, calls=%fused_computation.17 | loop fusion | bytes 196608 | tf_op jit(solution)/shard_map/slice | solution.py:305
  8.2 4.3 %collective-permute-start = (f32[6,2,8,256]{3,2,1,0:T(8,128)S(1)}, f32[6,2,8,256]{3,2,1,0:T(8,128)S(1)}, u32[]{:S(2)}, u32[]{:S(2)}) collective-permute-start(f32[6,2,8,256]{3,2,1,0:T(8,128)S(1)} %pad_maximum_fusion), channel_id=1, source_target_pairs={{0,8},{8,16},{16,24},{1,9},{9,17},{17,25},{2,10},{10,18},{18,26},{... | collective-permute-start | bytes 294920 | tf_op jit(solution)/shard_map/ppermute | solution.py:312
  12.5 1.3 %collective-permute-start.1 = (f32[6,2,8,256]{3,2,1,0:T(8,128)S(1)}, f32[6,2,8,256]{3,2,1,0:T(8,128)S(1)}, u32[]{:S(2)}, u32[]{:S(2)}) collective-permute-start(f32[6,2,8,256]{3,2,1,0:T(8,128)S(1)} %pad_maximum_fusion.1), channel_id=1, source_target_pairs={{8,0},{16,8},{24,16},{9,1},{17,9},{25,17},{10,2},{18,10},{26,18},{... | collective-permute-start | bytes 294920 | tf_op jit(solution)/shard_map/ppermute | solution.py:312
  13.8 1.3 %collective-permute-start.3 = (f32[6,4,2,256]{3,2,1,0:T(2,128)S(1)}, f32[6,4,2,256]{3,2,1,0:T(2,128)S(1)}, u32[]{:S(2)}, u32[]{:S(2)}) collective-permute-start(f32[6,4,2,256]{3,2,1,0:T(2,128)S(1)} %pad_maximum_fusion.3), channel_id=1, source_target_pairs={{1,0},{2,1},{3,2},{4,3},{5,4},{6,5},{7,6},{9,8},{10,9},{11,10},{12... | collective-permute-start | bytes 147464 | tf_op jit(solution)/shard_map/ppermute | solution.py:312
  15.1 0.0 copy-start
  15.1 1.4 %copy-done = f32[3,128,1024]{2,1,0:T(8,128)S(1)} copy-done((f32[3,128,1024]{2,1,0:T(8,128)S(1)}, f32[3,128,1024]{2,1,0:T(8,128)}, u32[]{:S(2)}) %copy-start) | copy-done | bytes 1572888
  16.5 1.0 %copy-done.3 = s32[128,1024]{1,0:T(8,128)S(1)} copy-done((s32[128,1024]{1,0:T(8,128)S(1)}, s32[128,1024]{1,0:T(8,128)}, u32[]{:S(2)}) %copy-start.3) | copy-done | bytes 524312
  17.6 1.0 %prepare_points.1 = (s32[1024,128]{1,0:T(8,128)S(1)}, f32[1024,128]{1,0:T(8,128)S(1)}, f32[1024,128]{1,0:T(8,128)S(1)}, f32[4,1024,128]{2,1,0:T(8,128)S(1)}) custom-call(s32[128,1024]{1,0:T(8,128)S(1)} %copy-done.3, f32[3,128,1024]{2,1,0:T(8,128)S(1)} %copy-done), custom_call_target="tpu_custom_call" | custom-call | flops 2621440 | bytes 5767168 | tf_op jit(solution)/shard_map/prepare_points/pallas_call | solution.py:52
  18.6 0.0 collective-permute-done.2.left_ref
  18.6 0.0 collective-permute-done.3.right_ref
  18.6 0.0 collective-permute-done.before_ref
  18.7 0.9 %collective-permute-done.1.after_ref = f32[6,2,8,256]{3,2,1,0:T(8,128)S(1)} collective-permute-done((f32[6,2,8,256]{3,2,1,0:T(8,128)S(1)}, f32[6,2,8,256]{3,2,1,0:T(8,128)S(1)}, u32[]{:S(2)}, u32[]{:S(2)}) %collective-permute-start.1) | collective-permute-done | bytes 98336 | tf_op jit(solution)/shard_map/ppermute | solution.py:312
  19.6 0.0 copy-done.1
  19.6 0.0 copy-done.4
  19.6 0.0 copy-done.2
  19.6 0.0 copy-done.5
  19.6 0.0 copy-done.6
  19.6 0.0 copy-done.7
  19.7 5.9 %section_and_disk.1 = (f32[3,4,8,256]{3,2,1,0:T(8,128)}, f32[4,8,256]{2,1,0:T(8,128)}, f32[4,8,256]{2,1,0:T(8,128)}, f32[128,768]{1,0:T(8,128)S(1)}) custom-call(s32[64]{0:T(128)S(1)} %bitcast.25, f32[3,4,8,256]{3,2,1,0:T(8,128)S(1)} %copy-done.2, f32[4,8,256]{2,1,0:T(8,128)S(1)} %copy-done.4, f32[4,8,256]{2,1,0:T(8,128)S(1)} %copy-done.5, ...), custom_call_target="tpu_custom_call" | custom-call | tf_op jit(solution)/shard_map/section_and_disk/pallas_call | solution.py:268
  25.5 0.1 reshape.11
  25.6 40.5 %all_to_all.5 = f32[32,4,768]{2,1,0:T(4,128)S(1)} all-to-all(f32[32,4,768]{2,1,0:T(4,128)S(1)} %reshape.11), channel_id=1, replica_groups=mesh['stream'=4,'girth'=8] {'stream','girth'}, dimensions={0} | all-to-all | bytes 786432 | tf_op jit(solution)/shard_map/all_to_all | solution.py:333
  66.2 0.7 %reduce_sum.9 = f32[4,768]{1,0:T(4,128)} reduce(f32[32,4,768]{2,1,0:T(4,128)S(1)} %all_to_all.5, f32[]{:T(128)} %constant.1.clone.1), dimensions={0}, to_apply=%region_0.0 | reduce | flops 95232 | bytes 405508 | tf_op jit(solution)/shard_map/reduce_sum | solution.py:340
  (7 shorter events, 0.1 us)
Async XLA Ops:
  0.6 19.0 %copy-start.1 = (f32[1024,256]{1,0:T(8,128)S(1)}, f32[1024,256]{1,0:T(8,128)}, u32[]{:S(2)}) copy-start(f32[1024,256]{1,0:T(8,128)} %constant.4.clone.table_ref) | copy-start | bytes 3145732
  0.6 19.0 %copy-start.4 = (f32[4,8,256]{2,1,0:T(8,128)S(1)}, f32[4,8,256]{2,1,0:T(8,128)}, u32[]{:S(2)}) copy-start(f32[4,8,256]{2,1,0:T(8,128)} %p_ref.1) | copy-start | bytes 98308
  0.7 19.0 %copy-start.2 = (f32[3,4,8,256]{3,2,1,0:T(8,128)S(1)}, f32[3,4,8,256]{3,2,1,0:T(8,128)}, u32[]{:S(2)}) copy-start(f32[3,4,8,256]{3,2,1,0:T(8,128)} %vel_ref.1) | copy-start | bytes 294916
  0.7 19.0 %copy-start.5 = (f32[4,8,256]{2,1,0:T(8,128)S(1)}, f32[4,8,256]{2,1,0:T(8,128)}, u32[]{:S(2)}) copy-start(f32[4,8,256]{2,1,0:T(8,128)} %k_ref.1) | copy-start | bytes 98308
  3.4 15.2 %collective-permute-start.2 = (f32[6,4,2,256]{3,2,1,0:T(2,128)S(1)}, f32[6,4,2,256]{3,2,1,0:T(2,128)S(1)}, u32[]{:S(2)}, u32[]{:S(2)}) collective-permute-start(f32[6,4,2,256]{3,2,1,0:T(2,128)S(1)} %pad_maximum_fusion.2), channel_id=1, source_target_pairs={{0,1},{1,2},{2,3},{3,4},{4,5},{5,6},{6,7},{8,9},{9,10},{10,11},{11... | collective-permute-start | bytes 147464 | tf_op jit(solution)/shard_map/ppermute | solution.py:312
  8.2 10.5 %collective-permute-start = (f32[6,2,8,256]{3,2,1,0:T(8,128)S(1)}, f32[6,2,8,256]{3,2,1,0:T(8,128)S(1)}, u32[]{:S(2)}, u32[]{:S(2)}) collective-permute-start(f32[6,2,8,256]{3,2,1,0:T(8,128)S(1)} %pad_maximum_fusion), channel_id=1, source_target_pairs={{0,8},{8,16},{16,24},{1,9},{9,17},{17,25},{2,10},{10,18},{18,26},{... | collective-permute-start | bytes 294920 | tf_op jit(solution)/shard_map/ppermute | solution.py:312
  12.5 7.1 %collective-permute-start.1 = (f32[6,2,8,256]{3,2,1,0:T(8,128)S(1)}, f32[6,2,8,256]{3,2,1,0:T(8,128)S(1)}, u32[]{:S(2)}, u32[]{:S(2)}) collective-permute-start(f32[6,2,8,256]{3,2,1,0:T(8,128)S(1)} %pad_maximum_fusion.1), channel_id=1, source_target_pairs={{8,0},{16,8},{24,16},{9,1},{17,9},{25,17},{10,2},{18,10},{26,18},{... | collective-permute-start | bytes 294920 | tf_op jit(solution)/shard_map/ppermute | solution.py:312
  13.8 4.8 %collective-permute-start.3 = (f32[6,4,2,256]{3,2,1,0:T(2,128)S(1)}, f32[6,4,2,256]{3,2,1,0:T(2,128)S(1)}, u32[]{:S(2)}, u32[]{:S(2)}) collective-permute-start(f32[6,4,2,256]{3,2,1,0:T(2,128)S(1)} %pad_maximum_fusion.3), channel_id=1, source_target_pairs={{1,0},{2,1},{3,2},{4,3},{5,4},{6,5},{7,6},{9,8},{10,9},{11,10},{12... | collective-permute-start | bytes 147464 | tf_op jit(solution)/shard_map/ppermute | solution.py:312
  15.1 1.4 %copy-start = (f32[3,128,1024]{2,1,0:T(8,128)S(1)}, f32[3,128,1024]{2,1,0:T(8,128)}, u32[]{:S(2)}) copy-start(f32[3,128,1024]{2,1,0:T(8,128)} %frac_ref.1) | copy-start | bytes 4718596
  16.5 1.0 %copy-start.3 = (s32[128,1024]{1,0:T(8,128)S(1)}, s32[128,1024]{1,0:T(8,128)}, u32[]{:S(2)}) copy-start(s32[128,1024]{1,0:T(8,128)} %ids_ref.1) | copy-start | bytes 1572868
  17.6 2.0 %copy-start.6 = (f32[4,8,256]{2,1,0:T(8,128)S(1)}, f32[4,8,256]{2,1,0:T(8,128)}, u32[]{:S(2)}) copy-start(f32[4,8,256]{2,1,0:T(8,128)} %w_ref.1) | copy-start | bytes 98308
  17.6 2.1 %copy-start.7 = (s32[64,1]{0,1:T(1,128)S(1)}, s32[64,1]{0,1:T(1,128)}, u32[]{:S(2)}) copy-start(s32[64,1]{0,1:T(1,128)} %param.14) | copy-start | bytes 772

commit v2 on v1

--- a/solution.py
+++ b/solution.py
@@ -20,49 +20,178 @@
 
 LANES = 128
 ROWS = 8
+SHIFT = 10
+CHUNK = 64
 VMEM_LIMIT = 48 * 1024 * 1024
 
 
-def prepare_kernel(cells_s, cells_g, cells_r, ids_ref, frac_ref, q_ref, fr_ref, xg_ref, hs_ref):
+def pack_kernel(vel_ref, p_ref, k_ref, w_ref, last_ref, first_ref, right_ref, left_ref):
+    cells_s, cells_g, _ = p_ref.shape
+    for f in range(6):
+        own = vel_ref.at[f] if f < 3 else (p_ref, k_ref, w_ref)[f - 3]
+        last_ref[f] = own[cells_s - 2 : cells_s]
+        first_ref[f] = own[0:2]
+        right_ref[f] = own[:, cells_g - 2 : cells_g, :]
+        left_ref[f] = own[:, 0:2, :]
+
+
+def pack(velocity, pressure, energy, rate):
+    _, cells_s, cells_g, cells_r = velocity.shape
+    stream = jax.ShapeDtypeStruct((6, 2, cells_g, cells_r), jnp.float32)
+    girth = jax.ShapeDtypeStruct((6, cells_s, 2, cells_r), jnp.float32)
+    return pl.pallas_call(
+        pack_kernel, out_shape=(stream, stream, girth, girth), name="pack_halos"
+    )(velocity, pressure, energy, rate)
+
+
+def prepare_kernel(
+    cells_s,
+    cells_g,
+    cells_r,
+    owner_ref,
+    ids_ref,
+    frac_ref,
+    table_ref,
+    key_ref,
+    fr_ref,
+    xs_ref,
+    xg_ref,
+    moves_ref,
+    chosen_ref,
+    count_ref,
+    all_key,
+    all_fr,
+    all_xs,
+    all_xg,
+    keys,
+    frs,
+    xss,
+    xgs,
+):
     stream_first = lax.axis_index("stream") * cells_s
+    me = lax.axis_index("girth")
     plane_cells = cells_g * cells_r
+    sectors = owner_ref.shape[0]
     azimuths = ids_ref.shape[1]
+    width = azimuths // sectors
+    halves, rows, _ = fr_ref.shape
+    pad = moves_ref.shape[1] - rows
+    steps = (rows - 1).bit_length()
     for block in range(azimuths // LANES):
         cols = pl.ds(block * LANES, LANES)
         ids = ids_ref[:, cols].T
-        fs = frac_ref[0, :, cols].T
-        fg = frac_ref[1, :, cols].T
-        fr = frac_ref[2, :, cols].T
         stream_cell = ids // plane_cells
         remainder = ids - stream_cell * plane_cells
         girth_cell = remainder // cells_r
-        q_ref[cols, :] = remainder - girth_cell * cells_r
-        fr_ref[cols, :] = fr
-        xg_ref[cols, :] = girth_cell.astype(jnp.float32) + fg
+        all_key[cols, :] = (remainder - girth_cell * cells_r) << SHIFT
+        all_fr[cols, :] = frac_ref[2, :, cols].T
+        all_xg[cols, :] = girth_cell.astype(jnp.float32) + frac_ref[1, :, cols].T
         local = stream_cell - stream_first
-        for layer in range(cells_s):
-            hs_ref[layer, cols, :] = jnp.where(
-                local == layer, 1.0 - fs, jnp.where(local == layer - 1, fs, 0.0)
-            )
-
-
-def prepare(corner_ids, fractions, cells_s, cells_g, cells_r):
+        all_xs[cols, :] = local.astype(jnp.float32) + frac_ref[0, :, cols].T
+
+    chosen_ref[...] = jnp.zeros_like(chosen_ref)
+    keys[...] = jnp.zeros_like(keys)
+    frs[0] = jnp.zeros_like(frs[0])
+    xgs[0] = jnp.zeros_like(xgs[0])
+    xss[0] = jnp.full_like(xss[0], -2.0)
+
+    def sector(number, count):
+        mine = owner_ref[number] == me
+
+        @pl.when(mine)
+        def _():
+            source = pl.ds(pl.multiple_of(number * width, width), width)
+            target = pl.ds(pl.multiple_of(count * width, width), width)
+            chosen_ref[target, :] = table_ref[source, :]
+            keys[0, target, :] = all_key[source, :]
+            frs[0, target, :] = all_fr[source, :]
+            xss[0, target, :] = all_xs[source, :]
+            xgs[0, target, :] = all_xg[source, :]
+
+        return count + mine.astype(jnp.int32)
+
+    lax.fori_loop(0, sectors, sector, jnp.int32(0))
+
+    held = pl.ds(0, rows)
+    earlier = lax.broadcasted_iota(jnp.int32, (rows, rows), 0) > lax.broadcasted_iota(
+        jnp.int32, (rows, rows), 1
+    )
+    earlier = earlier.astype(jnp.float32).astype(jnp.bfloat16)
+    xs = xss[0, held, :]
+    touched = (xs > -1.0) & (xs < float(cells_s))
+    fresh = keys[0, held, :]
+    for half in range(halves):
+        first = half * LANES << SHIFT
+        kept = touched & (fresh >= first) & (fresh < first + (LANES << SHIFT))
+        skipped = jnp.where(kept, 0.0, 1.0)
+        before = jnp.dot(
+            earlier, skipped.astype(jnp.bfloat16), preferred_element_type=jnp.float32
+        ).astype(jnp.int32)
+        counts = rows - jnp.sum(skipped, axis=0, keepdims=True).astype(jnp.int32)
+        count_ref[half] = jnp.max(counts)
+        moves_ref[half, 0:pad, :] = jnp.zeros((pad, LANES), jnp.int32)
+        moves_ref[half, pad : pad + rows, :] = jnp.where(kept, 1 << steps, 0)
+        keys[1, held, :] = fresh + jnp.where(kept, before, 0)
+        for step in range(steps):
+            bit = 1 << step
+            a, b = (1, 2) if step % 2 == 0 else (2, 1)
+            data = 0 if step == 0 else a
+            last = step == steps - 1
+            for at in range(0, rows, CHUNK):
+                here, there = pl.ds(at, CHUNK), pl.ds(at + bit, CHUNK)
+                key, arriving = keys[a, here, :], keys[a, there, :]
+                moved = (arriving & bit) != 0
+                target = pl.ds(pad + at, CHUNK)
+                moves_ref[half, target, :] = moves_ref[half, target, :] | jnp.where(moved, bit, 0)
+                stays = jnp.where((key & bit) != 0, key & -(1 << SHIFT), key)
+                key = jnp.where(moved, arriving, stays)
+                out = [jnp.where(moved, r[data, there, :], r[data, here, :]) for r in (frs, xss, xgs)]
+                if last:
+                    key_ref[half, here, :] = key >> SHIFT
+                    fr_ref[half, here, :] = out[0]
+                    xs_ref[half, here, :] = out[1]
+                    xg_ref[half, here, :] = out[2]
+                else:
+                    keys[b, here, :] = key
+                    frs[b, here, :] = out[0]
+                    xss[b, here, :] = out[1]
+                    xgs[b, here, :] = out[2]
+
+
+def prepare(owners, corner_ids, fractions, table, cells, girth_count):
+    cells_s, cells_g, cells_r = cells
     radii, azimuths = corner_ids.shape
+    sectors = owners.shape[0]
+    rows = 3 * sectors // girth_count * (azimuths // sectors)
+    halves = cells_r // LANES
+    pad = 1 << ((rows - 1).bit_length() - 1)
     shape = jax.ShapeDtypeStruct
+    lists = (halves, rows, radii)
+    vmem = pl.BlockSpec(memory_space=pltpu.VMEM)
+    smem = pl.BlockSpec(memory_space=pltpu.SMEM)
     return pl.pallas_call(
         functools.partial(prepare_kernel, cells_s, cells_g, cells_r),
         out_shape=(
-            shape((azimuths, radii), jnp.int32),
-            shape((azimuths, radii), jnp.float32),
-            shape((azimuths, radii), jnp.float32),
-            shape((cells_s, azimuths, radii), jnp.float32),
-        ),
+            shape(lists, jnp.int32),
+            shape(lists, jnp.float32),
+            shape(lists, jnp.float32),
+            shape(lists, jnp.float32),
+            shape((halves, pad + rows, radii), jnp.int32),
+            shape((rows, 2 * NH), jnp.float32),
+            shape((halves,), jnp.int32),
+        ),
+        in_specs=[smem, vmem, vmem, vmem],
+        out_specs=[vmem] * 6 + [smem],
+        scratch_shapes=[pltpu.VMEM((azimuths, radii), jnp.int32)]
+        + [pltpu.VMEM((azimuths, radii), jnp.float32)] * 3
+        + [pltpu.VMEM((3, rows + pad, radii), jnp.int32)]
+        + [pltpu.VMEM((3, rows + pad, radii), jnp.float32)] * 3,
         compiler_params=pltpu.CompilerParams(vmem_limit_bytes=VMEM_LIMIT),
         cost_estimate=pl.CostEstimate(
             flops=20 * radii * azimuths, bytes_accessed=44 * radii * azimuths, transcendentals=0
         ),
         name="prepare_points",
-    )(corner_ids, fractions)
+    )(owners, corner_ids, fractions, table)
 
 
 def radial(values, amount, fill):
@@ -143,8 +272,28 @@
     return updated, own[4] + time_step * energy, own[5] + time_step * rate
 
 
+def girth_sums(parts):
+    row = lax.broadcasted_iota(jnp.int32, parts[0].shape, 0)
+
+    def swapped(values, distance):
+        up = pltpu.roll(values, distance, 0)
+        if 2 * distance == ROWS:
+            return up
+        return jnp.where((row & distance) != 0, up, pltpu.roll(values, ROWS - distance, 0))
+
+    distance = ROWS // 2
+    while distance > 0:
+        low = (row & distance) == 0
+        parts = [
+            jnp.where(low, x, y) + swapped(jnp.where(low, y, x), distance)
+            for x, y in zip(parts[:distance], parts[distance:])
+        ]
+        distance //= 2
+    return parts[0]
+
+
 def section_kernel(
-    owner_ref,
+    count_ref,
     vel_ref,
     p_ref,
     k_ref,
@@ -153,11 +302,12 @@
     after_ref,
     left_ref,
     right_ref,
-    q_ref,
+    key_ref,
     fr_ref,
+    xs_ref,
     xg_ref,
-    hs_ref,
-    table_ref,
+    moves_ref,
+    chosen_ref,
     new_vel_ref,
     new_k_ref,
     new_w_ref,
@@ -166,14 +316,13 @@
     visc_ref,
     field_ref,
     slope_ref,
+    value_ref,
     disk_ref,
-    chosen_ref,
 ):
-    cells_s, cells_g, cells_r = p_ref.shape
-    halves = cells_r // LANES
-    sectors = owner_ref.shape[0]
-    width = q_ref.shape[0] // sectors
-    me = lax.axis_index("girth")
+    cells_s, cells_g, _ = p_ref.shape
+    halves, rows, _ = fr_ref.shape
+    pad = moves_ref.shape[1] - rows
+    steps = (rows - 1).bit_length()
 
     own = [vel_ref[0], vel_ref[1], vel_ref[2], p_ref[...], k_ref[...], w_ref[...]]
     six = range(6)
@@ -193,56 +342,61 @@
         slope = radial(updated[c], 1, 0.0) - updated[c]
         for h in range(halves):
             lanes = slice(h * LANES, (h + 1) * LANES)
-            field_ref[c, :, h] = updated[c][:, :, lanes]
-            slope_ref[c, :, h] = slope[:, :, lanes]
-
-    disk_ref[...] = jnp.zeros_like(disk_ref)
-    chosen_ref[...] = jnp.zeros_like(chosen_ref)
+            field_ref[h, c] = updated[c][:, :, lanes]
+            slope_ref[h, c] = slope[:, :, lanes]
+
     girth_row = lax.broadcasted_iota(jnp.int32, (cells_g, LANES), 0).astype(jnp.float32)
 
-    def pick(ref, c, s, index, half_of):
-        out = None
-        for h in range(halves):
-            got = jnp.take_along_axis(ref[c, s, h], index, axis=1, mode="promise_in_bounds")
-            out = got if out is None else jnp.where(half_of[h], got, out)
-        return out
+    def pick(table, index):
+        return jnp.take_along_axis(table, index, axis=1, mode="promise_in_bounds")
 
     def spread(row):
         return jnp.broadcast_to(row, (cells_g, LANES))
 
-    def eight(source, target):
-        rows = pl.ds(pl.multiple_of(source, ROWS), ROWS)
-        q8, fr8, xg8 = q_ref[rows, :], fr_ref[rows, :], xg_ref[rows, :]
-        hs8 = [hs_ref[s, rows, :] for s in range(cells_s)]
-        for j in range(ROWS):
-            q = spread(q8[j : j + 1])
-            fr = spread(fr8[j : j + 1])
-            hg = jnp.maximum(1.0 - jnp.abs(spread(xg8[j : j + 1]) - girth_row), 0.0)
-            hs = [spread(hs8[s][j : j + 1]) for s in range(cells_s)]
-            index = q % LANES
-            half_of = [q >= h * LANES for h in range(halves)]
+    for half in range(halves):
+
+        def eight(group, carry):
+            at = pl.multiple_of(group * ROWS, ROWS)
+            here = pl.ds(at, ROWS)
+            q8, fr8, xg8, xs8 = (r[half, here, :] for r in (key_ref, fr_ref, xg_ref, xs_ref))
+            index8 = q8 % LANES
+            hs8 = [jnp.maximum(1.0 - jnp.abs(xs8 - float(s)), 0.0) for s in range(cells_s)]
+            sums = [[], [], []]
+            for j in range(ROWS):
+                one = slice(j, j + 1)
+                fr, index = spread(fr8[one]), spread(index8[one])
+                hg = jnp.maximum(1.0 - jnp.abs(spread(xg8[one]) - girth_row), 0.0)
+                hs = [spread(hs8[s][one]) for s in range(cells_s)]
+                for c in range(3):
+                    total = None
+                    for s in range(cells_s):
+                        value = pick(field_ref[half, c, s], index)
+                        value = hs[s] * (value + fr * pick(slope_ref[half, c, s], index))
+                        total = value if total is None else total + value
+                    sums[c].append(hg * total)
             for c in range(3):
-                total = None
-                for s in range(cells_s):
-                    value = pick(field_ref, c, s, index, half_of)
-                    value = value + fr * pick(slope_ref, c, s, index, half_of)
-                    total = hs[s] * value if total is None else total + hs[s] * value
-                disk_ref[c, pl.ds(target + j, 1), :] = jnp.sum(hg * total, axis=0, keepdims=True)
-
-    def sector(number, count):
-        mine = owner_ref[number] == me
-
-        @pl.when(mine)
-        def _():
-            source = pl.multiple_of(number * width, width)
-            target = pl.multiple_of(count * width, width)
-            chosen_ref[pl.ds(target, width), :] = table_ref[pl.ds(source, width), :]
-            for part in range(width // ROWS):
-                eight(source + part * ROWS, target + part * ROWS)
-
-        return count + mine.astype(jnp.int32)
-
-    lax.fori_loop(0, sectors, sector, jnp.int32(0))
+                value_ref[0, c, pl.ds(pad + at, ROWS), :] = girth_sums(sums[c])
+            return carry
+
+        lax.fori_loop(0, (count_ref[half] + ROWS - 1) // ROWS, eight, jnp.int32(0))
+
+        for step in reversed(range(steps)):
+            bit = 1 << step
+            a, b = (0, 1) if (steps - 1 - step) % 2 == 0 else (1, 0)
+            for at in range(0, rows, CHUNK):
+                here, there = pl.ds(pad + at, CHUNK), pl.ds(pad + at - bit, CHUNK)
+                moved = (moves_ref[half, there, :] & bit) != 0
+                if step == 0:
+                    kept = moves_ref[half, here, :] >= 1 << steps
+                for c in range(3):
+                    value = jnp.where(moved, value_ref[a, c, there, :], value_ref[a, c, here, :])
+                    if step > 0:
+                        value_ref[b, c, here, :] = value
+                    elif half == 0:
+                        disk_ref[c, pl.ds(at, CHUNK), :] = jnp.where(kept, value, 0.0)
+                    else:
+                        other = disk_ref[c, pl.ds(at, CHUNK), :]
+                        disk_ref[c, pl.ds(at, CHUNK), :] = jnp.where(kept, value, other)
 
     for c in range(3):
         harm_ref[:, c * 2 * NH : (c + 1) * 2 * NH] = lax.dot_general(
@@ -254,13 +408,10 @@
         )
 
 
-def section(
-    owners, velocity, pressure, energy, rate, before, after, left, right, points, table, girth_count
-):
+def section(velocity, pressure, energy, rate, before, after, left, right, points):
     _, cells_s, cells_g, cells_r = velocity.shape
-    azimuths, radii = points[0].shape
-    sectors = owners.shape[0]
-    columns = 3 * sectors // girth_count * (azimuths // sectors)
+    *lists, moves, chosen, counts = points
+    halves, rows, radii = lists[0].shape
     shape = functools.partial(jax.ShapeDtypeStruct, dtype=jnp.float32)
     scratch = lambda *dims: pltpu.VMEM(dims, jnp.float32)
     vmem = pl.BlockSpec(memory_space=pltpu.VMEM)
@@ -273,18 +424,18 @@
             shape(rate.shape),
             shape((radii, 6 * NH)),
         ),
-        in_specs=[smem] + [vmem] * 13,
+        in_specs=[smem] + [vmem] * 14,
         scratch_shapes=[
             scratch(6, cells_s, 3 * ROWS, cells_r),
             scratch(cells_s, 3 * ROWS, cells_r),
-            scratch(3, cells_s, cells_r // LANES, cells_g, LANES),
-            scratch(3, cells_s, cells_r // LANES, cells_g, LANES),
-            scratch(3, columns, radii),
-            scratch(columns, 2 * NH),
+            scratch(halves, 3, cells_s, cells_g, LANES),
+            scratch(halves, 3, cells_s, cells_g, LANES),
+            scratch(2, 3, moves.shape[1], radii),
+            scratch(3, rows, radii),
         ],
         compiler_params=pltpu.CompilerParams(vmem_limit_bytes=VMEM_LIMIT),
         name="section_and_disk",
-    )(owners, velocity, pressure, energy, rate, before, after, left, right, *points, table)
+    )(counts, velocity, pressure, energy, rate, before, after, left, right, *lists, moves, chosen)
 
 
 def fourier_table(azimuths, modes):
@@ -300,35 +451,25 @@
     stream_count, girth_count = lax.axis_size("stream"), lax.axis_size("girth")
     devices = stream_count * girth_count
 
-    def slab(dim, start):
-        def cut(values, at):
-            return lax.slice_in_dim(values, start, start + 2, axis=at)
-
-        scalars = [cut(x, dim)[None] for x in (pressure, kinetic_energy, dissipation_rate)]
-        return jnp.concatenate([cut(velocity, dim + 1)] + scalars, axis=0)
-
     def send(values, axis, count, step):
         pairs = [(i, i + step) for i in range(count) if 0 <= i + step < count]
         return lax.ppermute(values, axis, pairs)
 
-    before = send(slab(0, cells_s - 2), "stream", stream_count, 1)
-    after = send(slab(0, 0), "stream", stream_count, -1)
-    left = send(slab(1, cells_g - 2), "girth", girth_count, 1)
-    right = send(slab(1, 0), "girth", girth_count, -1)
-    points = prepare(corner_ids, fractions, cells_s, cells_g, cells_r)
+    last, first, rightmost, leftmost = pack(velocity, pressure, kinetic_energy, dissipation_rate)
+    before = send(last, "stream", stream_count, 1)
+    after = send(first, "stream", stream_count, -1)
+    left = send(rightmost, "girth", girth_count, 1)
+    right = send(leftmost, "girth", girth_count, -1)
+    points = prepare(
+        sector_owner[:, 0],
+        corner_ids,
+        fractions,
+        fourier_table(azimuths, NH),
+        (cells_s, cells_g, cells_r),
+        girth_count,
+    )
     new_velocity, new_energy, new_rate, partial = section(
-        sector_owner[:, 0],
-        velocity,
-        pressure,
-        kinetic_energy,
-        dissipation_rate,
-        before,
-        after,
-        left,
-        right,
-        points,
-        fourier_table(azimuths, NH),
-        girth_count,
+        velocity, pressure, kinetic_energy, dissipation_rate, before, after, left, right, points
     )
     shares = lax.all_to_all(
         partial.reshape(devices, radii // devices, 6 * NH),

time: 66.9 us -> 52.7 us (0.79)
  blocking collectives: 40.5 us -> 25.3 us
  Pallas kernels: 6.89 us -> 12 us
  local copies, waits for them, and re-layouts: 7.65 us -> 4.45 us
  waiting for transfers between devices: 0.96 us -> 0.01 us
    all_to_all x1, blocking collectives: 40.5 us -> 25.3 us  [body(): lax.all_to_all(partial.reshape(devices, radii // devices, 6 * NH), ('stre...]
    pallas_call x1, Pallas kernels: 1.03 us -> 4.82 us  [prepare(): pl.pallas_call(functools.partial(prepare_kernel, cells_s, cells_g, cells_...]
    broadcast_in_dim x4 -> x0, local copies, waits for them, and re-layouts: 3.25 us -> none  [slab(): cut(x, dim)[None]]
    unnamed x16, local copies, waits for them, and re-layouts: 2.48 us -> 4.34 us
    slice x2 -> x0, local copies, waits for them, and re-layouts: 1.82 us -> none  [cut(): return lax.slice_in_dim(values, start, start + 2, axis=at)]
    pallas_call x0 -> x1, Pallas kernels: none -> 1.62 us  [pack(): pl.pallas_call(pack_kernel, out_shape=(stream, stream, girth, girth), nam...]
    ppermute x4, waiting for transfers between devices: 0.96 us -> 0.01 us  [send(): return lax.ppermute(values, axis, pairs)]
  transfers between devices with their start and end apart: 4 -> 4, of which waited for: 1 -> 0; matrix products, arithmetic and copies ran while one was open for 4% -> 0% of each run, Pallas kernels for 2% -> 9%
where the time goes in v2:
time: 52.7 us; the launch traced here: 52.2 us
  blocking collectives  25.3 us (48%)
  Pallas kernels  12 us (23%)
  starting transfers between devices  8.97 us (17%)
  local copies, waits for them, and re-layouts  4.45 us (8%)
  between operations  0.75 us (1%)
  other arithmetic  0.68 us (1%)
    all_to_all x1, blocking collectives, body(): lax.all_to_all(partial.reshape(devices, radii // devices, 6 * NH), ('stre...  25.3 us
    ppermute x4, starting transfers between devices, send(): return lax.ppermute(values, axis, pairs)  8.97 us
    pallas_call x1, Pallas kernels, section(): pl.pallas_call(section_kernel, out_shape=(shape(velocity.shape), shape(en...  5.57 us
    pallas_call x1, Pallas kernels, prepare(): pl.pallas_call(functools.partial(prepare_kernel, cells_s, cells_g, cells_...  4.82 us
    unnamed x16, local copies, waits for them, and re-layouts  4.34 us
    pallas_call x1, Pallas kernels, pack(): pl.pallas_call(pack_kernel, out_shape=(stream, stream, girth, girth), nam...  1.62 us
  transfers between devices with their start and end apart: 4, of which 0 were waited for; matrix products, arithmetic and copies ran while one was open for 0% of the time, Pallas kernels for 9%

profile of v2, /device:TPU:0, one launch (start us, length us, event | category | flops | bytes accessed | tf_op | source)
XLA Modules:
  0.0 52.2 jit_solution(3718174181285438285)
XLA Ops:
  0.6 1.6 %pack_halos.1 = (f32[6,2,8,256]{3,2,1,0:T(8,128)}, f32[6,2,8,256]{3,2,1,0:T(8,128)}, f32[6,4,2,256]{3,2,1,0:T(2,128)}, f32[6,4,2,256]{3,2,1,0:T(2,128)}) custom-call(f32[3,4,8,256]{3,2,1,0:T(8,128)} %vel_ref.3, f32[4,8,256]{2,1,0:T(8,128)} %p_ref.3, f32[4,8,256]{2,1,0:T(8,128)} %k_ref.3, f32[4,8,256]{2,1,0:T(8,128)} %w_ref.3), custom_call_target="tpu_custom_call" | custom-call | tf_op jit(solution)/shard_map/pack_halos/pallas_call | solution.py:42
  2.3 4.9 %collective-permute-start = (f32[6,2,8,256]{3,2,1,0:T(8,128)}, f32[6,2,8,256]{3,2,1,0:T(8,128)S(1)}, u32[]{:S(2)}, u32[]{:S(2)}) collective-permute-start(f32[6,2,8,256]{3,2,1,0:T(8,128)} %get-tuple-element.20), channel_id=1, source_target_pairs={{0,8},{8,16},{16,24},{1,9},{9,17},{17,25},{2,10},{10,18},{18,26},{... | collective-permute-start | bytes 294920 | tf_op jit(solution)/shard_map/ppermute | solution.py:456
  7.2 1.3 %collective-permute-start.1 = (f32[6,2,8,256]{3,2,1,0:T(8,128)}, f32[6,2,8,256]{3,2,1,0:T(8,128)S(1)}, u32[]{:S(2)}, u32[]{:S(2)}) collective-permute-start(f32[6,2,8,256]{3,2,1,0:T(8,128)} %get-tuple-element.21), channel_id=1, source_target_pairs={{8,0},{16,8},{24,16},{9,1},{17,9},{25,17},{10,2},{18,10},{26,18},{... | collective-permute-start | bytes 294920 | tf_op jit(solution)/shard_map/ppermute | solution.py:456
  8.5 1.5 %collective-permute-start.2 = (f32[6,4,2,256]{3,2,1,0:T(2,128)}, f32[6,4,2,256]{3,2,1,0:T(2,128)S(1)}, u32[]{:S(2)}, u32[]{:S(2)}) collective-permute-start(f32[6,4,2,256]{3,2,1,0:T(2,128)} %get-tuple-element.22), channel_id=1, source_target_pairs={{0,1},{1,2},{2,3},{3,4},{4,5},{5,6},{6,7},{8,9},{9,10},{10,11},{11... | collective-permute-start | bytes 147464 | tf_op jit(solution)/shard_map/ppermute | solution.py:456
  9.9 1.3 %collective-permute-start.3 = (f32[6,4,2,256]{3,2,1,0:T(2,128)}, f32[6,4,2,256]{3,2,1,0:T(2,128)S(1)}, u32[]{:S(2)}, u32[]{:S(2)}) collective-permute-start(f32[6,4,2,256]{3,2,1,0:T(2,128)} %get-tuple-element.23), channel_id=1, source_target_pairs={{1,0},{2,1},{3,2},{4,3},{5,4},{6,5},{7,6},{9,8},{10,9},{11,10},{12... | collective-permute-start | bytes 147464 | tf_op jit(solution)/shard_map/ppermute | solution.py:456
  11.2 0.0 copy-start
  11.3 1.4 %copy-done = f32[3,128,1024]{2,1,0:T(8,128)S(1)} copy-done((f32[3,128,1024]{2,1,0:T(8,128)S(1)}, f32[3,128,1024]{2,1,0:T(8,128)}, u32[]{:S(2)}) %copy-start) | copy-done | bytes 1572888
  12.7 0.0 copy-start.1
  12.7 1.2 %copy-done.1 = f32[1024,256]{1,0:T(8,128)S(1)} copy-done((f32[1024,256]{1,0:T(8,128)S(1)}, f32[1024,256]{1,0:T(8,128)}, u32[]{:S(2)}) %copy-start.1) | copy-done | bytes 1048600
  13.9 0.0 copy-start.2
  13.9 1.0 %copy-done.2 = s32[128,1024]{1,0:T(8,128)S(1)} copy-done((s32[128,1024]{1,0:T(8,128)S(1)}, s32[128,1024]{1,0:T(8,128)}, u32[]{:S(2)}) %copy-start.2) | copy-done | bytes 524312
  14.9 0.0 copy-start.7
  14.9 0.7 %copy-done.7 = s32[64,1]{0,1:T(1,128)S(1)} copy-done((s32[64,1]{0,1:T(1,128)S(1)}, s32[64,1]{0,1:T(1,128)}, u32[]{:S(2)}) %copy-start.7) | copy-done | bytes 280
  15.6 0.0 copy-start.3
  15.6 0.0 copy-start.4
  15.6 0.0 copy-start.5
  15.6 0.0 copy-start.6
  15.6 4.8 %prepare_points.1 = (s32[2,384,128]{2,1,0:T(8,128)S(1)}, f32[2,384,128]{2,1,0:T(8,128)S(1)}, f32[2,384,128]{2,1,0:T(8,128)S(1)}, f32[2,384,128]{2,1,0:T(8,128)S(...) custom-call(s32[64]{0:T(128)S(1)} %bitcast.1, s32[128,1024]{1,0:T(8,128)S(1)} %copy-done.2, ...), custom_call_target="tpu_custom_call" | custom-call | flops 2621440 | bytes 5767168 | tf_op jit(solution)/shard_map/prepare_points/pallas_call | solution.py:172
  20.4 0.0 collective-permute-done.2.left_ref
  20.4 0.0 collective-permute-done.3.right_ref
  20.4 0.0 collective-permute-done.before_ref
  20.5 0.0 collective-permute-done.1.after_ref
  20.5 0.0 copy-done.3
  20.5 0.0 copy-done.4
  20.5 0.0 copy-done.5
  20.5 0.0 copy-done.6
  20.5 5.6 %section_and_disk.1 = (f32[3,4,8,256]{3,2,1,0:T(8,128)}, f32[4,8,256]{2,1,0:T(8,128)}, f32[4,8,256]{2,1,0:T(8,128)}, f32[128,768]{1,0:T(8,128)S(1)}) custom-call(s32[2]{0:T(128)S(1)} %get-tuple-element.19.count_ref, f32[3,4,8,256]{3,2,1,0:T(8,128)S(1)} %copy-done.3, f32[4,8,256]{2,1,0:T(8,128)S(1)} %copy-done.4, f32[4,8,256]{2,1,0:T(8,128)S(1)} %copy-done.5, ...), custom_call_target="tpu_custom_call" | custom-call | tf_op jit(solution)/shard_map/section_and_disk/pallas_call | solution.py:419
  26.1 0.1 reshape.11
  26.2 25.3 %all_to_all.5 = f32[32,4,768]{2,1,0:T(4,128)S(1)} all-to-all(f32[32,4,768]{2,1,0:T(4,128)S(1)} %reshape.11), channel_id=1, replica_groups=mesh['stream'=4,'girth'=8] {'stream','girth'}, dimensions={0} | all-to-all | bytes 786432 | tf_op jit(solution)/shard_map/all_to_all | solution.py:474
  51.5 0.7 %reduce_sum.9 = f32[4,768]{1,0:T(4,128)} reduce(f32[32,4,768]{2,1,0:T(4,128)S(1)} %all_to_all.5, f32[]{:T(128)} %constant.1.clone.1), dimensions={0}, to_apply=%region_0.0 | reduce | flops 95232 | bytes 405508 | tf_op jit(solution)/shard_map/reduce_sum | solution.py:481
Async XLA Ops:
  2.3 18.2 %collective-permute-start = (f32[6,2,8,256]{3,2,1,0:T(8,128)}, f32[6,2,8,256]{3,2,1,0:T(8,128)S(1)}, u32[]{:S(2)}, u32[]{:S(2)}) collective-permute-start(f32[6,2,8,256]{3,2,1,0:T(8,128)} %get-tuple-element.20), channel_id=1, source_target_pairs={{0,8},{8,16},{16,24},{1,9},{9,17},{17,25},{2,10},{10,18},{18,26},{... | collective-permute-start | bytes 294920 | tf_op jit(solution)/shard_map/ppermute | solution.py:456
  7.2 13.3 %collective-permute-start.1 = (f32[6,2,8,256]{3,2,1,0:T(8,128)}, f32[6,2,8,256]{3,2,1,0:T(8,128)S(1)}, u32[]{:S(2)}, u32[]{:S(2)}) collective-permute-start(f32[6,2,8,256]{3,2,1,0:T(8,128)} %get-tuple-element.21), channel_id=1, source_target_pairs={{8,0},{16,8},{24,16},{9,1},{17,9},{25,17},{10,2},{18,10},{26,18},{... | collective-permute-start | bytes 294920 | tf_op jit(solution)/shard_map/ppermute | solution.py:456
  8.5 11.9 %collective-permute-start.2 = (f32[6,4,2,256]{3,2,1,0:T(2,128)}, f32[6,4,2,256]{3,2,1,0:T(2,128)S(1)}, u32[]{:S(2)}, u32[]{:S(2)}) collective-permute-start(f32[6,4,2,256]{3,2,1,0:T(2,128)} %get-tuple-element.22), channel_id=1, source_target_pairs={{0,1},{1,2},{2,3},{3,4},{4,5},{5,6},{6,7},{8,9},{9,10},{10,11},{11... | collective-permute-start | bytes 147464 | tf_op jit(solution)/shard_map/ppermute | solution.py:456
  9.9 10.5 %collective-permute-start.3 = (f32[6,4,2,256]{3,2,1,0:T(2,128)}, f32[6,4,2,256]{3,2,1,0:T(2,128)S(1)}, u32[]{:S(2)}, u32[]{:S(2)}) collective-permute-start(f32[6,4,2,256]{3,2,1,0:T(2,128)} %get-tuple-element.23), channel_id=1, source_target_pairs={{1,0},{2,1},{3,2},{4,3},{5,4},{6,5},{7,6},{9,8},{10,9},{11,10},{12... | collective-permute-start | bytes 147464 | tf_op jit(solution)/shard_map/ppermute | solution.py:456
  11.2 1.4 %copy-start = (f32[3,128,1024]{2,1,0:T(8,128)S(1)}, f32[3,128,1024]{2,1,0:T(8,128)}, u32[]{:S(2)}) copy-start(f32[3,128,1024]{2,1,0:T(8,128)} %frac_ref.1) | copy-start | bytes 4718596
  12.7 1.2 %copy-start.1 = (f32[1024,256]{1,0:T(8,128)S(1)}, f32[1024,256]{1,0:T(8,128)}, u32[]{:S(2)}) copy-start(f32[1024,256]{1,0:T(8,128)} %constant.4.clone.table_ref) | copy-start | bytes 3145732
  13.9 1.0 %copy-start.2 = (s32[128,1024]{1,0:T(8,128)S(1)}, s32[128,1024]{1,0:T(8,128)}, u32[]{:S(2)}) copy-start(s32[128,1024]{1,0:T(8,128)} %ids_ref.1) | copy-start | bytes 1572868
  14.9 0.7 %copy-start.7 = (s32[64,1]{0,1:T(1,128)S(1)}, s32[64,1]{0,1:T(1,128)}, u32[]{:S(2)}) copy-start(s32[64,1]{0,1:T(1,128)} %param.14) | copy-start | bytes 772
  15.6 4.9 %copy-start.3 = (f32[3,4,8,256]{3,2,1,0:T(8,128)S(1)}, f32[3,4,8,256]{3,2,1,0:T(8,128)}, u32[]{:S(2)}) copy-start(f32[3,4,8,256]{3,2,1,0:T(8,128)} %vel_ref.3) | copy-start | bytes 294916
  15.6 4.9 %copy-start.4 = (f32[4,8,256]{2,1,0:T(8,128)S(1)}, f32[4,8,256]{2,1,0:T(8,128)}, u32[]{:S(2)}) copy-start(f32[4,8,256]{2,1,0:T(8,128)} %p_ref.3) | copy-start | bytes 98308
  15.6 4.9 %copy-start.5 = (f32[4,8,256]{2,1,0:T(8,128)S(1)}, f32[4,8,256]{2,1,0:T(8,128)}, u32[]{:S(2)}) copy-start(f32[4,8,256]{2,1,0:T(8,128)} %k_ref.3) | copy-start | bytes 98308
  15.6 4.9 %copy-start.6 = (f32[4,8,256]{2,1,0:T(8,128)S(1)}, f32[4,8,256]{2,1,0:T(8,128)}, u32[]{:S(2)}) copy-start(f32[4,8,256]{2,1,0:T(8,128)} %w_ref.3) | copy-start | bytes 98308

commit v3 on v2

v3 whole, which is shorter than its diff:
```python
import functools
import math

import jax
import jax.numpy as jnp
import numpy as np
from jax import lax
from jax.experimental import pallas as pl
from jax.experimental.pallas import tpu as pltpu
from jax.sharding import PartitionSpec as P

NH = 128

base_viscosity = 0.05
time_step = 0.2
beta_star = 0.09
beta_rate = 0.075
alpha_rate = 0.52
wall_rate = 1.0

LANES = 128
ROWS = 8
SHIFT = 10
CHUNK = 64
VMEM_LIMIT = 48 * 1024 * 1024


def pack_kernel(vel_ref, p_ref, k_ref, w_ref, *slabs):
    cells_s, cells_g, _ = p_ref.shape
    stream_odd = lax.axis_index("stream") % 2 == 1
    girth_odd = lax.axis_index("girth") % 2 == 1
    for f in range(6):
        own = vel_ref.at[f] if f < 3 else (p_ref, k_ref, w_ref)[f - 3]
        first, last = own[0:2], own[cells_s - 2 : cells_s]
        slabs[0][f] = jnp.where(stream_odd, first, last)
        slabs[1][f] = jnp.where(stream_odd, last, first)
        first, last = own[:, 0:2, :], own[:, cells_g - 2 : cells_g, :]
        slabs[2][f] = jnp.where(girth_odd, first, last)
        slabs[3][f] = jnp.where(girth_odd, last, first)


def pack(velocity, pressure, energy, rate):
    _, cells_s, cells_g, cells_r = velocity.shape
    stream = jax.ShapeDtypeStruct((6, 2, cells_g, cells_r), jnp.float32)
    girth = jax.ShapeDtypeStruct((6, cells_s, 2, cells_r), jnp.float32)
    return pl.pallas_call(
        pack_kernel, out_shape=(stream, stream, girth, girth), name="pack_halos"
    )(velocity, pressure, energy, rate)


def prepare_kernel(
    cells_s,
    cells_g,
    cells_r,
    owner_ref,
    ids_hbm,
    frac_hbm,
    table_hbm,
    q_ref,
    fr_ref,
    xs_ref,
    xg_ref,
    moves_ref,
    chosen_ref,
    count_ref,
    ids_ref,
    frac_ref,
    table_ref,
    all_q,
    all_fr,
    all_xs,
    all_xg,
    keys,
    frs,
    xss,
    xgs,
    arrived,
):
    copies = [pltpu.make_async_copy(ids_hbm, ids_ref, arrived.at[0])]
    for d in range(3):
        copies.append(pltpu.make_async_copy(frac_hbm.at[d], frac_ref.at[d], arrived.at[1 + d]))
    copies.append(pltpu.make_async_copy(table_hbm, table_ref, arrived.at[4]))
    for copy in copies:
        copy.start()
    stream_first = lax.axis_index("stream") * cells_s
    me = lax.axis_index("girth")
    plane_cells = cells_g * cells_r
    sectors = owner_ref.shape[0]
    azimuths = ids_ref.shape[1]
    width = azimuths // sectors
    rows = fr_ref.shape[0]
    pad = moves_ref.shape[0] - rows
    steps = (rows - 1).bit_length()

    keys[...] = jnp.zeros_like(keys)
    frs[0] = jnp.zeros_like(frs[0])
    xgs[0] = jnp.zeros_like(xgs[0])
    xss[0] = jnp.full_like(xss[0], -2.0)
    chosen_ref[...] = jnp.zeros_like(chosen_ref)
    moves_ref[0:pad, :] = jnp.zeros((pad, LANES), jnp.int32)

    blocks = [pl.ds(at, LANES) for at in range(0, azimuths, LANES)]
    copies[0].wait()
    for cols in blocks:
        ids = ids_ref[:, cols].T
        stream_cell = ids // plane_cells
        remainder = ids - stream_cell * plane_cells
        girth_cell = remainder // cells_r
        all_q[cols, :] = (remainder - girth_cell * cells_r) << SHIFT
        all_xg[cols, :] = girth_cell.astype(jnp.float32)
        all_xs[cols, :] = (stream_cell - stream_first).astype(jnp.float32)
    copies[1].wait()
    for cols in blocks:
        all_xs[cols, :] += frac_ref[0, :, cols].T
    copies[2].wait()
    for cols in blocks:
        all_xg[cols, :] += frac_ref[1, :, cols].T
    copies[3].wait()
    for cols in blocks:
        all_fr[cols, :] = frac_ref[2, :, cols].T
    copies[4].wait()

    def sector(number, count):
        mine = owner_ref[number] == me

        @pl.when(mine)
        def _():
            source = pl.ds(pl.multiple_of(number * width, width), width)
            target = pl.ds(pl.multiple_of(count * width, width), width)
            chosen_ref[target, :] = table_ref[source, :]
            keys[0, target, :] = all_q[source, :]
            frs[0, target, :] = all_fr[source, :]
            xss[0, target, :] = all_xs[source, :]
            xgs[0, target, :] = all_xg[source, :]

        return count + mine.astype(jnp.int32)

    lax.fori_loop(0, sectors, sector, jnp.int32(0))

    held = pl.ds(0, rows)
    earlier = lax.broadcasted_iota(jnp.int32, (rows, rows), 0) > lax.broadcasted_iota(
        jnp.int32, (rows, rows), 1
    )
    earlier = earlier.astype(jnp.float32).astype(jnp.bfloat16)
    xs = xss[0, held, :]
    kept = (xs > -1.0) & (xs < float(cells_s))
    skipped = jnp.where(kept, 0.0, 1.0)
    before = jnp.dot(
        earlier, skipped.astype(jnp.bfloat16), preferred_element_type=jnp.float32
    ).astype(jnp.int32)
    counts = rows - jnp.sum(skipped, axis=0, keepdims=True).astype(jnp.int32)
    count_ref[0] = jnp.max(counts)
    moves_ref[pad : pad + rows, :] = jnp.where(kept, 1 << steps, 0)
    keys[0, held, :] = keys[0, held, :] + jnp.where(kept, before, 0)
    for step in range(steps):
        bit = 1 << step
        a, b = step % 2, 1 - step % 2
        last = step == steps - 1
        for at in range(0, rows, CHUNK):
            here, there = pl.ds(at, CHUNK), pl.ds(at + bit, CHUNK)
            key, arriving = keys[a, here, :], keys[a, there, :]
            moved = (arriving & bit) != 0
            target = pl.ds(pad + at, CHUNK)
            moves_ref[target, :] = moves_ref[target, :] | jnp.where(moved, bit, 0)
            stays = jnp.where((key & bit) != 0, key & -(1 << SHIFT), key)
            key = jnp.where(moved, arriving, stays)
            out = [jnp.where(moved, r[a, there, :], r[a, here, :]) for r in (frs, xss, xgs)]
            if last:
                q_ref[here, :] = key >> SHIFT
                fr_ref[here, :] = out[0]
                xs_ref[here, :] = out[1]
                xg_ref[here, :] = out[2]
            else:
                keys[b, here, :] = key
                frs[b, here, :] = out[0]
                xss[b, here, :] = out[1]
                xgs[b, here, :] = out[2]


def prepare(owners, corner_ids, fractions, table, cells, girth_count):
    cells_s, cells_g, cells_r = cells
    radii, azimuths = corner_ids.shape
    sectors = owners.shape[0]
    rows = 3 * sectors // girth_count * (azimuths // sectors)
    pad = 1 << ((rows - 1).bit_length() - 1)
    shape = jax.ShapeDtypeStruct
    lists = (rows, radii)
    vmem = pl.BlockSpec(memory_space=pltpu.VMEM)
    smem = pl.BlockSpec(memory_space=pltpu.SMEM)
    hbm = pl.BlockSpec(memory_space=pl.ANY)
    return pl.pallas_call(
        functools.partial(prepare_kernel, cells_s, cells_g, cells_r),
        out_shape=(
            shape(lists, jnp.int32),
            shape(lists, jnp.float32),
            shape(lists, jnp.float32),
            shape(lists, jnp.float32),
            shape((pad + rows, radii), jnp.int32),
            shape((rows, 2 * NH), jnp.float32),
            shape((1,), jnp.int32),
        ),
        in_specs=[smem, hbm, hbm, hbm],
        out_specs=[vmem] * 6 + [smem],
        scratch_shapes=[
            pltpu.VMEM(corner_ids.shape, jnp.int32),
            pltpu.VMEM(fractions.shape, jnp.float32),
            pltpu.VMEM(table.shape, jnp.float32),
            pltpu.VMEM((azimuths, radii), jnp.int32),
        ]
        + [pltpu.VMEM((azimuths, radii), jnp.float32)] * 3
        + [pltpu.VMEM((2, rows + pad, radii), jnp.int32)]
        + [pltpu.VMEM((2, rows + pad, radii), jnp.float32)] * 3
        + [pltpu.SemaphoreType.DMA((5,))],
        compiler_params=pltpu.CompilerParams(vmem_limit_bytes=VMEM_LIMIT),
        cost_estimate=pl.CostEstimate(
            flops=20 * radii * azimuths, bytes_accessed=44 * radii * azimuths, transcendentals=0
        ),
        name="prepare_points",
    )(owners, corner_ids, fractions, table)


def radial(values, amount, fill):
    extent = values.shape[-1]
    rolled = pltpu.roll(values, (-amount) % extent, values.ndim - 1)
    position = lax.broadcasted_iota(jnp.int32, values.shape, values.ndim - 1) + amount
    return jnp.where((position >= 0) & (position < extent), rolled, fill)


def advance(own, before, after, left, right, ext_ref, visc_ref):
    cells_s, cells_g, _ = own[0].shape
    mid = ROWS

    def along_s(stack, amount):
        return stack[2 + amount : 2 + amount + cells_s]

    def along_g(ref, amount):
        return ref[:, mid + amount : mid + amount + cells_g, :]

    def viscosity(energy, rate):
        return base_viscosity + energy / (rate + wall_rate)

    stacks = [jnp.concatenate([before[f], own[f], after[f]], axis=0) for f in range(6)]
    for f in range(6):
        ext_ref[f, :, mid - 2 : mid, :] = left[f]
        ext_ref[f, :, mid : mid + cells_g, :] = own[f]
        ext_ref[f, :, mid + cells_g : mid + cells_g + 2, :] = right[f]
    middle = viscosity(own[4], own[5])
    visc_stack = viscosity(stacks[4], stacks[5])
    visc_ref[:, mid - 2 : mid, :] = viscosity(left[4], left[5])
    visc_ref[:, mid : mid + cells_g, :] = middle
    visc_ref[:, mid + cells_g : mid + cells_g + 2, :] = viscosity(right[4], right[5])
    faces = [
        (
            0.5 * (middle + along_s(visc_stack, 1)),
            0.5 * (middle + along_s(visc_stack, -1)),
        ),
        (
            0.5 * (middle + along_g(visc_ref, 1)),
            0.5 * (middle + along_g(visc_ref, -1)),
        ),
        (
            0.5 * (middle + radial(middle, 1, base_viscosity)),
            0.5 * (middle + radial(middle, -1, base_viscosity)),
        ),
    ]

    def neighbour(f, direction, amount):
        if direction == 0:
            return along_s(stacks[f], amount)
        if direction == 1:
            return along_g(ext_ref.at[f], amount)
        return radial(own[f], amount, 0.0)

    def terms(f, direction):
        up, down = neighbour(f, direction, 1), neighbour(f, direction, -1)
        far = neighbour(f, direction, 2) - neighbour(f, direction, -2)
        gradient = (8.0 * (up - down) - far) * (1.0 / 12.0)
        above, below = faces[direction]
        return gradient, above * (up - own[f]) - below * (own[f] - down)

    strain = None
    updated = []
    for f in range(3):
        change = -terms(3, f)[0]
        for direction in range(3):
            gradient, spread = terms(f, direction)
            strain = gradient * gradient if strain is None else strain + gradient * gradient
            change = change - own[direction] * gradient + spread
        updated.append(own[f] + time_step * change)
    energy = own[4] / (own[5] + wall_rate) * strain - beta_star * own[4] * own[5]
    rate = alpha_rate * strain - beta_rate * own[5] * own[5]
    for direction in range(3):
        gradient, spread = terms(4, direction)
        energy = energy - own[direction] * gradient + spread
        gradient, spread = terms(5, direction)
        rate = rate - own[direction] * gradient + spread
    return updated, own[4] + time_step * energy, own[5] + time_step * rate


def girth_sums(parts):
    row = lax.broadcasted_iota(jnp.int32, parts[0].shape, 0)

    def swapped(values, distance):
        up = pltpu.roll(values, distance, 0)
        if 2 * distance == ROWS:
            return up
        return jnp.where((row & distance) != 0, up, pltpu.roll(values, ROWS - distance, 0))

    distance = ROWS // 2
    while distance > 0:
        low = (row & distance) == 0
        parts = [
            jnp.where(low, x, y) + swapped(jnp.where(low, y, x), distance)
            for x, y in zip(parts[:distance], parts[distance:])
        ]
        distance //= 2
    return parts[0]


def section_kernel(
    count_ref,
    vel_ref,
    p_ref,
    k_ref,
    w_ref,
    stream_a,
    stream_b,
    girth_a,
    girth_b,
    q_ref,
    fr_ref,
    xs_ref,
    xg_ref,
    moves_ref,
    chosen_ref,
    new_vel_ref,
    new_k_ref,
    new_w_ref,
    harm_ref,
    ext_ref,
    visc_ref,
    field_ref,
    value_ref,
    disk_ref,
):
    cells_s, cells_g, cells_r = p_ref.shape
    rows = fr_ref.shape[0]
    pad = moves_ref.shape[0] - rows
    steps = (rows - 1).bit_length()
    stream_odd = lax.axis_index("stream") % 2 == 1
    girth_odd = lax.axis_index("girth") % 2 == 1

    own = [vel_ref[0], vel_ref[1], vel_ref[2], p_ref[...], k_ref[...], w_ref[...]]
    six = range(6)
    updated, energy, rate = advance(
        own,
        [jnp.where(stream_odd, stream_a[f], stream_b[f]) for f in six],
        [jnp.where(stream_odd, stream_b[f], stream_a[f]) for f in six],
        [jnp.where(girth_odd, girth_a[f], girth_b[f]) for f in six],
        [jnp.where(girth_odd, girth_b[f], girth_a[f]) for f in six],
        ext_ref,
        visc_ref,
    )
    new_k_ref[...] = energy
    new_w_ref[...] = rate

    def rounded(values):
        return values.astype(jnp.bfloat16).astype(jnp.float32)

    for c in range(3):
        new_vel_ref[c] = updated[c]
        slope = radial(updated[c], 1, 0.0) - updated[c]
        for kind, values in enumerate((updated[c], slope)):
            high = rounded(values)
            field_ref[c, :, 2 * kind] = high
            field_ref[c, :, 2 * kind + 1] = rounded(values - high)

    kinds = 4
    table = field_ref[...].reshape(3 * cells_s * kinds * cells_g, cells_r).astype(jnp.bfloat16)
    pair = 2 * LANES
    girth_row = lax.broadcasted_iota(jnp.int32, (cells_g, pair), 0).astype(jnp.float32)
    radial_row = lax.broadcasted_iota(jnp.int32, (cells_r, pair), 0)

    def two(values, j):
        return jnp.concatenate([values[j : j + 1], values[j + 1 : j + 2]], axis=1)

    def eight(group, carry):
        at = pl.multiple_of(group * ROWS, ROWS)
        here = pl.ds(at, ROWS)
        q8, fr8, xg8, xs8 = (r[here, :] for r in (q_ref, fr_ref, xg_ref, xs_ref))
        hs8 = [jnp.maximum(1.0 - jnp.abs(xs8 - float(s)), 0.0) for s in range(cells_s)]
        sums = [[], [], []]
        for j in range(0, ROWS, 2):
            hot = jnp.where(radial_row == two(q8, j), 1.0, 0.0).astype(jnp.bfloat16)
            got = jnp.dot(table, hot, preferred_element_type=jnp.float32)
            got = got.reshape(3, cells_s, kinds, cells_g, pair)
            fr = two(fr8, j)
            hg = jnp.maximum(1.0 - jnp.abs(two(xg8, j) - girth_row), 0.0)
            hs = [two(hs8[s], j) for s in range(cells_s)]
            for c in range(3):
                total = None
                for s in range(cells_s):
                    value = got[c, s, 0] + got[c, s, 1] + fr * (got[c, s, 2] + got[c, s, 3])
                    value = hs[s] * value
                    total = value if total is None else total + value
                total = hg * total
                sums[c] += [total[:, :LANES], total[:, LANES:]]
        for c in range(3):
            value_ref[0, c, pl.ds(pad + at, ROWS), :] = girth_sums(sums[c])
        return carry

    lax.fori_loop(0, (count_ref[0] + ROWS - 1) // ROWS, eight, jnp.int32(0))

    for step in reversed(range(steps)):
        bit = 1 << step
        a, b = (0, 1) if (steps - 1 - step) % 2 == 0 else (1, 0)
        for at in range(0, rows, CHUNK):
            here, there = pl.ds(pad + at, CHUNK), pl.ds(pad + at - bit, CHUNK)
            moved = (moves_ref[there, :] & bit) != 0
            if step == 0:
                kept = moves_ref[here, :] >= 1 << steps
            for c in range(3):
                value = jnp.where(moved, value_ref[a, c, there, :], value_ref[a, c, here, :])
                if step > 0:
                    value_ref[b, c, here, :] = value
                else:
                    disk_ref[c, pl.ds(at, CHUNK), :] = jnp.where(kept, value, 0.0)

    for c in range(3):
        harm_ref[:, c * 2 * NH : (c + 1) * 2 * NH] = lax.dot_general(
            disk_ref[c],
            chosen_ref[...],
            (((0,), (0,)), ((), ())),
            precision=lax.Precision.HIGHEST,
            preferred_element_type=jnp.float32,
        )


def section(velocity, pressure, energy, rate, halos, points):
    _, cells_s, cells_g, cells_r = velocity.shape
    *lists, moves, chosen, counts = points
    rows, radii = lists[0].shape
    shape = functools.partial(jax.ShapeDtypeStruct, dtype=jnp.float32)
    scratch = lambda *dims: pltpu.VMEM(dims, jnp.float32)
    vmem = pl.BlockSpec(memory_space=pltpu.VMEM)
    smem = pl.BlockSpec(memory_space=pltpu.SMEM)
    return pl.pallas_call(
        section_kernel,
        out_shape=(
            shape(velocity.shape),
            shape(energy.shape),
            shape(rate.shape),
            shape((radii, 6 * NH)),
        ),
        in_specs=[smem] + [vmem] * 14,
        scratch_shapes=[
            scratch(6, cells_s, 3 * ROWS, cells_r),
            scratch(cells_s, 3 * ROWS, cells_r),
            scratch(3, cells_s, 4, cells_g, cells_r),
            scratch(2, 3, moves.shape[0], radii),
            scratch(3, rows, radii),
        ],
        compiler_params=pltpu.CompilerParams(vmem_limit_bytes=VMEM_LIMIT),
        name="section_and_disk",
    )(counts, velocity, pressure, energy, rate, *halos, *lists, moves, chosen)


def fourier_table(azimuths, modes):
    phase = np.arange(azimuths)[:, None] * np.arange(modes)[None, :] % azimuths
    angles = phase * (2.0 * math.pi / azimuths)
    table = np.concatenate([np.cos(angles), -np.sin(angles)], axis=1) / math.sqrt(azimuths)
    return jnp.asarray(table.astype(np.float32))


def body(velocity, pressure, kinetic_energy, dissipation_rate, corner_ids, fractions, sector_owner):
    _, cells_s, cells_g, cells_r = velocity.shape
    radii, azimuths = corner_ids.shape
    stream_count, girth_count = lax.axis_size("stream"), lax.axis_size("girth")
    devices = stream_count * girth_count

    def swap(values, axis, count, start):
        pairs = []
        for i in range(start, count - 1, 2):
            pairs += [(i, i + 1), (i + 1, i)]
        return lax.ppermute(values, axis, pairs)

    slabs = pack(velocity, pressure, kinetic_energy, dissipation_rate)
    halos = (
        swap(slabs[0], "stream", stream_count, 0),
        swap(slabs[1], "stream", stream_count, 1),
        swap(slabs[2], "girth", girth_count, 0),
        swap(slabs[3], "girth", girth_count, 1),
    )
    points = prepare(
        sector_owner[:, 0],
        corner_ids,
        fractions,
        fourier_table(azimuths, NH),
        (cells_s, cells_g, cells_r),
        girth_count,
    )
    new_velocity, new_energy, new_rate, partial = section(
        velocity, pressure, kinetic_energy, dissipation_rate, halos, points
    )
    shares = lax.all_to_all(
        partial.reshape(devices, radii // devices, 6 * NH),
        ("stream", "girth"),
        split_axis=0,
        concat_axis=0,
        tiled=True,
    )
    return new_velocity, new_energy, new_rate, jnp.sum(shares, axis=0)


def solution(mesh):
    return jax.shard_map(
        body,
        mesh=mesh,
        in_specs=(
            P(None, "stream", "girth", None),
            P("stream", "girth", None),
            P("stream", "girth", None),
            P("stream", "girth", None),
            P(),
            P(),
            P(),
        ),
        out_specs=(
            P(None, "stream", "girth", None),
            P("stream", "girth", None),
            P("stream", "girth", None),
            P(("stream", "girth"), None),
        ),
        check_vma=False,
    )
```

time: 52.7 us -> 49.2 us (0.934)
  starting transfers between devices: 8.97 us -> 4.41 us
  blocking collectives: 25.3 us -> 27.1 us
  Pallas kernels: 12 us -> 11.3 us
    ppermute x4, starting transfers between devices: 8.97 us -> 4.41 us  [swap(): return lax.ppermute(values, axis, pairs)]
    all_to_all x1, blocking collectives: 25.3 us -> 27.1 us  [body(): lax.all_to_all(partial.reshape(devices, radii // devices, 6 * NH), ('stre...]
where the time goes in v3:
time: 49.2 us; the launch traced here: 48.7 us
  blocking collectives  27.1 us (55%)
  Pallas kernels  11.3 us (23%)
  local copies, waits for them, and re-layouts  4.45 us (9%)
  starting transfers between devices  4.41 us (9%)
  between operations  0.75 us (2%)
  other arithmetic  0.68 us (1%)
    all_to_all x1, blocking collectives, body(): lax.all_to_all(partial.reshape(devices, radii // devices, 6 * NH), ('stre...  27.1 us
    pallas_call x1, Pallas kernels, section(): pl.pallas_call(section_kernel, out_shape=(shape(velocity.shape), shape(en...  5.2 us
    pallas_call x1, Pallas kernels, prepare(): pl.pallas_call(functools.partial(prepare_kernel, cells_s, cells_g, cells_...  4.46 us
    ppermute x4, starting transfers between devices, swap(): return lax.ppermute(values, axis, pairs)  4.41 us
    unnamed x16, local copies, waits for them, and re-layouts  4.34 us
    pallas_call x1, Pallas kernels, pack(): pl.pallas_call(pack_kernel, out_shape=(stream, stream, girth, girth), nam...  1.64 us
  transfers between devices with their start and end apart: 4, of which 0 were waited for; matrix products, arithmetic and copies ran while one was open for 0% of the time, Pallas kernels for 9%

profile of v3, /device:TPU:0, one launch (start us, length us, event | category | flops | bytes accessed | tf_op | source)
XLA Modules:
  0.0 48.7 jit_solution(13097455081351802904)
XLA Ops:
  0.6 1.6 %pack_halos.1 = (f32[6,2,8,256]{3,2,1,0:T(8,128)}, f32[6,2,8,256]{3,2,1,0:T(8,128)}, f32[6,4,2,256]{3,2,1,0:T(2,128)}, f32[6,4,2,256]{3,2,1,0:T(2,128)}) custom-call(f32[3,4,8,256]{3,2,1,0:T(8,128)} %vel_ref.3, f32[4,8,256]{2,1,0:T(8,128)} %p_ref.3, f32[4,8,256]{2,1,0:T(8,128)} %k_ref.3, f32[4,8,256]{2,1,0:T(8,128)} %w_ref.3), custom_call_target="tpu_custom_call" | custom-call | tf_op jit(solution)/shard_map/pack_halos/pallas_call | solution.py:46
  2.3 3.0 %collective-permute-start = (f32[6,2,8,256]{3,2,1,0:T(8,128)}, f32[6,2,8,256]{3,2,1,0:T(8,128)S(1)}, u32[]{:S(2)}, u32[]{:S(2)}) collective-permute-start(f32[6,2,8,256]{3,2,1,0:T(8,128)} %get-tuple-element.20), channel_id=1, source_target_pairs={{0,8},{8,0},{16,24},{24,16},{1,9},{9,1},{17,25},{25,17},{2,10},{10... | collective-permute-start | bytes 294920 | tf_op jit(solution)/shard_map/ppermute | solution.py:485
  5.3 0.7 %collective-permute-start.1 = (f32[6,2,8,256]{3,2,1,0:T(8,128)}, f32[6,2,8,256]{3,2,1,0:T(8,128)S(1)}, u32[]{:S(2)}, u32[]{:S(2)}) collective-permute-start(f32[6,2,8,256]{3,2,1,0:T(8,128)} %get-tuple-element.21), channel_id=1, source_target_pairs={{8,16},{16,8},{9,17},{17,9},{10,18},{18,10},{11,19},{19,11},{12,20... | collective-permute-start | bytes 294920 | tf_op jit(solution)/shard_map/ppermute | solution.py:485
  6.0 0.1 collective-permute-start.2
  6.0 0.7 %collective-permute-start.3 = (f32[6,4,2,256]{3,2,1,0:T(2,128)}, f32[6,4,2,256]{3,2,1,0:T(2,128)S(1)}, u32[]{:S(2)}, u32[]{:S(2)}) collective-permute-start(f32[6,4,2,256]{3,2,1,0:T(2,128)} %get-tuple-element.23), channel_id=1, source_target_pairs={{1,2},{2,1},{3,4},{4,3},{5,6},{6,5},{9,10},{10,9},{11,12},{12,11},... | collective-permute-start | bytes 147464 | tf_op jit(solution)/shard_map/ppermute | solution.py:485
  6.7 0.0 copy-start
  6.7 1.4 %copy-done = f32[3,128,1024]{2,1,0:T(8,128)S(1)} copy-done((f32[3,128,1024]{2,1,0:T(8,128)S(1)}, f32[3,128,1024]{2,1,0:T(8,128)}, u32[]{:S(2)}) %copy-start) | copy-done | bytes 1572888
  8.1 0.0 copy-start.1
  8.1 1.2 %copy-done.1 = f32[1024,256]{1,0:T(8,128)S(1)} copy-done((f32[1024,256]{1,0:T(8,128)S(1)}, f32[1024,256]{1,0:T(8,128)}, u32[]{:S(2)}) %copy-start.1) | copy-done | bytes 1048600
  9.3 0.0 copy-start.2
  9.3 1.0 %copy-done.2 = s32[128,1024]{1,0:T(8,128)S(1)} copy-done((s32[128,1024]{1,0:T(8,128)S(1)}, s32[128,1024]{1,0:T(8,128)}, u32[]{:S(2)}) %copy-start.2) | copy-done | bytes 524312
  10.4 0.0 copy-start.7
  10.4 0.7 %copy-done.7 = s32[64,1]{0,1:T(1,128)S(1)} copy-done((s32[64,1]{0,1:T(1,128)S(1)}, s32[64,1]{0,1:T(1,128)}, u32[]{:S(2)}) %copy-start.7) | copy-done | bytes 280
  11.0 0.0 copy-start.3
  11.0 0.0 copy-start.4
  11.0 0.0 copy-start.5
  11.0 0.0 copy-start.6
  11.1 4.5 %prepare_points.1 = (s32[384,128]{1,0:T(8,128)S(1)}, f32[384,128]{1,0:T(8,128)S(1)}, f32[384,128]{1,0:T(8,128)S(1)}, f32[384,128]{1,0:T(8,128)S(1)}, s32[640,128...) custom-call(s32[64]{0:T(128)S(1)} %bitcast.1, s32[128,1024]{1,0:T(8,128)S(1)} %copy-done.2, ...), custom_call_target="tpu_custom_call" | custom-call | flops 2621440 | bytes 5767168 | tf_op jit(solution)/shard_map/prepare_points/pallas_call | solution.py:191
  15.5 0.0 collective-permute-done.2.girth_a
  15.5 0.0 collective-permute-done.3.girth_b
  15.5 0.0 collective-permute-done.stream_a
  15.6 0.0 collective-permute-done.1.stream_b
  15.6 0.0 copy-done.3
  15.6 0.0 copy-done.4
  15.6 0.0 copy-done.5
  15.6 0.0 copy-done.6
  15.6 5.2 %section_and_disk.1 = (f32[3,4,8,256]{3,2,1,0:T(8,128)}, f32[4,8,256]{2,1,0:T(8,128)}, f32[4,8,256]{2,1,0:T(8,128)}, f32[128,768]{1,0:T(8,128)S(1)}) custom-call(s32[1]{0:T(128)} %get-tuple-element.19.count_ref, f32[3,4,8,256]{3,2,1,0:T(8,128)S(1)} %copy-done.3, f32[4,8,256]{2,1,0:T(8,128)S(1)} %copy-done.4, f32[4,8,256]{2,1,0:T(8,128)S(1)} %copy-done.5, ...), custom_call_target="tpu_custom_call" | custom-call | tf_op jit(solution)/shard_map/section_and_disk/pallas_call | solution.py:447
  20.8 0.1 reshape.11
  20.9 27.1 %all_to_all.5 = f32[32,4,768]{2,1,0:T(4,128)S(1)} all-to-all(f32[32,4,768]{2,1,0:T(4,128)S(1)} %reshape.11), channel_id=1, replica_groups=mesh['stream'=4,'girth'=8] {'stream','girth'}, dimensions={0} | all-to-all | bytes 786432 | tf_op jit(solution)/shard_map/all_to_all | solution.py:505
  48.0 0.7 %reduce_sum.9 = f32[4,768]{1,0:T(4,128)} reduce(f32[32,4,768]{2,1,0:T(4,128)S(1)} %all_to_all.5, f32[]{:T(128)} %constant.1.clone.1), dimensions={0}, to_apply=%region_0.0 | reduce | flops 95232 | bytes 405508 | tf_op jit(solution)/shard_map/reduce_sum | solution.py:512
Async XLA Ops:
  2.3 13.3 %collective-permute-start = (f32[6,2,8,256]{3,2,1,0:T(8,128)}, f32[6,2,8,256]{3,2,1,0:T(8,128)S(1)}, u32[]{:S(2)}, u32[]{:S(2)}) collective-permute-start(f32[6,2,8,256]{3,2,1,0:T(8,128)} %get-tuple-element.20), channel_id=1, source_target_pairs={{0,8},{8,0},{16,24},{24,16},{1,9},{9,1},{17,25},{25,17},{2,10},{10... | collective-permute-start | bytes 294920 | tf_op jit(solution)/shard_map/ppermute | solution.py:485
  5.3 10.3 %collective-permute-start.1 = (f32[6,2,8,256]{3,2,1,0:T(8,128)}, f32[6,2,8,256]{3,2,1,0:T(8,128)S(1)}, u32[]{:S(2)}, u32[]{:S(2)}) collective-permute-start(f32[6,2,8,256]{3,2,1,0:T(8,128)} %get-tuple-element.21), channel_id=1, source_target_pairs={{8,16},{16,8},{9,17},{17,9},{10,18},{18,10},{11,19},{19,11},{12,20... | collective-permute-start | bytes 294920 | tf_op jit(solution)/shard_map/ppermute | solution.py:485
  6.0 9.6 %collective-permute-start.2 = (f32[6,4,2,256]{3,2,1,0:T(2,128)}, f32[6,4,2,256]{3,2,1,0:T(2,128)S(1)}, u32[]{:S(2)}, u32[]{:S(2)}) collective-permute-start(f32[6,4,2,256]{3,2,1,0:T(2,128)} %get-tuple-element.22), channel_id=1, source_target_pairs={{0,1},{1,0},{2,3},{3,2},{4,5},{5,4},{6,7},{7,6},{8,9},{9,8},{10,11... | collective-permute-start | bytes 147464 | tf_op jit(solution)/shard_map/ppermute | solution.py:485
  6.0 9.5 %collective-permute-start.3 = (f32[6,4,2,256]{3,2,1,0:T(2,128)}, f32[6,4,2,256]{3,2,1,0:T(2,128)S(1)}, u32[]{:S(2)}, u32[]{:S(2)}) collective-permute-start(f32[6,4,2,256]{3,2,1,0:T(2,128)} %get-tuple-element.23), channel_id=1, source_target_pairs={{1,2},{2,1},{3,4},{4,3},{5,6},{6,5},{9,10},{10,9},{11,12},{12,11},... | collective-permute-start | bytes 147464 | tf_op jit(solution)/shard_map/ppermute | solution.py:485
  6.7 1.4 %copy-start = (f32[3,128,1024]{2,1,0:T(8,128)S(1)}, f32[3,128,1024]{2,1,0:T(8,128)}, u32[]{:S(2)}) copy-start(f32[3,128,1024]{2,1,0:T(8,128)} %frac_hbm.1) | copy-start | bytes 4718596
  8.1 1.2 %copy-start.1 = (f32[1024,256]{1,0:T(8,128)S(1)}, f32[1024,256]{1,0:T(8,128)}, u32[]{:S(2)}) copy-start(f32[1024,256]{1,0:T(8,128)} %constant.4.clone.table_hbm) | copy-start | bytes 3145732
  9.3 1.0 %copy-start.2 = (s32[128,1024]{1,0:T(8,128)S(1)}, s32[128,1024]{1,0:T(8,128)}, u32[]{:S(2)}) copy-start(s32[128,1024]{1,0:T(8,128)} %ids_hbm.1) | copy-start | bytes 1572868
  10.4 0.7 %copy-start.7 = (s32[64,1]{0,1:T(1,128)S(1)}, s32[64,1]{0,1:T(1,128)}, u32[]{:S(2)}) copy-start(s32[64,1]{0,1:T(1,128)} %param.14) | copy-start | bytes 772
  11.0 4.5 %copy-start.3 = (f32[3,4,8,256]{3,2,1,0:T(8,128)S(1)}, f32[3,4,8,256]{3,2,1,0:T(8,128)}, u32[]{:S(2)}) copy-start(f32[3,4,8,256]{3,2,1,0:T(8,128)} %vel_ref.3) | copy-start | bytes 294916
  11.0 4.5 %copy-start.4 = (f32[4,8,256]{2,1,0:T(8,128)S(1)}, f32[4,8,256]{2,1,0:T(8,128)}, u32[]{:S(2)}) copy-start(f32[4,8,256]{2,1,0:T(8,128)} %p_ref.3) | copy-start | bytes 98308
  11.0 4.5 %copy-start.5 = (f32[4,8,256]{2,1,0:T(8,128)S(1)}, f32[4,8,256]{2,1,0:T(8,128)}, u32[]{:S(2)}) copy-start(f32[4,8,256]{2,1,0:T(8,128)} %k_ref.3) | copy-start | bytes 98308
  11.0 4.5 %copy-start.6 = (f32[4,8,256]{2,1,0:T(8,128)S(1)}, f32[4,8,256]{2,1,0:T(8,128)}, u32[]{:S(2)}) copy-start(f32[4,8,256]{2,1,0:T(8,128)} %w_ref.3) | copy-start | bytes 98308

commit v4 on v3

--- a/solution.py
+++ b/solution.py
@@ -22,7 +22,12 @@
 ROWS = 8
 SHIFT = 10
 CHUNK = 64
+PRODUCTS = 2
 VMEM_LIMIT = 48 * 1024 * 1024
+
+
+def in_hbm(values):
+    return pltpu.with_memory_space_constraint(values, pltpu.HBM)
 
 
 def pack_kernel(vel_ref, p_ref, k_ref, w_ref, *slabs):
@@ -41,8 +46,8 @@
 
 def pack(velocity, pressure, energy, rate):
     _, cells_s, cells_g, cells_r = velocity.shape
-    stream = jax.ShapeDtypeStruct((6, 2, cells_g, cells_r), jnp.float32)
-    girth = jax.ShapeDtypeStruct((6, cells_s, 2, cells_r), jnp.float32)
+    stream = pltpu.VMEM((6, 2, cells_g, cells_r), jnp.float32)
+    girth = pltpu.VMEM((6, cells_s, 2, cells_r), jnp.float32)
     return pl.pallas_call(
         pack_kernel, out_shape=(stream, stream, girth, girth), name="pack_halos"
     )(velocity, pressure, energy, rate)
@@ -187,7 +192,7 @@
     lists = (rows, radii)
     vmem = pl.BlockSpec(memory_space=pltpu.VMEM)
     smem = pl.BlockSpec(memory_space=pltpu.SMEM)
-    hbm = pl.BlockSpec(memory_space=pl.ANY)
+    hbm = pl.BlockSpec(memory_space=pltpu.HBM)
     return pl.pallas_call(
         functools.partial(prepare_kernel, cells_s, cells_g, cells_r),
         out_shape=(
@@ -216,7 +221,7 @@
             flops=20 * radii * azimuths, bytes_accessed=44 * radii * azimuths, transcendentals=0
         ),
         name="prepare_points",
-    )(owners, corner_ids, fractions, table)
+    )(*(in_hbm(x) for x in (owners, corner_ids, fractions, table)))
 
 
 def radial(values, amount, fill):
@@ -340,6 +345,7 @@
     ext_ref,
     visc_ref,
     field_ref,
+    gather_ref,
     value_ref,
     disk_ref,
 ):
@@ -364,40 +370,64 @@
     new_k_ref[...] = energy
     new_w_ref[...] = rate
 
+    def halved(values):
+        high = values.astype(jnp.bfloat16)
+        return high, (values - high.astype(jnp.float32)).astype(jnp.bfloat16)
+
     def rounded(values):
         return values.astype(jnp.bfloat16).astype(jnp.float32)
 
+    halves = cells_r // LANES
     for c in range(3):
         new_vel_ref[c] = updated[c]
         slope = radial(updated[c], 1, 0.0) - updated[c]
         for kind, values in enumerate((updated[c], slope)):
-            high = rounded(values)
-            field_ref[c, :, 2 * kind] = high
-            field_ref[c, :, 2 * kind + 1] = rounded(values - high)
+            if c < PRODUCTS:
+                high = rounded(values)
+                field_ref[c, :, 2 * kind] = high
+                field_ref[c, :, 2 * kind + 1] = rounded(values - high)
+            else:
+                for h in range(halves):
+                    lanes = slice(h * LANES, (h + 1) * LANES)
+                    gather_ref[c - PRODUCTS, :, kind, h] = values[:, :, lanes]
 
     kinds = 4
-    table = field_ref[...].reshape(3 * cells_s * kinds * cells_g, cells_r).astype(jnp.bfloat16)
+    table = field_ref[...].reshape(PRODUCTS * cells_s * kinds * cells_g, cells_r)
+    table = table.astype(jnp.bfloat16)
     pair = 2 * LANES
     girth_row = lax.broadcasted_iota(jnp.int32, (cells_g, pair), 0).astype(jnp.float32)
     radial_row = lax.broadcasted_iota(jnp.int32, (cells_r, pair), 0)
 
     def two(values, j):
         return jnp.concatenate([values[j : j + 1], values[j + 1 : j + 2]], axis=1)
+
+    def spread(values, j):
+        return jnp.broadcast_to(values[j : j + 1], (cells_g, LANES))
+
+    def pick(c, s, kind, index, half_of):
+        out = None
+        for h in range(halves):
+            got = jnp.take_along_axis(
+                gather_ref[c - PRODUCTS, s, kind, h], index, axis=1, mode="promise_in_bounds"
+            )
+            out = got if out is None else jnp.where(half_of[h], got, out)
+        return out
 
     def eight(group, carry):
         at = pl.multiple_of(group * ROWS, ROWS)
         here = pl.ds(at, ROWS)
         q8, fr8, xg8, xs8 = (r[here, :] for r in (q_ref, fr_ref, xg_ref, xs_ref))
         hs8 = [jnp.maximum(1.0 - jnp.abs(xs8 - float(s)), 0.0) for s in range(cells_s)]
+        index8 = q8 % LANES
         sums = [[], [], []]
         for j in range(0, ROWS, 2):
             hot = jnp.where(radial_row == two(q8, j), 1.0, 0.0).astype(jnp.bfloat16)
             got = jnp.dot(table, hot, preferred_element_type=jnp.float32)
-            got = got.reshape(3, cells_s, kinds, cells_g, pair)
+            got = got.reshape(PRODUCTS, cells_s, kinds, cells_g, pair)
             fr = two(fr8, j)
             hg = jnp.maximum(1.0 - jnp.abs(two(xg8, j) - girth_row), 0.0)
             hs = [two(hs8[s], j) for s in range(cells_s)]
-            for c in range(3):
+            for c in range(PRODUCTS):
                 total = None
                 for s in range(cells_s):
                     value = got[c, s, 0] + got[c, s, 1] + fr * (got[c, s, 2] + got[c, s, 3])
@@ -405,6 +435,18 @@
                     total = value if total is None else total + value
                 total = hg * total
                 sums[c] += [total[:, :LANES], total[:, LANES:]]
+            for i in (j, j + 1):
+                index, q = spread(index8, i), spread(q8, i)
+                half_of = [q >= h * LANES for h in range(halves)]
+                own_hg = hg[:, (i - j) * LANES : (i - j + 1) * LANES]
+                for c in range(PRODUCTS, 3):
+                    total = None
+                    for s in range(cells_s):
+                        value = pick(c, s, 0, index, half_of)
+                        value = value + fr8[i : i + 1] * pick(c, s, 1, index, half_of)
+                        value = hs8[s][i : i + 1] * value
+                        total = value if total is None else total + value
+                    sums[c].append(own_hg * total)
         for c in range(3):
             value_ref[0, c, pl.ds(pad + at, ROWS), :] = girth_sums(sums[c])
         return carry
@@ -426,14 +468,15 @@
                 else:
                     disk_ref[c, pl.ds(at, CHUNK), :] = jnp.where(kept, value, 0.0)
 
+    turned = jnp.concatenate([disk_ref[c].T for c in range(3)], axis=0)
+    high, low = halved(turned)
+    wave_high, wave_low = halved(chosen_ref[...])
+    waves = jnp.dot(high, wave_high, preferred_element_type=jnp.float32)
+    waves += jnp.dot(high, wave_low, preferred_element_type=jnp.float32)
+    waves += jnp.dot(low, wave_high, preferred_element_type=jnp.float32)
+    radii = harm_ref.shape[0]
     for c in range(3):
-        harm_ref[:, c * 2 * NH : (c + 1) * 2 * NH] = lax.dot_general(
-            disk_ref[c],
-            chosen_ref[...],
-            (((0,), (0,)), ((), ())),
-            precision=lax.Precision.HIGHEST,
-            preferred_element_type=jnp.float32,
-        )
+        harm_ref[:, c * 2 * NH : (c + 1) * 2 * NH] = waves[c * radii : (c + 1) * radii]
 
 
 def section(velocity, pressure, energy, rate, halos, points):
@@ -456,7 +499,8 @@
         scratch_shapes=[
             scratch(6, cells_s, 3 * ROWS, cells_r),
             scratch(cells_s, 3 * ROWS, cells_r),
-            scratch(3, cells_s, 4, cells_g, cells_r),
+            scratch(PRODUCTS, cells_s, 4, cells_g, cells_r),
+            scratch(3 - PRODUCTS, cells_s, 2, cells_r // LANES, cells_g, LANES),
             scratch(2, 3, moves.shape[0], radii),
             scratch(3, rows, radii),
         ],

time: 49.2 us -> 43.1 us (0.88)
  local copies, waits for them, and re-layouts: 4.45 us -> 0.14 us
  blocking collectives: 27.1 us -> 25.2 us
    unnamed x16 -> x8, local copies, waits for them, and re-layouts: 4.34 us -> 0.03 us
    all_to_all x1, blocking collectives: 27.1 us -> 25.2 us  [body(): lax.all_to_all(partial.reshape(devices, radii // devices, 6 * NH), ('stre...]
    pallas_call x1, Pallas kernels: 4.46 us -> 5.4 us  [prepare(): pl.pallas_call(functools.partial(prepare_kernel, cells_s, cells_g, cells_...]
    pallas_call x1, Pallas kernels: 1.64 us -> 0.98 us  [pack(): pl.pallas_call(pack_kernel, out_shape=(stream, stream, girth, girth), nam...]
  transfers between devices with their start and end apart: 4 -> 4, of which waited for: 0 -> 0; matrix products, arithmetic and copies ran while one was open for 0% -> 0% of each run, Pallas kernels for 9% -> 13%
where the time goes in v4:
time: 43.1 us; the launch traced here: 42.9 us
  blocking collectives  25.2 us (58%)
  Pallas kernels  11.6 us (27%)
  starting transfers between devices  4.48 us (10%)
  between operations  0.78 us (2%)
  other arithmetic  0.68 us (2%)
    all_to_all x1, blocking collectives, body(): lax.all_to_all(partial.reshape(devices, radii // devices, 6 * NH), ('stre...  25.2 us
    pallas_call x1, Pallas kernels, prepare(): pl.pallas_call(functools.partial(prepare_kernel, cells_s, cells_g, cells_...  5.4 us
    pallas_call x1, Pallas kernels, section(): pl.pallas_call(section_kernel, out_shape=(shape(velocity.shape), shape(en...  5.25 us
    ppermute x4, starting transfers between devices, swap(): return lax.ppermute(values, axis, pairs)  4.48 us
    pallas_call x1, Pallas kernels, pack(): pl.pallas_call(pack_kernel, out_shape=(stream, stream, girth, girth), nam...  0.98 us
  transfers between devices with their start and end apart: 4, of which 0 were waited for; matrix products, arithmetic and copies ran while one was open for 0% of the time, Pallas kernels for 13%

profile of v4, /device:TPU:0, one launch (start us, length us, event | category | flops | bytes accessed | tf_op | source)
XLA Modules:
  0.0 42.9 jit_solution(10378752268349732671)
XLA Ops:
  0.6 1.0 %pack_halos.1 = (f32[6,2,8,256]{3,2,1,0:T(8,128)S(1)}, f32[6,2,8,256]{3,2,1,0:T(8,128)S(1)}, f32[6,4,2,256]{3,2,1,0:T(2,128)S(1)}, f32[6,4,2,256]{3,2,1,0:T(2,128)S(1)}) custom-call(f32[3,4,8,256]{3,2,1,0:T(8,128)} %vel_ref.3, f32[4,8,256]{2,1,0:T(8,128)} %p_ref.3, f32[4,8,256]{2,1,0:T(8,128)} %k_ref.3, f32[4,8,256]{2,1,0:T(8,128)} %w_ref.3), custom_call_target="tpu_custom_call" | custom-call | tf_op jit(solution)/shard_map/pack_halos/pallas_call | solution.py:51
  1.6 3.1 %collective-permute-start = (f32[6,2,8,256]{3,2,1,0:T(8,128)S(1)}, f32[6,2,8,256]{3,2,1,0:T(8,128)S(1)}, u32[]{:S(2)}, u32[]{:S(2)}) collective-permute-start(f32[6,2,8,256]{3,2,1,0:T(8,128)S(1)} %get-tuple-element.20), channel_id=1, source_target_pairs={{0,8},{8,0},{16,24},{24,16},{1,9},{9,1},{17,25},{25,17},{2,10},{10... | collective-permute-start | bytes 294920 | tf_op jit(solution)/shard_map/ppermute | solution.py:529
  4.7 0.7 %collective-permute-start.1 = (f32[6,2,8,256]{3,2,1,0:T(8,128)S(1)}, f32[6,2,8,256]{3,2,1,0:T(8,128)S(1)}, u32[]{:S(2)}, u32[]{:S(2)}) collective-permute-start(f32[6,2,8,256]{3,2,1,0:T(8,128)S(1)} %get-tuple-element.21), channel_id=1, source_target_pairs={{8,16},{16,8},{9,17},{17,9},{10,18},{18,10},{11,19},{19,11},{12,20... | collective-permute-start | bytes 294920 | tf_op jit(solution)/shard_map/ppermute | solution.py:529
  5.4 0.1 collective-permute-start.2
  5.4 0.7 %collective-permute-start.3 = (f32[6,4,2,256]{3,2,1,0:T(2,128)S(1)}, f32[6,4,2,256]{3,2,1,0:T(2,128)S(1)}, u32[]{:S(2)}, u32[]{:S(2)}) collective-permute-start(f32[6,4,2,256]{3,2,1,0:T(2,128)S(1)} %get-tuple-element.23), channel_id=1, source_target_pairs={{1,2},{2,1},{3,4},{4,3},{5,6},{6,5},{9,10},{10,9},{11,12},{12,11},... | collective-permute-start | bytes 147464 | tf_op jit(solution)/shard_map/ppermute | solution.py:529
  6.1 0.0 copy-start
  6.1 0.0 copy-start.1
  6.1 0.0 copy-start.2
  6.2 0.0 copy-start.3
  6.2 5.4 %prepare_points.1 = (s32[384,128]{1,0:T(8,128)S(1)}, f32[384,128]{1,0:T(8,128)S(1)}, f32[384,128]{1,0:T(8,128)S(1)}, f32[384,128]{1,0:T(8,128)S(1)}, s32[640,128...) custom-call(s32[64]{0:T(128)} %bitcast.1, s32[128,1024]{1,0:T(8,128)} %ids_hbm.1, f32[3,128,1024]{2,1,0:T(8,128)} %frac_hbm.1, ...), custom_call_target="tpu_custom_call" | custom-call | flops 2621440 | bytes 5767168 | tf_op jit(solution)/shard_map/prepare_points/pallas_call | solution.py:196
  11.6 0.0 collective-permute-done.2.girth_a
  11.6 0.0 collective-permute-done.3.girth_b
  11.6 0.0 collective-permute-done.stream_a
  11.6 0.0 collective-permute-done.1.stream_b
  11.6 0.0 copy-done
  11.6 0.0 copy-done.1
  11.6 0.0 copy-done.2
  11.6 0.0 copy-done.3
  11.7 5.3 %section_and_disk.1 = (f32[3,4,8,256]{3,2,1,0:T(8,128)}, f32[4,8,256]{2,1,0:T(8,128)}, f32[4,8,256]{2,1,0:T(8,128)}, f32[128,768]{1,0:T(8,128)S(1)}) custom-call(s32[1]{0:T(128)} %get-tuple-element.19.count_ref, f32[3,4,8,256]{3,2,1,0:T(8,128)S(1)} %copy-done, f32[4,8,256]{2,1,0:T(8,128)S(1)} %copy-done.1, f32[4,8,256]{2,1,0:T(8,128)S(1)} %copy-done.2, ...), custom_call_target="tpu_custom_call" | custom-call | tf_op jit(solution)/shard_map/section_and_disk/pallas_call | solution.py:490
  16.9 0.1 reshape.11
  17.0 25.2 %all_to_all.5 = f32[32,4,768]{2,1,0:T(4,128)S(1)} all-to-all(f32[32,4,768]{2,1,0:T(4,128)S(1)} %reshape.11), channel_id=1, replica_groups=mesh['stream'=4,'girth'=8] {'stream','girth'}, dimensions={0} | all-to-all | bytes 786432 | tf_op jit(solution)/shard_map/all_to_all | solution.py:549
  42.2 0.7 %reduce_sum.9 = f32[4,768]{1,0:T(4,128)} reduce(f32[32,4,768]{2,1,0:T(4,128)S(1)} %all_to_all.5, f32[]{:T(128)} %constant.1.clone.1), dimensions={0}, to_apply=%region_0.0 | reduce | flops 95232 | bytes 405508 | tf_op jit(solution)/shard_map/reduce_sum | solution.py:556
Async XLA Ops:
  1.6 10.0 %collective-permute-start = (f32[6,2,8,256]{3,2,1,0:T(8,128)S(1)}, f32[6,2,8,256]{3,2,1,0:T(8,128)S(1)}, u32[]{:S(2)}, u32[]{:S(2)}) collective-permute-start(f32[6,2,8,256]{3,2,1,0:T(8,128)S(1)} %get-tuple-element.20), channel_id=1, source_target_pairs={{0,8},{8,0},{16,24},{24,16},{1,9},{9,1},{17,25},{25,17},{2,10},{10... | collective-permute-start | bytes 294920 | tf_op jit(solution)/shard_map/ppermute | solution.py:529
  4.7 6.9 %collective-permute-start.1 = (f32[6,2,8,256]{3,2,1,0:T(8,128)S(1)}, f32[6,2,8,256]{3,2,1,0:T(8,128)S(1)}, u32[]{:S(2)}, u32[]{:S(2)}) collective-permute-start(f32[6,2,8,256]{3,2,1,0:T(8,128)S(1)} %get-tuple-element.21), channel_id=1, source_target_pairs={{8,16},{16,8},{9,17},{17,9},{10,18},{18,10},{11,19},{19,11},{12,20... | collective-permute-start | bytes 294920 | tf_op jit(solution)/shard_map/ppermute | solution.py:529
  5.4 6.2 %collective-permute-start.2 = (f32[6,4,2,256]{3,2,1,0:T(2,128)S(1)}, f32[6,4,2,256]{3,2,1,0:T(2,128)S(1)}, u32[]{:S(2)}, u32[]{:S(2)}) collective-permute-start(f32[6,4,2,256]{3,2,1,0:T(2,128)S(1)} %get-tuple-element.22), channel_id=1, source_target_pairs={{0,1},{1,0},{2,3},{3,2},{4,5},{5,4},{6,7},{7,6},{8,9},{9,8},{10,11... | collective-permute-start | bytes 147464 | tf_op jit(solution)/shard_map/ppermute | solution.py:529
  5.4 6.1 %collective-permute-start.3 = (f32[6,4,2,256]{3,2,1,0:T(2,128)S(1)}, f32[6,4,2,256]{3,2,1,0:T(2,128)S(1)}, u32[]{:S(2)}, u32[]{:S(2)}) collective-permute-start(f32[6,4,2,256]{3,2,1,0:T(2,128)S(1)} %get-tuple-element.23), channel_id=1, source_target_pairs={{1,2},{2,1},{3,4},{4,3},{5,6},{6,5},{9,10},{10,9},{11,12},{12,11},... | collective-permute-start | bytes 147464 | tf_op jit(solution)/shard_map/ppermute | solution.py:529
  6.1 5.5 %copy-start = (f32[3,4,8,256]{3,2,1,0:T(8,128)S(1)}, f32[3,4,8,256]{3,2,1,0:T(8,128)}, u32[]{:S(2)}) copy-start(f32[3,4,8,256]{3,2,1,0:T(8,128)} %vel_ref.3) | copy-start | bytes 294916
  6.1 5.5 %copy-start.1 = (f32[4,8,256]{2,1,0:T(8,128)S(1)}, f32[4,8,256]{2,1,0:T(8,128)}, u32[]{:S(2)}) copy-start(f32[4,8,256]{2,1,0:T(8,128)} %p_ref.3) | copy-start | bytes 98308
  6.1 5.5 %copy-start.2 = (f32[4,8,256]{2,1,0:T(8,128)S(1)}, f32[4,8,256]{2,1,0:T(8,128)}, u32[]{:S(2)}) copy-start(f32[4,8,256]{2,1,0:T(8,128)} %k_ref.3) | copy-start | bytes 98308
  6.2 5.5 %copy-start.3 = (f32[4,8,256]{2,1,0:T(8,128)S(1)}, f32[4,8,256]{2,1,0:T(8,128)}, u32[]{:S(2)}) copy-start(f32[4,8,256]{2,1,0:T(8,128)} %w_ref.3) | copy-start | bytes 98308

commit v5 on v4

--- a/solution.py
+++ b/solution.py
@@ -21,7 +21,7 @@
 LANES = 128
 ROWS = 8
 SHIFT = 10
-CHUNK = 64
+CHUNK = 32
 PRODUCTS = 2
 VMEM_LIMIT = 48 * 1024 * 1024
 
@@ -30,7 +30,14 @@
     return pltpu.with_memory_space_constraint(values, pltpu.HBM)
 
 
-def pack_kernel(vel_ref, p_ref, k_ref, w_ref, *slabs):
+def pack_kernel(vel_ref, p_ref, k_ref, w_ref, ids_hbm, frac_hbm, *rest):
+    *slabs, ids_ref, frac_ref, arrived = rest
+    copies = [
+        pltpu.make_async_copy(ids_hbm, ids_ref, arrived.at[0]),
+        pltpu.make_async_copy(frac_hbm, frac_ref, arrived.at[1]),
+    ]
+    for copy in copies:
+        copy.start()
     cells_s, cells_g, _ = p_ref.shape
     stream_odd = lax.axis_index("stream") % 2 == 1
     girth_odd = lax.axis_index("girth") % 2 == 1
@@ -42,15 +49,41 @@
         first, last = own[:, 0:2, :], own[:, cells_g - 2 : cells_g, :]
         slabs[2][f] = jnp.where(girth_odd, first, last)
         slabs[3][f] = jnp.where(girth_odd, last, first)
-
-
-def pack(velocity, pressure, energy, rate):
+    for copy in copies:
+        copy.wait()
+
+
+def pack(velocity, pressure, energy, rate, corner_ids, fractions):
     _, cells_s, cells_g, cells_r = velocity.shape
     stream = pltpu.VMEM((6, 2, cells_g, cells_r), jnp.float32)
     girth = pltpu.VMEM((6, cells_s, 2, cells_r), jnp.float32)
+    vmem = pl.BlockSpec(memory_space=pltpu.VMEM)
+    hbm = pl.BlockSpec(memory_space=pltpu.HBM)
     return pl.pallas_call(
-        pack_kernel, out_shape=(stream, stream, girth, girth), name="pack_halos"
-    )(velocity, pressure, energy, rate)
+        pack_kernel,
+        out_shape=(stream, stream, girth, girth)
+        + (pltpu.VMEM(corner_ids.shape, jnp.int32), pltpu.VMEM(fractions.shape, jnp.float32)),
+        in_specs=[vmem] * 4 + [hbm] * 2,
+        out_specs=[vmem] * 6,
+        scratch_shapes=[pltpu.SemaphoreType.DMA((2,))],
+        compiler_params=pltpu.CompilerParams(vmem_limit_bytes=VMEM_LIMIT),
+        name="pack_halos",
+    )(velocity, pressure, energy, rate, in_hbm(corner_ids), in_hbm(fractions))
+
+
+def network(rows):
+    steps = (rows - 1).bit_length()
+    return [(low, 1 << min(2, steps - low)) for low in range(0, steps, 2)]
+
+
+def reach(rows):
+    return max((digits - 1) << low for low, digits in network(rows))
+
+
+def split(values, size):
+    if size & (size - 1) == 0:
+        return values >> (size.bit_length() - 1), values & (size - 1)
+    return values // size, values % size
 
 
 def prepare_kernel(
@@ -58,8 +91,8 @@
     cells_g,
     cells_r,
     owner_ref,
-    ids_hbm,
-    frac_hbm,
+    ids_ref,
+    frac_ref,
     table_hbm,
     q_ref,
     fr_ref,
@@ -68,108 +101,99 @@
     moves_ref,
     chosen_ref,
     count_ref,
-    ids_ref,
-    frac_ref,
     table_ref,
-    all_q,
-    all_fr,
-    all_xs,
-    all_xg,
+    turned,
+    picked,
     keys,
     frs,
     xss,
     xgs,
+    order,
     arrived,
 ):
-    copies = [pltpu.make_async_copy(ids_hbm, ids_ref, arrived.at[0])]
-    for d in range(3):
-        copies.append(pltpu.make_async_copy(frac_hbm.at[d], frac_ref.at[d], arrived.at[1 + d]))
-    copies.append(pltpu.make_async_copy(table_hbm, table_ref, arrived.at[4]))
-    for copy in copies:
-        copy.start()
+    copy = pltpu.make_async_copy(table_hbm, table_ref, arrived.at[0])
+    copy.start()
     stream_first = lax.axis_index("stream") * cells_s
     me = lax.axis_index("girth")
-    plane_cells = cells_g * cells_r
     sectors = owner_ref.shape[0]
     azimuths = ids_ref.shape[1]
     width = azimuths // sectors
     rows = fr_ref.shape[0]
     pad = moves_ref.shape[0] - rows
-    steps = (rows - 1).bit_length()
-
-    keys[...] = jnp.zeros_like(keys)
-    frs[0] = jnp.zeros_like(frs[0])
-    xgs[0] = jnp.zeros_like(xgs[0])
-    xss[0] = jnp.full_like(xss[0], -2.0)
+    passes = network(rows)
+    valid = 1 << SHIFT - 1
+
+    def listed(number, count):
+        order[jnp.minimum(count, rows // width)] = number
+        return count + (owner_ref[number] == me).astype(jnp.int32)
+
+    owned = lax.fori_loop(0, sectors, listed, jnp.int32(0), unroll=8)
+
+    for at in range(0, azimuths, LANES):
+        cols = pl.ds(at, LANES)
+        turned[0, cols, :] = ids_ref[:, cols].astype(jnp.float32).T
+        for d in range(3):
+            turned[1 + d, cols, :] = frac_ref[d, :, cols].T
+    for d in range(4):
+        picked[d] = jnp.full(picked.shape[1:], -1.0 if d == 0 else 0.0, jnp.float32)
     chosen_ref[...] = jnp.zeros_like(chosen_ref)
+    beyond = pl.ds(rows, pad)
+    for slot in range(2):
+        keys[slot, beyond, :] = jnp.zeros((pad, LANES), jnp.int32)
     moves_ref[0:pad, :] = jnp.zeros((pad, LANES), jnp.int32)
-
-    blocks = [pl.ds(at, LANES) for at in range(0, azimuths, LANES)]
-    copies[0].wait()
-    for cols in blocks:
-        ids = ids_ref[:, cols].T
-        stream_cell = ids // plane_cells
-        remainder = ids - stream_cell * plane_cells
-        girth_cell = remainder // cells_r
-        all_q[cols, :] = (remainder - girth_cell * cells_r) << SHIFT
-        all_xg[cols, :] = girth_cell.astype(jnp.float32)
-        all_xs[cols, :] = (stream_cell - stream_first).astype(jnp.float32)
-    copies[1].wait()
-    for cols in blocks:
-        all_xs[cols, :] += frac_ref[0, :, cols].T
-    copies[2].wait()
-    for cols in blocks:
-        all_xg[cols, :] += frac_ref[1, :, cols].T
-    copies[3].wait()
-    for cols in blocks:
-        all_fr[cols, :] = frac_ref[2, :, cols].T
-    copies[4].wait()
-
-    def sector(number, count):
-        mine = owner_ref[number] == me
-
-        @pl.when(mine)
-        def _():
-            source = pl.ds(pl.multiple_of(number * width, width), width)
-            target = pl.ds(pl.multiple_of(count * width, width), width)
-            chosen_ref[target, :] = table_ref[source, :]
-            keys[0, target, :] = all_q[source, :]
-            frs[0, target, :] = all_fr[source, :]
-            xss[0, target, :] = all_xs[source, :]
-            xgs[0, target, :] = all_xg[source, :]
-
-        return count + mine.astype(jnp.int32)
-
-    lax.fori_loop(0, sectors, sector, jnp.int32(0))
+    copy.wait()
+
+    def sector(place, carry):
+        source = pl.ds(pl.multiple_of(order[place] * width, width), width)
+        target = pl.ds(pl.multiple_of(place * width, width), width)
+        chosen_ref[target, :] = table_ref[source, :]
+        for d in range(4):
+            picked[d, target, :] = turned[d, source, :]
+        return carry
+
+    lax.fori_loop(0, owned, sector, jnp.int32(0))
 
     held = pl.ds(0, rows)
+    ids = picked[0].astype(jnp.int32)
+    stream_cell, rest = split(jnp.maximum(ids, 0), cells_g * cells_r)
+    girth_cell, radial_cell = split(rest, cells_r)
+    xs = (stream_cell - stream_first).astype(jnp.float32) + picked[1]
+    kept = (ids >= 0) & (xs > -1.0) & (xs < float(cells_s))
+    xss[0, held, :] = xs
+    xgs[0, held, :] = girth_cell.astype(jnp.float32) + picked[2]
+    frs[0, held, :] = picked[3]
     earlier = lax.broadcasted_iota(jnp.int32, (rows, rows), 0) > lax.broadcasted_iota(
         jnp.int32, (rows, rows), 1
     )
     earlier = earlier.astype(jnp.float32).astype(jnp.bfloat16)
-    xs = xss[0, held, :]
-    kept = (xs > -1.0) & (xs < float(cells_s))
     skipped = jnp.where(kept, 0.0, 1.0)
     before = jnp.dot(
         earlier, skipped.astype(jnp.bfloat16), preferred_element_type=jnp.float32
     ).astype(jnp.int32)
     counts = rows - jnp.sum(skipped, axis=0, keepdims=True).astype(jnp.int32)
     count_ref[0] = jnp.max(counts)
-    moves_ref[pad : pad + rows, :] = jnp.where(kept, 1 << steps, 0)
-    keys[0, held, :] = keys[0, held, :] + jnp.where(kept, before, 0)
-    for step in range(steps):
-        bit = 1 << step
-        a, b = step % 2, 1 - step % 2
-        last = step == steps - 1
+    moves_ref[pad : pad + rows, :] = jnp.where(kept, valid, 0)
+    keys[0, held, :] = (radial_cell << SHIFT) + jnp.where(kept, before, 0)
+    for number, (low, digits) in enumerate(passes):
+        a, b = number % 2, 1 - number % 2
+        mask = digits - 1 << low
+        last = number == len(passes) - 1
         for at in range(0, rows, CHUNK):
-            here, there = pl.ds(at, CHUNK), pl.ds(at + bit, CHUNK)
-            key, arriving = keys[a, here, :], keys[a, there, :]
-            moved = (arriving & bit) != 0
-            target = pl.ds(pad + at, CHUNK)
-            moves_ref[target, :] = moves_ref[target, :] | jnp.where(moved, bit, 0)
-            stays = jnp.where((key & bit) != 0, key & -(1 << SHIFT), key)
-            key = jnp.where(moved, arriving, stays)
-            out = [jnp.where(moved, r[a, there, :], r[a, here, :]) for r in (frs, xss, xgs)]
+            here, target = pl.ds(at, CHUNK), pl.ds(pad + at, CHUNK)
+            there = [pl.ds(at + (k << low), CHUNK) for k in range(1, digits)]
+            key = keys[a, here, :]
+            arriving = [keys[a, t, :] for t in there]
+            moved = [(arriving[k] & mask) == (k + 1 << low) for k in range(digits - 1)]
+            key = jnp.where((key & mask) != 0, key & -(1 << SHIFT), key)
+            came = moves_ref[target, :]
+            out = [r[a, here, :] for r in (frs, xss, xgs)]
+            for k in range(digits - 1):
+                key = jnp.where(moved[k], arriving[k], key)
+                came = came | jnp.where(moved[k], k + 1 << low, 0)
+                out = [
+                    jnp.where(moved[k], r[a, there[k], :], o) for r, o in zip((frs, xss, xgs), out)
+                ]
+            moves_ref[target, :] = came
             if last:
                 q_ref[here, :] = key >> SHIFT
                 fr_ref[here, :] = out[0]
@@ -187,7 +211,7 @@
     radii, azimuths = corner_ids.shape
     sectors = owners.shape[0]
     rows = 3 * sectors // girth_count * (azimuths // sectors)
-    pad = 1 << ((rows - 1).bit_length() - 1)
+    pad = reach(rows)
     shape = jax.ShapeDtypeStruct
     lists = (rows, radii)
     vmem = pl.BlockSpec(memory_space=pltpu.VMEM)
@@ -204,24 +228,23 @@
             shape((rows, 2 * NH), jnp.float32),
             shape((1,), jnp.int32),
         ),
-        in_specs=[smem, hbm, hbm, hbm],
+        in_specs=[smem, vmem, vmem, hbm],
         out_specs=[vmem] * 6 + [smem],
         scratch_shapes=[
-            pltpu.VMEM(corner_ids.shape, jnp.int32),
-            pltpu.VMEM(fractions.shape, jnp.float32),
             pltpu.VMEM(table.shape, jnp.float32),
-            pltpu.VMEM((azimuths, radii), jnp.int32),
+            pltpu.VMEM((4, azimuths, radii), jnp.float32),
+            pltpu.VMEM((4, rows, radii), jnp.float32),
+            pltpu.VMEM((2, rows + pad, radii), jnp.int32),
         ]
-        + [pltpu.VMEM((azimuths, radii), jnp.float32)] * 3
-        + [pltpu.VMEM((2, rows + pad, radii), jnp.int32)]
         + [pltpu.VMEM((2, rows + pad, radii), jnp.float32)] * 3
-        + [pltpu.SemaphoreType.DMA((5,))],
+        + [pltpu.SMEM((rows // (azimuths // sectors) + 1,), jnp.int32)]
+        + [pltpu.SemaphoreType.DMA((1,))],
         compiler_params=pltpu.CompilerParams(vmem_limit_bytes=VMEM_LIMIT),
         cost_estimate=pl.CostEstimate(
             flops=20 * radii * azimuths, bytes_accessed=44 * radii * azimuths, transcendentals=0
         ),
         name="prepare_points",
-    )(*(in_hbm(x) for x in (owners, corner_ids, fractions, table)))
+    )(in_hbm(owners), corner_ids, fractions, in_hbm(table))
 
 
 def radial(values, amount, fill):
@@ -338,21 +361,26 @@
     xg_ref,
     moves_ref,
     chosen_ref,
+    new_vel_hbm,
+    new_k_hbm,
+    new_w_hbm,
+    harm_ref,
     new_vel_ref,
     new_k_ref,
     new_w_ref,
-    harm_ref,
     ext_ref,
     visc_ref,
     field_ref,
     gather_ref,
     value_ref,
     disk_ref,
+    stored,
 ):
     cells_s, cells_g, cells_r = p_ref.shape
     rows = fr_ref.shape[0]
     pad = moves_ref.shape[0] - rows
-    steps = (rows - 1).bit_length()
+    passes = network(rows)
+    valid = 1 << SHIFT - 1
     stream_odd = lax.axis_index("stream") % 2 == 1
     girth_odd = lax.axis_index("girth") % 2 == 1
 
@@ -390,6 +418,13 @@
                 for h in range(halves):
                     lanes = slice(h * LANES, (h + 1) * LANES)
                     gather_ref[c - PRODUCTS, :, kind, h] = values[:, :, lanes]
+    results = ((new_vel_ref, new_vel_hbm), (new_k_ref, new_k_hbm), (new_w_ref, new_w_hbm))
+    copies = [
+        pltpu.make_async_copy(source, target, stored.at[i])
+        for i, (source, target) in enumerate(results)
+    ]
+    for copy in copies:
+        copy.start()
 
     kinds = 4
     table = field_ref[...].reshape(PRODUCTS * cells_s * kinds * cells_g, cells_r)
@@ -418,7 +453,7 @@
         here = pl.ds(at, ROWS)
         q8, fr8, xg8, xs8 = (r[here, :] for r in (q_ref, fr_ref, xg_ref, xs_ref))
         hs8 = [jnp.maximum(1.0 - jnp.abs(xs8 - float(s)), 0.0) for s in range(cells_s)]
-        index8 = q8 % LANES
+        index8 = q8 & (LANES - 1)
         sums = [[], [], []]
         for j in range(0, ROWS, 2):
             hot = jnp.where(radial_row == two(q8, j), 1.0, 0.0).astype(jnp.bfloat16)
@@ -453,20 +488,24 @@
 
     lax.fori_loop(0, (count_ref[0] + ROWS - 1) // ROWS, eight, jnp.int32(0))
 
-    for step in reversed(range(steps)):
-        bit = 1 << step
-        a, b = (0, 1) if (steps - 1 - step) % 2 == 0 else (1, 0)
+    for number, (low, digits) in enumerate(reversed(passes)):
+        a, b = number % 2, 1 - number % 2
+        mask = digits - 1 << low
+        last = number == len(passes) - 1
         for at in range(0, rows, CHUNK):
-            here, there = pl.ds(pad + at, CHUNK), pl.ds(pad + at - bit, CHUNK)
-            moved = (moves_ref[there, :] & bit) != 0
-            if step == 0:
-                kept = moves_ref[here, :] >= 1 << steps
+            here = pl.ds(pad + at, CHUNK)
+            there = [pl.ds(pad + at - (k << low), CHUNK) for k in range(1, digits)]
+            moved = [(moves_ref[there[k], :] & mask) == (k + 1 << low) for k in range(digits - 1)]
+            if last:
+                kept = (moves_ref[here, :] & valid) != 0
             for c in range(3):
-                value = jnp.where(moved, value_ref[a, c, there, :], value_ref[a, c, here, :])
-                if step > 0:
+                value = value_ref[a, c, here, :]
+                for k in range(digits - 1):
+                    value = jnp.where(moved[k], value_ref[a, c, there[k], :], value)
+                if last:
+                    disk_ref[c, pl.ds(at, CHUNK), :] = jnp.where(kept, value, 0.0)
+                else:
                     value_ref[b, c, here, :] = value
-                else:
-                    disk_ref[c, pl.ds(at, CHUNK), :] = jnp.where(kept, value, 0.0)
 
     turned = jnp.concatenate([disk_ref[c].T for c in range(3)], axis=0)
     high, low = halved(turned)
@@ -477,6 +516,8 @@
     radii = harm_ref.shape[0]
     for c in range(3):
         harm_ref[:, c * 2 * NH : (c + 1) * 2 * NH] = waves[c * radii : (c + 1) * radii]
+    for copy in copies:
+        copy.wait()
 
 
 def section(velocity, pressure, energy, rate, halos, points):
@@ -496,13 +537,18 @@
             shape((radii, 6 * NH)),
         ),
         in_specs=[smem] + [vmem] * 14,
+        out_specs=[pl.BlockSpec(memory_space=pl.ANY)] * 3 + [vmem],
         scratch_shapes=[
+            scratch(*velocity.shape),
+            scratch(*energy.shape),
+            scratch(*rate.shape),
             scratch(6, cells_s, 3 * ROWS, cells_r),
             scratch(cells_s, 3 * ROWS, cells_r),
             scratch(PRODUCTS, cells_s, 4, cells_g, cells_r),
             scratch(3 - PRODUCTS, cells_s, 2, cells_r // LANES, cells_g, LANES),
             scratch(2, 3, moves.shape[0], radii),
             scratch(3, rows, radii),
+            pltpu.SemaphoreType.DMA((3,)),
         ],
         compiler_params=pltpu.CompilerParams(vmem_limit_bytes=VMEM_LIMIT),
         name="section_and_disk",
@@ -528,17 +574,22 @@
             pairs += [(i, i + 1), (i + 1, i)]
         return lax.ppermute(values, axis, pairs)
 
-    slabs = pack(velocity, pressure, kinetic_energy, dissipation_rate)
-    halos = (
+    *slabs, ids, fracs = pack(
+        velocity, pressure, kinetic_energy, dissipation_rate, corner_ids, fractions
+    )
+    girth_halos = (
+        swap(slabs[2], "girth", girth_count, 0),
+        swap(slabs[3], "girth", girth_count, 1),
+    )
+    stream_halos = (
         swap(slabs[0], "stream", stream_count, 0),
         swap(slabs[1], "stream", stream_count, 1),
-        swap(slabs[2], "girth", girth_count, 0),
-        swap(slabs[3], "girth", girth_count, 1),
-    )
+    )
+    halos = stream_halos + girth_halos
     points = prepare(
         sector_owner[:, 0],
-        corner_ids,
-        fractions,
+        ids,
+        fracs,
         fourier_table(azimuths, NH),
         (cells_s, cells_g, cells_r),
         girth_count,

time: 43.1 us -> 45.2 us (1.049)
  local copies, waits for them, and re-layouts: 0.14 us -> 3.27 us
  Pallas kernels: 11.6 us -> 10.7 us
  blocking collectives: 25.2 us -> 24.7 us
    unnamed x8, local copies, waits for them, and re-layouts: 0.03 us -> 3.16 us
    pallas_call x1, Pallas kernels: 5.4 us -> 3.27 us  [prepare(): pl.pallas_call(functools.partial(prepare_kernel, cells_s, cells_g, cells_...]
    pallas_call x1, Pallas kernels: 5.25 us -> 5.88 us  [section(): pl.pallas_call(section_kernel, out_shape=(shape(velocity.shape), shape(en...]
    pallas_call x1, Pallas kernels: 0.98 us -> 1.6 us  [pack(): pl.pallas_call(pack_kernel, out_shape=(stream, stream, girth, girth) + (p...]
    all_to_all x1, blocking collectives: 25.2 us -> 24.7 us  [body(): lax.all_to_all(partial.reshape(devices, radii // devices, 6 * NH), ('stre...]
  transfers between devices with their start and end apart: 4 -> 4, of which waited for: 0 -> 0; matrix products, arithmetic and copies ran while one was open for 0% -> 0% of each run, Pallas kernels for 13% -> 7%
where the time goes in v5:
time: 45.2 us; the launch traced here: 44.6 us
  blocking collectives  24.7 us (55%)
  Pallas kernels  10.7 us (24%)
  starting transfers between devices  4.48 us (10%)
  local copies, waits for them, and re-layouts  3.27 us (7%)
  between operations  0.73 us (2%)
  other arithmetic  0.68 us (2%)
    all_to_all x1, blocking collectives, body(): lax.all_to_all(partial.reshape(devices, radii // devices, 6 * NH), ('stre...  24.7 us
    pallas_call x1, Pallas kernels, section(): pl.pallas_call(section_kernel, out_shape=(shape(velocity.shape), shape(en...  5.88 us
    ppermute x4, starting transfers between devices, swap(): return lax.ppermute(values, axis, pairs)  4.48 us
    pallas_call x1, Pallas kernels, prepare(): pl.pallas_call(functools.partial(prepare_kernel, cells_s, cells_g, cells_...  3.27 us
    unnamed x8, local copies, waits for them, and re-layouts  3.16 us
    pallas_call x1, Pallas kernels, pack(): pl.pallas_call(pack_kernel, out_shape=(stream, stream, girth, girth) + (p...  1.6 us
  transfers between devices with their start and end apart: 4, of which 0 were waited for; matrix products, arithmetic and copies ran while one was open for 0% of the time, Pallas kernels for 7%

profile of v5, /device:TPU:0, one launch (start us, length us, event | category | flops | bytes accessed | tf_op | source)
XLA Modules:
  0.0 44.6 jit_solution(6735581219417200637)
XLA Ops:
  0.6 0.0 copy-start
  0.6 0.9 %copy-done = f32[3,4,8,256]{3,2,1,0:T(8,128)S(1)} copy-done((f32[3,4,8,256]{3,2,1,0:T(8,128)S(1)}, f32[3,4,8,256]{3,2,1,0:T(8,128)}, u32[]{:S(2)}) %copy-start) | copy-done | bytes 98328
  1.5 0.0 copy-start.1
  1.5 0.8 %copy-done.1 = f32[4,8,256]{2,1,0:T(8,128)S(1)} copy-done((f32[4,8,256]{2,1,0:T(8,128)S(1)}, f32[4,8,256]{2,1,0:T(8,128)}, u32[]{:S(2)}) %copy-start.1) | copy-done | bytes 32792
  2.3 0.0 copy-start.2
  2.3 0.8 %copy-done.2 = f32[4,8,256]{2,1,0:T(8,128)S(1)} copy-done((f32[4,8,256]{2,1,0:T(8,128)S(1)}, f32[4,8,256]{2,1,0:T(8,128)}, u32[]{:S(2)}) %copy-start.2) | copy-done | bytes 32792
  3.0 0.0 copy-start.3
  3.0 0.8 %copy-done.3 = f32[4,8,256]{2,1,0:T(8,128)S(1)} copy-done((f32[4,8,256]{2,1,0:T(8,128)S(1)}, f32[4,8,256]{2,1,0:T(8,128)}, u32[]{:S(2)}) %copy-start.3) | copy-done | bytes 32792
  3.8 1.6 %pack_halos.1 = (f32[6,2,8,256]{3,2,1,0:T(8,128)S(1)}, f32[6,2,8,256]{3,2,1,0:T(8,128)S(1)}, f32[6,4,2,256]{3,2,1,0:T(2,128)S(1)}, f32[6,4,2,256]{3,2,1,0:T(2,12...) custom-call(f32[3,4,8,256]{3,2,1,0:T(8,128)S(1)} %copy-done, f32[4,8,256]{2,1,0:T(8,128)S(1)} %copy-done.1, ...), custom_call_target="tpu_custom_call" | custom-call | tf_op jit(solution)/shard_map/pack_halos/pallas_call | solution.py:62
  5.4 3.1 %collective-permute-start = (f32[6,2,8,256]{3,2,1,0:T(8,128)S(1)}, f32[6,2,8,256]{3,2,1,0:T(8,128)S(1)}, u32[]{:S(2)}, u32[]{:S(2)}) collective-permute-start(f32[6,2,8,256]{3,2,1,0:T(8,128)S(1)} %get-tuple-element.24), channel_id=1, source_target_pairs={{0,8},{8,0},{16,24},{24,16},{1,9},{9,1},{17,25},{25,17},{2,10},{10... | collective-permute-start | bytes 294920 | tf_op jit(solution)/shard_map/ppermute | solution.py:575
  8.5 0.7 %collective-permute-start.1 = (f32[6,2,8,256]{3,2,1,0:T(8,128)S(1)}, f32[6,2,8,256]{3,2,1,0:T(8,128)S(1)}, u32[]{:S(2)}, u32[]{:S(2)}) collective-permute-start(f32[6,2,8,256]{3,2,1,0:T(8,128)S(1)} %get-tuple-element.25), channel_id=1, source_target_pairs={{8,16},{16,8},{9,17},{17,9},{10,18},{18,10},{11,19},{19,11},{12,20... | collective-permute-start | bytes 294920 | tf_op jit(solution)/shard_map/ppermute | solution.py:575
  9.2 0.1 collective-permute-start.2
  9.2 0.7 %collective-permute-start.3 = (f32[6,4,2,256]{3,2,1,0:T(2,128)S(1)}, f32[6,4,2,256]{3,2,1,0:T(2,128)S(1)}, u32[]{:S(2)}, u32[]{:S(2)}) collective-permute-start(f32[6,4,2,256]{3,2,1,0:T(2,128)S(1)} %get-tuple-element.27), channel_id=1, source_target_pairs={{1,2},{2,1},{3,4},{4,3},{5,6},{6,5},{9,10},{10,9},{11,12},{12,11},... | collective-permute-start | bytes 147464 | tf_op jit(solution)/shard_map/ppermute | solution.py:575
  9.9 3.3 %prepare_points.1 = (s32[384,128]{1,0:T(8,128)S(1)}, f32[384,128]{1,0:T(8,128)S(1)}, f32[384,128]{1,0:T(8,128)S(1)}, f32[384,128]{1,0:T(8,128)S(1)}, s32[640,128...) custom-call(s32[64]{0:T(128)} %bitcast.1, s32[128,1024]{1,0:T(8,128)S(1)} %get-tuple-element.21.ids_ref, ...), custom_call_target="tpu_custom_call" | custom-call | flops 2621440 | bytes 5767168 | tf_op jit(solution)/shard_map/prepare_points/pallas_call | solution.py:220
  13.2 0.0 collective-permute-done.2.girth_a
  13.2 0.0 collective-permute-done.3.girth_b
  13.2 0.0 collective-permute-done.stream_a
  13.2 0.0 collective-permute-done.1.stream_b
  13.2 5.9 %section_and_disk.1 = (f32[3,4,8,256]{3,2,1,0:T(8,128)}, f32[4,8,256]{2,1,0:T(8,128)}, f32[4,8,256]{2,1,0:T(8,128)}, f32[128,768]{1,0:T(8,128)S(1)}) custom-call(s32[1]{0:T(128)} %get-tuple-element.23.count_ref, f32[3,4,8,256]{3,2,1,0:T(8,128)S(1)} %copy-done, f32[4,8,256]{2,1,0:T(8,128)S(1)} %copy-done.1, f32[4,8,256]{2,1,0:T(8,128)S(1)} %copy-done.2, ...), custom_call_target="tpu_custom_call" | custom-call | tf_op jit(solution)/shard_map/section_and_disk/pallas_call | solution.py:531
  19.1 0.1 reshape.11
  19.2 24.7 %all_to_all.5 = f32[32,4,768]{2,1,0:T(4,128)S(1)} all-to-all(f32[32,4,768]{2,1,0:T(4,128)S(1)} %reshape.11), channel_id=1, replica_groups=mesh['stream'=4,'girth'=8] {'stream','girth'}, dimensions={0} | all-to-all | bytes 786432 | tf_op jit(solution)/shard_map/all_to_all | solution.py:600
  43.9 0.7 %reduce_sum.9 = f32[4,768]{1,0:T(4,128)} reduce(f32[32,4,768]{2,1,0:T(4,128)S(1)} %all_to_all.5, f32[]{:T(128)} %constant.1.clone.1), dimensions={0}, to_apply=%region_0.0 | reduce | flops 95232 | bytes 405508 | tf_op jit(solution)/shard_map/reduce_sum | solution.py:607
Async XLA Ops:
  0.6 0.9 %copy-start = (f32[3,4,8,256]{3,2,1,0:T(8,128)S(1)}, f32[3,4,8,256]{3,2,1,0:T(8,128)}, u32[]{:S(2)}) copy-start(f32[3,4,8,256]{3,2,1,0:T(8,128)} %vel_ref.3) | copy-start | bytes 294916
  1.5 0.8 %copy-start.1 = (f32[4,8,256]{2,1,0:T(8,128)S(1)}, f32[4,8,256]{2,1,0:T(8,128)}, u32[]{:S(2)}) copy-start(f32[4,8,256]{2,1,0:T(8,128)} %p_ref.3) | copy-start | bytes 98308
  2.3 0.8 %copy-start.2 = (f32[4,8,256]{2,1,0:T(8,128)S(1)}, f32[4,8,256]{2,1,0:T(8,128)}, u32[]{:S(2)}) copy-start(f32[4,8,256]{2,1,0:T(8,128)} %k_ref.3) | copy-start | bytes 98308
  3.0 0.8 %copy-start.3 = (f32[4,8,256]{2,1,0:T(8,128)S(1)}, f32[4,8,256]{2,1,0:T(8,128)}, u32[]{:S(2)}) copy-start(f32[4,8,256]{2,1,0:T(8,128)} %w_ref.3) | copy-start | bytes 98308
  5.4 7.8 %collective-permute-start = (f32[6,2,8,256]{3,2,1,0:T(8,128)S(1)}, f32[6,2,8,256]{3,2,1,0:T(8,128)S(1)}, u32[]{:S(2)}, u32[]{:S(2)}) collective-permute-start(f32[6,2,8,256]{3,2,1,0:T(8,128)S(1)} %get-tuple-element.24), channel_id=1, source_target_pairs={{0,8},{8,0},{16,24},{24,16},{1,9},{9,1},{17,25},{25,17},{2,10},{10... | collective-permute-start | bytes 294920 | tf_op jit(solution)/shard_map/ppermute | solution.py:575
  8.5 4.7 %collective-permute-start.1 = (f32[6,2,8,256]{3,2,1,0:T(8,128)S(1)}, f32[6,2,8,256]{3,2,1,0:T(8,128)S(1)}, u32[]{:S(2)}, u32[]{:S(2)}) collective-permute-start(f32[6,2,8,256]{3,2,1,0:T(8,128)S(1)} %get-tuple-element.25), channel_id=1, source_target_pairs={{8,16},{16,8},{9,17},{17,9},{10,18},{18,10},{11,19},{19,11},{12,20... | collective-permute-start | bytes 294920 | tf_op jit(solution)/shard_map/ppermute | solution.py:575
  9.2 4.0 %collective-permute-start.2 = (f32[6,4,2,256]{3,2,1,0:T(2,128)S(1)}, f32[6,4,2,256]{3,2,1,0:T(2,128)S(1)}, u32[]{:S(2)}, u32[]{:S(2)}) collective-permute-start(f32[6,4,2,256]{3,2,1,0:T(2,128)S(1)} %get-tuple-element.26), channel_id=1, source_target_pairs={{0,1},{1,0},{2,3},{3,2},{4,5},{5,4},{6,7},{7,6},{8,9},{9,8},{10,11... | collective-permute-start | bytes 147464 | tf_op jit(solution)/shard_map/ppermute | solution.py:575
  9.2 4.0 %collective-permute-start.3 = (f32[6,4,2,256]{3,2,1,0:T(2,128)S(1)}, f32[6,4,2,256]{3,2,1,0:T(2,128)S(1)}, u32[]{:S(2)}, u32[]{:S(2)}) collective-permute-start(f32[6,4,2,256]{3,2,1,0:T(2,128)S(1)} %get-tuple-element.27), channel_id=1, source_target_pairs={{1,2},{2,1},{3,4},{4,3},{5,6},{6,5},{9,10},{10,9},{11,12},{12,11},... | collective-permute-start | bytes 147464 | tf_op jit(solution)/shard_map/ppermute | solution.py:575

commit v6 on v5

--- a/solution.py
+++ b/solution.py
@@ -68,7 +68,7 @@
         scratch_shapes=[pltpu.SemaphoreType.DMA((2,))],
         compiler_params=pltpu.CompilerParams(vmem_limit_bytes=VMEM_LIMIT),
         name="pack_halos",
-    )(velocity, pressure, energy, rate, in_hbm(corner_ids), in_hbm(fractions))
+    )(*(in_hbm(x) for x in (velocity, pressure, energy, rate, corner_ids, fractions)))
 
 
 def network(rows):

time: 45.2 us -> 42.1 us (0.931); the launches traced: 44.6 us -> 42.6 us
  local copies, waits for them, and re-layouts: 3.27 us -> 0.14 us
  blocking collectives: 24.7 us -> 26.8 us
  Pallas kernels: 10.7 us -> 9.66 us
    unnamed x8, local copies, waits for them, and re-layouts: 3.16 us -> 0.03 us
    all_to_all x1, blocking collectives: 24.7 us -> 26.8 us  [body(): lax.all_to_all(partial.reshape(devices, radii // devices, 6 * NH), ('stre...]
    pallas_call x1, Pallas kernels: 5.88 us -> 3.82 us  [section(): pl.pallas_call(section_kernel, out_shape=(shape(velocity.shape), shape(en...]
    pallas_call x1, Pallas kernels: 1.6 us -> 2.52 us  [pack(): pl.pallas_call(pack_kernel, out_shape=(stream, stream, girth, girth) + (p...]
  transfers between devices with their start and end apart: 4 -> 4, of which waited for: 0 -> 0; matrix products, arithmetic and copies ran while one was open for 0% -> 0% of each run, Pallas kernels for 7% -> 8%
where the time goes in v6:
time: 42.1 us; the launch traced here: 42.6 us
  blocking collectives  26.8 us (64%)
  Pallas kernels  9.66 us (23%)
  starting transfers between devices  4.48 us (11%)
  between operations  0.78 us (2%)
  other arithmetic  0.68 us (2%)
    all_to_all x1, blocking collectives, body(): lax.all_to_all(partial.reshape(devices, radii // devices, 6 * NH), ('stre...  26.8 us
    ppermute x4, starting transfers between devices, swap(): return lax.ppermute(values, axis, pairs)  4.48 us
    pallas_call x1, Pallas kernels, section(): pl.pallas_call(section_kernel, out_shape=(shape(velocity.shape), shape(en...  3.82 us
    pallas_call x1, Pallas kernels, prepare(): pl.pallas_call(functools.partial(prepare_kernel, cells_s, cells_g, cells_...  3.32 us
    pallas_call x1, Pallas kernels, pack(): pl.pallas_call(pack_kernel, out_shape=(stream, stream, girth, girth) + (p...  2.52 us
  transfers between devices with their start and end apart: 4, of which 0 were waited for; matrix products, arithmetic and copies ran while one was open for 0% of the time, Pallas kernels for 8%

profile of v6, /device:TPU:0, one launch (start us, length us, event | category | flops | bytes accessed | tf_op | source)
XLA Modules:
  0.0 42.6 jit_solution(11382679677561997288)
XLA Ops:
  0.6 2.5 %pack_halos.1 = (f32[6,2,8,256]{3,2,1,0:T(8,128)S(1)}, f32[6,2,8,256]{3,2,1,0:T(8,128)S(1)}, f32[6,4,2,256]{3,2,1,0:T(2,128)S(1)}, f32[6,4,2,256]{3,2,1,0:T(2,12...) custom-call(f32[3,4,8,256]{3,2,1,0:T(8,128)} %vel_ref.3, f32[4,8,256]{2,1,0:T(8,128)} %p_ref.3, ...), custom_call_target="tpu_custom_call" | custom-call | tf_op jit(solution)/shard_map/pack_halos/pallas_call | solution.py:62
  3.2 3.1 %collective-permute-start = (f32[6,2,8,256]{3,2,1,0:T(8,128)S(1)}, f32[6,2,8,256]{3,2,1,0:T(8,128)S(1)}, u32[]{:S(2)}, u32[]{:S(2)}) collective-permute-start(f32[6,2,8,256]{3,2,1,0:T(8,128)S(1)} %get-tuple-element.24), channel_id=1, source_target_pairs={{0,8},{8,0},{16,24},{24,16},{1,9},{9,1},{17,25},{25,17},{2,10},{10... | collective-permute-start | bytes 294920 | tf_op jit(solution)/shard_map/ppermute | solution.py:575
  6.2 0.7 %collective-permute-start.1 = (f32[6,2,8,256]{3,2,1,0:T(8,128)S(1)}, f32[6,2,8,256]{3,2,1,0:T(8,128)S(1)}, u32[]{:S(2)}, u32[]{:S(2)}) collective-permute-start(f32[6,2,8,256]{3,2,1,0:T(8,128)S(1)} %get-tuple-element.25), channel_id=1, source_target_pairs={{8,16},{16,8},{9,17},{17,9},{10,18},{18,10},{11,19},{19,11},{12,20... | collective-permute-start | bytes 294920 | tf_op jit(solution)/shard_map/ppermute | solution.py:575
  6.9 0.1 collective-permute-start.2
  7.0 0.7 %collective-permute-start.3 = (f32[6,4,2,256]{3,2,1,0:T(2,128)S(1)}, f32[6,4,2,256]{3,2,1,0:T(2,128)S(1)}, u32[]{:S(2)}, u32[]{:S(2)}) collective-permute-start(f32[6,4,2,256]{3,2,1,0:T(2,128)S(1)} %get-tuple-element.27), channel_id=1, source_target_pairs={{1,2},{2,1},{3,4},{4,3},{5,6},{6,5},{9,10},{10,9},{11,12},{12,11},... | collective-permute-start | bytes 147464 | tf_op jit(solution)/shard_map/ppermute | solution.py:575
  7.7 0.0 copy-start
  7.7 0.0 copy-start.1
  7.7 0.0 copy-start.2
  7.7 0.0 copy-start.3
  7.7 3.3 %prepare_points.1 = (s32[384,128]{1,0:T(8,128)S(1)}, f32[384,128]{1,0:T(8,128)S(1)}, f32[384,128]{1,0:T(8,128)S(1)}, f32[384,128]{1,0:T(8,128)S(1)}, s32[640,128...) custom-call(s32[64]{0:T(128)} %bitcast.1, s32[128,1024]{1,0:T(8,128)S(1)} %get-tuple-element.21.ids_ref, ...), custom_call_target="tpu_custom_call" | custom-call | flops 2621440 | bytes 5767168 | tf_op jit(solution)/shard_map/prepare_points/pallas_call | solution.py:220
  11.0 0.0 collective-permute-done.2.girth_a
  11.0 0.0 collective-permute-done.3.girth_b
  11.1 0.0 collective-permute-done.stream_a
  11.1 0.0 collective-permute-done.1.stream_b
  11.1 0.0 copy-done
  11.1 0.0 copy-done.1
  11.1 0.0 copy-done.2
  11.1 0.0 copy-done.3
  11.1 3.8 %section_and_disk.1 = (f32[3,4,8,256]{3,2,1,0:T(8,128)}, f32[4,8,256]{2,1,0:T(8,128)}, f32[4,8,256]{2,1,0:T(8,128)}, f32[128,768]{1,0:T(8,128)S(1)}) custom-call(s32[1]{0:T(128)} %get-tuple-element.23.count_ref, f32[3,4,8,256]{3,2,1,0:T(8,128)S(1)} %copy-done, f32[4,8,256]{2,1,0:T(8,128)S(1)} %copy-done.1, f32[4,8,256]{2,1,0:T(8,128)S(1)} %copy-done.2, ...), custom_call_target="tpu_custom_call" | custom-call | tf_op jit(solution)/shard_map/section_and_disk/pallas_call | solution.py:531
  14.9 0.1 reshape.11
  15.1 26.8 %all_to_all.5 = f32[32,4,768]{2,1,0:T(4,128)S(1)} all-to-all(f32[32,4,768]{2,1,0:T(4,128)S(1)} %reshape.11), channel_id=1, replica_groups=mesh['stream'=4,'girth'=8] {'stream','girth'}, dimensions={0} | all-to-all | bytes 786432 | tf_op jit(solution)/shard_map/all_to_all | solution.py:600
  41.9 0.7 %reduce_sum.9 = f32[4,768]{1,0:T(4,128)} reduce(f32[32,4,768]{2,1,0:T(4,128)S(1)} %all_to_all.5, f32[]{:T(128)} %constant.1.clone.1), dimensions={0}, to_apply=%region_0.0 | reduce | flops 95232 | bytes 405508 | tf_op jit(solution)/shard_map/reduce_sum | solution.py:607
Async XLA Ops:
  3.2 7.9 %collective-permute-start = (f32[6,2,8,256]{3,2,1,0:T(8,128)S(1)}, f32[6,2,8,256]{3,2,1,0:T(8,128)S(1)}, u32[]{:S(2)}, u32[]{:S(2)}) collective-permute-start(f32[6,2,8,256]{3,2,1,0:T(8,128)S(1)} %get-tuple-element.24), channel_id=1, source_target_pairs={{0,8},{8,0},{16,24},{24,16},{1,9},{9,1},{17,25},{25,17},{2,10},{10... | collective-permute-start | bytes 294920 | tf_op jit(solution)/shard_map/ppermute | solution.py:575
  6.2 4.8 %collective-permute-start.1 = (f32[6,2,8,256]{3,2,1,0:T(8,128)S(1)}, f32[6,2,8,256]{3,2,1,0:T(8,128)S(1)}, u32[]{:S(2)}, u32[]{:S(2)}) collective-permute-start(f32[6,2,8,256]{3,2,1,0:T(8,128)S(1)} %get-tuple-element.25), channel_id=1, source_target_pairs={{8,16},{16,8},{9,17},{17,9},{10,18},{18,10},{11,19},{19,11},{12,20... | collective-permute-start | bytes 294920 | tf_op jit(solution)/shard_map/ppermute | solution.py:575
  6.9 4.1 %collective-permute-start.2 = (f32[6,4,2,256]{3,2,1,0:T(2,128)S(1)}, f32[6,4,2,256]{3,2,1,0:T(2,128)S(1)}, u32[]{:S(2)}, u32[]{:S(2)}) collective-permute-start(f32[6,4,2,256]{3,2,1,0:T(2,128)S(1)} %get-tuple-element.26), channel_id=1, source_target_pairs={{0,1},{1,0},{2,3},{3,2},{4,5},{5,4},{6,7},{7,6},{8,9},{9,8},{10,11... | collective-permute-start | bytes 147464 | tf_op jit(solution)/shard_map/ppermute | solution.py:575
  7.0 4.1 %collective-permute-start.3 = (f32[6,4,2,256]{3,2,1,0:T(2,128)S(1)}, f32[6,4,2,256]{3,2,1,0:T(2,128)S(1)}, u32[]{:S(2)}, u32[]{:S(2)}) collective-permute-start(f32[6,4,2,256]{3,2,1,0:T(2,128)S(1)} %get-tuple-element.27), channel_id=1, source_target_pairs={{1,2},{2,1},{3,4},{4,3},{5,6},{6,5},{9,10},{10,9},{11,12},{12,11},... | collective-permute-start | bytes 147464 | tf_op jit(solution)/shard_map/ppermute | solution.py:575
  7.7 3.4 %copy-start = (f32[3,4,8,256]{3,2,1,0:T(8,128)S(1)}, f32[3,4,8,256]{3,2,1,0:T(8,128)}, u32[]{:S(2)}) copy-start(f32[3,4,8,256]{3,2,1,0:T(8,128)} %vel_ref.3) | copy-start | bytes 294916
  7.7 3.4 %copy-start.1 = (f32[4,8,256]{2,1,0:T(8,128)S(1)}, f32[4,8,256]{2,1,0:T(8,128)}, u32[]{:S(2)}) copy-start(f32[4,8,256]{2,1,0:T(8,128)} %p_ref.3) | copy-start | bytes 98308
  7.7 3.4 %copy-start.2 = (f32[4,8,256]{2,1,0:T(8,128)S(1)}, f32[4,8,256]{2,1,0:T(8,128)}, u32[]{:S(2)}) copy-start(f32[4,8,256]{2,1,0:T(8,128)} %k_ref.3) | copy-start | bytes 98308
  7.7 3.4 %copy-start.3 = (f32[4,8,256]{2,1,0:T(8,128)S(1)}, f32[4,8,256]{2,1,0:T(8,128)}, u32[]{:S(2)}) copy-start(f32[4,8,256]{2,1,0:T(8,128)} %w_ref.3) | copy-start | bytes 98308

commit v7 on v6

--- a/solution.py
+++ b/solution.py
@@ -30,14 +30,7 @@
     return pltpu.with_memory_space_constraint(values, pltpu.HBM)
 
 
-def pack_kernel(vel_ref, p_ref, k_ref, w_ref, ids_hbm, frac_hbm, *rest):
-    *slabs, ids_ref, frac_ref, arrived = rest
-    copies = [
-        pltpu.make_async_copy(ids_hbm, ids_ref, arrived.at[0]),
-        pltpu.make_async_copy(frac_hbm, frac_ref, arrived.at[1]),
-    ]
-    for copy in copies:
-        copy.start()
+def pack_kernel(vel_ref, p_ref, k_ref, w_ref, *slabs):
     cells_s, cells_g, _ = p_ref.shape
     stream_odd = lax.axis_index("stream") % 2 == 1
     girth_odd = lax.axis_index("girth") % 2 == 1
@@ -49,26 +42,20 @@
         first, last = own[:, 0:2, :], own[:, cells_g - 2 : cells_g, :]
         slabs[2][f] = jnp.where(girth_odd, first, last)
         slabs[3][f] = jnp.where(girth_odd, last, first)
-    for copy in copies:
-        copy.wait()
-
-
-def pack(velocity, pressure, energy, rate, corner_ids, fractions):
+
+
+def pack(velocity, pressure, energy, rate):
     _, cells_s, cells_g, cells_r = velocity.shape
     stream = pltpu.VMEM((6, 2, cells_g, cells_r), jnp.float32)
     girth = pltpu.VMEM((6, cells_s, 2, cells_r), jnp.float32)
     vmem = pl.BlockSpec(memory_space=pltpu.VMEM)
-    hbm = pl.BlockSpec(memory_space=pltpu.HBM)
     return pl.pallas_call(
         pack_kernel,
-        out_shape=(stream, stream, girth, girth)
-        + (pltpu.VMEM(corner_ids.shape, jnp.int32), pltpu.VMEM(fractions.shape, jnp.float32)),
-        in_specs=[vmem] * 4 + [hbm] * 2,
-        out_specs=[vmem] * 6,
-        scratch_shapes=[pltpu.SemaphoreType.DMA((2,))],
-        compiler_params=pltpu.CompilerParams(vmem_limit_bytes=VMEM_LIMIT),
+        out_shape=(stream, stream, girth, girth),
+        in_specs=[vmem] * 4,
+        out_specs=[vmem] * 4,
         name="pack_halos",
-    )(*(in_hbm(x) for x in (velocity, pressure, energy, rate, corner_ids, fractions)))
+    )(*(in_hbm(x) for x in (velocity, pressure, energy, rate)))
 
 
 def network(rows):
@@ -91,8 +78,8 @@
     cells_g,
     cells_r,
     owner_ref,
-    ids_ref,
-    frac_ref,
+    ids_hbm,
+    frac_hbm,
     table_hbm,
     q_ref,
     fr_ref,
@@ -101,6 +88,8 @@
     moves_ref,
     chosen_ref,
     count_ref,
+    ids_ref,
+    frac_ref,
     table_ref,
     turned,
     picked,
@@ -111,8 +100,12 @@
     order,
     arrived,
 ):
-    copy = pltpu.make_async_copy(table_hbm, table_ref, arrived.at[0])
-    copy.start()
+    copies = [pltpu.make_async_copy(ids_hbm, ids_ref, arrived.at[0])]
+    for d in range(3):
+        copies.append(pltpu.make_async_copy(frac_hbm.at[d], frac_ref.at[d], arrived.at[1 + d]))
+    copies.append(pltpu.make_async_copy(table_hbm, table_ref, arrived.at[4]))
+    for copy in copies:
+        copy.start()
     stream_first = lax.axis_index("stream") * cells_s
     me = lax.axis_index("girth")
     sectors = owner_ref.shape[0]
@@ -129,11 +122,6 @@
 
     owned = lax.fori_loop(0, sectors, listed, jnp.int32(0), unroll=8)
 
-    for at in range(0, azimuths, LANES):
-        cols = pl.ds(at, LANES)
-        turned[0, cols, :] = ids_ref[:, cols].astype(jnp.float32).T
-        for d in range(3):
-            turned[1 + d, cols, :] = frac_ref[d, :, cols].T
     for d in range(4):
         picked[d] = jnp.full(picked.shape[1:], -1.0 if d == 0 else 0.0, jnp.float32)
     chosen_ref[...] = jnp.zeros_like(chosen_ref)
@@ -141,7 +129,13 @@
     for slot in range(2):
         keys[slot, beyond, :] = jnp.zeros((pad, LANES), jnp.int32)
     moves_ref[0:pad, :] = jnp.zeros((pad, LANES), jnp.int32)
-    copy.wait()
+    for d in range(4):
+        copies[d].wait()
+        for at in range(0, azimuths, LANES):
+            cols = pl.ds(at, LANES)
+            plane = ids_ref[:, cols].astype(jnp.float32) if d == 0 else frac_ref[d - 1, :, cols]
+            turned[d, cols, :] = plane.T
+    copies[4].wait()
 
     def sector(place, carry):
         source = pl.ds(pl.multiple_of(order[place] * width, width), width)
@@ -228,9 +222,11 @@
             shape((rows, 2 * NH), jnp.float32),
             shape((1,), jnp.int32),
         ),
-        in_specs=[smem, vmem, vmem, hbm],
+        in_specs=[smem, hbm, hbm, hbm],
         out_specs=[vmem] * 6 + [smem],
         scratch_shapes=[
+            pltpu.VMEM(corner_ids.shape, jnp.int32),
+            pltpu.VMEM(fractions.shape, jnp.float32),
             pltpu.VMEM(table.shape, jnp.float32),
             pltpu.VMEM((4, azimuths, radii), jnp.float32),
             pltpu.VMEM((4, rows, radii), jnp.float32),
@@ -238,13 +234,13 @@
         ]
         + [pltpu.VMEM((2, rows + pad, radii), jnp.float32)] * 3
         + [pltpu.SMEM((rows // (azimuths // sectors) + 1,), jnp.int32)]
-        + [pltpu.SemaphoreType.DMA((1,))],
+        + [pltpu.SemaphoreType.DMA((5,))],
         compiler_params=pltpu.CompilerParams(vmem_limit_bytes=VMEM_LIMIT),
         cost_estimate=pl.CostEstimate(
             flops=20 * radii * azimuths, bytes_accessed=44 * radii * azimuths, transcendentals=0
         ),
         name="prepare_points",
-    )(in_hbm(owners), corner_ids, fractions, in_hbm(table))
+    )(*(in_hbm(x) for x in (owners, corner_ids, fractions, table)))
 
 
 def radial(values, amount, fill):
@@ -574,9 +570,7 @@
             pairs += [(i, i + 1), (i + 1, i)]
         return lax.ppermute(values, axis, pairs)
 
-    *slabs, ids, fracs = pack(
-        velocity, pressure, kinetic_energy, dissipation_rate, corner_ids, fractions
-    )
+    slabs = pack(velocity, pressure, kinetic_energy, dissipation_rate)
     girth_halos = (
         swap(slabs[2], "girth", girth_count, 0),
         swap(slabs[3], "girth", girth_count, 1),
@@ -588,8 +582,8 @@
     halos = stream_halos + girth_halos
     points = prepare(
         sector_owner[:, 0],
-        ids,
-        fracs,
+        corner_ids,
+        fractions,
         fourier_table(azimuths, NH),
         (cells_s, cells_g, cells_r),
         girth_count,

time: 42.1 us -> 41.4 us (0.983)
  blocking collectives: 26.8 us -> 25.8 us
    pallas_call x1, Pallas kernels: 2.52 us -> 0.98 us  [pack(): pl.pallas_call(pack_kernel, out_shape=(stream, stream, girth, girth), in_...]
    pallas_call x1, Pallas kernels: 3.82 us -> 4.86 us  [section(): pl.pallas_call(section_kernel, out_shape=(shape(velocity.shape), shape(en...]
    all_to_all x1, blocking collectives: 26.8 us -> 25.8 us  [body(): lax.all_to_all(partial.reshape(devices, radii // devices, 6 * NH), ('stre...]
    pallas_call x1, Pallas kernels: 3.32 us -> 4.02 us  [prepare(): pl.pallas_call(functools.partial(prepare_kernel, cells_s, cells_g, cells_...]
  transfers between devices with their start and end apart: 4 -> 4, of which waited for: 0 -> 0; matrix products, arithmetic and copies ran while one was open for 0% -> 0% of each run, Pallas kernels for 8% -> 10%
where the time goes in v7:
time: 41.4 us; the launch traced here: 41.7 us
  blocking collectives  25.8 us (62%)
  Pallas kernels  9.86 us (24%)
  starting transfers between devices  4.48 us (11%)
  between operations  0.78 us (2%)
  other arithmetic  0.68 us (2%)
    all_to_all x1, blocking collectives, body(): lax.all_to_all(partial.reshape(devices, radii // devices, 6 * NH), ('stre...  25.8 us
    pallas_call x1, Pallas kernels, section(): pl.pallas_call(section_kernel, out_shape=(shape(velocity.shape), shape(en...  4.86 us
    ppermute x4, starting transfers between devices, swap(): return lax.ppermute(values, axis, pairs)  4.48 us
    pallas_call x1, Pallas kernels, prepare(): pl.pallas_call(functools.partial(prepare_kernel, cells_s, cells_g, cells_...  4.02 us
    pallas_call x1, Pallas kernels, pack(): pl.pallas_call(pack_kernel, out_shape=(stream, stream, girth, girth), in_...  0.98 us
  transfers between devices with their start and end apart: 4, of which 0 were waited for; matrix products, arithmetic and copies ran while one was open for 0% of the time, Pallas kernels for 10%

profile of v7, /device:TPU:0, one launch (start us, length us, event | category | flops | bytes accessed | tf_op | source)
XLA Modules:
  0.0 41.7 jit_solution(9149241630655901786)
XLA Ops:
  0.6 1.0 %pack_halos.1 = (f32[6,2,8,256]{3,2,1,0:T(8,128)S(1)}, f32[6,2,8,256]{3,2,1,0:T(8,128)S(1)}, f32[6,4,2,256]{3,2,1,0:T(2,128)S(1)}, f32[6,4,2,256]{3,2,1,0:T(2,128)S(1)}) custom-call(f32[3,4,8,256]{3,2,1,0:T(8,128)} %vel_ref.3, f32[4,8,256]{2,1,0:T(8,128)} %p_ref.3, f32[4,8,256]{2,1,0:T(8,128)} %k_ref.3, f32[4,8,256]{2,1,0:T(8,128)} %w_ref.3), custom_call_target="tpu_custom_call" | custom-call | tf_op jit(solution)/shard_map/pack_halos/pallas_call | solution.py:52
  1.6 3.1 %collective-permute-start = (f32[6,2,8,256]{3,2,1,0:T(8,128)S(1)}, f32[6,2,8,256]{3,2,1,0:T(8,128)S(1)}, u32[]{:S(2)}, u32[]{:S(2)}) collective-permute-start(f32[6,2,8,256]{3,2,1,0:T(8,128)S(1)} %get-tuple-element.20), channel_id=1, source_target_pairs={{0,8},{8,0},{16,24},{24,16},{1,9},{9,1},{17,25},{25,17},{2,10},{10... | collective-permute-start | bytes 294920 | tf_op jit(solution)/shard_map/ppermute | solution.py:571
  4.7 0.7 %collective-permute-start.1 = (f32[6,2,8,256]{3,2,1,0:T(8,128)S(1)}, f32[6,2,8,256]{3,2,1,0:T(8,128)S(1)}, u32[]{:S(2)}, u32[]{:S(2)}) collective-permute-start(f32[6,2,8,256]{3,2,1,0:T(8,128)S(1)} %get-tuple-element.21), channel_id=1, source_target_pairs={{8,16},{16,8},{9,17},{17,9},{10,18},{18,10},{11,19},{19,11},{12,20... | collective-permute-start | bytes 294920 | tf_op jit(solution)/shard_map/ppermute | solution.py:571
  5.4 0.1 collective-permute-start.2
  5.4 0.7 %collective-permute-start.3 = (f32[6,4,2,256]{3,2,1,0:T(2,128)S(1)}, f32[6,4,2,256]{3,2,1,0:T(2,128)S(1)}, u32[]{:S(2)}, u32[]{:S(2)}) collective-permute-start(f32[6,4,2,256]{3,2,1,0:T(2,128)S(1)} %get-tuple-element.23), channel_id=1, source_target_pairs={{1,2},{2,1},{3,4},{4,3},{5,6},{6,5},{9,10},{10,9},{11,12},{12,11},... | collective-permute-start | bytes 147464 | tf_op jit(solution)/shard_map/ppermute | solution.py:571
  6.1 0.0 copy-start
  6.1 0.0 copy-start.1
  6.1 0.0 copy-start.2
  6.2 0.0 copy-start.3
  6.2 4.0 %prepare_points.1 = (s32[384,128]{1,0:T(8,128)S(1)}, f32[384,128]{1,0:T(8,128)S(1)}, f32[384,128]{1,0:T(8,128)S(1)}, f32[384,128]{1,0:T(8,128)S(1)}, s32[640,128...) custom-call(s32[64]{0:T(128)} %bitcast.1, s32[128,1024]{1,0:T(8,128)} %ids_hbm.1, f32[3,128,1024]{2,1,0:T(8,128)} %frac_hbm.1, ...), custom_call_target="tpu_custom_call" | custom-call | flops 2621440 | bytes 5767168 | tf_op jit(solution)/shard_map/prepare_points/pallas_call | solution.py:214
  10.2 0.0 collective-permute-done.2.girth_a
  10.2 0.0 collective-permute-done.3.girth_b
  10.2 0.0 collective-permute-done.stream_a
  10.2 0.0 collective-permute-done.1.stream_b
  10.2 0.0 copy-done
  10.3 0.0 copy-done.1
  10.3 0.0 copy-done.2
  10.3 0.0 copy-done.3
  10.3 4.9 %section_and_disk.1 = (f32[3,4,8,256]{3,2,1,0:T(8,128)}, f32[4,8,256]{2,1,0:T(8,128)}, f32[4,8,256]{2,1,0:T(8,128)}, f32[128,768]{1,0:T(8,128)S(1)}) custom-call(s32[1]{0:T(128)} %get-tuple-element.19.count_ref, f32[3,4,8,256]{3,2,1,0:T(8,128)S(1)} %copy-done, f32[4,8,256]{2,1,0:T(8,128)S(1)} %copy-done.1, f32[4,8,256]{2,1,0:T(8,128)S(1)} %copy-done.2, ...), custom_call_target="tpu_custom_call" | custom-call | tf_op jit(solution)/shard_map/section_and_disk/pallas_call | solution.py:527
  15.1 0.1 reshape.11
  15.3 25.8 %all_to_all.5 = f32[32,4,768]{2,1,0:T(4,128)S(1)} all-to-all(f32[32,4,768]{2,1,0:T(4,128)S(1)} %reshape.11), channel_id=1, replica_groups=mesh['stream'=4,'girth'=8] {'stream','girth'}, dimensions={0} | all-to-all | bytes 786432 | tf_op jit(solution)/shard_map/all_to_all | solution.py:594
  41.0 0.7 %reduce_sum.9 = f32[4,768]{1,0:T(4,128)} reduce(f32[32,4,768]{2,1,0:T(4,128)S(1)} %all_to_all.5, f32[]{:T(128)} %constant.1.clone.1), dimensions={0}, to_apply=%region_0.0 | reduce | flops 95232 | bytes 405508 | tf_op jit(solution)/shard_map/reduce_sum | solution.py:601
Async XLA Ops:
  1.6 8.6 %collective-permute-start = (f32[6,2,8,256]{3,2,1,0:T(8,128)S(1)}, f32[6,2,8,256]{3,2,1,0:T(8,128)S(1)}, u32[]{:S(2)}, u32[]{:S(2)}) collective-permute-start(f32[6,2,8,256]{3,2,1,0:T(8,128)S(1)} %get-tuple-element.20), channel_id=1, source_target_pairs={{0,8},{8,0},{16,24},{24,16},{1,9},{9,1},{17,25},{25,17},{2,10},{10... | collective-permute-start | bytes 294920 | tf_op jit(solution)/shard_map/ppermute | solution.py:571
  4.7 5.5 %collective-permute-start.1 = (f32[6,2,8,256]{3,2,1,0:T(8,128)S(1)}, f32[6,2,8,256]{3,2,1,0:T(8,128)S(1)}, u32[]{:S(2)}, u32[]{:S(2)}) collective-permute-start(f32[6,2,8,256]{3,2,1,0:T(8,128)S(1)} %get-tuple-element.21), channel_id=1, source_target_pairs={{8,16},{16,8},{9,17},{17,9},{10,18},{18,10},{11,19},{19,11},{12,20... | collective-permute-start | bytes 294920 | tf_op jit(solution)/shard_map/ppermute | solution.py:571
  5.4 4.8 %collective-permute-start.2 = (f32[6,4,2,256]{3,2,1,0:T(2,128)S(1)}, f32[6,4,2,256]{3,2,1,0:T(2,128)S(1)}, u32[]{:S(2)}, u32[]{:S(2)}) collective-permute-start(f32[6,4,2,256]{3,2,1,0:T(2,128)S(1)} %get-tuple-element.22), channel_id=1, source_target_pairs={{0,1},{1,0},{2,3},{3,2},{4,5},{5,4},{6,7},{7,6},{8,9},{9,8},{10,11... | collective-permute-start | bytes 147464 | tf_op jit(solution)/shard_map/ppermute | solution.py:571
  5.4 4.8 %collective-permute-start.3 = (f32[6,4,2,256]{3,2,1,0:T(2,128)S(1)}, f32[6,4,2,256]{3,2,1,0:T(2,128)S(1)}, u32[]{:S(2)}, u32[]{:S(2)}) collective-permute-start(f32[6,4,2,256]{3,2,1,0:T(2,128)S(1)} %get-tuple-element.23), channel_id=1, source_target_pairs={{1,2},{2,1},{3,4},{4,3},{5,6},{6,5},{9,10},{10,9},{11,12},{12,11},... | collective-permute-start | bytes 147464 | tf_op jit(solution)/shard_map/ppermute | solution.py:571
  6.1 4.1 %copy-start = (f32[3,4,8,256]{3,2,1,0:T(8,128)S(1)}, f32[3,4,8,256]{3,2,1,0:T(8,128)}, u32[]{:S(2)}) copy-start(f32[3,4,8,256]{3,2,1,0:T(8,128)} %vel_ref.3) | copy-start | bytes 294916
  6.1 4.1 %copy-start.1 = (f32[4,8,256]{2,1,0:T(8,128)S(1)}, f32[4,8,256]{2,1,0:T(8,128)}, u32[]{:S(2)}) copy-start(f32[4,8,256]{2,1,0:T(8,128)} %p_ref.3) | copy-start | bytes 98308
  6.1 4.1 %copy-start.2 = (f32[4,8,256]{2,1,0:T(8,128)S(1)}, f32[4,8,256]{2,1,0:T(8,128)}, u32[]{:S(2)}) copy-start(f32[4,8,256]{2,1,0:T(8,128)} %k_ref.3) | copy-start | bytes 98308
  6.2 4.1 %copy-start.3 = (f32[4,8,256]{2,1,0:T(8,128)S(1)}, f32[4,8,256]{2,1,0:T(8,128)}, u32[]{:S(2)}) copy-start(f32[4,8,256]{2,1,0:T(8,128)} %w_ref.3) | copy-start | bytes 98308

commit v8 on v7

--- a/solution.py
+++ b/solution.py
@@ -342,6 +342,7 @@
 
 
 def section_kernel(
+    devices,
     count_ref,
     vel_ref,
     p_ref,
@@ -360,7 +361,8 @@
     new_vel_hbm,
     new_k_hbm,
     new_w_hbm,
-    harm_ref,
+    keep_ref,
+    give_ref,
     new_vel_ref,
     new_k_ref,
     new_w_ref,
@@ -370,6 +372,7 @@
     gather_ref,
     value_ref,
     disk_ref,
+    harm_ref,
     stored,
 ):
     cells_s, cells_g, cells_r = p_ref.shape
@@ -512,11 +515,17 @@
     radii = harm_ref.shape[0]
     for c in range(3):
         harm_ref[:, c * 2 * NH : (c + 1) * 2 * NH] = waves[c * radii : (c + 1) * radii]
+    block = radii // devices
+    for place in range(devices // 2):
+        even = harm_ref[2 * place * block : (2 * place + 1) * block, :]
+        odd = harm_ref[(2 * place + 1) * block : (2 * place + 2) * block, :]
+        keep_ref[place * block : (place + 1) * block, :] = jnp.where(girth_odd, odd, even)
+        give_ref[place * block : (place + 1) * block, :] = jnp.where(girth_odd, even, odd)
     for copy in copies:
         copy.wait()
 
 
-def section(velocity, pressure, energy, rate, halos, points):
+def section(velocity, pressure, energy, rate, halos, points, devices):
     _, cells_s, cells_g, cells_r = velocity.shape
     *lists, moves, chosen, counts = points
     rows, radii = lists[0].shape
@@ -525,15 +534,16 @@
     vmem = pl.BlockSpec(memory_space=pltpu.VMEM)
     smem = pl.BlockSpec(memory_space=pltpu.SMEM)
     return pl.pallas_call(
-        section_kernel,
+        functools.partial(section_kernel, devices),
         out_shape=(
             shape(velocity.shape),
             shape(energy.shape),
             shape(rate.shape),
-            shape((radii, 6 * NH)),
+            shape((radii // 2, 6 * NH)),
+            shape((radii // 2, 6 * NH)),
         ),
         in_specs=[smem] + [vmem] * 14,
-        out_specs=[pl.BlockSpec(memory_space=pl.ANY)] * 3 + [vmem],
+        out_specs=[pl.BlockSpec(memory_space=pl.ANY)] * 3 + [vmem] * 2,
         scratch_shapes=[
             scratch(*velocity.shape),
             scratch(*energy.shape),
@@ -544,6 +554,7 @@
             scratch(3 - PRODUCTS, cells_s, 2, cells_r // LANES, cells_g, LANES),
             scratch(2, 3, moves.shape[0], radii),
             scratch(3, rows, radii),
+            scratch(radii, 6 * NH),
             pltpu.SemaphoreType.DMA((3,)),
         ],
         compiler_params=pltpu.CompilerParams(vmem_limit_bytes=VMEM_LIMIT),
@@ -588,15 +599,17 @@
         (cells_s, cells_g, cells_r),
         girth_count,
     )
-    new_velocity, new_energy, new_rate, partial = section(
-        velocity, pressure, kinetic_energy, dissipation_rate, halos, points
-    )
+    new_velocity, new_energy, new_rate, keep, give = section(
+        velocity, pressure, kinetic_energy, dissipation_rate, halos, points, devices
+    )
+    total = keep + swap(give, "girth", girth_count, 0)
     shares = lax.all_to_all(
-        partial.reshape(devices, radii // devices, 6 * NH),
+        total.reshape(devices // 2, radii // devices, 6 * NH),
         ("stream", "girth"),
         split_axis=0,
         concat_axis=0,
         tiled=True,
+        axis_index_groups=[list(range(parity, devices, 2)) for parity in (0, 1)],
     )
     return new_velocity, new_energy, new_rate, jnp.sum(shares, axis=0)
 

time: 41.4 us -> 39.7 us (0.959)
  blocking collectives: 25.8 us -> 20.5 us
  starting transfers between devices: 4.48 us -> 7.01 us
  waiting for transfers between devices: 0.01 us -> 1.08 us
    all_to_all x1, blocking collectives: 25.8 us -> 20.5 us  [body(): lax.all_to_all(total.reshape(devices // 2, radii // devices, 6 * NH), ('s...]
    ppermute x4 -> x5, starting transfers between devices: 4.48 us -> 7.01 us  [swap(): return lax.ppermute(values, axis, pairs)]
    ppermute x4 -> x5, waiting for transfers between devices: 0.01 us -> 1.08 us  [swap(): return lax.ppermute(values, axis, pairs)]
  transfers between devices with their start and end apart: 4 -> 5, of which waited for: 0 -> 1; matrix products, arithmetic and copies ran while one was open for 0% -> 0% of each run, Pallas kernels for 10% -> 10%
where the time goes in v8:
time: 39.7 us
  blocking collectives  20.5 us (52%)
  Pallas kernels  9.56 us (24%)
  starting transfers between devices  7.01 us (18%)
  waiting for transfers between devices  1.08 us (3%)
  between operations  0.79 us (2%)
  other arithmetic  0.67 us (2%)
    all_to_all x1, blocking collectives, body(): lax.all_to_all(total.reshape(devices // 2, radii // devices, 6 * NH), ('s...  20.5 us
    ppermute x5, starting transfers between devices, swap(): return lax.ppermute(values, axis, pairs)  7.01 us
    pallas_call x1, Pallas kernels, section(): pl.pallas_call(functools.partial(section_kernel, devices), out_shape=(sha...  4.57 us
    pallas_call x1, Pallas kernels, prepare(): pl.pallas_call(functools.partial(prepare_kernel, cells_s, cells_g, cells_...  4.02 us
    ppermute x5, waiting for transfers between devices, swap(): return lax.ppermute(values, axis, pairs)  1.08 us
    pallas_call x1, Pallas kernels, pack(): pl.pallas_call(pack_kernel, out_shape=(stream, stream, girth, girth), in_...  0.98 us
  transfers between devices with their start and end apart: 5, of which 1 were waited for; matrix products, arithmetic and copies ran while one was open for 0% of the time, Pallas kernels for 10%

profile of v8, /device:TPU:0, one launch (start us, length us, event | category | flops | bytes accessed | tf_op | source)
XLA Modules:
  0.0 39.7 jit_solution(14108684226361325450)
XLA Ops:
  0.6 1.0 %pack_halos.1 = (f32[6,2,8,256]{3,2,1,0:T(8,128)S(1)}, f32[6,2,8,256]{3,2,1,0:T(8,128)S(1)}, f32[6,4,2,256]{3,2,1,0:T(2,128)S(1)}, f32[6,4,2,256]{3,2,1,0:T(2,128)S(1)}) custom-call(f32[3,4,8,256]{3,2,1,0:T(8,128)} %vel_ref.3, f32[4,8,256]{2,1,0:T(8,128)} %p_ref.3, f32[4,8,256]{2,1,0:T(8,128)} %k_ref.3, f32[4,8,256]{2,1,0:T(8,128)} %w_ref.3), custom_call_target="tpu_custom_call" | custom-call | tf_op jit(solution)/shard_map/pack_halos/pallas_call | solution.py:52
  1.6 3.1 %collective-permute-start = (f32[6,2,8,256]{3,2,1,0:T(8,128)S(1)}, f32[6,2,8,256]{3,2,1,0:T(8,128)S(1)}, u32[]{:S(2)}, u32[]{:S(2)}) collective-permute-start(f32[6,2,8,256]{3,2,1,0:T(8,128)S(1)} %get-tuple-element.21), channel_id=1, source_target_pairs={{0,8},{8,0},{16,24},{24,16},{1,9},{9,1},{17,25},{25,17},{2,10},{10... | collective-permute-start | bytes 294920 | tf_op jit(solution)/shard_map/ppermute | solution.py:582
  4.7 0.7 %collective-permute-start.1 = (f32[6,2,8,256]{3,2,1,0:T(8,128)S(1)}, f32[6,2,8,256]{3,2,1,0:T(8,128)S(1)}, u32[]{:S(2)}, u32[]{:S(2)}) collective-permute-start(f32[6,2,8,256]{3,2,1,0:T(8,128)S(1)} %get-tuple-element.22), channel_id=1, source_target_pairs={{8,16},{16,8},{9,17},{17,9},{10,18},{18,10},{11,19},{19,11},{12,20... | collective-permute-start | bytes 294920 | tf_op jit(solution)/shard_map/ppermute | solution.py:582
  5.4 0.1 collective-permute-start.2
  5.4 0.7 %collective-permute-start.3 = (f32[6,4,2,256]{3,2,1,0:T(2,128)S(1)}, f32[6,4,2,256]{3,2,1,0:T(2,128)S(1)}, u32[]{:S(2)}, u32[]{:S(2)}) collective-permute-start(f32[6,4,2,256]{3,2,1,0:T(2,128)S(1)} %get-tuple-element.24), channel_id=1, source_target_pairs={{1,2},{2,1},{3,4},{4,3},{5,6},{6,5},{9,10},{10,9},{11,12},{12,11},... | collective-permute-start | bytes 147464 | tf_op jit(solution)/shard_map/ppermute | solution.py:582
  6.1 0.0 copy-start
  6.1 0.0 copy-start.1
  6.1 0.0 copy-start.2
  6.2 0.0 copy-start.3
  6.2 4.0 %prepare_points.1 = (s32[384,128]{1,0:T(8,128)S(1)}, f32[384,128]{1,0:T(8,128)S(1)}, f32[384,128]{1,0:T(8,128)S(1)}, f32[384,128]{1,0:T(8,128)S(1)}, s32[640,128...) custom-call(s32[64]{0:T(128)} %bitcast.1, s32[128,1024]{1,0:T(8,128)} %ids_hbm.1, f32[3,128,1024]{2,1,0:T(8,128)} %frac_hbm.1, ...), custom_call_target="tpu_custom_call" | custom-call | flops 2621440 | bytes 5767168 | tf_op jit(solution)/shard_map/prepare_points/pallas_call | solution.py:214
  10.2 0.0 collective-permute-done.2.girth_a
  10.2 0.0 collective-permute-done.3.girth_b
  10.2 0.0 collective-permute-done.stream_a
  10.2 0.0 collective-permute-done.1.stream_b
  10.2 0.0 copy-done
  10.2 0.0 copy-done.1
  10.3 0.0 copy-done.2
  10.3 0.0 copy-done.3
  10.3 4.6 %section_and_disk.1 = (f32[3,4,8,256]{3,2,1,0:T(8,128)}, f32[4,8,256]{2,1,0:T(8,128)}, f32[4,8,256]{2,1,0:T(8,128)}, f32[64,768]{1,0:T(8,128)S(1)}, f32[64,768]{1,0:T(8,128)S(1)}) custom-call(s32[1]{0:T(128)} %get-tuple-element.20.count_ref, f32[3,4,8,256]{3,2,1,0:T(8,128)S(1)} %copy-done, f32[4,8,256]{2,1,0:T(8,128)S(1)} %copy-done.1, ...), custom_call_target="tpu_custom_call" | custom-call | tf_op jit(solution)/shard_map/section_and_disk/pallas_call | solution.py:536
  14.8 2.5 %collective-permute-start.4 = (f32[64,768]{1,0:T(8,128)S(1)}, f32[64,768]{1,0:T(8,128)S(1)}, u32[]{:S(2)}, u32[]{:S(2)}) collective-permute-start(f32[64,768]{1,0:T(8,128)S(1)} %get-tuple-element.35), channel_id=1, source_target_pairs={{0,1},{1,0},{2,3},{3,2},{4,5},{5,4},{6,7},{7,6},{8,9},{9,8},{10,11... | collective-permute-start | bytes 589832 | tf_op jit(solution)/shard_map/ppermute | solution.py:582
  17.4 1.1 %collective-permute-done.4 = f32[64,768]{1,0:T(8,128)S(1)} collective-permute-done((f32[64,768]{1,0:T(8,128)S(1)}, f32[64,768]{1,0:T(8,128)S(1)}, u32[]{:S(2)}, u32[]{:S(2)}) %collective-permute-start.4) | collective-permute-done | bytes 196640 | tf_op jit(solution)/shard_map/ppermute | solution.py:582
  18.5 0.1 reshape.11
  18.5 20.5 %all_to_all.5 = f32[16,4,768]{2,1,0:T(4,128)S(1)} all-to-all(f32[16,4,768]{2,1,0:T(4,128)S(1)} %reshape.11), channel_id=1, replica_groups={{0,2,4,6,8,10,12,14,16,18,20,22,24,26,28,30},{1,3,5,7,9,11,13,15,17,19,..., dimensions={0} | all-to-all | bytes 393216 | tf_op jit(solution)/shard_map/all_to_all | solution.py:606
  39.0 0.6 %reduce_sum.9 = f32[4,768]{1,0:T(4,128)} reduce(f32[16,4,768]{2,1,0:T(4,128)S(1)} %all_to_all.5, f32[]{:T(128)} %constant.1.clone.1), dimensions={0}, to_apply=%region_0.0 | reduce | flops 46080 | bytes 208900 | tf_op jit(solution)/shard_map/reduce_sum | solution.py:614
  (1 shorter events, 0.0 us)
Async XLA Ops:
  1.6 8.6 %collective-permute-start = (f32[6,2,8,256]{3,2,1,0:T(8,128)S(1)}, f32[6,2,8,256]{3,2,1,0:T(8,128)S(1)}, u32[]{:S(2)}, u32[]{:S(2)}) collective-permute-start(f32[6,2,8,256]{3,2,1,0:T(8,128)S(1)} %get-tuple-element.21), channel_id=1, source_target_pairs={{0,8},{8,0},{16,24},{24,16},{1,9},{9,1},{17,25},{25,17},{2,10},{10... | collective-permute-start | bytes 294920 | tf_op jit(solution)/shard_map/ppermute | solution.py:582
  4.7 5.5 %collective-permute-start.1 = (f32[6,2,8,256]{3,2,1,0:T(8,128)S(1)}, f32[6,2,8,256]{3,2,1,0:T(8,128)S(1)}, u32[]{:S(2)}, u32[]{:S(2)}) collective-permute-start(f32[6,2,8,256]{3,2,1,0:T(8,128)S(1)} %get-tuple-element.22), channel_id=1, source_target_pairs={{8,16},{16,8},{9,17},{17,9},{10,18},{18,10},{11,19},{19,11},{12,20... | collective-permute-start | bytes 294920 | tf_op jit(solution)/shard_map/ppermute | solution.py:582
  5.4 4.8 %collective-permute-start.2 = (f32[6,4,2,256]{3,2,1,0:T(2,128)S(1)}, f32[6,4,2,256]{3,2,1,0:T(2,128)S(1)}, u32[]{:S(2)}, u32[]{:S(2)}) collective-permute-start(f32[6,4,2,256]{3,2,1,0:T(2,128)S(1)} %get-tuple-element.23), channel_id=1, source_target_pairs={{0,1},{1,0},{2,3},{3,2},{4,5},{5,4},{6,7},{7,6},{8,9},{9,8},{10,11... | collective-permute-start | bytes 147464 | tf_op jit(solution)/shard_map/ppermute | solution.py:582
  5.4 4.8 %collective-permute-start.3 = (f32[6,4,2,256]{3,2,1,0:T(2,128)S(1)}, f32[6,4,2,256]{3,2,1,0:T(2,128)S(1)}, u32[]{:S(2)}, u32[]{:S(2)}) collective-permute-start(f32[6,4,2,256]{3,2,1,0:T(2,128)S(1)} %get-tuple-element.24), channel_id=1, source_target_pairs={{1,2},{2,1},{3,4},{4,3},{5,6},{6,5},{9,10},{10,9},{11,12},{12,11},... | collective-permute-start | bytes 147464 | tf_op jit(solution)/shard_map/ppermute | solution.py:582
  6.1 4.1 %copy-start = (f32[3,4,8,256]{3,2,1,0:T(8,128)S(1)}, f32[3,4,8,256]{3,2,1,0:T(8,128)}, u32[]{:S(2)}) copy-start(f32[3,4,8,256]{3,2,1,0:T(8,128)} %vel_ref.3) | copy-start | bytes 294916
  6.1 4.1 %copy-start.1 = (f32[4,8,256]{2,1,0:T(8,128)S(1)}, f32[4,8,256]{2,1,0:T(8,128)}, u32[]{:S(2)}) copy-start(f32[4,8,256]{2,1,0:T(8,128)} %p_ref.3) | copy-start | bytes 98308
  6.1 4.1 %copy-start.2 = (f32[4,8,256]{2,1,0:T(8,128)S(1)}, f32[4,8,256]{2,1,0:T(8,128)}, u32[]{:S(2)}) copy-start(f32[4,8,256]{2,1,0:T(8,128)} %k_ref.3) | copy-start | bytes 98308
  6.2 4.1 %copy-start.3 = (f32[4,8,256]{2,1,0:T(8,128)S(1)}, f32[4,8,256]{2,1,0:T(8,128)}, u32[]{:S(2)}) copy-start(f32[4,8,256]{2,1,0:T(8,128)} %w_ref.3) | copy-start | bytes 98308
  14.8 3.6 %collective-permute-start.4 = (f32[64,768]{1,0:T(8,128)S(1)}, f32[64,768]{1,0:T(8,128)S(1)}, u32[]{:S(2)}, u32[]{:S(2)}) collective-permute-start(f32[64,768]{1,0:T(8,128)S(1)} %get-tuple-element.35), channel_id=1, source_target_pairs={{0,1},{1,0},{2,3},{3,2},{4,5},{5,4},{6,7},{7,6},{8,9},{9,8},{10,11... | collective-permute-start | bytes 589832 | tf_op jit(solution)/shard_map/ppermute | solution.py:582

commit v9 on v8

--- a/solution.py
+++ b/solution.py
@@ -430,7 +430,10 @@
     table = table.astype(jnp.bfloat16)
     pair = 2 * LANES
     girth_row = lax.broadcasted_iota(jnp.int32, (cells_g, pair), 0).astype(jnp.float32)
-    radial_row = lax.broadcasted_iota(jnp.int32, (cells_r, pair), 0)
+    index_type = jnp.bfloat16 if cells_r <= 256 else jnp.float32
+    radial_row = lax.broadcasted_iota(jnp.int32, (cells_r, pair), 0).astype(jnp.float32)
+    radial_row = radial_row.astype(index_type)
+    one, none = jnp.ones((), jnp.bfloat16), jnp.zeros((), jnp.bfloat16)
 
     def two(values, j):
         return jnp.concatenate([values[j : j + 1], values[j + 1 : j + 2]], axis=1)
@@ -447,15 +450,16 @@
             out = got if out is None else jnp.where(half_of[h], got, out)
         return out
 
-    def eight(group, carry):
-        at = pl.multiple_of(group * ROWS, ROWS)
+    def eight(at):
         here = pl.ds(at, ROWS)
         q8, fr8, xg8, xs8 = (r[here, :] for r in (q_ref, fr_ref, xg_ref, xs_ref))
         hs8 = [jnp.maximum(1.0 - jnp.abs(xs8 - float(s)), 0.0) for s in range(cells_s)]
         index8 = q8 & (LANES - 1)
+        qf8 = q8.astype(jnp.float32)
         sums = [[], [], []]
         for j in range(0, ROWS, 2):
-            hot = jnp.where(radial_row == two(q8, j), 1.0, 0.0).astype(jnp.bfloat16)
+            chosen_q = jnp.broadcast_to(two(qf8, j), (cells_r, pair)).astype(index_type)
+            hot = jnp.where(radial_row == chosen_q, one, none)
             got = jnp.dot(table, hot, preferred_element_type=jnp.float32)
             got = got.reshape(PRODUCTS, cells_s, kinds, cells_g, pair)
             fr = two(fr8, j)
@@ -483,9 +487,13 @@
                     sums[c].append(own_hg * total)
         for c in range(3):
             value_ref[0, c, pl.ds(pad + at, ROWS), :] = girth_sums(sums[c])
+
+    def step(group, carry):
+        for part in range(2):
+            eight(pl.multiple_of((2 * group + part) * ROWS, ROWS))
         return carry
 
-    lax.fori_loop(0, (count_ref[0] + ROWS - 1) // ROWS, eight, jnp.int32(0))
+    lax.fori_loop(0, (count_ref[0] + 2 * ROWS - 1) // (2 * ROWS), step, jnp.int32(0))
 
     for number, (low, digits) in enumerate(reversed(passes)):
         a, b = number % 2, 1 - number % 2

time: 39.7 us -> 37.1 us (0.935); the launches traced: 39.7 us -> 37.6 us
  blocking collectives: 20.5 us -> 15.7 us
  starting transfers between devices: 7.01 us -> 9.46 us
    all_to_all x1, blocking collectives: 20.5 us -> 15.7 us  [body(): lax.all_to_all(total.reshape(devices // 2, radii // devices, 6 * NH), ('s...]
    ppermute x5, starting transfers between devices: 7.01 us -> 9.46 us  [swap(): return lax.ppermute(values, axis, pairs)]
  transfers between devices with their start and end apart: 5 -> 5, of which waited for: 1 -> 1; matrix products, arithmetic and copies ran while one was open for 0% -> 0% of each run, Pallas kernels for 10% -> 11%
where the time goes in v9:
time: 37.1 us; the launch traced here: 37.6 us
  blocking collectives  15.7 us (42%)
  Pallas kernels  9.8 us (26%)
  starting transfers between devices  9.46 us (25%)
  waiting for transfers between devices  1.08 us (3%)
  between operations  0.79 us (2%)
  other arithmetic  0.67 us (2%)
    all_to_all x1, blocking collectives, body(): lax.all_to_all(total.reshape(devices // 2, radii // devices, 6 * NH), ('s...  15.7 us
    ppermute x5, starting transfers between devices, swap(): return lax.ppermute(values, axis, pairs)  9.46 us
    pallas_call x1, Pallas kernels, section(): pl.pallas_call(functools.partial(section_kernel, devices), out_shape=(sha...  4.79 us
    pallas_call x1, Pallas kernels, prepare(): pl.pallas_call(functools.partial(prepare_kernel, cells_s, cells_g, cells_...  4.03 us
    ppermute x5, waiting for transfers between devices, swap(): return lax.ppermute(values, axis, pairs)  1.08 us
    pallas_call x1, Pallas kernels, pack(): pl.pallas_call(pack_kernel, out_shape=(stream, stream, girth, girth), in_...  0.98 us
  transfers between devices with their start and end apart: 5, of which 1 were waited for; matrix products, arithmetic and copies ran while one was open for 0% of the time, Pallas kernels for 11%

profile of v9, /device:TPU:0, one launch (start us, length us, event | category | flops | bytes accessed | tf_op | source)
XLA Modules:
  0.0 37.6 jit_solution(16912885153652955552)
XLA Ops:
  0.6 1.0 %pack_halos.1 = (f32[6,2,8,256]{3,2,1,0:T(8,128)S(1)}, f32[6,2,8,256]{3,2,1,0:T(8,128)S(1)}, f32[6,4,2,256]{3,2,1,0:T(2,128)S(1)}, f32[6,4,2,256]{3,2,1,0:T(2,128)S(1)}) custom-call(f32[3,4,8,256]{3,2,1,0:T(8,128)} %vel_ref.3, f32[4,8,256]{2,1,0:T(8,128)} %p_ref.3, f32[4,8,256]{2,1,0:T(8,128)} %k_ref.3, f32[4,8,256]{2,1,0:T(8,128)} %w_ref.3), custom_call_target="tpu_custom_call" | custom-call | tf_op jit(solution)/shard_map/pack_halos/pallas_call | solution.py:52
  1.6 3.1 %collective-permute-start = (f32[6,2,8,256]{3,2,1,0:T(8,128)S(1)}, f32[6,2,8,256]{3,2,1,0:T(8,128)S(1)}, u32[]{:S(2)}, u32[]{:S(2)}) collective-permute-start(f32[6,2,8,256]{3,2,1,0:T(8,128)S(1)} %get-tuple-element.21), channel_id=1, source_target_pairs={{0,8},{8,0},{16,24},{24,16},{1,9},{9,1},{17,25},{25,17},{2,10},{10... | collective-permute-start | bytes 294920 | tf_op jit(solution)/shard_map/ppermute | solution.py:590
  4.7 0.7 %collective-permute-start.1 = (f32[6,2,8,256]{3,2,1,0:T(8,128)S(1)}, f32[6,2,8,256]{3,2,1,0:T(8,128)S(1)}, u32[]{:S(2)}, u32[]{:S(2)}) collective-permute-start(f32[6,2,8,256]{3,2,1,0:T(8,128)S(1)} %get-tuple-element.22), channel_id=1, source_target_pairs={{8,16},{16,8},{9,17},{17,9},{10,18},{18,10},{11,19},{19,11},{12,20... | collective-permute-start | bytes 294920 | tf_op jit(solution)/shard_map/ppermute | solution.py:590
  5.4 0.1 collective-permute-start.2
  5.4 0.7 %collective-permute-start.3 = (f32[6,4,2,256]{3,2,1,0:T(2,128)S(1)}, f32[6,4,2,256]{3,2,1,0:T(2,128)S(1)}, u32[]{:S(2)}, u32[]{:S(2)}) collective-permute-start(f32[6,4,2,256]{3,2,1,0:T(2,128)S(1)} %get-tuple-element.24), channel_id=1, source_target_pairs={{1,2},{2,1},{3,4},{4,3},{5,6},{6,5},{9,10},{10,9},{11,12},{12,11},... | collective-permute-start | bytes 147464 | tf_op jit(solution)/shard_map/ppermute | solution.py:590
  6.1 0.0 copy-start
  6.1 0.0 copy-start.1
  6.1 0.0 copy-start.2
  6.2 0.0 copy-start.3
  6.2 4.0 %prepare_points.1 = (s32[384,128]{1,0:T(8,128)S(1)}, f32[384,128]{1,0:T(8,128)S(1)}, f32[384,128]{1,0:T(8,128)S(1)}, f32[384,128]{1,0:T(8,128)S(1)}, s32[640,128...) custom-call(s32[64]{0:T(128)} %bitcast.1, s32[128,1024]{1,0:T(8,128)} %ids_hbm.1, f32[3,128,1024]{2,1,0:T(8,128)} %frac_hbm.1, ...), custom_call_target="tpu_custom_call" | custom-call | flops 2621440 | bytes 5767168 | tf_op jit(solution)/shard_map/prepare_points/pallas_call | solution.py:214
  10.2 0.0 collective-permute-done.2.girth_a
  10.2 0.0 collective-permute-done.3.girth_b
  10.2 0.0 collective-permute-done.stream_a
  10.2 0.0 collective-permute-done.1.stream_b
  10.2 0.0 copy-done
  10.3 0.0 copy-done.1
  10.3 0.0 copy-done.2
  10.3 0.0 copy-done.3
  10.3 4.8 %section_and_disk.1 = (f32[3,4,8,256]{3,2,1,0:T(8,128)}, f32[4,8,256]{2,1,0:T(8,128)}, f32[4,8,256]{2,1,0:T(8,128)}, f32[64,768]{1,0:T(8,128)S(1)}, f32[64,768]{1,0:T(8,128)S(1)}) custom-call(s32[1]{0:T(128)} %get-tuple-element.20.count_ref, f32[3,4,8,256]{3,2,1,0:T(8,128)S(1)} %copy-done, f32[4,8,256]{2,1,0:T(8,128)S(1)} %copy-done.1, ...), custom_call_target="tpu_custom_call" | custom-call | tf_op jit(solution)/shard_map/section_and_disk/pallas_call | solution.py:544
  15.1 5.0 %collective-permute-start.4 = (f32[64,768]{1,0:T(8,128)S(1)}, f32[64,768]{1,0:T(8,128)S(1)}, u32[]{:S(2)}, u32[]{:S(2)}) collective-permute-start(f32[64,768]{1,0:T(8,128)S(1)} %get-tuple-element.35), channel_id=1, source_target_pairs={{0,1},{1,0},{2,3},{3,2},{4,5},{5,4},{6,7},{7,6},{8,9},{9,8},{10,11... | collective-permute-start | bytes 589832 | tf_op jit(solution)/shard_map/ppermute | solution.py:590
  20.1 1.1 %collective-permute-done.4 = f32[64,768]{1,0:T(8,128)S(1)} collective-permute-done((f32[64,768]{1,0:T(8,128)S(1)}, f32[64,768]{1,0:T(8,128)S(1)}, u32[]{:S(2)}, u32[]{:S(2)}) %collective-permute-start.4) | collective-permute-done | bytes 196640 | tf_op jit(solution)/shard_map/ppermute | solution.py:590
  21.2 0.1 reshape.11
  21.2 15.7 %all_to_all.5 = f32[16,4,768]{2,1,0:T(4,128)S(1)} all-to-all(f32[16,4,768]{2,1,0:T(4,128)S(1)} %reshape.11), channel_id=1, replica_groups={{0,2,4,6,8,10,12,14,16,18,20,22,24,26,28,30},{1,3,5,7,9,11,13,15,17,19,..., dimensions={0} | all-to-all | bytes 393216 | tf_op jit(solution)/shard_map/all_to_all | solution.py:614
  36.9 0.6 %reduce_sum.9 = f32[4,768]{1,0:T(4,128)} reduce(f32[16,4,768]{2,1,0:T(4,128)S(1)} %all_to_all.5, f32[]{:T(128)} %constant.1.clone.1), dimensions={0}, to_apply=%region_0.0 | reduce | flops 46080 | bytes 208900 | tf_op jit(solution)/shard_map/reduce_sum | solution.py:622
  (1 shorter events, 0.0 us)
Async XLA Ops:
  1.6 8.6 %collective-permute-start = (f32[6,2,8,256]{3,2,1,0:T(8,128)S(1)}, f32[6,2,8,256]{3,2,1,0:T(8,128)S(1)}, u32[]{:S(2)}, u32[]{:S(2)}) collective-permute-start(f32[6,2,8,256]{3,2,1,0:T(8,128)S(1)} %get-tuple-element.21), channel_id=1, source_target_pairs={{0,8},{8,0},{16,24},{24,16},{1,9},{9,1},{17,25},{25,17},{2,10},{10... | collective-permute-start | bytes 294920 | tf_op jit(solution)/shard_map/ppermute | solution.py:590
  4.7 5.5 %collective-permute-start.1 = (f32[6,2,8,256]{3,2,1,0:T(8,128)S(1)}, f32[6,2,8,256]{3,2,1,0:T(8,128)S(1)}, u32[]{:S(2)}, u32[]{:S(2)}) collective-permute-start(f32[6,2,8,256]{3,2,1,0:T(8,128)S(1)} %get-tuple-element.22), channel_id=1, source_target_pairs={{8,16},{16,8},{9,17},{17,9},{10,18},{18,10},{11,19},{19,11},{12,20... | collective-permute-start | bytes 294920 | tf_op jit(solution)/shard_map/ppermute | solution.py:590
  5.4 4.8 %collective-permute-start.2 = (f32[6,4,2,256]{3,2,1,0:T(2,128)S(1)}, f32[6,4,2,256]{3,2,1,0:T(2,128)S(1)}, u32[]{:S(2)}, u32[]{:S(2)}) collective-permute-start(f32[6,4,2,256]{3,2,1,0:T(2,128)S(1)} %get-tuple-element.23), channel_id=1, source_target_pairs={{0,1},{1,0},{2,3},{3,2},{4,5},{5,4},{6,7},{7,6},{8,9},{9,8},{10,11... | collective-permute-start | bytes 147464 | tf_op jit(solution)/shard_map/ppermute | solution.py:590
  5.4 4.8 %collective-permute-start.3 = (f32[6,4,2,256]{3,2,1,0:T(2,128)S(1)}, f32[6,4,2,256]{3,2,1,0:T(2,128)S(1)}, u32[]{:S(2)}, u32[]{:S(2)}) collective-permute-start(f32[6,4,2,256]{3,2,1,0:T(2,128)S(1)} %get-tuple-element.24), channel_id=1, source_target_pairs={{1,2},{2,1},{3,4},{4,3},{5,6},{6,5},{9,10},{10,9},{11,12},{12,11},... | collective-permute-start | bytes 147464 | tf_op jit(solution)/shard_map/ppermute | solution.py:590
  6.1 4.1 %copy-start = (f32[3,4,8,256]{3,2,1,0:T(8,128)S(1)}, f32[3,4,8,256]{3,2,1,0:T(8,128)}, u32[]{:S(2)}) copy-start(f32[3,4,8,256]{3,2,1,0:T(8,128)} %vel_ref.3) | copy-start | bytes 294916
  6.1 4.1 %copy-start.1 = (f32[4,8,256]{2,1,0:T(8,128)S(1)}, f32[4,8,256]{2,1,0:T(8,128)}, u32[]{:S(2)}) copy-start(f32[4,8,256]{2,1,0:T(8,128)} %p_ref.3) | copy-start | bytes 98308
  6.1 4.1 %copy-start.2 = (f32[4,8,256]{2,1,0:T(8,128)S(1)}, f32[4,8,256]{2,1,0:T(8,128)}, u32[]{:S(2)}) copy-start(f32[4,8,256]{2,1,0:T(8,128)} %k_ref.3) | copy-start | bytes 98308
  6.2 4.1 %copy-start.3 = (f32[4,8,256]{2,1,0:T(8,128)S(1)}, f32[4,8,256]{2,1,0:T(8,128)}, u32[]{:S(2)}) copy-start(f32[4,8,256]{2,1,0:T(8,128)} %w_ref.3) | copy-start | bytes 98308
  15.1 6.1 %collective-permute-start.4 = (f32[64,768]{1,0:T(8,128)S(1)}, f32[64,768]{1,0:T(8,128)S(1)}, u32[]{:S(2)}, u32[]{:S(2)}) collective-permute-start(f32[64,768]{1,0:T(8,128)S(1)} %get-tuple-element.35), channel_id=1, source_target_pairs={{0,1},{1,0},{2,3},{3,2},{4,5},{5,4},{6,7},{7,6},{8,9},{9,8},{10,11... | collective-permute-start | bytes 589832 | tf_op jit(solution)/shard_map/ppermute | solution.py:590

commit v10 on v9

--- a/solution.py
+++ b/solution.py
@@ -73,30 +73,21 @@
     return values // size, values % size
 
 
-def prepare_kernel(
-    cells_s,
-    cells_g,
-    cells_r,
+def choose_kernel(
     owner_ref,
     ids_hbm,
     frac_hbm,
     table_hbm,
-    q_ref,
-    fr_ref,
-    xs_ref,
-    xg_ref,
-    moves_ref,
+    slab_a,
+    slab_b,
+    picked,
     chosen_ref,
-    count_ref,
+    out_a,
+    out_b,
     ids_ref,
     frac_ref,
     table_ref,
     turned,
-    picked,
-    keys,
-    frs,
-    xss,
-    xgs,
     order,
     arrived,
 ):
@@ -106,15 +97,13 @@
     copies.append(pltpu.make_async_copy(table_hbm, table_ref, arrived.at[4]))
     for copy in copies:
         copy.start()
-    stream_first = lax.axis_index("stream") * cells_s
+    out_a[...] = slab_a[...]
+    out_b[...] = slab_b[...]
     me = lax.axis_index("girth")
     sectors = owner_ref.shape[0]
     azimuths = ids_ref.shape[1]
     width = azimuths // sectors
-    rows = fr_ref.shape[0]
-    pad = moves_ref.shape[0] - rows
-    passes = network(rows)
-    valid = 1 << SHIFT - 1
+    rows = picked.shape[1]
 
     def listed(number, count):
         order[jnp.minimum(count, rows // width)] = number
@@ -125,10 +114,6 @@
     for d in range(4):
         picked[d] = jnp.full(picked.shape[1:], -1.0 if d == 0 else 0.0, jnp.float32)
     chosen_ref[...] = jnp.zeros_like(chosen_ref)
-    beyond = pl.ds(rows, pad)
-    for slot in range(2):
-        keys[slot, beyond, :] = jnp.zeros((pad, LANES), jnp.int32)
-    moves_ref[0:pad, :] = jnp.zeros((pad, LANES), jnp.int32)
     for d in range(4):
         copies[d].wait()
         for at in range(0, azimuths, LANES):
@@ -147,6 +132,64 @@
 
     lax.fori_loop(0, owned, sector, jnp.int32(0))
 
+
+def choose(owners, corner_ids, fractions, table, slabs, girth_count):
+    radii, azimuths = corner_ids.shape
+    sectors = owners.shape[0]
+    rows = 3 * sectors // girth_count * (azimuths // sectors)
+    vmem = pl.BlockSpec(memory_space=pltpu.VMEM)
+    smem = pl.BlockSpec(memory_space=pltpu.SMEM)
+    hbm = pl.BlockSpec(memory_space=pltpu.HBM)
+    return pl.pallas_call(
+        choose_kernel,
+        out_shape=[
+            jax.ShapeDtypeStruct((4, rows, radii), jnp.float32),
+            jax.ShapeDtypeStruct((rows, 2 * NH), jnp.float32),
+        ]
+        + [pltpu.VMEM(slab.shape, jnp.float32) for slab in slabs],
+        in_specs=[smem, hbm, hbm, hbm, vmem, vmem],
+        out_specs=[vmem] * 4,
+        scratch_shapes=[
+            pltpu.VMEM(corner_ids.shape, jnp.int32),
+            pltpu.VMEM(fractions.shape, jnp.float32),
+            pltpu.VMEM(table.shape, jnp.float32),
+            pltpu.VMEM((4, azimuths, radii), jnp.float32),
+            pltpu.SMEM((rows // (azimuths // sectors) + 1,), jnp.int32),
+            pltpu.SemaphoreType.DMA((5,)),
+        ],
+        compiler_params=pltpu.CompilerParams(vmem_limit_bytes=VMEM_LIMIT),
+        cost_estimate=pl.CostEstimate(
+            flops=8 * radii * azimuths, bytes_accessed=32 * radii * azimuths, transcendentals=0
+        ),
+        name="choose_points",
+    )(*(in_hbm(x) for x in (owners, corner_ids, fractions, table)), *slabs)
+
+
+def prepare_kernel(
+    cells_s,
+    cells_g,
+    cells_r,
+    picked,
+    q_ref,
+    fr_ref,
+    xs_ref,
+    xg_ref,
+    moves_ref,
+    count_ref,
+    keys,
+    frs,
+    xss,
+    xgs,
+):
+    stream_first = lax.axis_index("stream") * cells_s
+    rows = fr_ref.shape[0]
+    pad = moves_ref.shape[0] - rows
+    passes = network(rows)
+    valid = 1 << SHIFT - 1
+    beyond = pl.ds(rows, pad)
+    for slot in range(2):
+        keys[slot, beyond, :] = jnp.zeros((pad, LANES), jnp.int32)
+    moves_ref[0:pad, :] = jnp.zeros((pad, LANES), jnp.int32)
     held = pl.ds(0, rows)
     ids = picked[0].astype(jnp.int32)
     stream_cell, rest = split(jnp.maximum(ids, 0), cells_g * cells_r)
@@ -200,47 +243,33 @@
                 xgs[b, here, :] = out[2]
 
 
-def prepare(owners, corner_ids, fractions, table, cells, girth_count):
-    cells_s, cells_g, cells_r = cells
-    radii, azimuths = corner_ids.shape
-    sectors = owners.shape[0]
-    rows = 3 * sectors // girth_count * (azimuths // sectors)
+def prepare(picked, cells):
+    _, rows, radii = picked.shape
     pad = reach(rows)
     shape = jax.ShapeDtypeStruct
     lists = (rows, radii)
     vmem = pl.BlockSpec(memory_space=pltpu.VMEM)
     smem = pl.BlockSpec(memory_space=pltpu.SMEM)
-    hbm = pl.BlockSpec(memory_space=pltpu.HBM)
     return pl.pallas_call(
-        functools.partial(prepare_kernel, cells_s, cells_g, cells_r),
+        functools.partial(prepare_kernel, *cells),
         out_shape=(
             shape(lists, jnp.int32),
             shape(lists, jnp.float32),
             shape(lists, jnp.float32),
             shape(lists, jnp.float32),
             shape((pad + rows, radii), jnp.int32),
-            shape((rows, 2 * NH), jnp.float32),
             shape((1,), jnp.int32),
         ),
-        in_specs=[smem, hbm, hbm, hbm],
-        out_specs=[vmem] * 6 + [smem],
-        scratch_shapes=[
-            pltpu.VMEM(corner_ids.shape, jnp.int32),
-            pltpu.VMEM(fractions.shape, jnp.float32),
-            pltpu.VMEM(table.shape, jnp.float32),
-            pltpu.VMEM((4, azimuths, radii), jnp.float32),
-            pltpu.VMEM((4, rows, radii), jnp.float32),
-            pltpu.VMEM((2, rows + pad, radii), jnp.int32),
-        ]
-        + [pltpu.VMEM((2, rows + pad, radii), jnp.float32)] * 3
-        + [pltpu.SMEM((rows // (azimuths // sectors) + 1,), jnp.int32)]
-        + [pltpu.SemaphoreType.DMA((5,))],
+        in_specs=[vmem],
+        out_specs=[vmem] * 5 + [smem],
+        scratch_shapes=[pltpu.VMEM((2, rows + pad, radii), jnp.int32)]
+        + [pltpu.VMEM((2, rows + pad, radii), jnp.float32)] * 3,
         compiler_params=pltpu.CompilerParams(vmem_limit_bytes=VMEM_LIMIT),
         cost_estimate=pl.CostEstimate(
-            flops=20 * radii * azimuths, bytes_accessed=44 * radii * azimuths, transcendentals=0
+            flops=200 * rows * radii, bytes_accessed=44 * rows * radii, transcendentals=0
         ),
         name="prepare_points",
-    )(*(in_hbm(x) for x in (owners, corner_ids, fractions, table)))
+    )(picked)
 
 
 def radial(values, amount, fill):
@@ -590,23 +619,25 @@
         return lax.ppermute(values, axis, pairs)
 
     slabs = pack(velocity, pressure, kinetic_energy, dissipation_rate)
-    girth_halos = (
-        swap(slabs[2], "girth", girth_count, 0),
-        swap(slabs[3], "girth", girth_count, 1),
-    )
     stream_halos = (
         swap(slabs[0], "stream", stream_count, 0),
         swap(slabs[1], "stream", stream_count, 1),
     )
-    halos = stream_halos + girth_halos
-    points = prepare(
+    picked, chosen, *girth_slabs = choose(
         sector_owner[:, 0],
         corner_ids,
         fractions,
         fourier_table(azimuths, NH),
-        (cells_s, cells_g, cells_r),
+        slabs[2:],
         girth_count,
     )
+    girth_halos = (
+        swap(girth_slabs[0], "girth", girth_count, 0),
+        swap(girth_slabs[1], "girth", girth_count, 1),
+    )
+    *lists, counts = prepare(picked, (cells_s, cells_g, cells_r))
+    halos = stream_halos + girth_halos
+    points = (*lists, chosen, counts)
     new_velocity, new_energy, new_rate, keep, give = section(
         velocity, pressure, kinetic_energy, dissipation_rate, halos, points, devices
     )

time: 37.1 us -> 39.9 us (1.075)
  blocking collectives: 15.7 us -> 19.7 us
  starting transfers between devices: 9.46 us -> 8.71 us
  Pallas kernels: 9.8 us -> 9.3 us
    all_to_all x1, blocking collectives: 15.7 us -> 19.7 us  [body(): lax.all_to_all(total.reshape(devices // 2, radii // devices, 6 * NH), ('s...]
    ppermute x5, starting transfers between devices: 9.46 us -> 8.71 us  [swap(): return lax.ppermute(values, axis, pairs)]
    pallas_call x1, Pallas kernels: 4.79 us -> 4.32 us  [section(): pl.pallas_call(functools.partial(section_kernel, devices), out_shape=(sha...]
    pallas_call x1 -> x2, Pallas kernels: 4.03 us -> 4 us  [the longest x1 2.74 us: choose(): pl.pallas_call(choose_kernel, out_shape=[jax.ShapeDtypeStruct((4, rows, r...]
  transfers between devices with their start and end apart: 5 -> 5, of which waited for: 1 -> 1; matrix products, arithmetic and copies ran while one was open for 0% -> 0% of each run, Pallas kernels for 11% -> 10%
where the time goes in v10:
time: 39.9 us; the launch traced here: 40.4 us
  blocking collectives  19.7 us (49%)
  Pallas kernels  9.3 us (23%)
  starting transfers between devices  8.71 us (22%)
  waiting for transfers between devices  1.08 us (3%)
  between operations  0.79 us (2%)
  other arithmetic  0.68 us (2%)
    all_to_all x1, blocking collectives, body(): lax.all_to_all(total.reshape(devices // 2, radii // devices, 6 * NH), ('s...  19.7 us
    ppermute x5, starting transfers between devices, swap(): return lax.ppermute(values, axis, pairs)  8.71 us
    pallas_call x1, Pallas kernels, section(): pl.pallas_call(functools.partial(section_kernel, devices), out_shape=(sha...  4.32 us
    pallas_call x1, Pallas kernels, choose(): pl.pallas_call(choose_kernel, out_shape=[jax.ShapeDtypeStruct((4, rows, r...  2.74 us
    pallas_call x1, Pallas kernels, prepare(): pl.pallas_call(functools.partial(prepare_kernel, *cells), out_shape=(shap...  1.26 us
    ppermute x5, waiting for transfers between devices, swap(): return lax.ppermute(values, axis, pairs)  1.08 us
    pallas_call x1, Pallas kernels, pack(): pl.pallas_call(pack_kernel, out_shape=(stream, stream, girth, girth), in_...  0.98 us
  transfers between devices with their start and end apart: 5, of which 1 were waited for; matrix products, arithmetic and copies ran while one was open for 0% of the time, Pallas kernels for 10%

profile of v10, /device:TPU:0, one launch (start us, length us, event | category | flops | bytes accessed | tf_op | source)
XLA Modules:
  0.0 40.4 jit_solution(15504157339553126259)
XLA Ops:
  0.6 1.0 %pack_halos.1 = (f32[6,2,8,256]{3,2,1,0:T(8,128)S(1)}, f32[6,2,8,256]{3,2,1,0:T(8,128)S(1)}, f32[6,4,2,256]{3,2,1,0:T(2,128)S(1)}, f32[6,4,2,256]{3,2,1,0:T(2,128)S(1)}) custom-call(f32[3,4,8,256]{3,2,1,0:T(8,128)} %vel_ref.3, f32[4,8,256]{2,1,0:T(8,128)} %p_ref.3, f32[4,8,256]{2,1,0:T(8,128)} %k_ref.3, f32[4,8,256]{2,1,0:T(8,128)} %w_ref.3), custom_call_target="tpu_custom_call" | custom-call | tf_op jit(solution)/shard_map/pack_halos/pallas_call | solution.py:52
  1.6 3.1 %collective-permute-start = (f32[6,2,8,256]{3,2,1,0:T(8,128)S(1)}, f32[6,2,8,256]{3,2,1,0:T(8,128)S(1)}, u32[]{:S(2)}, u32[]{:S(2)}) collective-permute-start(f32[6,2,8,256]{3,2,1,0:T(8,128)S(1)} %get-tuple-element.27), channel_id=1, source_target_pairs={{0,8},{8,0},{16,24},{24,16},{1,9},{9,1},{17,25},{25,17},{2,10},{10... | collective-permute-start | bytes 294920 | tf_op jit(solution)/shard_map/ppermute | solution.py:619
  4.7 0.7 %collective-permute-start.1 = (f32[6,2,8,256]{3,2,1,0:T(8,128)S(1)}, f32[6,2,8,256]{3,2,1,0:T(8,128)S(1)}, u32[]{:S(2)}, u32[]{:S(2)}) collective-permute-start(f32[6,2,8,256]{3,2,1,0:T(8,128)S(1)} %get-tuple-element.28), channel_id=1, source_target_pairs={{8,16},{16,8},{9,17},{17,9},{10,18},{18,10},{11,19},{19,11},{12,20... | collective-permute-start | bytes 294920 | tf_op jit(solution)/shard_map/ppermute | solution.py:619
  5.4 0.0 copy-start
  5.4 0.0 copy-start.1
  5.4 0.0 copy-start.2
  5.4 0.0 copy-start.3
  5.4 2.7 %choose_points.1 = (f32[4,384,128]{2,1,0:T(8,128)S(1)}, f32[384,256]{1,0:T(8,128)S(1)}, f32[6,4,2,256]{3,2,1,0:T(2,128)S(1)}, f32[6,4,2,256]{3,2,1,0:T(2,128)S(1)}) custom-call(s32[64]{0:T(128)} %bitcast.1, s32[128,1024]{1,0:T(8,128)} %ids_hbm.1, f32[3,128,1024]{2,1,0:T(8,128)} %frac_hbm.1, f32[1024,256]{1,0:T(8,128)} %constant.4.clone.table_hbm, ...), custom_call_target="tpu_custom_call" | custom-call | flops 1048576 | bytes 4194304 | tf_op jit(solution)/shard_map/choose_points/pallas_call | solution.py:143
  8.2 0.1 collective-permute-start.2
  8.2 0.7 %collective-permute-start.3 = (f32[6,4,2,256]{3,2,1,0:T(2,128)S(1)}, f32[6,4,2,256]{3,2,1,0:T(2,128)S(1)}, u32[]{:S(2)}, u32[]{:S(2)}) collective-permute-start(f32[6,4,2,256]{3,2,1,0:T(2,128)S(1)} %get-tuple-element.30), channel_id=1, source_target_pairs={{1,2},{2,1},{3,4},{4,3},{5,6},{6,5},{9,10},{10,9},{11,12},{12,11},... | collective-permute-start | bytes 147464 | tf_op jit(solution)/shard_map/ppermute | solution.py:619
  8.9 1.3 %prepare_points.1 = (s32[384,128]{1,0:T(8,128)S(1)}, f32[384,128]{1,0:T(8,128)S(1)}, f32[384,128]{1,0:T(8,128)S(1)}, f32[384,128]{1,0:T(8,128)S(1)}, s32[640,128]{1,0:T(8,128)S(1)}, /*index=5*/s32[1]{0:T(128)}) custom-call(f32[4,384,128]{2,1,0:T(8,128)S(1)} %get-tuple-element.25.picked), custom_call_target="tpu_custom_call" | custom-call | flops 9830400 | bytes 2162688 | tf_op jit(solution)/shard_map/prepare_points/pallas_call | solution.py:253
  10.2 0.0 collective-permute-done.2.girth_a
  10.2 0.0 collective-permute-done.3.girth_b
  10.2 0.0 collective-permute-done.stream_a
  10.2 0.0 collective-permute-done.1.stream_b
  10.2 0.0 copy-done
  10.2 0.0 copy-done.1
  10.2 0.0 copy-done.2
  10.3 0.0 copy-done.3
  10.3 4.3 %section_and_disk.1 = (f32[3,4,8,256]{3,2,1,0:T(8,128)}, f32[4,8,256]{2,1,0:T(8,128)}, f32[4,8,256]{2,1,0:T(8,128)}, f32[64,768]{1,0:T(8,128)S(1)}, f32[64,768]{1,0:T(8,128)S(1)}) custom-call(s32[1]{0:T(128)} %get-tuple-element.26.count_ref, f32[3,4,8,256]{3,2,1,0:T(8,128)S(1)} %copy-done, f32[4,8,256]{2,1,0:T(8,128)S(1)} %copy-done.1, ...), custom_call_target="tpu_custom_call" | custom-call | tf_op jit(solution)/shard_map/section_and_disk/pallas_call | solution.py:573
  14.6 4.2 %collective-permute-start.4 = (f32[64,768]{1,0:T(8,128)S(1)}, f32[64,768]{1,0:T(8,128)S(1)}, u32[]{:S(2)}, u32[]{:S(2)}) collective-permute-start(f32[64,768]{1,0:T(8,128)S(1)} %get-tuple-element.41), channel_id=1, source_target_pairs={{0,1},{1,0},{2,3},{3,2},{4,5},{5,4},{6,7},{7,6},{8,9},{9,8},{10,11... | collective-permute-start | bytes 589832 | tf_op jit(solution)/shard_map/ppermute | solution.py:619
  18.8 1.1 %collective-permute-done.4 = f32[64,768]{1,0:T(8,128)S(1)} collective-permute-done((f32[64,768]{1,0:T(8,128)S(1)}, f32[64,768]{1,0:T(8,128)S(1)}, u32[]{:S(2)}, u32[]{:S(2)}) %collective-permute-start.4) | collective-permute-done | bytes 196640 | tf_op jit(solution)/shard_map/ppermute | solution.py:619
  19.9 0.1 reshape.11
  20.0 19.7 %all_to_all.5 = f32[16,4,768]{2,1,0:T(4,128)S(1)} all-to-all(f32[16,4,768]{2,1,0:T(4,128)S(1)} %reshape.11), channel_id=1, replica_groups={{0,2,4,6,8,10,12,14,16,18,20,22,24,26,28,30},{1,3,5,7,9,11,13,15,17,19,..., dimensions={0} | all-to-all | bytes 393216 | tf_op jit(solution)/shard_map/all_to_all | solution.py:645
  39.7 0.6 %reduce_sum.9 = f32[4,768]{1,0:T(4,128)} reduce(f32[16,4,768]{2,1,0:T(4,128)S(1)} %all_to_all.5, f32[]{:T(128)} %constant.1.clone.1), dimensions={0}, to_apply=%region_0.0 | reduce | flops 46080 | bytes 208900 | tf_op jit(solution)/shard_map/reduce_sum | solution.py:653
  (1 shorter events, 0.0 us)
Async XLA Ops:
  1.6 8.6 %collective-permute-start = (f32[6,2,8,256]{3,2,1,0:T(8,128)S(1)}, f32[6,2,8,256]{3,2,1,0:T(8,128)S(1)}, u32[]{:S(2)}, u32[]{:S(2)}) collective-permute-start(f32[6,2,8,256]{3,2,1,0:T(8,128)S(1)} %get-tuple-element.27), channel_id=1, source_target_pairs={{0,8},{8,0},{16,24},{24,16},{1,9},{9,1},{17,25},{25,17},{2,10},{10... | collective-permute-start | bytes 294920 | tf_op jit(solution)/shard_map/ppermute | solution.py:619
  4.7 5.5 %collective-permute-start.1 = (f32[6,2,8,256]{3,2,1,0:T(8,128)S(1)}, f32[6,2,8,256]{3,2,1,0:T(8,128)S(1)}, u32[]{:S(2)}, u32[]{:S(2)}) collective-permute-start(f32[6,2,8,256]{3,2,1,0:T(8,128)S(1)} %get-tuple-element.28), channel_id=1, source_target_pairs={{8,16},{16,8},{9,17},{17,9},{10,18},{18,10},{11,19},{19,11},{12,20... | collective-permute-start | bytes 294920 | tf_op jit(solution)/shard_map/ppermute | solution.py:619
  5.4 4.9 %copy-start = (f32[3,4,8,256]{3,2,1,0:T(8,128)S(1)}, f32[3,4,8,256]{3,2,1,0:T(8,128)}, u32[]{:S(2)}) copy-start(f32[3,4,8,256]{3,2,1,0:T(8,128)} %vel_ref.3) | copy-start | bytes 294916
  5.4 4.9 %copy-start.1 = (f32[4,8,256]{2,1,0:T(8,128)S(1)}, f32[4,8,256]{2,1,0:T(8,128)}, u32[]{:S(2)}) copy-start(f32[4,8,256]{2,1,0:T(8,128)} %p_ref.3) | copy-start | bytes 98308
  5.4 4.9 %copy-start.2 = (f32[4,8,256]{2,1,0:T(8,128)S(1)}, f32[4,8,256]{2,1,0:T(8,128)}, u32[]{:S(2)}) copy-start(f32[4,8,256]{2,1,0:T(8,128)} %k_ref.3) | copy-start | bytes 98308
  5.4 4.9 %copy-start.3 = (f32[4,8,256]{2,1,0:T(8,128)S(1)}, f32[4,8,256]{2,1,0:T(8,128)}, u32[]{:S(2)}) copy-start(f32[4,8,256]{2,1,0:T(8,128)} %w_ref.3) | copy-start | bytes 98308
  8.2 2.0 %collective-permute-start.2 = (f32[6,4,2,256]{3,2,1,0:T(2,128)S(1)}, f32[6,4,2,256]{3,2,1,0:T(2,128)S(1)}, u32[]{:S(2)}, u32[]{:S(2)}) collective-permute-start(f32[6,4,2,256]{3,2,1,0:T(2,128)S(1)} %get-tuple-element.29), channel_id=1, source_target_pairs={{0,1},{1,0},{2,3},{3,2},{4,5},{5,4},{6,7},{7,6},{8,9},{9,8},{10,11... | collective-permute-start | bytes 147464 | tf_op jit(solution)/shard_map/ppermute | solution.py:619
  8.2 2.0 %collective-permute-start.3 = (f32[6,4,2,256]{3,2,1,0:T(2,128)S(1)}, f32[6,4,2,256]{3,2,1,0:T(2,128)S(1)}, u32[]{:S(2)}, u32[]{:S(2)}) collective-permute-start(f32[6,4,2,256]{3,2,1,0:T(2,128)S(1)} %get-tuple-element.30), channel_id=1, source_target_pairs={{1,2},{2,1},{3,4},{4,3},{5,6},{6,5},{9,10},{10,9},{11,12},{12,11},... | collective-permute-start | bytes 147464 | tf_op jit(solution)/shard_map/ppermute | solution.py:619
  14.6 5.3 %collective-permute-start.4 = (f32[64,768]{1,0:T(8,128)S(1)}, f32[64,768]{1,0:T(8,128)S(1)}, u32[]{:S(2)}, u32[]{:S(2)}) collective-permute-start(f32[64,768]{1,0:T(8,128)S(1)} %get-tuple-element.41), channel_id=1, source_target_pairs={{0,1},{1,0},{2,3},{3,2},{4,5},{5,4},{6,7},{7,6},{8,9},{9,8},{10,11... | collective-permute-start | bytes 589832 | tf_op jit(solution)/shard_map/ppermute | solution.py:619

commit v11 on v9

--- a/solution.py
+++ b/solution.py
@@ -22,7 +22,7 @@
 ROWS = 8
 SHIFT = 10
 CHUNK = 32
-PRODUCTS = 2
+PRODUCTS = 3
 VMEM_LIMIT = 48 * 1024 * 1024
 
 
@@ -559,7 +559,7 @@
             scratch(6, cells_s, 3 * ROWS, cells_r),
             scratch(cells_s, 3 * ROWS, cells_r),
             scratch(PRODUCTS, cells_s, 4, cells_g, cells_r),
-            scratch(3 - PRODUCTS, cells_s, 2, cells_r // LANES, cells_g, LANES),
+            scratch(max(1, 3 - PRODUCTS), cells_s, 2, cells_r // LANES, cells_g, LANES),
             scratch(2, 3, moves.shape[0], radii),
             scratch(3, rows, radii),
             scratch(radii, 6 * NH),

time: 37.1 us -> 38.8 us (1.046); the launches traced: 37.6 us -> 38.8 us
  starting transfers between devices: 9.46 us -> 10.6 us
    ppermute x5, starting transfers between devices: 9.46 us -> 10.6 us  [swap(): return lax.ppermute(values, axis, pairs)]
  transfers between devices with their start and end apart: 5 -> 5, of which waited for: 1 -> 1; matrix products, arithmetic and copies ran while one was open for 0% -> 0% of each run, Pallas kernels for 11% -> 10%
where the time goes in v11:
time: 38.8 us
  blocking collectives  16 us (41%)
  starting transfers between devices  10.6 us (27%)
  Pallas kernels  9.67 us (25%)
  waiting for transfers between devices  1.08 us (3%)
  between operations  0.79 us (2%)
  other arithmetic  0.67 us (2%)
    all_to_all x1, blocking collectives, body(): lax.all_to_all(total.reshape(devices // 2, radii // devices, 6 * NH), ('s...  16 us
    ppermute x5, starting transfers between devices, swap(): return lax.ppermute(values, axis, pairs)  10.6 us
    pallas_call x1, Pallas kernels, section(): pl.pallas_call(functools.partial(section_kernel, devices), out_shape=(sha...  4.67 us
    pallas_call x1, Pallas kernels, prepare(): pl.pallas_call(functools.partial(prepare_kernel, cells_s, cells_g, cells_...  4.01 us
    ppermute x5, waiting for transfers between devices, swap(): return lax.ppermute(values, axis, pairs)  1.08 us
    pallas_call x1, Pallas kernels, pack(): pl.pallas_call(pack_kernel, out_shape=(stream, stream, girth, girth), in_...  0.98 us
  transfers between devices with their start and end apart: 5, of which 1 were waited for; matrix products, arithmetic and copies ran while one was open for 0% of the time, Pallas kernels for 10%

profile of v11, /device:TPU:0, one launch (start us, length us, event | category | flops | bytes accessed | tf_op | source)
XLA Modules:
  0.0 38.8 jit_solution(1321201383012146574)
XLA Ops:
  0.6 1.0 %pack_halos.1 = (f32[6,2,8,256]{3,2,1,0:T(8,128)S(1)}, f32[6,2,8,256]{3,2,1,0:T(8,128)S(1)}, f32[6,4,2,256]{3,2,1,0:T(2,128)S(1)}, f32[6,4,2,256]{3,2,1,0:T(2,128)S(1)}) custom-call(f32[3,4,8,256]{3,2,1,0:T(8,128)} %vel_ref.3, f32[4,8,256]{2,1,0:T(8,128)} %p_ref.3, f32[4,8,256]{2,1,0:T(8,128)} %k_ref.3, f32[4,8,256]{2,1,0:T(8,128)} %w_ref.3), custom_call_target="tpu_custom_call" | custom-call | tf_op jit(solution)/shard_map/pack_halos/pallas_call | solution.py:52
  1.6 3.1 %collective-permute-start = (f32[6,2,8,256]{3,2,1,0:T(8,128)S(1)}, f32[6,2,8,256]{3,2,1,0:T(8,128)S(1)}, u32[]{:S(2)}, u32[]{:S(2)}) collective-permute-start(f32[6,2,8,256]{3,2,1,0:T(8,128)S(1)} %get-tuple-element.21), channel_id=1, source_target_pairs={{0,8},{8,0},{16,24},{24,16},{1,9},{9,1},{17,25},{25,17},{2,10},{10... | collective-permute-start | bytes 294920 | tf_op jit(solution)/shard_map/ppermute | solution.py:590
  4.7 0.7 %collective-permute-start.1 = (f32[6,2,8,256]{3,2,1,0:T(8,128)S(1)}, f32[6,2,8,256]{3,2,1,0:T(8,128)S(1)}, u32[]{:S(2)}, u32[]{:S(2)}) collective-permute-start(f32[6,2,8,256]{3,2,1,0:T(8,128)S(1)} %get-tuple-element.22), channel_id=1, source_target_pairs={{8,16},{16,8},{9,17},{17,9},{10,18},{18,10},{11,19},{19,11},{12,20... | collective-permute-start | bytes 294920 | tf_op jit(solution)/shard_map/ppermute | solution.py:590
  5.4 0.1 collective-permute-start.2
  5.4 0.7 %collective-permute-start.3 = (f32[6,4,2,256]{3,2,1,0:T(2,128)S(1)}, f32[6,4,2,256]{3,2,1,0:T(2,128)S(1)}, u32[]{:S(2)}, u32[]{:S(2)}) collective-permute-start(f32[6,4,2,256]{3,2,1,0:T(2,128)S(1)} %get-tuple-element.24), channel_id=1, source_target_pairs={{1,2},{2,1},{3,4},{4,3},{5,6},{6,5},{9,10},{10,9},{11,12},{12,11},... | collective-permute-start | bytes 147464 | tf_op jit(solution)/shard_map/ppermute | solution.py:590
  6.1 0.0 copy-start
  6.1 0.0 copy-start.1
  6.1 0.0 copy-start.2
  6.2 0.0 copy-start.3
  6.2 4.0 %prepare_points.1 = (s32[384,128]{1,0:T(8,128)S(1)}, f32[384,128]{1,0:T(8,128)S(1)}, f32[384,128]{1,0:T(8,128)S(1)}, f32[384,128]{1,0:T(8,128)S(1)}, s32[640,128...) custom-call(s32[64]{0:T(128)} %bitcast.1, s32[128,1024]{1,0:T(8,128)} %ids_hbm.1, f32[3,128,1024]{2,1,0:T(8,128)} %frac_hbm.1, ...), custom_call_target="tpu_custom_call" | custom-call | flops 2621440 | bytes 5767168 | tf_op jit(solution)/shard_map/prepare_points/pallas_call | solution.py:214
  10.2 0.0 collective-permute-done.2.girth_a
  10.2 0.0 collective-permute-done.3.girth_b
  10.2 0.0 collective-permute-done.stream_a
  10.2 0.0 collective-permute-done.1.stream_b
  10.2 0.0 copy-done
  10.2 0.0 copy-done.1
  10.3 0.0 copy-done.2
  10.3 0.0 copy-done.3
  10.3 4.7 %section_and_disk.1 = (f32[3,4,8,256]{3,2,1,0:T(8,128)}, f32[4,8,256]{2,1,0:T(8,128)}, f32[4,8,256]{2,1,0:T(8,128)}, f32[64,768]{1,0:T(8,128)S(1)}, f32[64,768]{1,0:T(8,128)S(1)}) custom-call(s32[1]{0:T(128)} %get-tuple-element.20.count_ref, f32[3,4,8,256]{3,2,1,0:T(8,128)S(1)} %copy-done, f32[4,8,256]{2,1,0:T(8,128)S(1)} %copy-done.1, ...), custom_call_target="tpu_custom_call" | custom-call | tf_op jit(solution)/shard_map/section_and_disk/pallas_call | solution.py:544
  15.0 6.1 %collective-permute-start.4 = (f32[64,768]{1,0:T(8,128)S(1)}, f32[64,768]{1,0:T(8,128)S(1)}, u32[]{:S(2)}, u32[]{:S(2)}) collective-permute-start(f32[64,768]{1,0:T(8,128)S(1)} %get-tuple-element.35), channel_id=1, source_target_pairs={{0,1},{1,0},{2,3},{3,2},{4,5},{5,4},{6,7},{7,6},{8,9},{9,8},{10,11... | collective-permute-start | bytes 589832 | tf_op jit(solution)/shard_map/ppermute | solution.py:590
  21.0 1.1 %collective-permute-done.4 = f32[64,768]{1,0:T(8,128)S(1)} collective-permute-done((f32[64,768]{1,0:T(8,128)S(1)}, f32[64,768]{1,0:T(8,128)S(1)}, u32[]{:S(2)}, u32[]{:S(2)}) %collective-permute-start.4) | collective-permute-done | bytes 196640 | tf_op jit(solution)/shard_map/ppermute | solution.py:590
  22.1 0.1 reshape.11
  22.2 16.0 %all_to_all.5 = f32[16,4,768]{2,1,0:T(4,128)S(1)} all-to-all(f32[16,4,768]{2,1,0:T(4,128)S(1)} %reshape.11), channel_id=1, replica_groups={{0,2,4,6,8,10,12,14,16,18,20,22,24,26,28,30},{1,3,5,7,9,11,13,15,17,19,..., dimensions={0} | all-to-all | bytes 393216 | tf_op jit(solution)/shard_map/all_to_all | solution.py:614
  38.1 0.6 %reduce_sum.9 = f32[4,768]{1,0:T(4,128)} reduce(f32[16,4,768]{2,1,0:T(4,128)S(1)} %all_to_all.5, f32[]{:T(128)} %constant.1.clone.1), dimensions={0}, to_apply=%region_0.0 | reduce | flops 46080 | bytes 208900 | tf_op jit(solution)/shard_map/reduce_sum | solution.py:622
  (1 shorter events, 0.0 us)
Async XLA Ops:
  1.6 8.6 %collective-permute-start = (f32[6,2,8,256]{3,2,1,0:T(8,128)S(1)}, f32[6,2,8,256]{3,2,1,0:T(8,128)S(1)}, u32[]{:S(2)}, u32[]{:S(2)}) collective-permute-start(f32[6,2,8,256]{3,2,1,0:T(8,128)S(1)} %get-tuple-element.21), channel_id=1, source_target_pairs={{0,8},{8,0},{16,24},{24,16},{1,9},{9,1},{17,25},{25,17},{2,10},{10... | collective-permute-start | bytes 294920 | tf_op jit(solution)/shard_map/ppermute | solution.py:590
  4.7 5.5 %collective-permute-start.1 = (f32[6,2,8,256]{3,2,1,0:T(8,128)S(1)}, f32[6,2,8,256]{3,2,1,0:T(8,128)S(1)}, u32[]{:S(2)}, u32[]{:S(2)}) collective-permute-start(f32[6,2,8,256]{3,2,1,0:T(8,128)S(1)} %get-tuple-element.22), channel_id=1, source_target_pairs={{8,16},{16,8},{9,17},{17,9},{10,18},{18,10},{11,19},{19,11},{12,20... | collective-permute-start | bytes 294920 | tf_op jit(solution)/shard_map/ppermute | solution.py:590
  5.4 4.8 %collective-permute-start.2 = (f32[6,4,2,256]{3,2,1,0:T(2,128)S(1)}, f32[6,4,2,256]{3,2,1,0:T(2,128)S(1)}, u32[]{:S(2)}, u32[]{:S(2)}) collective-permute-start(f32[6,4,2,256]{3,2,1,0:T(2,128)S(1)} %get-tuple-element.23), channel_id=1, source_target_pairs={{0,1},{1,0},{2,3},{3,2},{4,5},{5,4},{6,7},{7,6},{8,9},{9,8},{10,11... | collective-permute-start | bytes 147464 | tf_op jit(solution)/shard_map/ppermute | solution.py:590
  5.4 4.8 %collective-permute-start.3 = (f32[6,4,2,256]{3,2,1,0:T(2,128)S(1)}, f32[6,4,2,256]{3,2,1,0:T(2,128)S(1)}, u32[]{:S(2)}, u32[]{:S(2)}) collective-permute-start(f32[6,4,2,256]{3,2,1,0:T(2,128)S(1)} %get-tuple-element.24), channel_id=1, source_target_pairs={{1,2},{2,1},{3,4},{4,3},{5,6},{6,5},{9,10},{10,9},{11,12},{12,11},... | collective-permute-start | bytes 147464 | tf_op jit(solution)/shard_map/ppermute | solution.py:590
  6.1 4.1 %copy-start = (f32[3,4,8,256]{3,2,1,0:T(8,128)S(1)}, f32[3,4,8,256]{3,2,1,0:T(8,128)}, u32[]{:S(2)}) copy-start(f32[3,4,8,256]{3,2,1,0:T(8,128)} %vel_ref.3) | copy-start | bytes 294916
  6.1 4.1 %copy-start.1 = (f32[4,8,256]{2,1,0:T(8,128)S(1)}, f32[4,8,256]{2,1,0:T(8,128)}, u32[]{:S(2)}) copy-start(f32[4,8,256]{2,1,0:T(8,128)} %p_ref.3) | copy-start | bytes 98308
  6.1 4.1 %copy-start.2 = (f32[4,8,256]{2,1,0:T(8,128)S(1)}, f32[4,8,256]{2,1,0:T(8,128)}, u32[]{:S(2)}) copy-start(f32[4,8,256]{2,1,0:T(8,128)} %k_ref.3) | copy-start | bytes 98308
  6.2 4.1 %copy-start.3 = (f32[4,8,256]{2,1,0:T(8,128)S(1)}, f32[4,8,256]{2,1,0:T(8,128)}, u32[]{:S(2)}) copy-start(f32[4,8,256]{2,1,0:T(8,128)} %w_ref.3) | copy-start | bytes 98308
  15.0 7.1 %collective-permute-start.4 = (f32[64,768]{1,0:T(8,128)S(1)}, f32[64,768]{1,0:T(8,128)S(1)}, u32[]{:S(2)}, u32[]{:S(2)}) collective-permute-start(f32[64,768]{1,0:T(8,128)S(1)} %get-tuple-element.35), channel_id=1, source_target_pairs={{0,1},{1,0},{2,3},{3,2},{4,5},{5,4},{6,7},{7,6},{8,9},{9,8},{10,11... | collective-permute-start | bytes 589832 | tf_op jit(solution)/shard_map/ppermute | solution.py:590

commit v12 on v11

--- a/solution.py
+++ b/solution.py
@@ -22,7 +22,7 @@
 ROWS = 8
 SHIFT = 10
 CHUNK = 32
-PRODUCTS = 3
+PRODUCTS = 6
 VMEM_LIMIT = 48 * 1024 * 1024
 
 
@@ -81,7 +81,7 @@
     ids_hbm,
     frac_hbm,
     table_hbm,
-    q_ref,
+    key_ref,
     fr_ref,
     xs_ref,
     xg_ref,
@@ -93,10 +93,6 @@
     table_ref,
     turned,
     picked,
-    keys,
-    frs,
-    xss,
-    xgs,
     order,
     arrived,
 ):
@@ -111,7 +107,7 @@
     sectors = owner_ref.shape[0]
     azimuths = ids_ref.shape[1]
     width = azimuths // sectors
-    rows = fr_ref.shape[0]
+    rows = chosen_ref.shape[0]
     pad = moves_ref.shape[0] - rows
     passes = network(rows)
     valid = 1 << SHIFT - 1
@@ -125,9 +121,7 @@
     for d in range(4):
         picked[d] = jnp.full(picked.shape[1:], -1.0 if d == 0 else 0.0, jnp.float32)
     chosen_ref[...] = jnp.zeros_like(chosen_ref)
-    beyond = pl.ds(rows, pad)
-    for slot in range(2):
-        keys[slot, beyond, :] = jnp.zeros((pad, LANES), jnp.int32)
+    key_ref[rows : rows + pad, :] = jnp.zeros((pad, LANES), jnp.int32)
     moves_ref[0:pad, :] = jnp.zeros((pad, LANES), jnp.int32)
     for d in range(4):
         copies[d].wait()
@@ -153,9 +147,9 @@
     girth_cell, radial_cell = split(rest, cells_r)
     xs = (stream_cell - stream_first).astype(jnp.float32) + picked[1]
     kept = (ids >= 0) & (xs > -1.0) & (xs < float(cells_s))
-    xss[0, held, :] = xs
-    xgs[0, held, :] = girth_cell.astype(jnp.float32) + picked[2]
-    frs[0, held, :] = picked[3]
+    xs_ref[held, :] = xs
+    xg_ref[held, :] = girth_cell.astype(jnp.float32) + picked[2]
+    fr_ref[held, :] = picked[3]
     earlier = lax.broadcasted_iota(jnp.int32, (rows, rows), 0) > lax.broadcasted_iota(
         jnp.int32, (rows, rows), 1
     )
@@ -167,37 +161,31 @@
     counts = rows - jnp.sum(skipped, axis=0, keepdims=True).astype(jnp.int32)
     count_ref[0] = jnp.max(counts)
     moves_ref[pad : pad + rows, :] = jnp.where(kept, valid, 0)
-    keys[0, held, :] = (radial_cell << SHIFT) + jnp.where(kept, before, 0)
-    for number, (low, digits) in enumerate(passes):
-        a, b = number % 2, 1 - number % 2
+    key_ref[held, :] = (radial_cell << SHIFT) + jnp.where(kept, before, 0)
+    for low, digits in passes:
         mask = digits - 1 << low
-        last = number == len(passes) - 1
         for at in range(0, rows, CHUNK):
             here, target = pl.ds(at, CHUNK), pl.ds(pad + at, CHUNK)
-            there = [pl.ds(at + (k << low), CHUNK) for k in range(1, digits)]
-            key = keys[a, here, :]
-            arriving = [keys[a, t, :] for t in there]
-            moved = [(arriving[k] & mask) == (k + 1 << low) for k in range(digits - 1)]
+            there = {k: pl.ds(at + (k << low), CHUNK) for k in range(1, digits) if at + (k << low) < rows}
+            if not there and (low, digits) == passes[-1]:
+                continue
+            key = key_ref[here, :]
+            arriving = {k: key_ref[t, :] for k, t in there.items()}
+            moved = {k: (arriving[k] & mask) == k << low for k in there}
             key = jnp.where((key & mask) != 0, key & -(1 << SHIFT), key)
-            came = moves_ref[target, :]
-            out = [r[a, here, :] for r in (frs, xss, xgs)]
-            for k in range(digits - 1):
+            for k in there:
                 key = jnp.where(moved[k], arriving[k], key)
-                came = came | jnp.where(moved[k], k + 1 << low, 0)
-                out = [
-                    jnp.where(moved[k], r[a, there[k], :], o) for r, o in zip((frs, xss, xgs), out)
-                ]
-            moves_ref[target, :] = came
-            if last:
-                q_ref[here, :] = key >> SHIFT
-                fr_ref[here, :] = out[0]
-                xs_ref[here, :] = out[1]
-                xg_ref[here, :] = out[2]
-            else:
-                keys[b, here, :] = key
-                frs[b, here, :] = out[0]
-                xss[b, here, :] = out[1]
-                xgs[b, here, :] = out[2]
+            key_ref[here, :] = key
+            if there:
+                came = moves_ref[target, :]
+                for k in there:
+                    came = came | jnp.where(moved[k], k << low, 0)
+                moves_ref[target, :] = came
+                for ref in (fr_ref, xs_ref, xg_ref):
+                    value = ref[here, :]
+                    for k, t in there.items():
+                        value = jnp.where(moved[k], ref[t, :], value)
+                    ref[here, :] = value
 
 
 def prepare(owners, corner_ids, fractions, table, cells, girth_count):
@@ -207,7 +195,7 @@
     rows = 3 * sectors // girth_count * (azimuths // sectors)
     pad = reach(rows)
     shape = jax.ShapeDtypeStruct
-    lists = (rows, radii)
+    lists = (rows + pad, radii)
     vmem = pl.BlockSpec(memory_space=pltpu.VMEM)
     smem = pl.BlockSpec(memory_space=pltpu.SMEM)
     hbm = pl.BlockSpec(memory_space=pltpu.HBM)
@@ -230,9 +218,7 @@
             pltpu.VMEM(table.shape, jnp.float32),
             pltpu.VMEM((4, azimuths, radii), jnp.float32),
             pltpu.VMEM((4, rows, radii), jnp.float32),
-            pltpu.VMEM((2, rows + pad, radii), jnp.int32),
         ]
-        + [pltpu.VMEM((2, rows + pad, radii), jnp.float32)] * 3
         + [pltpu.SMEM((rows // (azimuths // sectors) + 1,), jnp.int32)]
         + [pltpu.SemaphoreType.DMA((5,))],
         compiler_params=pltpu.CompilerParams(vmem_limit_bytes=VMEM_LIMIT),
@@ -352,7 +338,7 @@
     stream_b,
     girth_a,
     girth_b,
-    q_ref,
+    key_ref,
     fr_ref,
     xs_ref,
     xg_ref,
@@ -376,7 +362,7 @@
     stored,
 ):
     cells_s, cells_g, cells_r = p_ref.shape
-    rows = fr_ref.shape[0]
+    rows = chosen_ref.shape[0]
     pad = moves_ref.shape[0] - rows
     passes = network(rows)
     valid = 1 << SHIFT - 1
@@ -409,14 +395,16 @@
         new_vel_ref[c] = updated[c]
         slope = radial(updated[c], 1, 0.0) - updated[c]
         for kind, values in enumerate((updated[c], slope)):
-            if c < PRODUCTS:
-                high = rounded(values)
-                field_ref[c, :, 2 * kind] = high
-                field_ref[c, :, 2 * kind + 1] = rounded(values - high)
-            else:
-                for h in range(halves):
-                    lanes = slice(h * LANES, (h + 1) * LANES)
-                    gather_ref[c - PRODUCTS, :, kind, h] = values[:, :, lanes]
+            for layer in range(cells_s):
+                place = c * cells_s + layer
+                if place < PRODUCTS:
+                    high = rounded(values[layer])
+                    field_ref[place, 2 * kind] = high
+                    field_ref[place, 2 * kind + 1] = rounded(values[layer] - high)
+                else:
+                    for h in range(halves):
+                        lanes = slice(h * LANES, (h + 1) * LANES)
+                        gather_ref[place - PRODUCTS, kind, h] = values[layer, :, lanes]
     results = ((new_vel_ref, new_vel_hbm), (new_k_ref, new_k_hbm), (new_w_ref, new_w_hbm))
     copies = [
         pltpu.make_async_copy(source, target, stored.at[i])
@@ -426,7 +414,7 @@
         copy.start()
 
     kinds = 4
-    table = field_ref[...].reshape(PRODUCTS * cells_s * kinds * cells_g, cells_r)
+    table = field_ref[...].reshape(PRODUCTS * kinds * cells_g, cells_r)
     table = table.astype(jnp.bfloat16)
     pair = 2 * LANES
     girth_row = lax.broadcasted_iota(jnp.int32, (cells_g, pair), 0).astype(jnp.float32)
@@ -441,18 +429,19 @@
     def spread(values, j):
         return jnp.broadcast_to(values[j : j + 1], (cells_g, LANES))
 
-    def pick(c, s, kind, index, half_of):
+    def pick(place, kind, index, half_of):
         out = None
         for h in range(halves):
             got = jnp.take_along_axis(
-                gather_ref[c - PRODUCTS, s, kind, h], index, axis=1, mode="promise_in_bounds"
+                gather_ref[place - PRODUCTS, kind, h], index, axis=1, mode="promise_in_bounds"
             )
             out = got if out is None else jnp.where(half_of[h], got, out)
         return out
 
     def eight(at):
         here = pl.ds(at, ROWS)
-        q8, fr8, xg8, xs8 = (r[here, :] for r in (q_ref, fr_ref, xg_ref, xs_ref))
+        key8, fr8, xg8, xs8 = (r[here, :] for r in (key_ref, fr_ref, xg_ref, xs_ref))
+        q8 = key8 >> SHIFT
         hs8 = [jnp.maximum(1.0 - jnp.abs(xs8 - float(s)), 0.0) for s in range(cells_s)]
         index8 = q8 & (LANES - 1)
         qf8 = q8.astype(jnp.float32)
@@ -461,32 +450,38 @@
             chosen_q = jnp.broadcast_to(two(qf8, j), (cells_r, pair)).astype(index_type)
             hot = jnp.where(radial_row == chosen_q, one, none)
             got = jnp.dot(table, hot, preferred_element_type=jnp.float32)
-            got = got.reshape(PRODUCTS, cells_s, kinds, cells_g, pair)
+            got = got.reshape(PRODUCTS, kinds, cells_g, pair)
             fr = two(fr8, j)
             hg = jnp.maximum(1.0 - jnp.abs(two(xg8, j) - girth_row), 0.0)
             hs = [two(hs8[s], j) for s in range(cells_s)]
-            for c in range(PRODUCTS):
-                total = None
-                for s in range(cells_s):
-                    value = got[c, s, 0] + got[c, s, 1] + fr * (got[c, s, 2] + got[c, s, 3])
-                    value = hs[s] * value
-                    total = value if total is None else total + value
-                total = hg * total
-                sums[c] += [total[:, :LANES], total[:, LANES:]]
+            gathered = []
             for i in (j, j + 1):
                 index, q = spread(index8, i), spread(q8, i)
                 half_of = [q >= h * LANES for h in range(halves)]
-                own_hg = hg[:, (i - j) * LANES : (i - j + 1) * LANES]
-                for c in range(PRODUCTS, 3):
-                    total = None
-                    for s in range(cells_s):
-                        value = pick(c, s, 0, index, half_of)
-                        value = value + fr8[i : i + 1] * pick(c, s, 1, index, half_of)
-                        value = hs8[s][i : i + 1] * value
+                parts = {}
+                for place in range(PRODUCTS, 3 * cells_s):
+                    c, s = divmod(place, cells_s)
+                    value = pick(place, 0, index, half_of)
+                    value = value + fr8[i : i + 1] * pick(place, 1, index, half_of)
+                    value = hs8[s][i : i + 1] * value
+                    parts[c] = value if c not in parts else parts[c] + value
+                gathered.append(parts)
+            for c in range(3):
+                total = None
+                for s in range(cells_s):
+                    place = c * cells_s + s
+                    if place < PRODUCTS:
+                        value = got[place, 0] + got[place, 1] + fr * (got[place, 2] + got[place, 3])
+                        value = hs[s] * value
                         total = value if total is None else total + value
-                    sums[c].append(own_hg * total)
+                for i in range(2):
+                    lanes = slice(i * LANES, (i + 1) * LANES)
+                    both = [] if total is None else [total[:, lanes]]
+                    if c in gathered[i]:
+                        both.append(gathered[i][c])
+                    sums[c].append(hg[:, lanes] * sum(both[1:], both[0]))
         for c in range(3):
-            value_ref[0, c, pl.ds(pad + at, ROWS), :] = girth_sums(sums[c])
+            value_ref[c, pl.ds(pad + at, ROWS), :] = girth_sums(sums[c])
 
     def step(group, carry):
         for part in range(2):
@@ -495,24 +490,29 @@
 
     lax.fori_loop(0, (count_ref[0] + 2 * ROWS - 1) // (2 * ROWS), step, jnp.int32(0))
 
-    for number, (low, digits) in enumerate(reversed(passes)):
-        a, b = number % 2, 1 - number % 2
+    for low, digits in reversed(passes):
         mask = digits - 1 << low
-        last = number == len(passes) - 1
-        for at in range(0, rows, CHUNK):
+        last = (low, digits) == passes[0]
+        for at in range(rows - CHUNK, -1, -CHUNK):
             here = pl.ds(pad + at, CHUNK)
-            there = [pl.ds(pad + at - (k << low), CHUNK) for k in range(1, digits)]
-            moved = [(moves_ref[there[k], :] & mask) == (k + 1 << low) for k in range(digits - 1)]
+            there = {
+                k: pl.ds(pad + at - (k << low), CHUNK)
+                for k in range(1, digits)
+                if at + CHUNK > k << low
+            }
+            if not there and not last:
+                continue
+            moved = {k: (moves_ref[t, :] & mask) == k << low for k, t in there.items()}
             if last:
                 kept = (moves_ref[here, :] & valid) != 0
             for c in range(3):
-                value = value_ref[a, c, here, :]
-                for k in range(digits - 1):
-                    value = jnp.where(moved[k], value_ref[a, c, there[k], :], value)
+                value = value_ref[c, here, :]
+                for k, t in there.items():
+                    value = jnp.where(moved[k], value_ref[c, t, :], value)
                 if last:
                     disk_ref[c, pl.ds(at, CHUNK), :] = jnp.where(kept, value, 0.0)
                 else:
-                    value_ref[b, c, here, :] = value
+                    value_ref[c, here, :] = value
 
     turned = jnp.concatenate([disk_ref[c].T for c in range(3)], axis=0)
     high, low = halved(turned)
@@ -536,7 +536,7 @@
 def section(velocity, pressure, energy, rate, halos, points, devices):
     _, cells_s, cells_g, cells_r = velocity.shape
     *lists, moves, chosen, counts = points
-    rows, radii = lists[0].shape
+    rows, radii = chosen.shape[0], lists[0].shape[1]
     shape = functools.partial(jax.ShapeDtypeStruct, dtype=jnp.float32)
     scratch = lambda *dims: pltpu.VMEM(dims, jnp.float32)
     vmem = pl.BlockSpec(memory_space=pltpu.VMEM)
@@ -558,9 +558,9 @@
             scratch(*rate.shape),
             scratch(6, cells_s, 3 * ROWS, cells_r),
             scratch(cells_s, 3 * ROWS, cells_r),
-            scratch(PRODUCTS, cells_s, 4, cells_g, cells_r),
-            scratch(max(1, 3 - PRODUCTS), cells_s, 2, cells_r // LANES, cells_g, LANES),
-            scratch(2, 3, moves.shape[0], radii),
+            scratch(PRODUCTS, 4, cells_g, cells_r),
+            scratch(3 * cells_s - PRODUCTS, 2, cells_r // LANES, cells_g, LANES),
+            scratch(3, moves.shape[0], radii),
             scratch(3, rows, radii),
             scratch(radii, 6 * NH),
             pltpu.SemaphoreType.DMA((3,)),

time: 38.8 us -> 39.3 us (1.013)
  blocking collectives: 16 us -> 20.7 us
  starting transfers between devices: 10.6 us -> 6.77 us
    all_to_all x1, blocking collectives: 16 us -> 20.7 us  [body(): lax.all_to_all(total.reshape(devices // 2, radii // devices, 6 * NH), ('s...]
    ppermute x5, starting transfers between devices: 10.6 us -> 6.77 us  [swap(): return lax.ppermute(values, axis, pairs)]
where the time goes in v12:
time: 39.3 us; the launch traced here: 39.6 us
  blocking collectives  20.7 us (53%)
  Pallas kernels  9.52 us (24%)
  starting transfers between devices  6.77 us (17%)
  waiting for transfers between devices  1.08 us (3%)
  between operations  0.79 us (2%)
  other arithmetic  0.67 us (2%)
    all_to_all x1, blocking collectives, body(): lax.all_to_all(total.reshape(devices // 2, radii // devices, 6 * NH), ('s...  20.7 us
    ppermute x5, starting transfers between devices, swap(): return lax.ppermute(values, axis, pairs)  6.77 us
    pallas_call x1, Pallas kernels, section(): pl.pallas_call(functools.partial(section_kernel, devices), out_shape=(sha...  4.5 us
    pallas_call x1, Pallas kernels, prepare(): pl.pallas_call(functools.partial(prepare_kernel, cells_s, cells_g, cells_...  4.04 us
    ppermute x5, waiting for transfers between devices, swap(): return lax.ppermute(values, axis, pairs)  1.08 us
    pallas_call x1, Pallas kernels, pack(): pl.pallas_call(pack_kernel, out_shape=(stream, stream, girth, girth), in_...  0.98 us
  transfers between devices with their start and end apart: 5, of which 1 were waited for; matrix products, arithmetic and copies ran while one was open for 0% of the time, Pallas kernels for 10%

profile of v12, /device:TPU:0, one launch (start us, length us, event | category | flops | bytes accessed | tf_op | source)
XLA Modules:
  0.0 39.6 jit_solution(13193590533956121335)
XLA Ops:
  0.6 1.0 %pack_halos.1 = (f32[6,2,8,256]{3,2,1,0:T(8,128)S(1)}, f32[6,2,8,256]{3,2,1,0:T(8,128)S(1)}, f32[6,4,2,256]{3,2,1,0:T(2,128)S(1)}, f32[6,4,2,256]{3,2,1,0:T(2,128)S(1)}) custom-call(f32[3,4,8,256]{3,2,1,0:T(8,128)} %vel_ref.3, f32[4,8,256]{2,1,0:T(8,128)} %p_ref.3, f32[4,8,256]{2,1,0:T(8,128)} %k_ref.3, f32[4,8,256]{2,1,0:T(8,128)} %w_ref.3), custom_call_target="tpu_custom_call" | custom-call | tf_op jit(solution)/shard_map/pack_halos/pallas_call | solution.py:52
  1.6 3.1 %collective-permute-start = (f32[6,2,8,256]{3,2,1,0:T(8,128)S(1)}, f32[6,2,8,256]{3,2,1,0:T(8,128)S(1)}, u32[]{:S(2)}, u32[]{:S(2)}) collective-permute-start(f32[6,2,8,256]{3,2,1,0:T(8,128)S(1)} %get-tuple-element.21), channel_id=1, source_target_pairs={{0,8},{8,0},{16,24},{24,16},{1,9},{9,1},{17,25},{25,17},{2,10},{10... | collective-permute-start | bytes 294920 | tf_op jit(solution)/shard_map/ppermute | solution.py:590
  4.7 0.7 %collective-permute-start.1 = (f32[6,2,8,256]{3,2,1,0:T(8,128)S(1)}, f32[6,2,8,256]{3,2,1,0:T(8,128)S(1)}, u32[]{:S(2)}, u32[]{:S(2)}) collective-permute-start(f32[6,2,8,256]{3,2,1,0:T(8,128)S(1)} %get-tuple-element.22), channel_id=1, source_target_pairs={{8,16},{16,8},{9,17},{17,9},{10,18},{18,10},{11,19},{19,11},{12,20... | collective-permute-start | bytes 294920 | tf_op jit(solution)/shard_map/ppermute | solution.py:590
  5.4 0.1 collective-permute-start.2
  5.4 0.7 %collective-permute-start.3 = (f32[6,4,2,256]{3,2,1,0:T(2,128)S(1)}, f32[6,4,2,256]{3,2,1,0:T(2,128)S(1)}, u32[]{:S(2)}, u32[]{:S(2)}) collective-permute-start(f32[6,4,2,256]{3,2,1,0:T(2,128)S(1)} %get-tuple-element.24), channel_id=1, source_target_pairs={{1,2},{2,1},{3,4},{4,3},{5,6},{6,5},{9,10},{10,9},{11,12},{12,11},... | collective-permute-start | bytes 147464 | tf_op jit(solution)/shard_map/ppermute | solution.py:590
  6.1 0.0 copy-start
  6.1 0.0 copy-start.1
  6.1 0.0 copy-start.2
  6.2 0.0 copy-start.3
  6.2 4.0 %prepare_points.1 = (s32[640,128]{1,0:T(8,128)S(1)}, f32[640,128]{1,0:T(8,128)S(1)}, f32[640,128]{1,0:T(8,128)S(1)}, f32[640,128]{1,0:T(8,128)S(1)}, s32[640,128...) custom-call(s32[64]{0:T(128)} %bitcast.1, s32[128,1024]{1,0:T(8,128)} %ids_hbm.1, f32[3,128,1024]{2,1,0:T(8,128)} %frac_hbm.1, ...), custom_call_target="tpu_custom_call" | custom-call | flops 2621440 | bytes 5767168 | tf_op jit(solution)/shard_map/prepare_points/pallas_call | solution.py:202
  10.2 0.0 collective-permute-done.2.girth_a
  10.2 0.0 collective-permute-done.3.girth_b
  10.2 0.0 collective-permute-done.stream_a
  10.2 0.0 collective-permute-done.1.stream_b
  10.3 0.0 copy-done
  10.3 0.0 copy-done.1
  10.3 0.0 copy-done.2
  10.3 0.0 copy-done.3
  10.3 4.5 %section_and_disk.1 = (f32[3,4,8,256]{3,2,1,0:T(8,128)}, f32[4,8,256]{2,1,0:T(8,128)}, f32[4,8,256]{2,1,0:T(8,128)}, f32[64,768]{1,0:T(8,128)S(1)}, f32[64,768]{1,0:T(8,128)S(1)}) custom-call(s32[1]{0:T(128)} %get-tuple-element.20.count_ref, f32[3,4,8,256]{3,2,1,0:T(8,128)S(1)} %copy-done, f32[4,8,256]{2,1,0:T(8,128)S(1)} %copy-done.1, ...), custom_call_target="tpu_custom_call" | custom-call | tf_op jit(solution)/shard_map/section_and_disk/pallas_call | solution.py:544
  14.8 2.3 %collective-permute-start.4 = (f32[64,768]{1,0:T(8,128)S(1)}, f32[64,768]{1,0:T(8,128)S(1)}, u32[]{:S(2)}, u32[]{:S(2)}) collective-permute-start(f32[64,768]{1,0:T(8,128)S(1)} %get-tuple-element.35), channel_id=1, source_target_pairs={{0,1},{1,0},{2,3},{3,2},{4,5},{5,4},{6,7},{7,6},{8,9},{9,8},{10,11... | collective-permute-start | bytes 589832 | tf_op jit(solution)/shard_map/ppermute | solution.py:590
  17.1 1.1 %collective-permute-done.4 = f32[64,768]{1,0:T(8,128)S(1)} collective-permute-done((f32[64,768]{1,0:T(8,128)S(1)}, f32[64,768]{1,0:T(8,128)S(1)}, u32[]{:S(2)}, u32[]{:S(2)}) %collective-permute-start.4) | collective-permute-done | bytes 196640 | tf_op jit(solution)/shard_map/ppermute | solution.py:590
  18.2 0.1 reshape.11
  18.3 20.7 %all_to_all.5 = f32[16,4,768]{2,1,0:T(4,128)S(1)} all-to-all(f32[16,4,768]{2,1,0:T(4,128)S(1)} %reshape.11), channel_id=1, replica_groups={{0,2,4,6,8,10,12,14,16,18,20,22,24,26,28,30},{1,3,5,7,9,11,13,15,17,19,..., dimensions={0} | all-to-all | bytes 393216 | tf_op jit(solution)/shard_map/all_to_all | solution.py:614
  39.0 0.6 %reduce_sum.9 = f32[4,768]{1,0:T(4,128)} reduce(f32[16,4,768]{2,1,0:T(4,128)S(1)} %all_to_all.5, f32[]{:T(128)} %constant.1.clone.1), dimensions={0}, to_apply=%region_0.0 | reduce | flops 46080 | bytes 208900 | tf_op jit(solution)/shard_map/reduce_sum | solution.py:622
  (1 shorter events, 0.0 us)
Async XLA Ops:
  1.6 8.6 %collective-permute-start = (f32[6,2,8,256]{3,2,1,0:T(8,128)S(1)}, f32[6,2,8,256]{3,2,1,0:T(8,128)S(1)}, u32[]{:S(2)}, u32[]{:S(2)}) collective-permute-start(f32[6,2,8,256]{3,2,1,0:T(8,128)S(1)} %get-tuple-element.21), channel_id=1, source_target_pairs={{0,8},{8,0},{16,24},{24,16},{1,9},{9,1},{17,25},{25,17},{2,10},{10... | collective-permute-start | bytes 294920 | tf_op jit(solution)/shard_map/ppermute | solution.py:590
  4.7 5.5 %collective-permute-start.1 = (f32[6,2,8,256]{3,2,1,0:T(8,128)S(1)}, f32[6,2,8,256]{3,2,1,0:T(8,128)S(1)}, u32[]{:S(2)}, u32[]{:S(2)}) collective-permute-start(f32[6,2,8,256]{3,2,1,0:T(8,128)S(1)} %get-tuple-element.22), channel_id=1, source_target_pairs={{8,16},{16,8},{9,17},{17,9},{10,18},{18,10},{11,19},{19,11},{12,20... | collective-permute-start | bytes 294920 | tf_op jit(solution)/shard_map/ppermute | solution.py:590
  5.4 4.8 %collective-permute-start.2 = (f32[6,4,2,256]{3,2,1,0:T(2,128)S(1)}, f32[6,4,2,256]{3,2,1,0:T(2,128)S(1)}, u32[]{:S(2)}, u32[]{:S(2)}) collective-permute-start(f32[6,4,2,256]{3,2,1,0:T(2,128)S(1)} %get-tuple-element.23), channel_id=1, source_target_pairs={{0,1},{1,0},{2,3},{3,2},{4,5},{5,4},{6,7},{7,6},{8,9},{9,8},{10,11... | collective-permute-start | bytes 147464 | tf_op jit(solution)/shard_map/ppermute | solution.py:590
  5.4 4.8 %collective-permute-start.3 = (f32[6,4,2,256]{3,2,1,0:T(2,128)S(1)}, f32[6,4,2,256]{3,2,1,0:T(2,128)S(1)}, u32[]{:S(2)}, u32[]{:S(2)}) collective-permute-start(f32[6,4,2,256]{3,2,1,0:T(2,128)S(1)} %get-tuple-element.24), channel_id=1, source_target_pairs={{1,2},{2,1},{3,4},{4,3},{5,6},{6,5},{9,10},{10,9},{11,12},{12,11},... | collective-permute-start | bytes 147464 | tf_op jit(solution)/shard_map/ppermute | solution.py:590
  6.1 4.1 %copy-start = (f32[3,4,8,256]{3,2,1,0:T(8,128)S(1)}, f32[3,4,8,256]{3,2,1,0:T(8,128)}, u32[]{:S(2)}) copy-start(f32[3,4,8,256]{3,2,1,0:T(8,128)} %vel_ref.3) | copy-start | bytes 294916
  6.1 4.1 %copy-start.1 = (f32[4,8,256]{2,1,0:T(8,128)S(1)}, f32[4,8,256]{2,1,0:T(8,128)}, u32[]{:S(2)}) copy-start(f32[4,8,256]{2,1,0:T(8,128)} %p_ref.3) | copy-start | bytes 98308
  6.1 4.1 %copy-start.2 = (f32[4,8,256]{2,1,0:T(8,128)S(1)}, f32[4,8,256]{2,1,0:T(8,128)}, u32[]{:S(2)}) copy-start(f32[4,8,256]{2,1,0:T(8,128)} %k_ref.3) | copy-start | bytes 98308
  6.2 4.1 %copy-start.3 = (f32[4,8,256]{2,1,0:T(8,128)S(1)}, f32[4,8,256]{2,1,0:T(8,128)}, u32[]{:S(2)}) copy-start(f32[4,8,256]{2,1,0:T(8,128)} %w_ref.3) | copy-start | bytes 98308
  14.8 3.4 %collective-permute-start.4 = (f32[64,768]{1,0:T(8,128)S(1)}, f32[64,768]{1,0:T(8,128)S(1)}, u32[]{:S(2)}, u32[]{:S(2)}) collective-permute-start(f32[64,768]{1,0:T(8,128)S(1)} %get-tuple-element.35), channel_id=1, source_target_pairs={{0,1},{1,0},{2,3},{3,2},{4,5},{5,4},{6,7},{7,6},{8,9},{9,8},{10,11... | collective-permute-start | bytes 589832 | tf_op jit(solution)/shard_map/ppermute | solution.py:590

commit v13 on v9

--- a/solution.py
+++ b/solution.py
@@ -370,6 +370,7 @@
     visc_ref,
     field_ref,
     gather_ref,
+    weight_ref,
     value_ref,
     disk_ref,
     harm_ref,
@@ -429,17 +430,17 @@
     table = field_ref[...].reshape(PRODUCTS * cells_s * kinds * cells_g, cells_r)
     table = table.astype(jnp.bfloat16)
     pair = 2 * LANES
-    girth_row = lax.broadcasted_iota(jnp.int32, (cells_g, pair), 0).astype(jnp.float32)
+    girth_row = lax.broadcasted_iota(jnp.int32, (cells_g, LANES), 0).astype(jnp.float32)
     index_type = jnp.bfloat16 if cells_r <= 256 else jnp.float32
     radial_row = lax.broadcasted_iota(jnp.int32, (cells_r, pair), 0).astype(jnp.float32)
     radial_row = radial_row.astype(index_type)
     one, none = jnp.ones((), jnp.bfloat16), jnp.zeros((), jnp.bfloat16)
 
-    def two(values, j):
-        return jnp.concatenate([values[j : j + 1], values[j + 1 : j + 2]], axis=1)
-
-    def spread(values, j):
-        return jnp.broadcast_to(values[j : j + 1], (cells_g, LANES))
+    def row(ref, at):
+        return jnp.broadcast_to(ref[pl.ds(at, 1), :], (cells_g, LANES))
+
+    def wide(parts):
+        return jnp.concatenate(parts, axis=1)
 
     def pick(c, s, kind, index, half_of):
         out = None
@@ -450,47 +451,44 @@
             out = got if out is None else jnp.where(half_of[h], got, out)
         return out
 
-    def eight(at):
-        here = pl.ds(at, ROWS)
-        q8, fr8, xg8, xs8 = (r[here, :] for r in (q_ref, fr_ref, xg_ref, xs_ref))
-        hs8 = [jnp.maximum(1.0 - jnp.abs(xs8 - float(s)), 0.0) for s in range(cells_s)]
-        index8 = q8 & (LANES - 1)
-        qf8 = q8.astype(jnp.float32)
+    def eight(at, part):
+        xs8 = xs_ref[pl.ds(at, ROWS), :]
+        for s in range(cells_s):
+            weight_ref[part, s] = jnp.maximum(1.0 - jnp.abs(xs8 - float(s)), 0.0)
         sums = [[], [], []]
         for j in range(0, ROWS, 2):
-            chosen_q = jnp.broadcast_to(two(qf8, j), (cells_r, pair)).astype(index_type)
-            hot = jnp.where(radial_row == chosen_q, one, none)
+            both = (j, j + 1)
+            q = [row(q_ref, at + i) for i in both]
+            fr = [row(fr_ref, at + i) for i in both]
+            hs = [[row(weight_ref.at[part, s], i) for i in both] for s in range(cells_s)]
+            hg = [jnp.maximum(1.0 - jnp.abs(row(xg_ref, at + i) - girth_row), 0.0) for i in both]
+            spread = wide(q).astype(jnp.float32)
+            spread = jnp.concatenate([spread] * (cells_r // cells_g), axis=0).astype(index_type)
+            hot = jnp.where(radial_row == spread, one, none)
             got = jnp.dot(table, hot, preferred_element_type=jnp.float32)
             got = got.reshape(PRODUCTS, cells_s, kinds, cells_g, pair)
-            fr = two(fr8, j)
-            hg = jnp.maximum(1.0 - jnp.abs(two(xg8, j) - girth_row), 0.0)
-            hs = [two(hs8[s], j) for s in range(cells_s)]
-            for c in range(PRODUCTS):
-                total = None
-                for s in range(cells_s):
-                    value = got[c, s, 0] + got[c, s, 1] + fr * (got[c, s, 2] + got[c, s, 3])
-                    value = hs[s] * value
-                    total = value if total is None else total + value
-                total = hg * total
-                sums[c] += [total[:, :LANES], total[:, LANES:]]
-            for i in (j, j + 1):
-                index, q = spread(index8, i), spread(q8, i)
-                half_of = [q >= h * LANES for h in range(halves)]
-                own_hg = hg[:, (i - j) * LANES : (i - j + 1) * LANES]
-                for c in range(PRODUCTS, 3):
+            for i in range(2):
+                lanes = slice(i * LANES, (i + 1) * LANES)
+                index = q[i] & (LANES - 1)
+                half_of = [q[i] >= h * LANES for h in range(halves)]
+                for c in range(3):
                     total = None
                     for s in range(cells_s):
-                        value = pick(c, s, 0, index, half_of)
-                        value = value + fr8[i : i + 1] * pick(c, s, 1, index, half_of)
-                        value = hs8[s][i : i + 1] * value
+                        if c < PRODUCTS:
+                            high, low, slope_high, slope_low = (got[c, s, k, :, lanes] for k in range(kinds))
+                            value = high + low + fr[i] * (slope_high + slope_low)
+                        else:
+                            value = pick(c, s, 0, index, half_of)
+                            value = value + fr[i] * pick(c, s, 1, index, half_of)
+                        value = hs[s][i] * value
                         total = value if total is None else total + value
-                    sums[c].append(own_hg * total)
+                    sums[c].append(hg[i] * total)
         for c in range(3):
             value_ref[0, c, pl.ds(pad + at, ROWS), :] = girth_sums(sums[c])
 
     def step(group, carry):
         for part in range(2):
-            eight(pl.multiple_of((2 * group + part) * ROWS, ROWS))
+            eight(pl.multiple_of((2 * group + part) * ROWS, ROWS), part)
         return carry
 
     lax.fori_loop(0, (count_ref[0] + 2 * ROWS - 1) // (2 * ROWS), step, jnp.int32(0))
@@ -560,6 +558,7 @@
             scratch(cells_s, 3 * ROWS, cells_r),
             scratch(PRODUCTS, cells_s, 4, cells_g, cells_r),
             scratch(3 - PRODUCTS, cells_s, 2, cells_r // LANES, cells_g, LANES),
+            scratch(2, cells_s, ROWS, radii),
             scratch(2, 3, moves.shape[0], radii),
             scratch(3, rows, radii),
             scratch(radii, 6 * NH),

time: 37.1 us -> 37.8 us (1.019); the launches traced: 37.6 us -> 37.6 us
  blocking collectives: 15.7 us -> 18.3 us
  starting transfers between devices: 9.46 us -> 7.89 us
  Pallas kernels: 9.8 us -> 8.79 us
    all_to_all x1, blocking collectives: 15.7 us -> 18.3 us  [body(): lax.all_to_all(total.reshape(devices // 2, radii // devices, 6 * NH), ('s...]
    ppermute x5, starting transfers between devices: 9.46 us -> 7.89 us  [swap(): return lax.ppermute(values, axis, pairs)]
    pallas_call x1, Pallas kernels: 4.79 us -> 3.82 us  [section(): pl.pallas_call(functools.partial(section_kernel, devices), out_shape=(sha...]
where the time goes in v13:
time: 37.8 us; the launch traced here: 37.6 us
  blocking collectives  18.3 us (48%)
  Pallas kernels  8.79 us (23%)
  starting transfers between devices  7.89 us (21%)
  waiting for transfers between devices  1.08 us (3%)
  between operations  0.79 us (2%)
  other arithmetic  0.67 us (2%)
    all_to_all x1, blocking collectives, body(): lax.all_to_all(total.reshape(devices // 2, radii // devices, 6 * NH), ('s...  18.3 us
    ppermute x5, starting transfers between devices, swap(): return lax.ppermute(values, axis, pairs)  7.89 us
    pallas_call x1, Pallas kernels, prepare(): pl.pallas_call(functools.partial(prepare_kernel, cells_s, cells_g, cells_...  3.99 us
    pallas_call x1, Pallas kernels, section(): pl.pallas_call(functools.partial(section_kernel, devices), out_shape=(sha...  3.82 us
    ppermute x5, waiting for transfers between devices, swap(): return lax.ppermute(values, axis, pairs)  1.08 us
    pallas_call x1, Pallas kernels, pack(): pl.pallas_call(pack_kernel, out_shape=(stream, stream, girth, girth), in_...  0.98 us
  transfers between devices with their start and end apart: 5, of which 1 were waited for; matrix products, arithmetic and copies ran while one was open for 0% of the time, Pallas kernels for 11%

profile of v13, /device:TPU:0, one launch (start us, length us, event | category | flops | bytes accessed | tf_op | source)
XLA Modules:
  0.0 37.6 jit_solution(8315787618679005284)
XLA Ops:
  0.6 1.0 %pack_halos.1 = (f32[6,2,8,256]{3,2,1,0:T(8,128)S(1)}, f32[6,2,8,256]{3,2,1,0:T(8,128)S(1)}, f32[6,4,2,256]{3,2,1,0:T(2,128)S(1)}, f32[6,4,2,256]{3,2,1,0:T(2,128)S(1)}) custom-call(f32[3,4,8,256]{3,2,1,0:T(8,128)} %vel_ref.3, f32[4,8,256]{2,1,0:T(8,128)} %p_ref.3, f32[4,8,256]{2,1,0:T(8,128)} %k_ref.3, f32[4,8,256]{2,1,0:T(8,128)} %w_ref.3), custom_call_target="tpu_custom_call" | custom-call | tf_op jit(solution)/shard_map/pack_halos/pallas_call | solution.py:52
  1.6 3.1 %collective-permute-start = (f32[6,2,8,256]{3,2,1,0:T(8,128)S(1)}, f32[6,2,8,256]{3,2,1,0:T(8,128)S(1)}, u32[]{:S(2)}, u32[]{:S(2)}) collective-permute-start(f32[6,2,8,256]{3,2,1,0:T(8,128)S(1)} %get-tuple-element.21), channel_id=1, source_target_pairs={{0,8},{8,0},{16,24},{24,16},{1,9},{9,1},{17,25},{25,17},{2,10},{10... | collective-permute-start | bytes 294920 | tf_op jit(solution)/shard_map/ppermute | solution.py:589
  4.7 0.7 %collective-permute-start.1 = (f32[6,2,8,256]{3,2,1,0:T(8,128)S(1)}, f32[6,2,8,256]{3,2,1,0:T(8,128)S(1)}, u32[]{:S(2)}, u32[]{:S(2)}) collective-permute-start(f32[6,2,8,256]{3,2,1,0:T(8,128)S(1)} %get-tuple-element.22), channel_id=1, source_target_pairs={{8,16},{16,8},{9,17},{17,9},{10,18},{18,10},{11,19},{19,11},{12,20... | collective-permute-start | bytes 294920 | tf_op jit(solution)/shard_map/ppermute | solution.py:589
  5.4 0.1 collective-permute-start.2
  5.4 0.7 %collective-permute-start.3 = (f32[6,4,2,256]{3,2,1,0:T(2,128)S(1)}, f32[6,4,2,256]{3,2,1,0:T(2,128)S(1)}, u32[]{:S(2)}, u32[]{:S(2)}) collective-permute-start(f32[6,4,2,256]{3,2,1,0:T(2,128)S(1)} %get-tuple-element.24), channel_id=1, source_target_pairs={{1,2},{2,1},{3,4},{4,3},{5,6},{6,5},{9,10},{10,9},{11,12},{12,11},... | collective-permute-start | bytes 147464 | tf_op jit(solution)/shard_map/ppermute | solution.py:589
  6.1 0.0 copy-start
  6.1 0.0 copy-start.1
  6.1 0.0 copy-start.2
  6.2 0.0 copy-start.3
  6.2 4.0 %prepare_points.1 = (s32[384,128]{1,0:T(8,128)S(1)}, f32[384,128]{1,0:T(8,128)S(1)}, f32[384,128]{1,0:T(8,128)S(1)}, f32[384,128]{1,0:T(8,128)S(1)}, s32[640,128...) custom-call(s32[64]{0:T(128)} %bitcast.1, s32[128,1024]{1,0:T(8,128)} %ids_hbm.1, f32[3,128,1024]{2,1,0:T(8,128)} %frac_hbm.1, ...), custom_call_target="tpu_custom_call" | custom-call | flops 2621440 | bytes 5767168 | tf_op jit(solution)/shard_map/prepare_points/pallas_call | solution.py:214
  10.2 0.0 collective-permute-done.2.girth_a
  10.2 0.0 collective-permute-done.3.girth_b
  10.2 0.0 collective-permute-done.stream_a
  10.2 0.0 collective-permute-done.1.stream_b
  10.2 0.0 copy-done
  10.2 0.0 copy-done.1
  10.2 0.0 copy-done.2
  10.2 0.0 copy-done.3
  10.3 3.8 %section_and_disk.1 = (f32[3,4,8,256]{3,2,1,0:T(8,128)}, f32[4,8,256]{2,1,0:T(8,128)}, f32[4,8,256]{2,1,0:T(8,128)}, f32[64,768]{1,0:T(8,128)S(1)}, f32[64,768]{1,0:T(8,128)S(1)}) custom-call(s32[1]{0:T(128)} %get-tuple-element.20.count_ref, f32[3,4,8,256]{3,2,1,0:T(8,128)S(1)} %copy-done, f32[4,8,256]{2,1,0:T(8,128)S(1)} %copy-done.1, ...), custom_call_target="tpu_custom_call" | custom-call | tf_op jit(solution)/shard_map/section_and_disk/pallas_call | solution.py:542
  14.1 3.4 %collective-permute-start.4 = (f32[64,768]{1,0:T(8,128)S(1)}, f32[64,768]{1,0:T(8,128)S(1)}, u32[]{:S(2)}, u32[]{:S(2)}) collective-permute-start(f32[64,768]{1,0:T(8,128)S(1)} %get-tuple-element.35), channel_id=1, source_target_pairs={{0,1},{1,0},{2,3},{3,2},{4,5},{5,4},{6,7},{7,6},{8,9},{9,8},{10,11... | collective-permute-start | bytes 589832 | tf_op jit(solution)/shard_map/ppermute | solution.py:589
  17.5 1.1 %collective-permute-done.4 = f32[64,768]{1,0:T(8,128)S(1)} collective-permute-done((f32[64,768]{1,0:T(8,128)S(1)}, f32[64,768]{1,0:T(8,128)S(1)}, u32[]{:S(2)}, u32[]{:S(2)}) %collective-permute-start.4) | collective-permute-done | bytes 196640 | tf_op jit(solution)/shard_map/ppermute | solution.py:589
  18.6 0.1 reshape.11
  18.7 18.3 %all_to_all.5 = f32[16,4,768]{2,1,0:T(4,128)S(1)} all-to-all(f32[16,4,768]{2,1,0:T(4,128)S(1)} %reshape.11), channel_id=1, replica_groups={{0,2,4,6,8,10,12,14,16,18,20,22,24,26,28,30},{1,3,5,7,9,11,13,15,17,19,..., dimensions={0} | all-to-all | bytes 393216 | tf_op jit(solution)/shard_map/all_to_all | solution.py:613
  37.0 0.6 %reduce_sum.9 = f32[4,768]{1,0:T(4,128)} reduce(f32[16,4,768]{2,1,0:T(4,128)S(1)} %all_to_all.5, f32[]{:T(128)} %constant.1.clone.1), dimensions={0}, to_apply=%region_0.0 | reduce | flops 46080 | bytes 208900 | tf_op jit(solution)/shard_map/reduce_sum | solution.py:621
  (1 shorter events, 0.0 us)
Async XLA Ops:
  1.6 8.6 %collective-permute-start = (f32[6,2,8,256]{3,2,1,0:T(8,128)S(1)}, f32[6,2,8,256]{3,2,1,0:T(8,128)S(1)}, u32[]{:S(2)}, u32[]{:S(2)}) collective-permute-start(f32[6,2,8,256]{3,2,1,0:T(8,128)S(1)} %get-tuple-element.21), channel_id=1, source_target_pairs={{0,8},{8,0},{16,24},{24,16},{1,9},{9,1},{17,25},{25,17},{2,10},{10... | collective-permute-start | bytes 294920 | tf_op jit(solution)/shard_map/ppermute | solution.py:589
  4.7 5.5 %collective-permute-start.1 = (f32[6,2,8,256]{3,2,1,0:T(8,128)S(1)}, f32[6,2,8,256]{3,2,1,0:T(8,128)S(1)}, u32[]{:S(2)}, u32[]{:S(2)}) collective-permute-start(f32[6,2,8,256]{3,2,1,0:T(8,128)S(1)} %get-tuple-element.22), channel_id=1, source_target_pairs={{8,16},{16,8},{9,17},{17,9},{10,18},{18,10},{11,19},{19,11},{12,20... | collective-permute-start | bytes 294920 | tf_op jit(solution)/shard_map/ppermute | solution.py:589
  5.4 4.8 %collective-permute-start.2 = (f32[6,4,2,256]{3,2,1,0:T(2,128)S(1)}, f32[6,4,2,256]{3,2,1,0:T(2,128)S(1)}, u32[]{:S(2)}, u32[]{:S(2)}) collective-permute-start(f32[6,4,2,256]{3,2,1,0:T(2,128)S(1)} %get-tuple-element.23), channel_id=1, source_target_pairs={{0,1},{1,0},{2,3},{3,2},{4,5},{5,4},{6,7},{7,6},{8,9},{9,8},{10,11... | collective-permute-start | bytes 147464 | tf_op jit(solution)/shard_map/ppermute | solution.py:589
  5.4 4.7 %collective-permute-start.3 = (f32[6,4,2,256]{3,2,1,0:T(2,128)S(1)}, f32[6,4,2,256]{3,2,1,0:T(2,128)S(1)}, u32[]{:S(2)}, u32[]{:S(2)}) collective-permute-start(f32[6,4,2,256]{3,2,1,0:T(2,128)S(1)} %get-tuple-element.24), channel_id=1, source_target_pairs={{1,2},{2,1},{3,4},{4,3},{5,6},{6,5},{9,10},{10,9},{11,12},{12,11},... | collective-permute-start | bytes 147464 | tf_op jit(solution)/shard_map/ppermute | solution.py:589
  6.1 4.1 %copy-start = (f32[3,4,8,256]{3,2,1,0:T(8,128)S(1)}, f32[3,4,8,256]{3,2,1,0:T(8,128)}, u32[]{:S(2)}) copy-start(f32[3,4,8,256]{3,2,1,0:T(8,128)} %vel_ref.3) | copy-start | bytes 294916
  6.1 4.1 %copy-start.1 = (f32[4,8,256]{2,1,0:T(8,128)S(1)}, f32[4,8,256]{2,1,0:T(8,128)}, u32[]{:S(2)}) copy-start(f32[4,8,256]{2,1,0:T(8,128)} %p_ref.3) | copy-start | bytes 98308
  6.1 4.1 %copy-start.2 = (f32[4,8,256]{2,1,0:T(8,128)S(1)}, f32[4,8,256]{2,1,0:T(8,128)}, u32[]{:S(2)}) copy-start(f32[4,8,256]{2,1,0:T(8,128)} %k_ref.3) | copy-start | bytes 98308
  6.2 4.1 %copy-start.3 = (f32[4,8,256]{2,1,0:T(8,128)S(1)}, f32[4,8,256]{2,1,0:T(8,128)}, u32[]{:S(2)}) copy-start(f32[4,8,256]{2,1,0:T(8,128)} %w_ref.3) | copy-start | bytes 98308
  14.1 4.5 %collective-permute-start.4 = (f32[64,768]{1,0:T(8,128)S(1)}, f32[64,768]{1,0:T(8,128)S(1)}, u32[]{:S(2)}, u32[]{:S(2)}) collective-permute-start(f32[64,768]{1,0:T(8,128)S(1)} %get-tuple-element.35), channel_id=1, source_target_pairs={{0,1},{1,0},{2,3},{3,2},{4,5},{5,4},{6,7},{7,6},{8,9},{9,8},{10,11... | collective-permute-start | bytes 589832 | tf_op jit(solution)/shard_map/ppermute | solution.py:589

commit v14 on v9

--- a/solution.py
+++ b/solution.py
@@ -30,32 +30,50 @@
     return pltpu.with_memory_space_constraint(values, pltpu.HBM)
 
 
-def pack_kernel(vel_ref, p_ref, k_ref, w_ref, *slabs):
-    cells_s, cells_g, _ = p_ref.shape
+def pack_kernel(vel_hbm, p_hbm, k_hbm, w_hbm, ids_hbm, frac_hbm, *rest):
+    *slabs, ids_ref, frac_ref, fields, arrived = rest
+    moves = [(vel_hbm, fields.at[0:3]), (p_hbm, fields.at[3]), (k_hbm, fields.at[4])]
+    moves += [(w_hbm, fields.at[5]), (ids_hbm, ids_ref), (frac_hbm, frac_ref)]
+    copies = [
+        pltpu.make_async_copy(source, target, arrived.at[i])
+        for i, (source, target) in enumerate(moves)
+    ]
+    for copy in copies:
+        copy.start()
+    _, cells_s, cells_g, _ = fields.shape
     stream_odd = lax.axis_index("stream") % 2 == 1
     girth_odd = lax.axis_index("girth") % 2 == 1
+    for copy in copies[:4]:
+        copy.wait()
     for f in range(6):
-        own = vel_ref.at[f] if f < 3 else (p_ref, k_ref, w_ref)[f - 3]
-        first, last = own[0:2], own[cells_s - 2 : cells_s]
+        first, last = fields[f, 0:2], fields[f, cells_s - 2 : cells_s]
         slabs[0][f] = jnp.where(stream_odd, first, last)
         slabs[1][f] = jnp.where(stream_odd, last, first)
-        first, last = own[:, 0:2, :], own[:, cells_g - 2 : cells_g, :]
+        first, last = fields[f, :, 0:2, :], fields[f, :, cells_g - 2 : cells_g, :]
         slabs[2][f] = jnp.where(girth_odd, first, last)
         slabs[3][f] = jnp.where(girth_odd, last, first)
-
-
-def pack(velocity, pressure, energy, rate):
+    for copy in copies[4:]:
+        copy.wait()
+
+
+def pack(velocity, pressure, energy, rate, corner_ids, fractions):
     _, cells_s, cells_g, cells_r = velocity.shape
     stream = pltpu.VMEM((6, 2, cells_g, cells_r), jnp.float32)
     girth = pltpu.VMEM((6, cells_s, 2, cells_r), jnp.float32)
-    vmem = pl.BlockSpec(memory_space=pltpu.VMEM)
+    points = [pltpu.VMEM(x.shape, x.dtype) for x in (corner_ids, fractions)]
+    inputs = (velocity, pressure, energy, rate, corner_ids, fractions)
     return pl.pallas_call(
         pack_kernel,
-        out_shape=(stream, stream, girth, girth),
-        in_specs=[vmem] * 4,
-        out_specs=[vmem] * 4,
+        out_shape=[stream, stream, girth, girth] + points,
+        in_specs=[pl.BlockSpec(memory_space=pltpu.HBM)] * 6,
+        out_specs=[pl.BlockSpec(memory_space=pltpu.VMEM)] * 6,
+        scratch_shapes=[
+            pltpu.VMEM((6, cells_s, cells_g, cells_r), jnp.float32),
+            pltpu.SemaphoreType.DMA((6,)),
+        ],
+        compiler_params=pltpu.CompilerParams(vmem_limit_bytes=VMEM_LIMIT),
         name="pack_halos",
-    )(*(in_hbm(x) for x in (velocity, pressure, energy, rate)))
+    )(*(in_hbm(x) for x in inputs))
 
 
 def network(rows):
@@ -78,8 +96,8 @@
     cells_g,
     cells_r,
     owner_ref,
-    ids_hbm,
-    frac_hbm,
+    ids_ref,
+    frac_ref,
     table_hbm,
     q_ref,
     fr_ref,
@@ -88,9 +106,6 @@
     moves_ref,
     chosen_ref,
     count_ref,
-    ids_ref,
-    frac_ref,
-    table_ref,
     turned,
     picked,
     keys,
@@ -100,12 +115,6 @@
     order,
     arrived,
 ):
-    copies = [pltpu.make_async_copy(ids_hbm, ids_ref, arrived.at[0])]
-    for d in range(3):
-        copies.append(pltpu.make_async_copy(frac_hbm.at[d], frac_ref.at[d], arrived.at[1 + d]))
-    copies.append(pltpu.make_async_copy(table_hbm, table_ref, arrived.at[4]))
-    for copy in copies:
-        copy.start()
     stream_first = lax.axis_index("stream") * cells_s
     me = lax.axis_index("girth")
     sectors = owner_ref.shape[0]
@@ -116,31 +125,35 @@
     passes = network(rows)
     valid = 1 << SHIFT - 1
 
+    for place in range(rows // width):
+        order[place] = 0
+
     def listed(number, count):
         order[jnp.minimum(count, rows // width)] = number
         return count + (owner_ref[number] == me).astype(jnp.int32)
 
     owned = lax.fori_loop(0, sectors, listed, jnp.int32(0), unroll=8)
+    for place in range(rows // width):
+        source = pl.ds(pl.multiple_of(order[place] * width, width), width)
+        pltpu.make_async_copy(
+            table_hbm.at[source, :], chosen_ref.at[pl.ds(place * width, width), :], arrived.at[0]
+        ).start()
 
     for d in range(4):
         picked[d] = jnp.full(picked.shape[1:], -1.0 if d == 0 else 0.0, jnp.float32)
-    chosen_ref[...] = jnp.zeros_like(chosen_ref)
     beyond = pl.ds(rows, pad)
     for slot in range(2):
         keys[slot, beyond, :] = jnp.zeros((pad, LANES), jnp.int32)
     moves_ref[0:pad, :] = jnp.zeros((pad, LANES), jnp.int32)
     for d in range(4):
-        copies[d].wait()
         for at in range(0, azimuths, LANES):
             cols = pl.ds(at, LANES)
             plane = ids_ref[:, cols].astype(jnp.float32) if d == 0 else frac_ref[d - 1, :, cols]
             turned[d, cols, :] = plane.T
-    copies[4].wait()
 
     def sector(place, carry):
         source = pl.ds(pl.multiple_of(order[place] * width, width), width)
         target = pl.ds(pl.multiple_of(place * width, width), width)
-        chosen_ref[target, :] = table_ref[source, :]
         for d in range(4):
             picked[d, target, :] = turned[d, source, :]
         return carry
@@ -198,6 +211,7 @@
                 frs[b, here, :] = out[0]
                 xss[b, here, :] = out[1]
                 xgs[b, here, :] = out[2]
+    pltpu.make_async_copy(table_hbm.at[pl.ds(0, rows), :], chosen_ref, arrived.at[0]).wait()
 
 
 def prepare(owners, corner_ids, fractions, table, cells, girth_count):
@@ -222,25 +236,22 @@
             shape((rows, 2 * NH), jnp.float32),
             shape((1,), jnp.int32),
         ),
-        in_specs=[smem, hbm, hbm, hbm],
+        in_specs=[smem, vmem, vmem, hbm],
         out_specs=[vmem] * 6 + [smem],
         scratch_shapes=[
-            pltpu.VMEM(corner_ids.shape, jnp.int32),
-            pltpu.VMEM(fractions.shape, jnp.float32),
-            pltpu.VMEM(table.shape, jnp.float32),
             pltpu.VMEM((4, azimuths, radii), jnp.float32),
             pltpu.VMEM((4, rows, radii), jnp.float32),
             pltpu.VMEM((2, rows + pad, radii), jnp.int32),
         ]
         + [pltpu.VMEM((2, rows + pad, radii), jnp.float32)] * 3
         + [pltpu.SMEM((rows // (azimuths // sectors) + 1,), jnp.int32)]
-        + [pltpu.SemaphoreType.DMA((5,))],
+        + [pltpu.SemaphoreType.DMA((1,))],
         compiler_params=pltpu.CompilerParams(vmem_limit_bytes=VMEM_LIMIT),
         cost_estimate=pl.CostEstimate(
             flops=20 * radii * azimuths, bytes_accessed=44 * radii * azimuths, transcendentals=0
         ),
         name="prepare_points",
-    )(*(in_hbm(x) for x in (owners, corner_ids, fractions, table)))
+    )(in_hbm(owners), corner_ids, fractions, in_hbm(table))
 
 
 def radial(values, amount, fill):
@@ -589,7 +600,9 @@
             pairs += [(i, i + 1), (i + 1, i)]
         return lax.ppermute(values, axis, pairs)
 
-    slabs = pack(velocity, pressure, kinetic_energy, dissipation_rate)
+    *slabs, ids, fracs = pack(
+        velocity, pressure, kinetic_energy, dissipation_rate, corner_ids, fractions
+    )
     girth_halos = (
         swap(slabs[2], "girth", girth_count, 0),
         swap(slabs[3], "girth", girth_count, 1),
@@ -601,8 +614,8 @@
     halos = stream_halos + girth_halos
     points = prepare(
         sector_owner[:, 0],
-        corner_ids,
-        fractions,
+        ids,
+        fracs,
         fourier_table(azimuths, NH),
         (cells_s, cells_g, cells_r),
         girth_count,

time: 37.1 us -> 38.1 us (1.027); the launches traced: 37.6 us -> 37.8 us
  starting transfers between devices: 9.46 us -> 9.94 us
    pallas_call x1, Pallas kernels: 0.98 us -> 1.74 us  [pack(): pl.pallas_call(pack_kernel, out_shape=[stream, stream, girth, girth] + po...]
    pallas_call x1, Pallas kernels: 4.03 us -> 3.45 us  [prepare(): pl.pallas_call(functools.partial(prepare_kernel, cells_s, cells_g, cells_...]
    pallas_call x1, Pallas kernels: 4.79 us -> 4.31 us  [section(): pl.pallas_call(functools.partial(section_kernel, devices), out_shape=(sha...]
    ppermute x5, starting transfers between devices: 9.46 us -> 9.94 us  [swap(): return lax.ppermute(values, axis, pairs)]
  transfers between devices with their start and end apart: 5 -> 5, of which waited for: 1 -> 1; matrix products, arithmetic and copies ran while one was open for 0% -> 0% of each run, Pallas kernels for 11% -> 9%
where the time goes in v14:
time: 38.1 us; the launch traced here: 37.8 us
  blocking collectives  15.7 us (41%)
  starting transfers between devices  9.94 us (26%)
  Pallas kernels  9.5 us (25%)
  waiting for transfers between devices  1.08 us (3%)
  between operations  0.79 us (2%)
  other arithmetic  0.67 us (2%)
    all_to_all x1, blocking collectives, body(): lax.all_to_all(total.reshape(devices // 2, radii // devices, 6 * NH), ('s...  15.7 us
    ppermute x5, starting transfers between devices, swap(): return lax.ppermute(values, axis, pairs)  9.94 us
    pallas_call x1, Pallas kernels, section(): pl.pallas_call(functools.partial(section_kernel, devices), out_shape=(sha...  4.31 us
    pallas_call x1, Pallas kernels, prepare(): pl.pallas_call(functools.partial(prepare_kernel, cells_s, cells_g, cells_...  3.45 us
    pallas_call x1, Pallas kernels, pack(): pl.pallas_call(pack_kernel, out_shape=[stream, stream, girth, girth] + po...  1.74 us
    ppermute x5, waiting for transfers between devices, swap(): return lax.ppermute(values, axis, pairs)  1.08 us
  transfers between devices with their start and end apart: 5, of which 1 were waited for; matrix products, arithmetic and copies ran while one was open for 0% of the time, Pallas kernels for 9%

profile of v14, /device:TPU:0, one launch (start us, length us, event | category | flops | bytes accessed | tf_op | source)
XLA Modules:
  0.0 37.8 jit_solution(10494171833089364524)
XLA Ops:
  0.6 1.7 %pack_halos.1 = (f32[6,2,8,256]{3,2,1,0:T(8,128)S(1)}, f32[6,2,8,256]{3,2,1,0:T(8,128)S(1)}, f32[6,4,2,256]{3,2,1,0:T(2,128)S(1)}, f32[6,4,2,256]{3,2,1,0:T(2,12...) custom-call(f32[3,4,8,256]{3,2,1,0:T(8,128)} %vel_ref.1, f32[4,8,256]{2,1,0:T(8,128)} %p_ref.1, ...), custom_call_target="tpu_custom_call" | custom-call | tf_op jit(solution)/shard_map/pack_halos/pallas_call | solution.py:65
  2.4 3.1 %collective-permute-start = (f32[6,2,8,256]{3,2,1,0:T(8,128)S(1)}, f32[6,2,8,256]{3,2,1,0:T(8,128)S(1)}, u32[]{:S(2)}, u32[]{:S(2)}) collective-permute-start(f32[6,2,8,256]{3,2,1,0:T(8,128)S(1)} %get-tuple-element.25), channel_id=1, source_target_pairs={{0,8},{8,0},{16,24},{24,16},{1,9},{9,1},{17,25},{25,17},{2,10},{10... | collective-permute-start | bytes 294920 | tf_op jit(solution)/shard_map/ppermute | solution.py:601
  5.5 0.7 %collective-permute-start.1 = (f32[6,2,8,256]{3,2,1,0:T(8,128)S(1)}, f32[6,2,8,256]{3,2,1,0:T(8,128)S(1)}, u32[]{:S(2)}, u32[]{:S(2)}) collective-permute-start(f32[6,2,8,256]{3,2,1,0:T(8,128)S(1)} %get-tuple-element.26), channel_id=1, source_target_pairs={{8,16},{16,8},{9,17},{17,9},{10,18},{18,10},{11,19},{19,11},{12,20... | collective-permute-start | bytes 294920 | tf_op jit(solution)/shard_map/ppermute | solution.py:601
  6.1 0.1 collective-permute-start.2
  6.2 0.7 %collective-permute-start.3 = (f32[6,4,2,256]{3,2,1,0:T(2,128)S(1)}, f32[6,4,2,256]{3,2,1,0:T(2,128)S(1)}, u32[]{:S(2)}, u32[]{:S(2)}) collective-permute-start(f32[6,4,2,256]{3,2,1,0:T(2,128)S(1)} %get-tuple-element.28), channel_id=1, source_target_pairs={{1,2},{2,1},{3,4},{4,3},{5,6},{6,5},{9,10},{10,9},{11,12},{12,11},... | collective-permute-start | bytes 147464 | tf_op jit(solution)/shard_map/ppermute | solution.py:601
  6.9 0.0 copy-start
  6.9 0.0 copy-start.1
  6.9 0.0 copy-start.2
  6.9 0.0 copy-start.3
  6.9 3.4 %prepare_points.1 = (s32[384,128]{1,0:T(8,128)S(1)}, f32[384,128]{1,0:T(8,128)S(1)}, f32[384,128]{1,0:T(8,128)S(1)}, f32[384,128]{1,0:T(8,128)S(1)}, s32[640,128...) custom-call(s32[64]{0:T(128)} %bitcast.1, s32[128,1024]{1,0:T(8,128)S(1)} %get-tuple-element.22.ids_ref, ...), custom_call_target="tpu_custom_call" | custom-call | flops 2621440 | bytes 5767168 | tf_op jit(solution)/shard_map/prepare_points/pallas_call | solution.py:228
  10.4 0.0 collective-permute-done.2.girth_a
  10.4 0.0 collective-permute-done.3.girth_b
  10.4 0.0 collective-permute-done.stream_a
  10.4 0.0 collective-permute-done.1.stream_b
  10.4 0.0 copy-done
  10.4 0.0 copy-done.1
  10.4 0.0 copy-done.2
  10.5 0.0 copy-done.3
  10.5 4.3 %section_and_disk.1 = (f32[3,4,8,256]{3,2,1,0:T(8,128)}, f32[4,8,256]{2,1,0:T(8,128)}, f32[4,8,256]{2,1,0:T(8,128)}, f32[64,768]{1,0:T(8,128)S(1)}, f32[64,768]{1,0:T(8,128)S(1)}) custom-call(s32[1]{0:T(128)} %get-tuple-element.24.count_ref, f32[3,4,8,256]{3,2,1,0:T(8,128)S(1)} %copy-done, f32[4,8,256]{2,1,0:T(8,128)S(1)} %copy-done.1, ...), custom_call_target="tpu_custom_call" | custom-call | tf_op jit(solution)/shard_map/section_and_disk/pallas_call | solution.py:555
  14.8 5.5 %collective-permute-start.4 = (f32[64,768]{1,0:T(8,128)S(1)}, f32[64,768]{1,0:T(8,128)S(1)}, u32[]{:S(2)}, u32[]{:S(2)}) collective-permute-start(f32[64,768]{1,0:T(8,128)S(1)} %get-tuple-element.39), channel_id=1, source_target_pairs={{0,1},{1,0},{2,3},{3,2},{4,5},{5,4},{6,7},{7,6},{8,9},{9,8},{10,11... | collective-permute-start | bytes 589832 | tf_op jit(solution)/shard_map/ppermute | solution.py:601
  20.2 1.1 %collective-permute-done.4 = f32[64,768]{1,0:T(8,128)S(1)} collective-permute-done((f32[64,768]{1,0:T(8,128)S(1)}, f32[64,768]{1,0:T(8,128)S(1)}, u32[]{:S(2)}, u32[]{:S(2)}) %collective-permute-start.4) | collective-permute-done | bytes 196640 | tf_op jit(solution)/shard_map/ppermute | solution.py:601
  21.3 0.1 reshape.11
  21.4 15.7 %all_to_all.5 = f32[16,4,768]{2,1,0:T(4,128)S(1)} all-to-all(f32[16,4,768]{2,1,0:T(4,128)S(1)} %reshape.11), channel_id=1, replica_groups={{0,2,4,6,8,10,12,14,16,18,20,22,24,26,28,30},{1,3,5,7,9,11,13,15,17,19,..., dimensions={0} | all-to-all | bytes 393216 | tf_op jit(solution)/shard_map/all_to_all | solution.py:627
  37.1 0.6 %reduce_sum.9 = f32[4,768]{1,0:T(4,128)} reduce(f32[16,4,768]{2,1,0:T(4,128)S(1)} %all_to_all.5, f32[]{:T(128)} %constant.1.clone.1), dimensions={0}, to_apply=%region_0.0 | reduce | flops 46080 | bytes 208900 | tf_op jit(solution)/shard_map/reduce_sum | solution.py:635
  (1 shorter events, 0.0 us)
Async XLA Ops:
  2.4 8.0 %collective-permute-start = (f32[6,2,8,256]{3,2,1,0:T(8,128)S(1)}, f32[6,2,8,256]{3,2,1,0:T(8,128)S(1)}, u32[]{:S(2)}, u32[]{:S(2)}) collective-permute-start(f32[6,2,8,256]{3,2,1,0:T(8,128)S(1)} %get-tuple-element.25), channel_id=1, source_target_pairs={{0,8},{8,0},{16,24},{24,16},{1,9},{9,1},{17,25},{25,17},{2,10},{10... | collective-permute-start | bytes 294920 | tf_op jit(solution)/shard_map/ppermute | solution.py:601
  5.5 5.0 %collective-permute-start.1 = (f32[6,2,8,256]{3,2,1,0:T(8,128)S(1)}, f32[6,2,8,256]{3,2,1,0:T(8,128)S(1)}, u32[]{:S(2)}, u32[]{:S(2)}) collective-permute-start(f32[6,2,8,256]{3,2,1,0:T(8,128)S(1)} %get-tuple-element.26), channel_id=1, source_target_pairs={{8,16},{16,8},{9,17},{17,9},{10,18},{18,10},{11,19},{19,11},{12,20... | collective-permute-start | bytes 294920 | tf_op jit(solution)/shard_map/ppermute | solution.py:601
  6.1 4.3 %collective-permute-start.2 = (f32[6,4,2,256]{3,2,1,0:T(2,128)S(1)}, f32[6,4,2,256]{3,2,1,0:T(2,128)S(1)}, u32[]{:S(2)}, u32[]{:S(2)}) collective-permute-start(f32[6,4,2,256]{3,2,1,0:T(2,128)S(1)} %get-tuple-element.27), channel_id=1, source_target_pairs={{0,1},{1,0},{2,3},{3,2},{4,5},{5,4},{6,7},{7,6},{8,9},{9,8},{10,11... | collective-permute-start | bytes 147464 | tf_op jit(solution)/shard_map/ppermute | solution.py:601
  6.2 4.2 %collective-permute-start.3 = (f32[6,4,2,256]{3,2,1,0:T(2,128)S(1)}, f32[6,4,2,256]{3,2,1,0:T(2,128)S(1)}, u32[]{:S(2)}, u32[]{:S(2)}) collective-permute-start(f32[6,4,2,256]{3,2,1,0:T(2,128)S(1)} %get-tuple-element.28), channel_id=1, source_target_pairs={{1,2},{2,1},{3,4},{4,3},{5,6},{6,5},{9,10},{10,9},{11,12},{12,11},... | collective-permute-start | bytes 147464 | tf_op jit(solution)/shard_map/ppermute | solution.py:601
  6.9 3.5 %copy-start = (f32[3,4,8,256]{3,2,1,0:T(8,128)S(1)}, f32[3,4,8,256]{3,2,1,0:T(8,128)}, u32[]{:S(2)}) copy-start(f32[3,4,8,256]{3,2,1,0:T(8,128)} %vel_ref.1) | copy-start | bytes 294916
  6.9 3.5 %copy-start.1 = (f32[4,8,256]{2,1,0:T(8,128)S(1)}, f32[4,8,256]{2,1,0:T(8,128)}, u32[]{:S(2)}) copy-start(f32[4,8,256]{2,1,0:T(8,128)} %p_ref.1) | copy-start | bytes 98308
  6.9 3.5 %copy-start.2 = (f32[4,8,256]{2,1,0:T(8,128)S(1)}, f32[4,8,256]{2,1,0:T(8,128)}, u32[]{:S(2)}) copy-start(f32[4,8,256]{2,1,0:T(8,128)} %k_ref.1) | copy-start | bytes 98308
  6.9 3.5 %copy-start.3 = (f32[4,8,256]{2,1,0:T(8,128)S(1)}, f32[4,8,256]{2,1,0:T(8,128)}, u32[]{:S(2)}) copy-start(f32[4,8,256]{2,1,0:T(8,128)} %w_ref.1) | copy-start | bytes 98308
  14.8 6.5 %collective-permute-start.4 = (f32[64,768]{1,0:T(8,128)S(1)}, f32[64,768]{1,0:T(8,128)S(1)}, u32[]{:S(2)}, u32[]{:S(2)}) collective-permute-start(f32[64,768]{1,0:T(8,128)S(1)} %get-tuple-element.39), channel_id=1, source_target_pairs={{0,1},{1,0},{2,3},{3,2},{4,5},{5,4},{6,7},{7,6},{8,9},{9,8},{10,11... | collective-permute-start | bytes 589832 | tf_op jit(solution)/shard_map/ppermute | solution.py:601

commit v15 on v14

--- a/solution.py
+++ b/solution.py
@@ -31,9 +31,9 @@
 
 
 def pack_kernel(vel_hbm, p_hbm, k_hbm, w_hbm, ids_hbm, frac_hbm, *rest):
-    *slabs, ids_ref, frac_ref, fields, arrived = rest
+    *slabs, ids_ref, first_ref, fields, arrived = rest
     moves = [(vel_hbm, fields.at[0:3]), (p_hbm, fields.at[3]), (k_hbm, fields.at[4])]
-    moves += [(w_hbm, fields.at[5]), (ids_hbm, ids_ref), (frac_hbm, frac_ref)]
+    moves += [(w_hbm, fields.at[5]), (ids_hbm, ids_ref), (frac_hbm.at[0], first_ref)]
     copies = [
         pltpu.make_async_copy(source, target, arrived.at[i])
         for i, (source, target) in enumerate(moves)
@@ -60,7 +60,7 @@
     _, cells_s, cells_g, cells_r = velocity.shape
     stream = pltpu.VMEM((6, 2, cells_g, cells_r), jnp.float32)
     girth = pltpu.VMEM((6, cells_s, 2, cells_r), jnp.float32)
-    points = [pltpu.VMEM(x.shape, x.dtype) for x in (corner_ids, fractions)]
+    points = [pltpu.VMEM(corner_ids.shape, x.dtype) for x in (corner_ids, fractions)]
     inputs = (velocity, pressure, energy, rate, corner_ids, fractions)
     return pl.pallas_call(
         pack_kernel,
@@ -97,7 +97,8 @@
     cells_r,
     owner_ref,
     ids_ref,
-    frac_ref,
+    first_ref,
+    frac_hbm,
     table_hbm,
     q_ref,
     fr_ref,
@@ -106,6 +107,8 @@
     moves_ref,
     chosen_ref,
     count_ref,
+    frac_ref,
+    table_ref,
     turned,
     picked,
     keys,
@@ -115,6 +118,13 @@
     order,
     arrived,
 ):
+    copies = [
+        pltpu.make_async_copy(frac_hbm.at[1], frac_ref.at[0], arrived.at[0]),
+        pltpu.make_async_copy(frac_hbm.at[2], frac_ref.at[1], arrived.at[1]),
+        pltpu.make_async_copy(table_hbm, table_ref, arrived.at[2]),
+    ]
+    for copy in copies:
+        copy.start()
     stream_first = lax.axis_index("stream") * cells_s
     me = lax.axis_index("girth")
     sectors = owner_ref.shape[0]
@@ -125,35 +135,31 @@
     passes = network(rows)
     valid = 1 << SHIFT - 1
 
-    for place in range(rows // width):
-        order[place] = 0
-
     def listed(number, count):
         order[jnp.minimum(count, rows // width)] = number
         return count + (owner_ref[number] == me).astype(jnp.int32)
 
     owned = lax.fori_loop(0, sectors, listed, jnp.int32(0), unroll=8)
-    for place in range(rows // width):
-        source = pl.ds(pl.multiple_of(order[place] * width, width), width)
-        pltpu.make_async_copy(
-            table_hbm.at[source, :], chosen_ref.at[pl.ds(place * width, width), :], arrived.at[0]
-        ).start()
-
     for d in range(4):
         picked[d] = jnp.full(picked.shape[1:], -1.0 if d == 0 else 0.0, jnp.float32)
+    chosen_ref[...] = jnp.zeros_like(chosen_ref)
     beyond = pl.ds(rows, pad)
     for slot in range(2):
         keys[slot, beyond, :] = jnp.zeros((pad, LANES), jnp.int32)
     moves_ref[0:pad, :] = jnp.zeros((pad, LANES), jnp.int32)
+    planes = (ids_ref, first_ref, frac_ref.at[0], frac_ref.at[1])
     for d in range(4):
+        if d >= 2:
+            copies[d - 2].wait()
         for at in range(0, azimuths, LANES):
             cols = pl.ds(at, LANES)
-            plane = ids_ref[:, cols].astype(jnp.float32) if d == 0 else frac_ref[d - 1, :, cols]
-            turned[d, cols, :] = plane.T
+            turned[d, cols, :] = planes[d][:, cols].astype(jnp.float32).T
+    copies[2].wait()
 
     def sector(place, carry):
         source = pl.ds(pl.multiple_of(order[place] * width, width), width)
         target = pl.ds(pl.multiple_of(place * width, width), width)
+        chosen_ref[target, :] = table_ref[source, :]
         for d in range(4):
             picked[d, target, :] = turned[d, source, :]
         return carry
@@ -211,10 +217,9 @@
                 frs[b, here, :] = out[0]
                 xss[b, here, :] = out[1]
                 xgs[b, here, :] = out[2]
-    pltpu.make_async_copy(table_hbm.at[pl.ds(0, rows), :], chosen_ref, arrived.at[0]).wait()
-
-
-def prepare(owners, corner_ids, fractions, table, cells, girth_count):
+
+
+def prepare(owners, corner_ids, first, fractions, table, cells, girth_count):
     cells_s, cells_g, cells_r = cells
     radii, azimuths = corner_ids.shape
     sectors = owners.shape[0]
@@ -236,22 +241,24 @@
             shape((rows, 2 * NH), jnp.float32),
             shape((1,), jnp.int32),
         ),
-        in_specs=[smem, vmem, vmem, hbm],
+        in_specs=[smem, vmem, vmem, hbm, hbm],
         out_specs=[vmem] * 6 + [smem],
         scratch_shapes=[
+            pltpu.VMEM((2, radii, azimuths), jnp.float32),
+            pltpu.VMEM(table.shape, jnp.float32),
             pltpu.VMEM((4, azimuths, radii), jnp.float32),
             pltpu.VMEM((4, rows, radii), jnp.float32),
             pltpu.VMEM((2, rows + pad, radii), jnp.int32),
         ]
         + [pltpu.VMEM((2, rows + pad, radii), jnp.float32)] * 3
         + [pltpu.SMEM((rows // (azimuths // sectors) + 1,), jnp.int32)]
-        + [pltpu.SemaphoreType.DMA((1,))],
+        + [pltpu.SemaphoreType.DMA((3,))],
         compiler_params=pltpu.CompilerParams(vmem_limit_bytes=VMEM_LIMIT),
         cost_estimate=pl.CostEstimate(
             flops=20 * radii * azimuths, bytes_accessed=44 * radii * azimuths, transcendentals=0
         ),
         name="prepare_points",
-    )(in_hbm(owners), corner_ids, fractions, in_hbm(table))
+    )(in_hbm(owners), corner_ids, first, in_hbm(fractions), in_hbm(table))
 
 
 def radial(values, amount, fill):
@@ -600,7 +607,7 @@
             pairs += [(i, i + 1), (i + 1, i)]
         return lax.ppermute(values, axis, pairs)
 
-    *slabs, ids, fracs = pack(
+    *slabs, ids, first = pack(
         velocity, pressure, kinetic_energy, dissipation_rate, corner_ids, fractions
     )
     girth_halos = (
@@ -615,7 +622,8 @@
     points = prepare(
         sector_owner[:, 0],
         ids,
-        fracs,
+        first,
+        fractions,
         fourier_table(azimuths, NH),
         (cells_s, cells_g, cells_r),
         girth_count,

time: 38.1 us -> 37.2 us (0.976)
  starting transfers between devices: 9.94 us -> 4.55 us
  Pallas kernels: 9.5 us -> 12.4 us
  blocking collectives: 15.7 us -> 16.6 us
    ppermute x5, starting transfers between devices: 9.94 us -> 4.55 us  [swap(): return lax.ppermute(values, axis, pairs)]
    pallas_call x1, Pallas kernels: 4.31 us -> 7.22 us  [section(): pl.pallas_call(functools.partial(section_kernel, devices), out_shape=(sha...]
    all_to_all x1, blocking collectives: 15.7 us -> 16.6 us  [body(): lax.all_to_all(total.reshape(devices // 2, radii // devices, 6 * NH), ('s...]
    pallas_call x1, Pallas kernels: 3.45 us -> 3.84 us  [prepare(): pl.pallas_call(functools.partial(prepare_kernel, cells_s, cells_g, cells_...]
  transfers between devices with their start and end apart: 5 -> 5, of which waited for: 1 -> 1; matrix products, arithmetic and copies ran while one was open for 0% -> 0% of each run, Pallas kernels for 9% -> 10%
where the time goes in v15:
time: 37.2 us; the launch traced here: 36.6 us
  blocking collectives  16.6 us (45%)
  Pallas kernels  12.4 us (33%)
  starting transfers between devices  4.55 us (12%)
  waiting for transfers between devices  1.44 us (4%)
  between operations  0.79 us (2%)
  other arithmetic  0.68 us (2%)
    all_to_all x1, blocking collectives, body(): lax.all_to_all(total.reshape(devices // 2, radii // devices, 6 * NH), ('s...  16.6 us
    pallas_call x1, Pallas kernels, section(): pl.pallas_call(functools.partial(section_kernel, devices), out_shape=(sha...  7.22 us
    ppermute x5, starting transfers between devices, swap(): return lax.ppermute(values, axis, pairs)  4.55 us
    pallas_call x1, Pallas kernels, prepare(): pl.pallas_call(functools.partial(prepare_kernel, cells_s, cells_g, cells_...  3.84 us
    ppermute x5, waiting for transfers between devices, swap(): return lax.ppermute(values, axis, pairs)  1.44 us
    pallas_call x1, Pallas kernels, pack(): pl.pallas_call(pack_kernel, out_shape=[stream, stream, girth, girth] + po...  1.37 us
  transfers between devices with their start and end apart: 5, of which 1 were waited for; matrix products, arithmetic and copies ran while one was open for 0% of the time, Pallas kernels for 10%

profile of v15, /device:TPU:0, one launch (start us, length us, event | category | flops | bytes accessed | tf_op | source)
XLA Modules:
  0.0 36.6 jit_solution(4798901815260666086)
XLA Ops:
  0.6 1.4 %pack_halos.1 = (f32[6,2,8,256]{3,2,1,0:T(8,128)S(1)}, f32[6,2,8,256]{3,2,1,0:T(8,128)S(1)}, f32[6,4,2,256]{3,2,1,0:T(2,128)S(1)}, f32[6,4,2,256]{3,2,1,0:T(2,12...) custom-call(f32[3,4,8,256]{3,2,1,0:T(8,128)} %vel_ref.1, f32[4,8,256]{2,1,0:T(8,128)} %p_ref.1, ...), custom_call_target="tpu_custom_call" | custom-call | tf_op jit(solution)/shard_map/pack_halos/pallas_call | solution.py:65
  2.0 3.1 %collective-permute-start = (f32[6,2,8,256]{3,2,1,0:T(8,128)S(1)}, f32[6,2,8,256]{3,2,1,0:T(8,128)S(1)}, u32[]{:S(2)}, u32[]{:S(2)}) collective-permute-start(f32[6,2,8,256]{3,2,1,0:T(8,128)S(1)} %get-tuple-element.25), channel_id=1, source_target_pairs={{0,8},{8,0},{16,24},{24,16},{1,9},{9,1},{17,25},{25,17},{2,10},{10... | collective-permute-start | bytes 294920 | tf_op jit(solution)/shard_map/ppermute | solution.py:608
  5.1 0.7 %collective-permute-start.1 = (f32[6,2,8,256]{3,2,1,0:T(8,128)S(1)}, f32[6,2,8,256]{3,2,1,0:T(8,128)S(1)}, u32[]{:S(2)}, u32[]{:S(2)}) collective-permute-start(f32[6,2,8,256]{3,2,1,0:T(8,128)S(1)} %get-tuple-element.26), channel_id=1, source_target_pairs={{8,16},{16,8},{9,17},{17,9},{10,18},{18,10},{11,19},{19,11},{12,20... | collective-permute-start | bytes 294920 | tf_op jit(solution)/shard_map/ppermute | solution.py:608
  5.8 0.1 collective-permute-start.2
  5.8 0.7 %collective-permute-start.3 = (f32[6,4,2,256]{3,2,1,0:T(2,128)S(1)}, f32[6,4,2,256]{3,2,1,0:T(2,128)S(1)}, u32[]{:S(2)}, u32[]{:S(2)}) collective-permute-start(f32[6,4,2,256]{3,2,1,0:T(2,128)S(1)} %get-tuple-element.28), channel_id=1, source_target_pairs={{1,2},{2,1},{3,4},{4,3},{5,6},{6,5},{9,10},{10,9},{11,12},{12,11},... | collective-permute-start | bytes 147464 | tf_op jit(solution)/shard_map/ppermute | solution.py:608
  6.5 0.0 copy-start
  6.5 0.0 copy-start.1
  6.5 0.0 copy-start.2
  6.6 0.0 copy-start.3
  6.6 3.8 %prepare_points.1 = (s32[384,128]{1,0:T(8,128)S(1)}, f32[384,128]{1,0:T(8,128)S(1)}, f32[384,128]{1,0:T(8,128)S(1)}, f32[384,128]{1,0:T(8,128)S(1)}, s32[640,128...) custom-call(s32[64]{0:T(128)} %bitcast.1, s32[128,1024]{1,0:T(8,128)S(1)} %get-tuple-element.22.ids_ref, ...), custom_call_target="tpu_custom_call" | custom-call | flops 2621440 | bytes 5767168 | tf_op jit(solution)/shard_map/prepare_points/pallas_call | solution.py:233
  10.4 0.0 collective-permute-done.2.girth_a
  10.4 0.0 collective-permute-done.3.girth_b
  10.4 0.0 collective-permute-done.stream_a
  10.4 0.0 collective-permute-done.1.stream_b
  10.5 0.0 copy-done
  10.5 0.0 copy-done.1
  10.5 0.0 copy-done.2
  10.5 0.0 copy-done.3
  10.5 7.2 %section_and_disk.1 = (f32[3,4,8,256]{3,2,1,0:T(8,128)}, f32[4,8,256]{2,1,0:T(8,128)}, f32[4,8,256]{2,1,0:T(8,128)}, f32[64,768]{1,0:T(8,128)S(1)}, f32[64,768]{1,0:T(8,128)S(1)}) custom-call(s32[1]{0:T(128)} %get-tuple-element.24.count_ref, f32[3,4,8,256]{3,2,1,0:T(8,128)S(1)} %copy-done, f32[4,8,256]{2,1,0:T(8,128)S(1)} %copy-done.1, ...), custom_call_target="tpu_custom_call" | custom-call | tf_op jit(solution)/shard_map/section_and_disk/pallas_call | solution.py:562
  17.7 0.1 collective-permute-start.4
  17.8 1.4 %collective-permute-done.4 = f32[64,768]{1,0:T(8,128)S(1)} collective-permute-done((f32[64,768]{1,0:T(8,128)S(1)}, f32[64,768]{1,0:T(8,128)S(1)}, u32[]{:S(2)}, u32[]{:S(2)}) %collective-permute-start.4) | collective-permute-done | bytes 196640 | tf_op jit(solution)/shard_map/ppermute | solution.py:608
  19.3 0.1 reshape.11
  19.3 16.6 %all_to_all.5 = f32[16,4,768]{2,1,0:T(4,128)S(1)} all-to-all(f32[16,4,768]{2,1,0:T(4,128)S(1)} %reshape.11), channel_id=1, replica_groups={{0,2,4,6,8,10,12,14,16,18,20,22,24,26,28,30},{1,3,5,7,9,11,13,15,17,19,..., dimensions={0} | all-to-all | bytes 393216 | tf_op jit(solution)/shard_map/all_to_all | solution.py:635
  36.0 0.6 %reduce_sum.9 = f32[4,768]{1,0:T(4,128)} reduce(f32[16,4,768]{2,1,0:T(4,128)S(1)} %all_to_all.5, f32[]{:T(128)} %constant.1.clone.1), dimensions={0}, to_apply=%region_0.0 | reduce | flops 46080 | bytes 208900 | tf_op jit(solution)/shard_map/reduce_sum | solution.py:643
  (1 shorter events, 0.0 us)
Async XLA Ops:
  2.0 8.4 %collective-permute-start = (f32[6,2,8,256]{3,2,1,0:T(8,128)S(1)}, f32[6,2,8,256]{3,2,1,0:T(8,128)S(1)}, u32[]{:S(2)}, u32[]{:S(2)}) collective-permute-start(f32[6,2,8,256]{3,2,1,0:T(8,128)S(1)} %get-tuple-element.25), channel_id=1, source_target_pairs={{0,8},{8,0},{16,24},{24,16},{1,9},{9,1},{17,25},{25,17},{2,10},{10... | collective-permute-start | bytes 294920 | tf_op jit(solution)/shard_map/ppermute | solution.py:608
  5.1 5.3 %collective-permute-start.1 = (f32[6,2,8,256]{3,2,1,0:T(8,128)S(1)}, f32[6,2,8,256]{3,2,1,0:T(8,128)S(1)}, u32[]{:S(2)}, u32[]{:S(2)}) collective-permute-start(f32[6,2,8,256]{3,2,1,0:T(8,128)S(1)} %get-tuple-element.26), channel_id=1, source_target_pairs={{8,16},{16,8},{9,17},{17,9},{10,18},{18,10},{11,19},{19,11},{12,20... | collective-permute-start | bytes 294920 | tf_op jit(solution)/shard_map/ppermute | solution.py:608
  5.8 4.7 %collective-permute-start.2 = (f32[6,4,2,256]{3,2,1,0:T(2,128)S(1)}, f32[6,4,2,256]{3,2,1,0:T(2,128)S(1)}, u32[]{:S(2)}, u32[]{:S(2)}) collective-permute-start(f32[6,4,2,256]{3,2,1,0:T(2,128)S(1)} %get-tuple-element.27), channel_id=1, source_target_pairs={{0,1},{1,0},{2,3},{3,2},{4,5},{5,4},{6,7},{7,6},{8,9},{9,8},{10,11... | collective-permute-start | bytes 147464 | tf_op jit(solution)/shard_map/ppermute | solution.py:608
  5.8 4.6 %collective-permute-start.3 = (f32[6,4,2,256]{3,2,1,0:T(2,128)S(1)}, f32[6,4,2,256]{3,2,1,0:T(2,128)S(1)}, u32[]{:S(2)}, u32[]{:S(2)}) collective-permute-start(f32[6,4,2,256]{3,2,1,0:T(2,128)S(1)} %get-tuple-element.28), channel_id=1, source_target_pairs={{1,2},{2,1},{3,4},{4,3},{5,6},{6,5},{9,10},{10,9},{11,12},{12,11},... | collective-permute-start | bytes 147464 | tf_op jit(solution)/shard_map/ppermute | solution.py:608
  6.5 3.9 %copy-start = (f32[3,4,8,256]{3,2,1,0:T(8,128)S(1)}, f32[3,4,8,256]{3,2,1,0:T(8,128)}, u32[]{:S(2)}) copy-start(f32[3,4,8,256]{3,2,1,0:T(8,128)} %vel_ref.1) | copy-start | bytes 294916
  6.5 3.9 %copy-start.1 = (f32[4,8,256]{2,1,0:T(8,128)S(1)}, f32[4,8,256]{2,1,0:T(8,128)}, u32[]{:S(2)}) copy-start(f32[4,8,256]{2,1,0:T(8,128)} %p_ref.1) | copy-start | bytes 98308
  6.5 3.9 %copy-start.2 = (f32[4,8,256]{2,1,0:T(8,128)S(1)}, f32[4,8,256]{2,1,0:T(8,128)}, u32[]{:S(2)}) copy-start(f32[4,8,256]{2,1,0:T(8,128)} %k_ref.1) | copy-start | bytes 98308
  6.6 3.9 %copy-start.3 = (f32[4,8,256]{2,1,0:T(8,128)S(1)}, f32[4,8,256]{2,1,0:T(8,128)}, u32[]{:S(2)}) copy-start(f32[4,8,256]{2,1,0:T(8,128)} %w_ref.1) | copy-start | bytes 98308
  17.7 1.5 %collective-permute-start.4 = (f32[64,768]{1,0:T(8,128)S(1)}, f32[64,768]{1,0:T(8,128)S(1)}, u32[]{:S(2)}, u32[]{:S(2)}) collective-permute-start(f32[64,768]{1,0:T(8,128)S(1)} %get-tuple-element.39), channel_id=1, source_target_pairs={{0,1},{1,0},{2,3},{3,2},{4,5},{5,4},{6,7},{7,6},{8,9},{9,8},{10,11... | collective-permute-start | bytes 589832 | tf_op jit(solution)/shard_map/ppermute | solution.py:608

commit v16 on v15

--- a/solution.py
+++ b/solution.py
@@ -361,6 +361,7 @@
 
 def section_kernel(
     devices,
+    girth_count,
     count_ref,
     vel_ref,
     p_ref,
@@ -543,15 +544,18 @@
         harm_ref[:, c * 2 * NH : (c + 1) * 2 * NH] = waves[c * radii : (c + 1) * radii]
     block = radii // devices
     for place in range(devices // 2):
-        even = harm_ref[2 * place * block : (2 * place + 1) * block, :]
-        odd = harm_ref[(2 * place + 1) * block : (2 * place + 2) * block, :]
-        keep_ref[place * block : (place + 1) * block, :] = jnp.where(girth_odd, odd, even)
-        give_ref[place * block : (place + 1) * block, :] = jnp.where(girth_odd, even, odd)
+        second, rest = divmod(place, devices // 4)
+        stream, high = divmod(rest, girth_count // 4)
+        at = (stream * girth_count + 4 * high + 2 * second) * block
+        even, odd = harm_ref[at : at + block, :], harm_ref[at + block : at + 2 * block, :]
+        target = slice(place * block, (place + 1) * block)
+        keep_ref[target, :] = jnp.where(girth_odd, odd, even)
+        give_ref[target, :] = jnp.where(girth_odd, even, odd)
     for copy in copies:
         copy.wait()
 
 
-def section(velocity, pressure, energy, rate, halos, points, devices):
+def section(velocity, pressure, energy, rate, halos, points, devices, girth_count):
     _, cells_s, cells_g, cells_r = velocity.shape
     *lists, moves, chosen, counts = points
     rows, radii = lists[0].shape
@@ -560,7 +564,7 @@
     vmem = pl.BlockSpec(memory_space=pltpu.VMEM)
     smem = pl.BlockSpec(memory_space=pltpu.SMEM)
     return pl.pallas_call(
-        functools.partial(section_kernel, devices),
+        functools.partial(section_kernel, devices, girth_count),
         out_shape=(
             shape(velocity.shape),
             shape(energy.shape),
@@ -629,16 +633,21 @@
         girth_count,
     )
     new_velocity, new_energy, new_rate, keep, give = section(
-        velocity, pressure, kinetic_energy, dissipation_rate, halos, points, devices
+        velocity, pressure, kinetic_energy, dissipation_rate, halos, points, devices, girth_count
     )
     total = keep + swap(give, "girth", girth_count, 0)
+    half = radii // 4
+    second = lax.axis_index("girth") // 2 % 2
+    give = lax.dynamic_slice_in_dim(total, (1 - second) * half, half, axis=0)
+    keep = lax.dynamic_slice_in_dim(total, second * half, half, axis=0)
+    total = keep + lax.ppermute(give, "girth", [(i, i ^ 2) for i in range(girth_count)])
     shares = lax.all_to_all(
-        total.reshape(devices // 2, radii // devices, 6 * NH),
+        total.reshape(devices // 4, radii // devices, 6 * NH),
         ("stream", "girth"),
         split_axis=0,
         concat_axis=0,
         tiled=True,
-        axis_index_groups=[list(range(parity, devices, 2)) for parity in (0, 1)],
+        axis_index_groups=[list(range(part, devices, 4)) for part in range(4)],
     )
     return new_velocity, new_energy, new_rate, jnp.sum(shares, axis=0)
 

time: 37.2 us -> 41.9 us (1.13)
  starting transfers between devices: 4.55 us -> 8.98 us
  waiting for transfers between devices: 1.44 us -> 5.68 us
  Pallas kernels: 12.4 us -> 8.89 us
    ppermute x0 -> x1, waiting for transfers between devices: none -> 4.6 us  [body(): lax.ppermute(give, 'girth', [(i, i ^ 2) for i in range(girth_count)])]
    ppermute x5, starting transfers between devices: 4.55 us -> 8.44 us  [swap(): return lax.ppermute(values, axis, pairs)]
    pallas_call x1, Pallas kernels: 7.22 us -> 3.85 us  [section(): pl.pallas_call(functools.partial(section_kernel, devices, girth_count), o...]
    ppermute x0 -> x1, starting transfers between devices: none -> 0.54 us  [body(): lax.ppermute(give, 'girth', [(i, i ^ 2) for i in range(girth_count)])]
  transfers between devices with their start and end apart: 5 -> 6, of which waited for: 1 -> 2; matrix products, arithmetic and copies ran while one was open for 0% -> 0% of each run, Pallas kernels for 10% -> 9%
where the time goes in v16:
time: 41.9 us; the launch traced here: 41.6 us
  blocking collectives  16.5 us (39%)
  starting transfers between devices  8.98 us (21%)
  Pallas kernels  8.89 us (21%)
  waiting for transfers between devices  5.68 us (14%)
  between operations  0.8 us (2%)
  other arithmetic  0.66 us (2%)
    all_to_all x1, blocking collectives, body(): lax.all_to_all(total.reshape(devices // 4, radii // devices, 6 * NH), ('s...  16.5 us
    ppermute x5, starting transfers between devices, swap(): return lax.ppermute(values, axis, pairs)  8.44 us
    ppermute x1, waiting for transfers between devices, body(): lax.ppermute(give, 'girth', [(i, i ^ 2) for i in range(girth_count)])  4.6 us
    pallas_call x1, Pallas kernels, section(): pl.pallas_call(functools.partial(section_kernel, devices, girth_count), o...  3.85 us
    pallas_call x1, Pallas kernels, prepare(): pl.pallas_call(functools.partial(prepare_kernel, cells_s, cells_g, cells_...  3.67 us
    pallas_call x1, Pallas kernels, pack(): pl.pallas_call(pack_kernel, out_shape=[stream, stream, girth, girth] + po...  1.37 us
    ppermute x5, waiting for transfers between devices, swap(): return lax.ppermute(values, axis, pairs)  1.08 us
  transfers between devices with their start and end apart: 6, of which 2 were waited for; matrix products, arithmetic and copies ran while one was open for 0% of the time, Pallas kernels for 9%

profile of v16, /device:TPU:0, one launch (start us, length us, event | category | flops | bytes accessed | tf_op | source)
XLA Modules:
  0.0 41.6 jit_solution(4743937443809986667)
XLA Ops:
  0.6 1.4 %pack_halos.1 = (f32[6,2,8,256]{3,2,1,0:T(8,128)S(1)}, f32[6,2,8,256]{3,2,1,0:T(8,128)S(1)}, f32[6,4,2,256]{3,2,1,0:T(2,128)S(1)}, f32[6,4,2,256]{3,2,1,0:T(2,12...) custom-call(f32[3,4,8,256]{3,2,1,0:T(8,128)} %vel_ref.1, f32[4,8,256]{2,1,0:T(8,128)} %p_ref.1, ...), custom_call_target="tpu_custom_call" | custom-call | tf_op jit(solution)/shard_map/pack_halos/pallas_call | solution.py:65
  2.0 3.1 %collective-permute-start = (f32[6,2,8,256]{3,2,1,0:T(8,128)S(1)}, f32[6,2,8,256]{3,2,1,0:T(8,128)S(1)}, u32[]{:S(2)}, u32[]{:S(2)}) collective-permute-start(f32[6,2,8,256]{3,2,1,0:T(8,128)S(1)} %get-tuple-element.25), channel_id=1, source_target_pairs={{0,8},{8,0},{16,24},{24,16},{1,9},{9,1},{17,25},{25,17},{2,10},{10... | collective-permute-start | bytes 294920 | tf_op jit(solution)/shard_map/ppermute | solution.py:612
  5.1 0.7 %collective-permute-start.1 = (f32[6,2,8,256]{3,2,1,0:T(8,128)S(1)}, f32[6,2,8,256]{3,2,1,0:T(8,128)S(1)}, u32[]{:S(2)}, u32[]{:S(2)}) collective-permute-start(f32[6,2,8,256]{3,2,1,0:T(8,128)S(1)} %get-tuple-element.26), channel_id=1, source_target_pairs={{8,16},{16,8},{9,17},{17,9},{10,18},{18,10},{11,19},{19,11},{12,20... | collective-permute-start | bytes 294920 | tf_op jit(solution)/shard_map/ppermute | solution.py:612
  5.8 0.1 collective-permute-start.2
  5.8 0.7 %collective-permute-start.3 = (f32[6,4,2,256]{3,2,1,0:T(2,128)S(1)}, f32[6,4,2,256]{3,2,1,0:T(2,128)S(1)}, u32[]{:S(2)}, u32[]{:S(2)}) collective-permute-start(f32[6,4,2,256]{3,2,1,0:T(2,128)S(1)} %get-tuple-element.28), channel_id=1, source_target_pairs={{1,2},{2,1},{3,4},{4,3},{5,6},{6,5},{9,10},{10,9},{11,12},{12,11},... | collective-permute-start | bytes 147464 | tf_op jit(solution)/shard_map/ppermute | solution.py:612
  6.5 0.0 copy-start
  6.5 0.0 copy-start.1
  6.5 0.0 copy-start.2
  6.6 0.0 copy-start.3
  6.6 3.7 %prepare_points.1 = (s32[384,128]{1,0:T(8,128)S(1)}, f32[384,128]{1,0:T(8,128)S(1)}, f32[384,128]{1,0:T(8,128)S(1)}, f32[384,128]{1,0:T(8,128)S(1)}, s32[640,128...) custom-call(s32[64]{0:T(128)} %bitcast.1, s32[128,1024]{1,0:T(8,128)S(1)} %get-tuple-element.22.ids_ref, ...), custom_call_target="tpu_custom_call" | custom-call | flops 2621440 | bytes 5767168 | tf_op jit(solution)/shard_map/prepare_points/pallas_call | solution.py:233
  10.2 0.0 collective-permute-done.2.girth_a
  10.3 0.0 collective-permute-done.3.girth_b
  10.3 0.0 collective-permute-done.stream_a
  10.3 0.0 collective-permute-done.1.stream_b
  10.3 0.0 copy-done
  10.3 0.0 copy-done.1
  10.3 0.0 copy-done.2
  10.3 0.0 copy-done.3
  10.3 3.8 %section_and_disk.1 = (f32[3,4,8,256]{3,2,1,0:T(8,128)}, f32[4,8,256]{2,1,0:T(8,128)}, f32[4,8,256]{2,1,0:T(8,128)}, f32[64,768]{1,0:T(8,128)S(1)}, f32[64,768]{1,0:T(8,128)S(1)}) custom-call(s32[1]{0:T(128)} %get-tuple-element.24.count_ref, f32[3,4,8,256]{3,2,1,0:T(8,128)S(1)} %copy-done, f32[4,8,256]{2,1,0:T(8,128)S(1)} %copy-done.1, ...), custom_call_target="tpu_custom_call" | custom-call | tf_op jit(solution)/shard_map/section_and_disk/pallas_call | solution.py:566
  14.2 4.0 %collective-permute-start.4 = (f32[64,768]{1,0:T(8,128)S(1)}, f32[64,768]{1,0:T(8,128)S(1)}, u32[]{:S(2)}, u32[]{:S(2)}) collective-permute-start(f32[64,768]{1,0:T(8,128)S(1)} %get-tuple-element.39), channel_id=1, source_target_pairs={{0,1},{1,0},{2,3},{3,2},{4,5},{5,4},{6,7},{7,6},{8,9},{9,8},{10,11... | collective-permute-start | bytes 589832 | tf_op jit(solution)/shard_map/ppermute | solution.py:612
  18.1 1.1 %collective-permute-done.4 = f32[64,768]{1,0:T(8,128)S(1)} collective-permute-done((f32[64,768]{1,0:T(8,128)S(1)}, f32[64,768]{1,0:T(8,128)S(1)}, u32[]{:S(2)}, u32[]{:S(2)}) %collective-permute-start.4) | collective-permute-done | bytes 196640 | tf_op jit(solution)/shard_map/ppermute | solution.py:612
  19.3 0.5 %collective-permute-start.5 = (f32[32,768]{1,0:T(8,128)S(1)}, f32[32,768]{1,0:T(8,128)S(1)}, u32[]{:S(2)}, u32[]{:S(2)}) collective-permute-start(f32[32,768]{1,0:T(8,128)S(1)} %constant_dynamic-slice_fusion), channel_id=1, source_target_pairs={{0,2},{1,3},{2,0},{3,1},{4,6},{5,7},{6,4},{7,5},{8,10},{9,11},{10,... | collective-permute-start | bytes 294920 | tf_op jit(solution)/shard_map/ppermute | solution.py:643
  19.8 4.6 %collective-permute-done.5 = f32[32,768]{1,0:T(8,128)S(1)} collective-permute-done((f32[32,768]{1,0:T(8,128)S(1)}, f32[32,768]{1,0:T(8,128)S(1)}, u32[]{:S(2)}, u32[]{:S(2)}) %collective-permute-start.5) | collective-permute-done | bytes 98336 | tf_op jit(solution)/shard_map/ppermute | solution.py:643
  24.4 16.5 %all_to_all.5 = f32[8,4,768]{2,1,0:T(4,128)S(1)} all-to-all(f32[8,4,768]{2,1,0:T(4,128)S(1)} %reshape.11), channel_id=1, replica_groups={{0,4,8,12,16,20,24,28},{1,5,9,13,17,21,25,29},{2,6,10,14,18,22,26,30},{..., dimensions={0} | all-to-all | bytes 196608 | tf_op jit(solution)/shard_map/all_to_all | solution.py:644
  41.0 0.6 %reduce_sum.9 = f32[4,768]{1,0:T(4,128)} reduce(f32[8,4,768]{2,1,0:T(4,128)S(1)} %all_to_all.5, f32[]{:T(128)} %constant.37.clone.1), dimensions={0}, to_apply=%region_0.1 | reduce | flops 21504 | bytes 110596 | tf_op jit(solution)/shard_map/reduce_sum | solution.py:652
  (4 shorter events, 0.1 us)
Async XLA Ops:
  2.0 8.3 %collective-permute-start = (f32[6,2,8,256]{3,2,1,0:T(8,128)S(1)}, f32[6,2,8,256]{3,2,1,0:T(8,128)S(1)}, u32[]{:S(2)}, u32[]{:S(2)}) collective-permute-start(f32[6,2,8,256]{3,2,1,0:T(8,128)S(1)} %get-tuple-element.25), channel_id=1, source_target_pairs={{0,8},{8,0},{16,24},{24,16},{1,9},{9,1},{17,25},{25,17},{2,10},{10... | collective-permute-start | bytes 294920 | tf_op jit(solution)/shard_map/ppermute | solution.py:612
  5.1 5.2 %collective-permute-start.1 = (f32[6,2,8,256]{3,2,1,0:T(8,128)S(1)}, f32[6,2,8,256]{3,2,1,0:T(8,128)S(1)}, u32[]{:S(2)}, u32[]{:S(2)}) collective-permute-start(f32[6,2,8,256]{3,2,1,0:T(8,128)S(1)} %get-tuple-element.26), channel_id=1, source_target_pairs={{8,16},{16,8},{9,17},{17,9},{10,18},{18,10},{11,19},{19,11},{12,20... | collective-permute-start | bytes 294920 | tf_op jit(solution)/shard_map/ppermute | solution.py:612
  5.8 4.5 %collective-permute-start.2 = (f32[6,4,2,256]{3,2,1,0:T(2,128)S(1)}, f32[6,4,2,256]{3,2,1,0:T(2,128)S(1)}, u32[]{:S(2)}, u32[]{:S(2)}) collective-permute-start(f32[6,4,2,256]{3,2,1,0:T(2,128)S(1)} %get-tuple-element.27), channel_id=1, source_target_pairs={{0,1},{1,0},{2,3},{3,2},{4,5},{5,4},{6,7},{7,6},{8,9},{9,8},{10,11... | collective-permute-start | bytes 147464 | tf_op jit(solution)/shard_map/ppermute | solution.py:612
  5.8 4.4 %collective-permute-start.3 = (f32[6,4,2,256]{3,2,1,0:T(2,128)S(1)}, f32[6,4,2,256]{3,2,1,0:T(2,128)S(1)}, u32[]{:S(2)}, u32[]{:S(2)}) collective-permute-start(f32[6,4,2,256]{3,2,1,0:T(2,128)S(1)} %get-tuple-element.28), channel_id=1, source_target_pairs={{1,2},{2,1},{3,4},{4,3},{5,6},{6,5},{9,10},{10,9},{11,12},{12,11},... | collective-permute-start | bytes 147464 | tf_op jit(solution)/shard_map/ppermute | solution.py:612
  6.5 3.8 %copy-start = (f32[3,4,8,256]{3,2,1,0:T(8,128)S(1)}, f32[3,4,8,256]{3,2,1,0:T(8,128)}, u32[]{:S(2)}) copy-start(f32[3,4,8,256]{3,2,1,0:T(8,128)} %vel_ref.1) | copy-start | bytes 294916
  6.5 3.8 %copy-start.1 = (f32[4,8,256]{2,1,0:T(8,128)S(1)}, f32[4,8,256]{2,1,0:T(8,128)}, u32[]{:S(2)}) copy-start(f32[4,8,256]{2,1,0:T(8,128)} %p_ref.1) | copy-start | bytes 98308
  6.5 3.8 %copy-start.2 = (f32[4,8,256]{2,1,0:T(8,128)S(1)}, f32[4,8,256]{2,1,0:T(8,128)}, u32[]{:S(2)}) copy-start(f32[4,8,256]{2,1,0:T(8,128)} %k_ref.1) | copy-start | bytes 98308
  6.6 3.8 %copy-start.3 = (f32[4,8,256]{2,1,0:T(8,128)S(1)}, f32[4,8,256]{2,1,0:T(8,128)}, u32[]{:S(2)}) copy-start(f32[4,8,256]{2,1,0:T(8,128)} %w_ref.1) | copy-start | bytes 98308
  14.2 5.0 %collective-permute-start.4 = (f32[64,768]{1,0:T(8,128)S(1)}, f32[64,768]{1,0:T(8,128)S(1)}, u32[]{:S(2)}, u32[]{:S(2)}) collective-permute-start(f32[64,768]{1,0:T(8,128)S(1)} %get-tuple-element.39), channel_id=1, source_target_pairs={{0,1},{1,0},{2,3},{3,2},{4,5},{5,4},{6,7},{7,6},{8,9},{9,8},{10,11... | collective-permute-start | bytes 589832 | tf_op jit(solution)/shard_map/ppermute | solution.py:612
  19.3 5.1 %collective-permute-start.5 = (f32[32,768]{1,0:T(8,128)S(1)}, f32[32,768]{1,0:T(8,128)S(1)}, u32[]{:S(2)}, u32[]{:S(2)}) collective-permute-start(f32[32,768]{1,0:T(8,128)S(1)} %constant_dynamic-slice_fusion), channel_id=1, source_target_pairs={{0,2},{1,3},{2,0},{3,1},{4,6},{5,7},{6,4},{7,5},{8,10},{9,11},{10,... | collective-permute-start | bytes 294920 | tf_op jit(solution)/shard_map/ppermute | solution.py:643

commit v17 on v15

--- a/solution.py
+++ b/solution.py
@@ -135,14 +135,15 @@
     passes = network(rows)
     valid = 1 << SHIFT - 1
 
+    places = rows // width
+    for place in range(places):
+        order[place] = 0
+
     def listed(number, count):
-        order[jnp.minimum(count, rows // width)] = number
+        order[jnp.minimum(count, places)] = number
         return count + (owner_ref[number] == me).astype(jnp.int32)
 
     owned = lax.fori_loop(0, sectors, listed, jnp.int32(0), unroll=8)
-    for d in range(4):
-        picked[d] = jnp.full(picked.shape[1:], -1.0 if d == 0 else 0.0, jnp.float32)
-    chosen_ref[...] = jnp.zeros_like(chosen_ref)
     beyond = pl.ds(rows, pad)
     for slot in range(2):
         keys[slot, beyond, :] = jnp.zeros((pad, LANES), jnp.int32)
@@ -156,15 +157,13 @@
             turned[d, cols, :] = planes[d][:, cols].astype(jnp.float32).T
     copies[2].wait()
 
-    def sector(place, carry):
+    for place in range(places):
         source = pl.ds(pl.multiple_of(order[place] * width, width), width)
-        target = pl.ds(pl.multiple_of(place * width, width), width)
+        target = pl.ds(place * width, width)
         chosen_ref[target, :] = table_ref[source, :]
-        for d in range(4):
+        picked[0, target, :] = jnp.where(place < owned, turned[0, source, :], -1.0)
+        for d in range(1, 4):
             picked[d, target, :] = turned[d, source, :]
-        return carry
-
-    lax.fori_loop(0, owned, sector, jnp.int32(0))
 
     held = pl.ds(0, rows)
     ids = picked[0].astype(jnp.int32)

time: 37.2 us -> 38 us (1.022); the launches traced: 36.6 us -> 38.5 us
  Pallas kernels: 12.4 us -> 9.36 us
  blocking collectives: 16.6 us -> 19.6 us
  starting transfers between devices: 4.55 us -> 6.91 us
    all_to_all x1, blocking collectives: 16.6 us -> 19.6 us  [body(): lax.all_to_all(total.reshape(devices // 2, radii // devices, 6 * NH), ('s...]
    pallas_call x1, Pallas kernels: 7.22 us -> 4.33 us  [section(): pl.pallas_call(functools.partial(section_kernel, devices), out_shape=(sha...]
    ppermute x5, starting transfers between devices: 4.55 us -> 6.91 us  [swap(): return lax.ppermute(values, axis, pairs)]
  transfers between devices with their start and end apart: 5 -> 5, of which waited for: 1 -> 1; matrix products, arithmetic and copies ran while one was open for 0% -> 0% of each run, Pallas kernels for 10% -> 9%
where the time goes in v17:
time: 38 us; the launch traced here: 38.5 us
  blocking collectives  19.6 us (52%)
  Pallas kernels  9.36 us (25%)
  starting transfers between devices  6.91 us (18%)
  waiting for transfers between devices  1.08 us (3%)
  between operations  0.78 us (2%)
  other arithmetic  0.68 us (2%)
    all_to_all x1, blocking collectives, body(): lax.all_to_all(total.reshape(devices // 2, radii // devices, 6 * NH), ('s...  19.6 us
    ppermute x5, starting transfers between devices, swap(): return lax.ppermute(values, axis, pairs)  6.91 us
    pallas_call x1, Pallas kernels, section(): pl.pallas_call(functools.partial(section_kernel, devices), out_shape=(sha...  4.33 us
    pallas_call x1, Pallas kernels, prepare(): pl.pallas_call(functools.partial(prepare_kernel, cells_s, cells_g, cells_...  3.66 us
    pallas_call x1, Pallas kernels, pack(): pl.pallas_call(pack_kernel, out_shape=[stream, stream, girth, girth] + po...  1.37 us
    ppermute x5, waiting for transfers between devices, swap(): return lax.ppermute(values, axis, pairs)  1.08 us
  transfers between devices with their start and end apart: 5, of which 1 were waited for; matrix products, arithmetic and copies ran while one was open for 0% of the time, Pallas kernels for 9%

profile of v17, /device:TPU:0, one launch (start us, length us, event | category | flops | bytes accessed | tf_op | source)
XLA Modules:
  0.0 38.5 jit_solution(2219855339488774769)
XLA Ops:
  0.6 1.4 %pack_halos.1 = (f32[6,2,8,256]{3,2,1,0:T(8,128)S(1)}, f32[6,2,8,256]{3,2,1,0:T(8,128)S(1)}, f32[6,4,2,256]{3,2,1,0:T(2,128)S(1)}, f32[6,4,2,256]{3,2,1,0:T(2,12...) custom-call(f32[3,4,8,256]{3,2,1,0:T(8,128)} %vel_ref.1, f32[4,8,256]{2,1,0:T(8,128)} %p_ref.1, ...), custom_call_target="tpu_custom_call" | custom-call | tf_op jit(solution)/shard_map/pack_halos/pallas_call | solution.py:65
  2.0 3.1 %collective-permute-start = (f32[6,2,8,256]{3,2,1,0:T(8,128)S(1)}, f32[6,2,8,256]{3,2,1,0:T(8,128)S(1)}, u32[]{:S(2)}, u32[]{:S(2)}) collective-permute-start(f32[6,2,8,256]{3,2,1,0:T(8,128)S(1)} %get-tuple-element.25), channel_id=1, source_target_pairs={{0,8},{8,0},{16,24},{24,16},{1,9},{9,1},{17,25},{25,17},{2,10},{10... | collective-permute-start | bytes 294920 | tf_op jit(solution)/shard_map/ppermute | solution.py:607
  5.1 0.7 %collective-permute-start.1 = (f32[6,2,8,256]{3,2,1,0:T(8,128)S(1)}, f32[6,2,8,256]{3,2,1,0:T(8,128)S(1)}, u32[]{:S(2)}, u32[]{:S(2)}) collective-permute-start(f32[6,2,8,256]{3,2,1,0:T(8,128)S(1)} %get-tuple-element.26), channel_id=1, source_target_pairs={{8,16},{16,8},{9,17},{17,9},{10,18},{18,10},{11,19},{19,11},{12,20... | collective-permute-start | bytes 294920 | tf_op jit(solution)/shard_map/ppermute | solution.py:607
  5.8 0.1 collective-permute-start.2
  5.8 0.7 %collective-permute-start.3 = (f32[6,4,2,256]{3,2,1,0:T(2,128)S(1)}, f32[6,4,2,256]{3,2,1,0:T(2,128)S(1)}, u32[]{:S(2)}, u32[]{:S(2)}) collective-permute-start(f32[6,4,2,256]{3,2,1,0:T(2,128)S(1)} %get-tuple-element.28), channel_id=1, source_target_pairs={{1,2},{2,1},{3,4},{4,3},{5,6},{6,5},{9,10},{10,9},{11,12},{12,11},... | collective-permute-start | bytes 147464 | tf_op jit(solution)/shard_map/ppermute | solution.py:607
  6.5 0.0 copy-start
  6.5 0.0 copy-start.1
  6.5 0.0 copy-start.2
  6.6 0.0 copy-start.3
  6.6 3.7 %prepare_points.1 = (s32[384,128]{1,0:T(8,128)S(1)}, f32[384,128]{1,0:T(8,128)S(1)}, f32[384,128]{1,0:T(8,128)S(1)}, f32[384,128]{1,0:T(8,128)S(1)}, s32[640,128...) custom-call(s32[64]{0:T(128)} %bitcast.1, s32[128,1024]{1,0:T(8,128)S(1)} %get-tuple-element.22.ids_ref, ...), custom_call_target="tpu_custom_call" | custom-call | flops 2621440 | bytes 5767168 | tf_op jit(solution)/shard_map/prepare_points/pallas_call | solution.py:232
  10.2 0.0 collective-permute-done.2.girth_a
  10.2 0.0 collective-permute-done.3.girth_b
  10.2 0.0 collective-permute-done.stream_a
  10.3 0.0 collective-permute-done.1.stream_b
  10.3 0.0 copy-done
  10.3 0.0 copy-done.1
  10.3 0.0 copy-done.2
  10.3 0.0 copy-done.3
  10.3 4.3 %section_and_disk.1 = (f32[3,4,8,256]{3,2,1,0:T(8,128)}, f32[4,8,256]{2,1,0:T(8,128)}, f32[4,8,256]{2,1,0:T(8,128)}, f32[64,768]{1,0:T(8,128)S(1)}, f32[64,768]{1,0:T(8,128)S(1)}) custom-call(s32[1]{0:T(128)} %get-tuple-element.24.count_ref, f32[3,4,8,256]{3,2,1,0:T(8,128)S(1)} %copy-done, f32[4,8,256]{2,1,0:T(8,128)S(1)} %copy-done.1, ...), custom_call_target="tpu_custom_call" | custom-call | tf_op jit(solution)/shard_map/section_and_disk/pallas_call | solution.py:561
  14.6 2.4 %collective-permute-start.4 = (f32[64,768]{1,0:T(8,128)S(1)}, f32[64,768]{1,0:T(8,128)S(1)}, u32[]{:S(2)}, u32[]{:S(2)}) collective-permute-start(f32[64,768]{1,0:T(8,128)S(1)} %get-tuple-element.39), channel_id=1, source_target_pairs={{0,1},{1,0},{2,3},{3,2},{4,5},{5,4},{6,7},{7,6},{8,9},{9,8},{10,11... | collective-permute-start | bytes 589832 | tf_op jit(solution)/shard_map/ppermute | solution.py:607
  17.1 1.1 %collective-permute-done.4 = f32[64,768]{1,0:T(8,128)S(1)} collective-permute-done((f32[64,768]{1,0:T(8,128)S(1)}, f32[64,768]{1,0:T(8,128)S(1)}, u32[]{:S(2)}, u32[]{:S(2)}) %collective-permute-start.4) | collective-permute-done | bytes 196640 | tf_op jit(solution)/shard_map/ppermute | solution.py:607
  18.2 0.1 reshape.11
  18.2 19.6 %all_to_all.5 = f32[16,4,768]{2,1,0:T(4,128)S(1)} all-to-all(f32[16,4,768]{2,1,0:T(4,128)S(1)} %reshape.11), channel_id=1, replica_groups={{0,2,4,6,8,10,12,14,16,18,20,22,24,26,28,30},{1,3,5,7,9,11,13,15,17,19,..., dimensions={0} | all-to-all | bytes 393216 | tf_op jit(solution)/shard_map/all_to_all | solution.py:634
  37.9 0.6 %reduce_sum.9 = f32[4,768]{1,0:T(4,128)} reduce(f32[16,4,768]{2,1,0:T(4,128)S(1)} %all_to_all.5, f32[]{:T(128)} %constant.1.clone.1), dimensions={0}, to_apply=%region_0.0 | reduce | flops 46080 | bytes 208900 | tf_op jit(solution)/shard_map/reduce_sum | solution.py:642
  (1 shorter events, 0.0 us)
Async XLA Ops:
  2.0 8.2 %collective-permute-start = (f32[6,2,8,256]{3,2,1,0:T(8,128)S(1)}, f32[6,2,8,256]{3,2,1,0:T(8,128)S(1)}, u32[]{:S(2)}, u32[]{:S(2)}) collective-permute-start(f32[6,2,8,256]{3,2,1,0:T(8,128)S(1)} %get-tuple-element.25), channel_id=1, source_target_pairs={{0,8},{8,0},{16,24},{24,16},{1,9},{9,1},{17,25},{25,17},{2,10},{10... | collective-permute-start | bytes 294920 | tf_op jit(solution)/shard_map/ppermute | solution.py:607
  5.1 5.2 %collective-permute-start.1 = (f32[6,2,8,256]{3,2,1,0:T(8,128)S(1)}, f32[6,2,8,256]{3,2,1,0:T(8,128)S(1)}, u32[]{:S(2)}, u32[]{:S(2)}) collective-permute-start(f32[6,2,8,256]{3,2,1,0:T(8,128)S(1)} %get-tuple-element.26), channel_id=1, source_target_pairs={{8,16},{16,8},{9,17},{17,9},{10,18},{18,10},{11,19},{19,11},{12,20... | collective-permute-start | bytes 294920 | tf_op jit(solution)/shard_map/ppermute | solution.py:607
  5.8 4.5 %collective-permute-start.2 = (f32[6,4,2,256]{3,2,1,0:T(2,128)S(1)}, f32[6,4,2,256]{3,2,1,0:T(2,128)S(1)}, u32[]{:S(2)}, u32[]{:S(2)}) collective-permute-start(f32[6,4,2,256]{3,2,1,0:T(2,128)S(1)} %get-tuple-element.27), channel_id=1, source_target_pairs={{0,1},{1,0},{2,3},{3,2},{4,5},{5,4},{6,7},{7,6},{8,9},{9,8},{10,11... | collective-permute-start | bytes 147464 | tf_op jit(solution)/shard_map/ppermute | solution.py:607
  5.8 4.4 %collective-permute-start.3 = (f32[6,4,2,256]{3,2,1,0:T(2,128)S(1)}, f32[6,4,2,256]{3,2,1,0:T(2,128)S(1)}, u32[]{:S(2)}, u32[]{:S(2)}) collective-permute-start(f32[6,4,2,256]{3,2,1,0:T(2,128)S(1)} %get-tuple-element.28), channel_id=1, source_target_pairs={{1,2},{2,1},{3,4},{4,3},{5,6},{6,5},{9,10},{10,9},{11,12},{12,11},... | collective-permute-start | bytes 147464 | tf_op jit(solution)/shard_map/ppermute | solution.py:607
  6.5 3.8 %copy-start = (f32[3,4,8,256]{3,2,1,0:T(8,128)S(1)}, f32[3,4,8,256]{3,2,1,0:T(8,128)}, u32[]{:S(2)}) copy-start(f32[3,4,8,256]{3,2,1,0:T(8,128)} %vel_ref.1) | copy-start | bytes 294916
  6.5 3.8 %copy-start.1 = (f32[4,8,256]{2,1,0:T(8,128)S(1)}, f32[4,8,256]{2,1,0:T(8,128)}, u32[]{:S(2)}) copy-start(f32[4,8,256]{2,1,0:T(8,128)} %p_ref.1) | copy-start | bytes 98308
  6.5 3.8 %copy-start.2 = (f32[4,8,256]{2,1,0:T(8,128)S(1)}, f32[4,8,256]{2,1,0:T(8,128)}, u32[]{:S(2)}) copy-start(f32[4,8,256]{2,1,0:T(8,128)} %k_ref.1) | copy-start | bytes 98308
  6.6 3.8 %copy-start.3 = (f32[4,8,256]{2,1,0:T(8,128)S(1)}, f32[4,8,256]{2,1,0:T(8,128)}, u32[]{:S(2)}) copy-start(f32[4,8,256]{2,1,0:T(8,128)} %w_ref.1) | copy-start | bytes 98308
  14.6 3.5 %collective-permute-start.4 = (f32[64,768]{1,0:T(8,128)S(1)}, f32[64,768]{1,0:T(8,128)S(1)}, u32[]{:S(2)}, u32[]{:S(2)}) collective-permute-start(f32[64,768]{1,0:T(8,128)S(1)} %get-tuple-element.39), channel_id=1, source_target_pairs={{0,1},{1,0},{2,3},{3,2},{4,5},{5,4},{6,7},{7,6},{8,9},{9,8},{10,11... | collective-permute-start | bytes 589832 | tf_op jit(solution)/shard_map/ppermute | solution.py:607
